TPU v7x, 32 devices: a whole 2x2x4 slice. The times are simulated.
32 devices in a mesh: rx: 4 (over x, core), ry: 8 (over z, y).
Axes of the slice: x: 2, y: 2, z: 4, core: 2. Of those that a mesh axis runs over, the one named last changes fastest.
Arguments:
- column_features: bfloat16 [4096, 1536], P(('rx', 'ry')), may hold values from -6 to 6
- column_route: int32 [4096], P(('rx', 'ry')), may hold values from 0 to 8191, as said below
- cotangent: bfloat16 [64, 128, 1536], P('rx', 'ry'), may hold values from -6 to 6
- first_weight: bfloat16 [27, 96, 96], replicated, may hold values from -0.125 to 0.125
- second_weight: bfloat16 [27, 96, 96], replicated, may hold values from -0.125 to 0.125
Outputs:
- block_output: bfloat16 [64, 128, 1536], P('rx', 'ry')
- feature_grads: bfloat16 [4096, 1536], P(('rx', 'ry'))
- first_grad: float32 [27, 96, 96], replicated
- second_grad: float32 [27, 96, 96], replicated
Inputs may be any that keep to these rules, and one draw needn't show every extreme that they name: `column_route`: entries are distinct; entry o * 256 + q names slot q of owner o, owner o = i * 8 + j being the device at rx index i and ry index j. The columns of one owner are spread over the devices' shards as evenly as possible: each shard holds the floor or the ceiling of that owner's count / 32. An owner holds at most 256 columns, and in every draw one owner holds exactly 256, so that it receives 8 from every shard.
All inputs are finite; a program needn't handle non-finite values.
Results may differ from a plain program's by a relative error of at most 0.0029.
Values may be sent and summed in bfloat16 or wider, within the bound.
No kernel may reach another device: no remote copies, remote signals or barrier semaphores. Data moves between devices by JAX's collectives and lax.ppermute only.
A program may use at most 256 MiB of HBM per device.

v0:
```python
import jax
import jax.numpy as jnp
from jax import lax
from jax.sharding import PartitionSpec as P


def extended(block, sides, width):
    for axis, dim in sides:
        count = lax.axis_size(axis)
        forward = [(i, i + 1) for i in range(count - 1)]
        backward = [(target, source) for source, target in forward]
        low = lax.ppermute(
            lax.slice_in_dim(block, block.shape[dim] - width, None, axis=dim), axis, forward
        )
        high = lax.ppermute(lax.slice_in_dim(block, 0, width, axis=dim), axis, backward)
        block = jnp.concatenate([low, block, high], axis=dim)
    return block


def pad_depth(widened, channels):
    shaped = widened.reshape(
        widened.shape[0], widened.shape[1], widened.shape[2] // channels, channels
    )
    return jnp.pad(shaped, ((0, 0), (0, 0), (1, 1), (0, 0)))


def face_field(rows, channels):
    widened = extended(rows, (("rx", 0), ("ry", 1)), 1)
    return pad_depth(widened, channels)


def conv_sum(padded, weights):
    size_x = padded.shape[0] - 2
    size_y = padded.shape[1] - 2
    size_z = padded.shape[2] - 2
    result = jnp.zeros((size_x, size_y, size_z, weights.shape[1]), jnp.float32)
    for a in range(3):
        for b in range(3):
            for c in range(3):
                piece = padded[a : a + size_x, b : b + size_y, c : c + size_z, :]
                result = result + jnp.einsum(
                    "xyzi,oi->xyzo",
                    piece,
                    weights[9 * a + 3 * b + c],
                    preferred_element_type=jnp.float32,
                )
    return result


def correlate(grads, padded):
    size_x, size_y, size_z, _ = grads.shape
    terms = []
    for a in range(3):
        for b in range(3):
            for c in range(3):
                piece = padded[a : a + size_x, b : b + size_y, c : c + size_z, :]
                terms.append(
                    jnp.einsum("xyzo,xyzi->oi", grads, piece, preferred_element_type=jnp.float32)
                )
    return jnp.stack(terms, axis=0)


def flipped(weights):
    return jnp.transpose(weights[::-1], (0, 2, 1))


def on_device(column_features, column_route, cotangent, first_weight, second_weight):
    count_x = lax.axis_size("rx")
    count_y = lax.axis_size("ry")
    count_all = count_x * count_y
    shard_rows = column_features.shape[0]
    row_width = column_features.shape[1]
    region_x = cotangent.shape[0]
    region_y = cotangent.shape[1]
    channels = first_weight.shape[1]
    depth = row_width // channels
    region_slots = region_x * region_y
    capacity = 2 * shard_rows // count_all
    owners = column_route // region_slots
    slot_ids = column_route % region_slots
    shard_index = jnp.arange(shard_rows, dtype=jnp.int32)
    earlier = shard_index[:, None] > shard_index[None, :]
    same_owner = owners[:, None] == owners[None, :]
    ranks = jnp.sum(jnp.logical_and(earlier, same_owner).astype(jnp.int32), axis=1)
    send_pos = owners * capacity + ranks
    buffer_index = jnp.arange(count_all * capacity, dtype=jnp.int32)
    send_hot = send_pos[:, None] == buffer_index[None, :]
    send_table = send_hot.astype(jnp.bfloat16)
    outgoing = jnp.einsum(
        "sr,sw->rw", send_table, column_features, preferred_element_type=jnp.float32
    ).astype(jnp.bfloat16)
    filled = jnp.sum(send_hot.astype(jnp.int32), axis=0)
    slot_total = jnp.sum(jnp.where(send_hot, slot_ids[:, None], 0), axis=0)
    out_slots = jnp.where(filled > 0, slot_total, region_slots)
    incoming, in_slots = (
        lax.all_to_all(
            outgoing.reshape(count_all, capacity, row_width),
            ("rx", "ry"),
            split_axis=0,
            concat_axis=0,
            tiled=True,
        ),
        lax.all_to_all(
            out_slots.reshape(count_all, capacity),
            ("rx", "ry"),
            split_axis=0,
            concat_axis=0,
            tiled=True,
        ),
    )
    incoming = incoming.reshape(count_all * capacity, row_width)
    in_slots = in_slots.reshape(count_all * capacity)
    slot_hot = in_slots[:, None] == jnp.arange(region_slots, dtype=jnp.int32)[None, :]
    slot_table = slot_hot.astype(jnp.bfloat16)
    region_rows = jnp.einsum(
        "rs,rw->sw", slot_table, incoming, preferred_element_type=jnp.float32
    ).astype(jnp.bfloat16)
    active = jnp.sum(slot_hot.astype(jnp.float32), axis=0)
    field = jnp.transpose(region_rows.reshape(region_x, region_y, channels, depth), (0, 1, 3, 2))
    mask = active.reshape(region_x, region_y, 1, 1)
    cot_field = jnp.transpose(
        cotangent.reshape(region_x, region_y, channels, depth), (0, 1, 3, 2)
    ).astype(jnp.float32)
    outer_grad = (mask * cot_field).astype(jnp.bfloat16)
    field_flat = field.reshape(region_x, region_y, row_width)
    outer_flat = outer_grad.reshape(region_x, region_y, row_width)
    padded_x = pad_depth(extended(field_flat, (("rx", 0), ("ry", 1)), 1), channels)
    padded_g = pad_depth(extended(outer_flat, (("rx", 0), ("ry", 1)), 1), channels)
    hidden = mask * conv_sum(padded_x, first_weight)
    act = jax.nn.silu(hidden).astype(jnp.bfloat16)
    padded_a = face_field(act.reshape(region_x, region_y, row_width), channels)
    second = conv_sum(padded_a, second_weight)
    summed = (field.astype(jnp.float32) + mask * second).astype(jnp.bfloat16)
    block_output = jnp.transpose(summed, (0, 1, 3, 2)).reshape(region_x, region_y, row_width)
    act_grad = conv_sum(padded_g, flipped(second_weight))
    sigma = jax.nn.sigmoid(hidden)
    hidden_grad = (mask * act_grad * sigma * (1.0 + hidden * (1.0 - sigma))).astype(jnp.bfloat16)
    padded_h = face_field(hidden_grad.reshape(region_x, region_y, row_width), channels)
    grid_grad = (mask * cot_field + conv_sum(padded_h, flipped(first_weight))).astype(jnp.bfloat16)
    grad_rows = jnp.transpose(grid_grad, (0, 1, 3, 2)).reshape(region_slots, row_width)
    backward = jnp.dot(slot_table, grad_rows, preferred_element_type=jnp.float32).astype(
        jnp.bfloat16
    )
    returned = lax.all_to_all(
        backward.reshape(count_all, capacity, row_width),
        ("rx", "ry"),
        split_axis=0,
        concat_axis=0,
        tiled=True,
    )
    returned_rows = returned.reshape(count_all * capacity, row_width)
    feature_grads = jnp.dot(send_table, returned_rows, preferred_element_type=jnp.float32).astype(
        jnp.bfloat16
    )
    second_local = correlate(outer_grad, padded_a)
    first_local = correlate(hidden_grad, padded_x)
    first_total, second_total = lax.psum((first_local, second_local), ("rx", "ry"))
    factor = 1.0 / jnp.sqrt(jnp.float32(count_all * shard_rows * depth))
    return (block_output, feature_grads, first_total * factor, second_total * factor)


def solution(mesh):
    in_specs = (P(("rx", "ry"), None), P(("rx", "ry")), P("rx", "ry", None), P(), P())
    out_specs = (P("rx", "ry", None), P(("rx", "ry"), None), P(), P())
    return jax.shard_map(
        on_device, mesh=mesh, in_specs=in_specs, out_specs=out_specs, check_vma=False
    )
```

profile of v0, /device:TPU:0, one launch (start us, length us, event | category | flops | bytes accessed | tf_op | source)
XLA Modules:
  0.0 637.5 jit_solution(11468231901222669993)
XLA Ops:
  9.0 7.3 %all-to-all-start = ((s32[32,1,8]{2,1,0:T(1,128)}), s32[32,1,8]{2,1,0:T(1,128)S(1)}, u32[]{:S(2)}, u32[]{:S(2)}) async-start(s32[32,1,8]{2,1,0:T(1,128)} %bitcast), calls=%async_computation | async-start | bytes 32768 | tf_op jit(solution)/shard_map/all_to_all | solution.py:103
  19.8 6.9 %reshape.118 = f32[16,16,96,16]{3,2,1,0:T(8,128)} reshape(bf16[16,16,1536]{2,1,0:T(8,128)(2,1)S(1)} %copy-done.16) | data formatting | bytes 2359296 | tf_op jit(solution)/shard_map/convert_element_type | solution.py:123
  26.7 8.4 %copy.37 = f32[16,16,96,16]{2,3,1,0:T(8,128)S(1)} copy(f32[16,16,96,16]{3,2,1,0:T(8,128)} %reshape.118) | data formatting | bytes 3145728 | tf_op jit(solution)/shard_map/convert_element_type | solution.py:123
  35.1 6.0 all-to-all-start.1
  51.3 2.9 collective-permute-done.9
  54.4 3.4 collective-permute-start.10
  61.1 3.3 collective-permute-done.11
  111.6 6.3 reshape.105
  119.9 4.8 collective-permute-start
  126.5 6.0 copy.34
  136.4 4.1 collective-permute-start.2
  144.4 6.1 copy.32
  152.2 2.7 reshape.107
  155.0 2.6 fusion.118
  202.3 20.1 %multiply_convert_fusion.1 = (bf16[16,16,16,96]{3,2,1,0:T(8,128)(2,1)}, f32[16,16,16,96]{3,2,1,0:T(8,128)}) fusion(bf16[27,96,96]{2,1,0:T(8,128)(2,1)} %param.8, bf16[18,18,16,96]{3,2,1,0:T(8,128)(2,1)S(1)} %reshape.107, f32[16,16,16,96]{3,2,1,0:T(8,128)} %fusion.212, f32[16,16,16,96]{3,2,1,0:T(8,128)} %fusion.133, f32[16,16,16,96]{3,2,1,0:T(8,128)} %fusion.132, ...), kind=kOutput, calls=%fused_computation.104 | convolution fusion | flops 88080384 | bytes 57906176 | tf_op jit(solution)/shard_map/xyzi,oi->xyzo/dot_general | solution.py:41
  222.4 20.1 %multiply_convert_fusion = bf16[16,16,16,96]{3,2,1,0:T(8,128)(2,1)} fusion(f32[16,16,16,96]{3,2,1,0:T(8,128)} %get-tuple-element.27, f32[16,16,16,96]{3,2,1,0:T(8,128)} %fusion.166, f32[16,16,16,96]{3,2,1,0:T(8,128)} %fusion.78, f32[16,16,16,96]{3,2,1,0:T(8,128)} %fusion.77, f32[16,16,16,96]{3,2,1,0:T(8,128)} %fusion.167, f32[16,16,16,96]{3,2,1,0:T(8,128)} %fusion.76, ...), kind=kOutput, calls=%fused_computation.103 | convolution fusion | flops 89653248 | bytes 58430464 | tf_op jit(solution)/shard_map/xyzi,oi->xyzo/dot_general | solution.py:41
  246.0 4.3 collective-permute-start.4
  250.5 2.7 collective-permute-start.12
  289.6 4.5 collective-permute-start.6
  295.8 4.6 collective-permute-start.14
  303.5 2.6 fusion.136
  353.7 2.9 reshape.114
  356.6 2.6 fusion.81
  433.0 19.9 %fusion.3 = bf16[16,16,96,16]{2,3,1,0:T(8,128)(2,1)} fusion(f32[16,16,16,96]{3,2,1,0:T(8,128)} %fusion.157, f32[16,16,16,96]{3,2,1,0:T(8,128)} %fusion.96, f32[16,16,16,96]{3,2,1,0:T(8,128)} %fusion.95, f32[16,16,16,96]{3,2,1,0:T(8,128)} %fusion.158, f32[16,16,16,96]{3,2,1,0:T(8,128)} %fusion.94, f32[16,16,16,96]{3,2,1,0:T(8,128)} %fusion.93, ...), kind=kOutput, calls=%fused_computation.80 | convolution fusion | flops 86900736 | bytes 58430464 | tf_op jit(solution)/shard_map/xyzi,oi->xyzo/dot_general | solution.py:41
  452.8 6.0 copy.40
  458.8 11.3 %reshape.115 = bf16[256,1536]{1,0:T(8,128)(2,1)S(1)} reshape(bf16[16,16,96,16]{3,2,1,0:T(8,128)(2,1)} %copy.40) | data formatting | bytes 1572864 | tf_op jit(solution)/shard_map/reshape | solution.py:140
  471.5 9.1 %all-to-all-start.2 = ((bf16[32,8,1536]{2,1,0:T(8,128)(2,1)}), bf16[32,8,1536]{2,1,0:T(8,128)(2,1)S(1)}, u32[]{:S(2)}, u32[]{:S(2)}) async-start(bf16[32,8,1536]{2,1,0:T(8,128)(2,1)} %fusion), calls=%async_computation.2 | async-start | bytes 1572864 | tf_op jit(solution)/shard_map/all_to_all | solution.py:144
  481.3 19.8 %fusion.6 = bf16[16,16,96,16]{2,3,1,0:T(8,128)(2,1)} fusion(f32[16,16,16,96]{3,2,1,0:T(8,128)} %fusion.176, f32[16,16,16,96]{3,2,1,0:T(8,128)} %fusion.151, f32[16,16,16,96]{3,2,1,0:T(8,128)} %fusion.150, f32[16,16,16,96]{3,2,1,0:T(8,128)} %fusion.180, f32[16,16,16,96]{3,2,1,0:T(8,128)} %fusion.149, f32[16,16,16,96]{3,2,1,0:T(8,128)} %fusion.148, ...), kind=kOutput, calls=%fused_computation.93 | convolution fusion | flops 87293952 | bytes 57119744 | tf_op jit(solution)/shard_map/xyzi,oi->xyzo/dot_general | solution.py:41
  501.1 6.0 copy.36
  507.1 11.8 %reshape.110 = bf16[16,16,1536]{2,1,0:T(8,128)(2,1)} reshape(bf16[16,16,96,16]{3,2,1,0:T(8,128)(2,1)} %copy.36) | data formatting | bytes 1572864 | tf_op jit(solution)/shard_map/reshape | solution.py:134
  518.8 106.8 %all-reduce.7.cloned.1.call-done = (f32[27,96,96]{2,1,0:T(8,128)}, f32[27,96,96]{2,1,0:T(8,128)}) async-done(((f32[27,96,96]{2,1,0:T(8,128)}, f32[27,96,96]{2,1,0:T(8,128)}), (f32[27,96,96]{2,1,0:T(8,128)}, f32[27,96,96]{2,1,0:T(8,128)})) %all-reduce.7.cloned.1.call-update) | async-done | bytes 1990672 | tf_op jit(solution)/shard_map/psum | solution.py:157
  625.7 3.5 broadcast_multiply_fusion
  (289 shorter events, 293.0 us)
Async XLA Ops:
  7.2 9.1 %copy-start = (bf16[128,1536]{1,0:T(8,128)(2,1)S(1)}, bf16[128,1536]{1,0:T(8,128)(2,1)}, u32[]{:S(2)}) copy-start(bf16[128,1536]{1,0:T(8,128)(2,1)} %param.5) | copy-start | bytes 1179652
  7.2 12.6 %copy-start.16 = (bf16[16,16,1536]{2,1,0:T(8,128)(2,1)S(1)}, bf16[16,16,1536]{2,1,0:T(8,128)(2,1)}, u32[]{:S(2)}) copy-start(bf16[16,16,1536]{2,1,0:T(8,128)(2,1)} %param.7) | copy-start | bytes 2359300
  8.1 11.7 %copy-start.21 = (s32[128]{0:T(128)}, s32[128]{0:T(128)S(1)}, u32[]{:S(2)}) copy-start(s32[128]{0:T(128)S(1)} %multiply_add_fusion) | copy-start | bytes 1540
  9.0 26.1 %all-to-all-start = ((s32[32,1,8]{2,1,0:T(1,128)}), s32[32,1,8]{2,1,0:T(1,128)S(1)}, u32[]{:S(2)}, u32[]{:S(2)}) async-start(s32[32,1,8]{2,1,0:T(1,128)} %bitcast), calls=%async_computation | async-start | bytes 32768 | tf_op jit(solution)/shard_map/all_to_all | solution.py:103
  35.1 7.8 %copy-start.2 = (f32[16,16,96,16]{2,3,1,0:T(8,128)}, f32[16,16,96,16]{2,3,1,0:T(8,128)S(1)}, u32[]{:S(2)}) copy-start(f32[16,16,96,16]{2,3,1,0:T(8,128)S(1)} %copy.37) | copy-start | bytes 4718596
  35.1 74.8 %all-to-all-start.1 = ((bf16[32,8,1536]{2,1,0:T(8,128)(2,1)}), bf16[32,8,1536]{2,1,0:T(8,128)(2,1)}, u32[]{:S(2)}, u32[]{:S(2)}) async-start(bf16[32,8,1536]{2,1,0:T(8,128)(2,1)} %fusion.1), calls=%async_computation.1 | async-start | bytes 1572864 | tf_op jit(solution)/shard_map/all_to_all | solution.py:96
  42.4 67.5 %copy-start.19 = (s32[256]{0:T(256)}, s32[256]{0:T(256)S(1)}, u32[]{:S(2)}) copy-start(s32[256]{0:T(256)S(1)} %eq.49) | copy-start | bytes 3076
  42.6 4.6 copy-start.17
  42.9 6.8 %copy-start.6 = (bf16[16,16,16,96]{3,2,1,0:T(8,128)(2,1)}, bf16[16,16,16,96]{3,2,1,0:T(8,128)(2,1)S(1)}, u32[]{:S(2)}) copy-start(bf16[16,16,16,96]{3,2,1,0:T(8,128)(2,1)S(1)} %fusion.61) | copy-start | bytes 2359300
  43.1 8.1 %collective-permute-start.8 = (bf16[1,16,1536]{2,1,0:T(8,128)(2,1)S(1)}, bf16[1,16,1536]{2,1,0:T(8,128)(2,1)S(1)}, u32[]{:S(2)}, u32[]{:S(2)}) collective-permute-start(bf16[1,16,1536]{2,1,0:T(8,128)(2,1)S(1)} %slice.931), channel_id=1, source_target_pairs={{0,8},{8,16},{16,24},{1,9},{9,17},{17,25},{2,10},{10,18},{18,26},{... | collective-permute-start | bytes 147464 | tf_op jit(solution)/shard_map/ppermute | solution.py:12
  49.9 4.3 collective-permute-start.9
  54.4 6.7 %collective-permute-start.10 = (bf16[18,1,1536]{2,1,0:T(2,128)(2,1)S(1)}, bf16[18,1,1536]{2,1,0:T(2,128)(2,1)S(1)}, u32[]{:S(2)}, u32[]{:S(2)}) collective-permute-start(bf16[18,1,1536]{2,1,0:T(2,128)(2,1)S(1)} %get-tuple-element.18), channel_id=1, source_target_pairs={{0,1},{1,2},{2,3},{3,4},{4,5},{5,6},{6,7},{8,9},{9,10},{10,11},{11... | collective-permute-start | bytes 165896 | tf_op jit(solution)/shard_map/ppermute | solution.py:12
  57.8 6.6 %collective-permute-start.11 = (bf16[18,1,1536]{2,1,0:T(2,128)(2,1)S(1)}, bf16[18,1,1536]{2,1,0:T(2,128)(2,1)S(1)}, u32[]{:S(2)}, u32[]{:S(2)}) collective-permute-start(bf16[18,1,1536]{2,1,0:T(2,128)(2,1)S(1)} %get-tuple-element.19), channel_id=1, source_target_pairs={{1,0},{2,1},{3,2},{4,3},{5,4},{6,5},{7,6},{9,8},{10,9},{11,10},{12... | collective-permute-start | bytes 165896 | tf_op jit(solution)/shard_map/ppermute | solution.py:15
  119.9 15.4 %collective-permute-start = (bf16[1,16,1536]{2,1,0:T(8,128)(2,1)}, bf16[1,16,1536]{2,1,0:T(8,128)(2,1)}, u32[]{:S(2)}, u32[]{:S(2)}) collective-permute-start(bf16[1,16,1536]{2,1,0:T(8,128)(2,1)} %slice.811), channel_id=1, source_target_pairs={{0,8},{8,16},{16,24},{1,9},{9,17},{17,25},{2,10},{10,18},{18,26},{... | collective-permute-start | bytes 147464 | tf_op jit(solution)/shard_map/ppermute | solution.py:12
  132.8 3.4 collective-permute-start.1
  136.4 14.1 %collective-permute-start.2 = (bf16[18,1,1536]{2,1,0:T(2,128)(2,1)S(1)}, bf16[18,1,1536]{2,1,0:T(2,128)(2,1)S(1)}, u32[]{:S(2)}, u32[]{:S(2)}) collective-permute-start(bf16[18,1,1536]{2,1,0:T(2,128)(2,1)S(1)} %get-tuple-element.22), channel_id=1, source_target_pairs={{0,1},{1,2},{2,3},{3,4},{4,5},{5,6},{6,7},{8,9},{9,10},{10,11},{11... | collective-permute-start | bytes 165896 | tf_op jit(solution)/shard_map/ppermute | solution.py:12
  140.5 10.0 %collective-permute-start.3 = (bf16[18,1,1536]{2,1,0:T(2,128)(2,1)S(1)}, bf16[18,1,1536]{2,1,0:T(2,128)(2,1)S(1)}, u32[]{:S(2)}, u32[]{:S(2)}) collective-permute-start(bf16[18,1,1536]{2,1,0:T(2,128)(2,1)S(1)} %get-tuple-element.23), channel_id=1, source_target_pairs={{1,0},{2,1},{3,2},{4,3},{5,4},{6,5},{7,6},{9,8},{10,9},{11,10},{12... | collective-permute-start | bytes 165896 | tf_op jit(solution)/shard_map/ppermute | solution.py:15
  246.0 43.0 %collective-permute-start.4 = (bf16[1,16,1536]{2,1,0:T(8,128)(2,1)S(1)}, bf16[1,16,1536]{2,1,0:T(8,128)(2,1)S(1)}, u32[]{:S(2)}, u32[]{:S(2)}) collective-permute-start(bf16[1,16,1536]{2,1,0:T(8,128)(2,1)S(1)} %slice.871), channel_id=1, source_target_pairs={{0,8},{8,16},{16,24},{1,9},{9,17},{17,25},{2,10},{10,18},{18,26},{... | collective-permute-start | bytes 147464 | tf_op jit(solution)/shard_map/ppermute | solution.py:12
  250.5 5.0 copy-start.4
  250.5 45.0 %collective-permute-start.12 = (bf16[1,16,1536]{2,1,0:T(8,128)(2,1)S(1)}, bf16[1,16,1536]{2,1,0:T(8,128)(2,1)S(1)}, u32[]{:S(2)}, u32[]{:S(2)}) collective-permute-start(bf16[1,16,1536]{2,1,0:T(8,128)(2,1)S(1)} %slice.991), channel_id=1, source_target_pairs={{0,8},{8,16},{16,24},{1,9},{9,17},{17,25},{2,10},{10,18},{18,26},{... | collective-permute-start | bytes 147464 | tf_op jit(solution)/shard_map/ppermute | solution.py:12
  286.3 3.1 collective-permute-start.5
  287.7 7.8 %collective-permute-start.13 = (bf16[1,16,1536]{2,1,0:T(8,128)(2,1)S(1)}, bf16[1,16,1536]{2,1,0:T(8,128)(2,1)S(1)}, u32[]{:S(2)}, u32[]{:S(2)}) collective-permute-start(bf16[1,16,1536]{2,1,0:T(8,128)(2,1)S(1)} %slice.993), channel_id=1, source_target_pairs={{8,0},{16,8},{24,16},{9,1},{17,9},{25,17},{10,2},{18,10},{26,18},{... | collective-permute-start | bytes 147464 | tf_op jit(solution)/shard_map/ppermute | solution.py:15
  289.6 12.0 %collective-permute-start.6 = (bf16[18,1,1536]{2,1,0:T(2,128)(2,1)S(1)}, bf16[18,1,1536]{2,1,0:T(2,128)(2,1)S(1)}, u32[]{:S(2)}, u32[]{:S(2)}) collective-permute-start(bf16[18,1,1536]{2,1,0:T(2,128)(2,1)S(1)} %get-tuple-element.20), channel_id=1, source_target_pairs={{0,1},{1,2},{2,3},{3,4},{4,5},{5,6},{6,7},{8,9},{9,10},{10,11},{11... | collective-permute-start | bytes 165896 | tf_op jit(solution)/shard_map/ppermute | solution.py:12
  294.2 7.5 %collective-permute-start.7 = (bf16[18,1,1536]{2,1,0:T(2,128)(2,1)S(1)}, bf16[18,1,1536]{2,1,0:T(2,128)(2,1)S(1)}, u32[]{:S(2)}, u32[]{:S(2)}) collective-permute-start(bf16[18,1,1536]{2,1,0:T(2,128)(2,1)S(1)} %get-tuple-element.21), channel_id=1, source_target_pairs={{1,0},{2,1},{3,2},{4,3},{5,4},{6,5},{7,6},{9,8},{10,9},{11,10},{12... | collective-permute-start | bytes 165896 | tf_op jit(solution)/shard_map/ppermute | solution.py:15
  295.6 6.1 copy-start.14
  295.8 56.2 %collective-permute-start.14 = (bf16[18,1,1536]{2,1,0:T(2,128)(2,1)S(1)}, bf16[18,1,1536]{2,1,0:T(2,128)(2,1)S(1)}, u32[]{:S(2)}, u32[]{:S(2)}) collective-permute-start(bf16[18,1,1536]{2,1,0:T(2,128)(2,1)S(1)} %get-tuple-element.16), channel_id=1, source_target_pairs={{0,1},{1,2},{2,3},{3,4},{4,5},{5,6},{6,7},{8,9},{9,10},{10,11},{11... | collective-permute-start | bytes 165896 | tf_op jit(solution)/shard_map/ppermute | solution.py:12
  300.3 51.6 %collective-permute-start.15 = (bf16[18,1,1536]{2,1,0:T(2,128)(2,1)S(1)}, bf16[18,1,1536]{2,1,0:T(2,128)(2,1)S(1)}, u32[]{:S(2)}, u32[]{:S(2)}) collective-permute-start(bf16[18,1,1536]{2,1,0:T(2,128)(2,1)S(1)} %get-tuple-element.17), channel_id=1, source_target_pairs={{1,0},{2,1},{3,2},{4,3},{5,4},{6,5},{7,6},{9,8},{10,9},{11,10},{12... | collective-permute-start | bytes 165896 | tf_op jit(solution)/shard_map/ppermute | solution.py:15
  458.8 11.3 %copy-start.20 = (s32[256]{0:T(256)S(1)}, s32[256]{0:T(256)}, u32[]{:S(2)}) copy-start(s32[256]{0:T(256)} %copy-done.19) | copy-start | bytes 3076
  471.5 9.8 %copy-start.9 = (bf16[16,16,96,16]{2,3,1,0:T(8,128)(2,1)S(1)}, bf16[16,16,96,16]{2,3,1,0:T(8,128)(2,1)}, u32[]{:S(2)}) copy-start(bf16[16,16,96,16]{2,3,1,0:T(8,128)(2,1)} %copy.32) | copy-start | bytes 2359300
  471.5 157.7 %all-to-all-start.2 = ((bf16[32,8,1536]{2,1,0:T(8,128)(2,1)}), bf16[32,8,1536]{2,1,0:T(8,128)(2,1)S(1)}, u32[]{:S(2)}, u32[]{:S(2)}) async-start(bf16[32,8,1536]{2,1,0:T(8,128)(2,1)} %fusion), calls=%async_computation.2 | async-start | bytes 1572864 | tf_op jit(solution)/shard_map/all_to_all | solution.py:144
  480.5 145.1 %all-reduce.7.cloned.1.call-start = ((), (), s32[]{:S(2)}) async-start(), calls=%async_computation.3 | async-start | bytes 5308416 | tf_op jit(solution)/shard_map/psum | solution.py:157
  625.7 4.5 copy-start.1
  (11 other events, 24.8 us)
Sparse Core Ops, SparseCore 0:
  487.6 138.0 all-reduce.6
where the time goes:
time: 644 us; the launch traced here: 638 us
  matrix products  338 us (52%)
  waiting for transfers between devices  115 us (18%)
  local copies, waits for them, and re-layouts  95.3 us (15%)
  starting transfers between devices  63.3 us (10%)
  between operations  15.2 us (2%)
  other arithmetic  10.4 us (2%)
    dot_general x108, matrix products, conv_sum(): jnp.einsum('xyzi,oi->xyzo', piece, weights[9 * a + 3 * b + c], preferred_...  270 us
    psum x1, waiting for transfers between devices, on_device(): lax.psum((first_local, second_local), ('rx', 'ry'))  107 us
    dot_general x54, matrix products, correlate(): jnp.einsum('xyzo,xyzi->oi', grads, piece, preferred_element_type=jnp.floa...  63.1 us
    ppermute x8, starting transfers between devices, extended(): lax.ppermute(lax.slice_in_dim(block, block.shape[dim] - width, None, axis...  30.4 us
    convert_element_type x2, local copies, waits for them, and re-layouts, on_device(): cot_field = jnp.transpose(cotangent.reshape(region_x, region_y, channels,...  15.3 us
  transfers between devices with their start and end apart: 20, of which 5 were waited for; matrix products, arithmetic and copies ran while one was open for 34% of the time, Pallas kernels for 0%

commit v1 on v0

v1 whole, which is shorter than its diff:
```python
import functools

import jax
import jax.numpy as jnp
import numpy as np
from jax import lax
from jax.experimental import pallas as pl
from jax.experimental.pallas import tpu as pltpu
from jax.sharding import PartitionSpec as P

LANES = 128
PAIR = 256
VMEM = 56 * 1024 * 1024
BF = jnp.bfloat16
F32 = jnp.float32


def call(body, out_shape, flops, moved, grid=None, in_specs=None, out_specs=None, scratch=()):
    extra = {}
    if grid is not None:
        extra = dict(grid=grid, in_specs=in_specs, out_specs=out_specs)
    return pl.pallas_call(
        body,
        out_shape=out_shape,
        scratch_shapes=list(scratch),
        compiler_params=pltpu.CompilerParams(vmem_limit_bytes=VMEM),
        cost_estimate=pl.CostEstimate(flops=int(flops), bytes_accessed=int(moved), transcendentals=0),
        **extra,
    )


def dot(left, right):
    return jnp.dot(left, right, preferred_element_type=F32)


def dot_nt(left, right):
    return lax.dot_general(left, right, (((1,), (1,)), ((), ())), preferred_element_type=F32)


def send_kernel(cap, slots, row_ref, col_ref, feat_ref, out_ref):
    rows = feat_ref.shape[0]
    owner_row = row_ref[...] // slots
    owner_col = col_ref[...] // slots
    first = lax.broadcasted_iota(jnp.int32, (rows, rows), 0)
    second = lax.broadcasted_iota(jnp.int32, (rows, rows), 1)
    same = jnp.where((owner_col == owner_row) & (first < second), 1.0, 0.0)
    rank = jnp.sum(same, axis=0, keepdims=True)
    pos = owner_row.astype(F32) * cap + rank
    place = lax.broadcasted_iota(jnp.int32, (out_ref.shape[0], rows), 0).astype(F32)
    hot = jnp.where(place == pos, 1.0, 0.0).astype(BF)
    out_ref[...] = dot(hot, feat_ref[...]).astype(BF)


def collect_kernel(cap, slots, row_ref, col_ref, back_ref, out_ref):
    rows = out_ref.shape[0]
    owner_row = row_ref[...] // slots
    owner_col = col_ref[...] // slots
    first = lax.broadcasted_iota(jnp.int32, (rows, rows), 0)
    second = lax.broadcasted_iota(jnp.int32, (rows, rows), 1)
    same = jnp.where((owner_col == owner_row) & (second < first), 1.0, 0.0)
    rank = jnp.sum(same, axis=1, keepdims=True)
    pos = owner_col.astype(F32) * cap + rank
    place = lax.broadcasted_iota(jnp.int32, (rows, back_ref.shape[0]), 1).astype(F32)
    hot = jnp.where(place == pos, 1.0, 0.0).astype(BF)
    out_ref[...] = dot(hot, back_ref[...]).astype(BF)


def mask_kernel(cap, slots, route_ref, rel_ref, codes_ref, mask_ref, take_ref, put_ref):
    count, rows = route_ref.shape
    total = mask_ref.shape[0]
    codes = jnp.broadcast_to(codes_ref[...], (total, rows))
    hits = jnp.zeros((total, rows), F32)
    for s in range(count):
        hits = hits + jnp.where(codes == route_ref[s : s + 1, :], 1.0, 0.0)
    mask_ref[...] = jnp.broadcast_to(jnp.sum(hits, axis=1, keepdims=True), (total, LANES))
    rel = rel_ref[...]
    mine = (rel >= 0) & (rel < slots)
    mine_f = jnp.where(mine, 1.0, 0.0)
    slot_f = jnp.where(mine, rel, 0).astype(F32)
    first = lax.broadcasted_iota(jnp.int32, (rows, rows), 0)
    second = lax.broadcasted_iota(jnp.int32, (rows, rows), 1)
    tri = jnp.where(first < second, 1.0, 0.0).astype(BF)
    rank = dot(mine_f.astype(BF), tri)
    lane = lax.broadcasted_iota(jnp.int32, (count, LANES), 1)
    held = jnp.zeros((count, LANES), F32)
    for j in range(cap):
        here = jnp.where(rank == j, mine_f, 0.0)
        number = jnp.sum(here, axis=1, keepdims=True)
        value = jnp.sum(here * slot_f, axis=1, keepdims=True)
        value = value + (1.0 - number) * slots
        held = jnp.where(lane == j, value, held)
    buffers = count * cap
    place = lax.broadcasted_iota(jnp.int32, (buffers, count), 0)
    source = lax.broadcasted_iota(jnp.int32, (buffers, count), 1)
    spread = jnp.where(place // cap == source, 1.0, 0.0).astype(BF)
    wide = dot(spread, held.astype(BF))
    place = lax.broadcasted_iota(jnp.int32, (buffers, LANES), 0)
    lane = lax.broadcasted_iota(jnp.int32, (buffers, LANES), 1)
    slot_col = jnp.sum(jnp.where(place % cap == lane, wide, 0.0), axis=1, keepdims=True)
    slot_id = lax.broadcasted_iota(jnp.int32, (buffers, slots), 1).astype(F32)
    take = jnp.where(slot_col == slot_id, 1.0, 0.0)
    take_ref[...] = take.astype(BF)
    put_ref[...] = take.T.astype(BF)


def to_pairs_kernel(rows_ref, perm_ref, face_ref, out_ref, faces_ref):
    block = dot(rows_ref[...], perm_ref[0]).astype(BF)
    out_ref[0] = block
    faces_ref[0] = dot(face_ref[...], block).astype(BF)


def place_kernel(put_ref, rows_ref, perm_ref, face_ref, out_ref, faces_ref, held_ref):
    @pl.when(pl.program_id(0) == 0)
    def _():
        held_ref[...] = dot(put_ref[...], rows_ref[...]).astype(BF)

    block = dot(held_ref[...], perm_ref[0]).astype(BF)
    out_ref[0] = block
    faces_ref[0] = dot(face_ref[...], block).astype(BF)


def band_kernel(first_ref, second_ref, w1_ref, w2_ref, f1_ref, f2_ref):
    channels = first_ref.shape[1]
    for ref in (w1_ref, w2_ref, f1_ref, f2_ref):
        ref[...] = jnp.zeros_like(ref)
    for a in range(3):
        for b in range(3):
            for c in range(3):
                tap = 9 * a + 3 * b + c
                back = 26 - tap
                parts = (
                    (w1_ref, first_ref[tap].T),
                    (w2_ref, second_ref[tap].T),
                    (f1_ref, first_ref[back]),
                    (f2_ref, second_ref[back]),
                )
                for zo in range(2):
                    row = ((a * 3 + b) * 4 + zo + c) * LANES
                    for ref, value in parts:
                        ref[row : row + channels, zo * LANES : zo * LANES + channels] = value


def widen(ext_ref, f_ref, xlo_ref, xhi_ref, ylo_ref, yhi_ref, mask_ref=None):
    pairs = f_ref.shape[0]
    nx = ext_ref.shape[2] - 2
    ny = ext_ref.shape[3]
    inner = nx * ny
    for b in range(3):
        ext_ref[b, 0, :, :, 0:LANES] = jnp.zeros((nx + 2, ny, LANES), BF)
        ext_ref[b, pairs, :, :, LANES:PAIR] = jnp.zeros((nx + 2, ny, LANES), BF)
    row = lax.broadcasted_iota(jnp.int32, (ny, PAIR), 0)

    def masked(value, start, size):
        if mask_ref is None:
            return value
        m = mask_ref[start : start + size, :]
        return value * jnp.concatenate([m, m], axis=1)

    def body(k, carry):
        low = masked(ylo_ref[k].astype(F32), inner + 2 * ny, nx + 2)
        high = masked(yhi_ref[k].astype(F32), inner + 4 * ny, nx + 2)
        for xp in range(nx + 2):
            if xp == 0:
                mid = masked(xlo_ref[k].astype(F32), inner, ny)
            elif xp == nx + 1:
                mid = masked(xhi_ref[k].astype(F32), inner + ny, ny)
            else:
                mid = masked(f_ref[k, (xp - 1) * ny : xp * ny, :].astype(F32), (xp - 1) * ny, ny)
            up = jnp.where(row == 0, low[xp : xp + 1, :], pltpu.roll(mid, 1, 0))
            down = jnp.where(row == ny - 1, high[xp : xp + 1, :], pltpu.roll(mid, ny - 1, 0))
            for b, value in enumerate((up, mid, down)):
                value = value.astype(BF)
                ext_ref[b, k, xp, :, LANES:PAIR] = value[:, 0:LANES]
                ext_ref[b, k + 1, xp, :, 0:LANES] = value[:, LANES:PAIR]
        return carry

    lax.fori_loop(0, pairs, body, 0)


def conv_block(ext_ref, w_ref, k):
    nx = ext_ref.shape[2] - 2
    ny = ext_ref.shape[3]
    pieces = []
    for a in range(3):
        for b in range(3):
            for j in range(2):
                pieces.append(ext_ref[b, k + j, a : a + nx].reshape(nx * ny, PAIR))
    return dot(jnp.concatenate(pieces, axis=1), w_ref[...])


def wide_mask(mask_ref, rows):
    m = mask_ref[0:rows, :]
    return jnp.concatenate([m, m], axis=1)


def act_grad_kernel(f_ref, xlo_ref, xhi_ref, ylo_ref, yhi_ref, mask_ref, w_ref, out_ref, outer_ref, ext_ref):
    k = pl.program_id(0)

    @pl.when(k == 0)
    def _():
        widen(ext_ref, f_ref, xlo_ref, xhi_ref, ylo_ref, yhi_ref, mask_ref)

    rows = out_ref.shape[1]
    out_ref[0] = conv_block(ext_ref, w_ref, k)
    outer_ref[0] = (f_ref[k].astype(F32) * wide_mask(mask_ref, rows)).astype(BF)


def hidden_kernel(f_ref, xlo_ref, xhi_ref, ylo_ref, yhi_ref, mask_ref, w_ref, grad_ref, face_ref,
                  act_ref, hg_ref, faces_ref, ext_ref):
    k = pl.program_id(0)

    @pl.when(k == 0)
    def _():
        widen(ext_ref, f_ref, xlo_ref, xhi_ref, ylo_ref, yhi_ref)

    rows = act_ref.shape[1]
    m = wide_mask(mask_ref, rows)
    hidden = m * conv_block(ext_ref, w_ref, k)
    sigma = jax.nn.sigmoid(hidden)
    act = (hidden * sigma).astype(BF)
    hg = (m * grad_ref[0] * sigma * (1.0 + hidden * (1.0 - sigma))).astype(BF)
    act_ref[0] = act
    hg_ref[0] = hg
    faces_ref[0, 0] = dot(face_ref[...], act).astype(BF)
    faces_ref[1, 0] = dot(face_ref[...], hg).astype(BF)


def grid_grad_kernel(f_ref, xlo_ref, xhi_ref, ylo_ref, yhi_ref, w_ref, outer_ref, perm_ref, take_ref,
                     out_ref, ext_ref, acc_ref):
    k = pl.program_id(0)

    @pl.when(k == 0)
    def _():
        widen(ext_ref, f_ref, xlo_ref, xhi_ref, ylo_ref, yhi_ref)
        acc_ref[...] = jnp.zeros_like(acc_ref)

    total = (outer_ref[0].astype(F32) + conv_block(ext_ref, w_ref, k)).astype(BF)
    acc_ref[...] += dot_nt(total, perm_ref[0])

    @pl.when(k == pl.num_programs(0) - 1)
    def _():
        out_ref[...] = dot(take_ref[...], acc_ref[...].astype(BF)).astype(BF)


def block_kernel(f_ref, xlo_ref, xhi_ref, ylo_ref, yhi_ref, mask_ref, w_ref, field_ref, perm_ref,
                 out_ref, ext_ref, acc_ref):
    k = pl.program_id(0)

    @pl.when(k == 0)
    def _():
        widen(ext_ref, f_ref, xlo_ref, xhi_ref, ylo_ref, yhi_ref)
        acc_ref[...] = jnp.zeros_like(acc_ref)

    m = wide_mask(mask_ref, f_ref.shape[1])
    total = (field_ref[0].astype(F32) + m * conv_block(ext_ref, w_ref, k)).astype(BF)
    acc_ref[...] += dot_nt(total, perm_ref[0])

    @pl.when(k == pl.num_programs(0) - 1)
    def _():
        out_ref[...] = acc_ref[...].astype(BF)


def corr_kernel(channels, f_ref, xlo_ref, xhi_ref, ylo_ref, yhi_ref, g_ref, out_ref, ext_ref, gt_ref, taps_ref):
    pairs, rows, _ = g_ref.shape
    nx = ext_ref.shape[2] - 2
    widen(ext_ref, f_ref, xlo_ref, xhi_ref, ylo_ref, yhi_ref)
    for k in range(pairs):
        gt_ref[:, k * rows : (k + 1) * rows] = g_ref[k].T
    taps_ref[27] = jnp.zeros((channels, LANES), F32)

    def body(ab, carry):
        a = ab // 3
        b = ab % 3
        left = gt_ref[...]
        near = dot(left, ext_ref[b, 0:pairs, pl.ds(a, nx)].reshape(pairs * rows, PAIR))
        far = dot(left, ext_ref[b, 1 : pairs + 1, pl.ds(a, nx)].reshape(pairs * rows, PAIR))
        low = slice(0, channels)
        high = slice(LANES, LANES + channels)
        taps_ref[3 * ab] = near[low, 0:LANES] + near[high, LANES:PAIR]
        taps_ref[3 * ab + 1] = near[low, LANES:PAIR] + far[high, 0:LANES]
        taps_ref[3 * ab + 2] = far[low, 0:LANES] + far[high, LANES:PAIR]
        return carry

    lax.fori_loop(0, 9, body, 0)
    lane = lax.broadcasted_iota(jnp.int32, (channels, LANES), 1)
    for g in range(7):
        t1 = pltpu.roll(taps_ref[4 * g + 1], 96, 1)
        t2 = pltpu.roll(taps_ref[4 * g + 2], 64, 1)
        t3 = pltpu.roll(taps_ref[4 * g + 3], 32, 1)
        blocks = (
            jnp.where(lane < 96, taps_ref[4 * g], t1),
            jnp.where(lane < 64, t1, t2),
            jnp.where(lane < 32, t2, t3),
        )
        for i, value in enumerate(blocks):
            start = (3 * g + i) * channels
            out_ref[start : start + channels, :] = value.astype(BF)
    rest = out_ref.shape[0] - 21 * channels
    if rest:
        out_ref[21 * channels :, :] = jnp.zeros((rest, LANES), BF)


def chunk_sum_kernel(in_ref, out_ref):
    total = in_ref[0].astype(F32)
    for s in range(1, in_ref.shape[0]):
        total = total + in_ref[s].astype(F32)
    out_ref[...] = total.astype(BF)


def unpack_kernel(factor, packed_ref, out_ref):
    channels = out_ref.shape[1]
    lane = lax.broadcasted_iota(jnp.int32, (channels, LANES), 1)
    for g in range(7):
        v = []
        for i in range(3):
            start = (3 * g + i) * channels
            v.append(packed_ref[start : start + channels, :].astype(F32) * factor)
        taps = (
            v[0],
            pltpu.roll(jnp.where(lane < 64, v[1], v[0]), 32, 1),
            pltpu.roll(jnp.where(lane < 32, v[2], v[1]), 64, 1),
            pltpu.roll(v[2], 96, 1),
        )
        for u in range(4):
            if 4 * g + u < 27:
                out_ref[4 * g + u] = taps[u][:, 0:channels]


def permutation(channels, depth):
    perm = np.zeros((depth // 2, channels * depth, PAIR), np.float32)
    for c in range(channels):
        for z in range(depth):
            perm[z // 2, c * depth + z, (z % 2) * LANES + c] = 1.0
    return perm


def exchange(field, faces, ny):
    axis = field.ndim - 2
    count = lax.axis_size("rx")
    ahead = [(i, i + 1) for i in range(count - 1)]
    behind = [(t, s) for s, t in ahead]
    size = field.shape[axis]

    def cut(value, start, stop):
        return lax.slice_in_dim(value, start, stop, axis=axis)

    xlo = lax.ppermute(cut(field, size - ny, size), "rx", ahead)
    xhi = lax.ppermute(cut(field, 0, ny), "rx", behind)
    nx = faces.shape[axis] // 2
    low = jnp.concatenate([cut(xlo, 0, 1), cut(faces, 0, nx), cut(xhi, 0, 1)], axis=axis)
    high = jnp.concatenate([cut(xlo, ny - 1, ny), cut(faces, nx, 2 * nx), cut(xhi, ny - 1, ny)], axis=axis)
    count = lax.axis_size("ry")
    ahead = [(i, i + 1) for i in range(count - 1)]
    behind = [(t, s) for s, t in ahead]
    ylo = lax.ppermute(high, "ry", ahead)
    yhi = lax.ppermute(low, "ry", behind)
    return xlo, xhi, ylo, yhi


def on_device(column_features, column_route, cotangent, first_weight, second_weight):
    count_x = lax.axis_size("rx")
    count_y = lax.axis_size("ry")
    count_all = count_x * count_y
    shard_rows, row_width = column_features.shape
    nx, ny, _ = cotangent.shape
    channels = first_weight.shape[1]
    depth = row_width // channels
    slots = nx * ny
    pairs = depth // 2
    cap = 2 * shard_rows // count_all
    buffers = count_all * cap
    me_x = lax.axis_index("rx")
    me_y = lax.axis_index("ry")
    conv_flops = 2 * slots * pairs * 36 * LANES * PAIR
    axes = ("rx", "ry")

    shape = jax.ShapeDtypeStruct
    whole = lambda *dims: pl.BlockSpec(dims, lambda k: (0,) * len(dims))
    by_pair = lambda *dims: pl.BlockSpec((1,) + dims, lambda k: (k,) + (0,) * len(dims))
    zeros_like_field = shape((pairs, slots, PAIR), BF)
    ext = pltpu.VMEM((3, pairs + 1, nx + 2, ny, PAIR), BF)

    perm = jnp.asarray(permutation(channels, depth), BF)
    face_np = np.zeros((2 * nx, slots), np.float32)
    for u in range(nx):
        face_np[u, u * ny] = 1.0
        face_np[nx + u, u * ny + ny - 1] = 1.0
    face = jnp.asarray(face_np, BF)

    route_row = column_route.reshape(1, shard_rows)
    route_col = column_route.reshape(shard_rows, 1)
    route_all = lax.all_gather(column_route, axes).reshape(count_all, shard_rows)
    outgoing = call(
        functools.partial(send_kernel, cap, slots), shape((buffers, row_width), BF),
        2 * buffers * shard_rows * row_width, 3 * shard_rows * row_width * 2,
    )(route_row, route_col, column_features)
    incoming = lax.all_to_all(
        outgoing.reshape(count_all, cap, row_width), axes, split_axis=0, concat_axis=0, tiled=True
    ).reshape(buffers, row_width)

    steps, cells = [], []
    for u in range(nx):
        for v in range(ny):
            steps.append((0, 0)), cells.append(u * ny + v)
    for dx, u in ((-1, nx - 1), (1, 0)):
        for v in range(ny):
            steps.append((dx, 0)), cells.append(u * ny + v)
    for dy, v in ((-1, ny - 1), (1, 0)):
        for u in range(-1, nx + 1):
            steps.append((-1 if u < 0 else 1 if u == nx else 0, dy)), cells.append((u % nx) * ny + v)
        for _ in range(2 * ny - nx - 2):
            steps.append((0, 0)), cells.append(-(1 << 30))
    steps_np = np.asarray(steps, np.int32)
    cells_np = np.asarray(cells, np.int32)
    to_x = me_x + steps_np[:, 0]
    to_y = me_y + steps_np[:, 1]
    inside = (to_x >= 0) & (to_x < count_x) & (to_y >= 0) & (to_y < count_y) & (cells_np >= 0)
    codes = jnp.where(inside, (to_x * count_y + to_y) * slots + cells_np, -1).astype(jnp.int32)[:, None]
    spots = codes.shape[0]

    cot, cot_faces = call(
        to_pairs_kernel, (zeros_like_field, shape((pairs, 2 * nx, PAIR), BF)),
        2 * slots * row_width * PAIR * pairs, 10e6, (pairs,),
        [whole(slots, row_width), by_pair(row_width, PAIR), whole(2 * nx, slots)],
        (by_pair(slots, PAIR), by_pair(2 * nx, PAIR)),
    )(cotangent.reshape(slots, row_width), perm, face)
    cot_halo = exchange(cot, cot_faces, ny)

    band = shape((36 * LANES, PAIR), BF)
    w1, w2, f1, f2 = call(band_kernel, (band,) * 4, 1e9, 12e6)(first_weight, second_weight)

    mask, take, put = call(
        functools.partial(mask_kernel, cap, slots),
        (shape((spots, LANES), F32), shape((buffers, slots), BF), shape((slots, buffers), BF)),
        1e8, 1e6,
    )(route_all, route_all - (me_x * count_y + me_y) * slots, codes)

    halo_specs = [
        whole(pairs, slots, PAIR), whole(pairs, ny, PAIR), whole(pairs, ny, PAIR),
        whole(pairs, nx + 2, PAIR), whole(pairs, nx + 2, PAIR),
    ]
    mask_spec = whole(spots, LANES)
    band_spec = whole(36 * LANES, PAIR)
    field_spec = by_pair(slots, PAIR)

    act_grad, outer = call(
        act_grad_kernel, (shape((pairs, slots, PAIR), F32), zeros_like_field),
        conv_flops, 7e6, (pairs,),
        halo_specs + [mask_spec, band_spec], (field_spec, field_spec), (ext,),
    )(cot, *cot_halo, mask, f2)

    field, field_faces = call(
        place_kernel, (zeros_like_field, shape((pairs, 2 * nx, PAIR), BF)),
        2 * slots * row_width * PAIR * pairs, 10e6, (pairs,),
        [whole(slots, buffers), whole(buffers, row_width), by_pair(row_width, PAIR), whole(2 * nx, slots)],
        (by_pair(slots, PAIR), by_pair(2 * nx, PAIR)),
        (pltpu.VMEM((slots, row_width), BF),),
    )(put, incoming, perm, face)
    field_halo = exchange(field, field_faces, ny)

    act, hg, faces = call(
        hidden_kernel,
        (zeros_like_field, zeros_like_field, shape((2, pairs, 2 * nx, PAIR), BF)),
        conv_flops, 10e6, (pairs,),
        halo_specs + [mask_spec, band_spec, field_spec, whole(2 * nx, slots)],
        (field_spec, field_spec, pl.BlockSpec((2, 1, 2 * nx, PAIR), lambda k: (0, k, 0, 0))),
        (ext,),
    )(field, *field_halo, mask, w1, act_grad, face)
    act_halo = exchange(act, faces[0], ny)
    hg_halo = exchange(hg, faces[1], ny)

    unit = 16 * count_all
    packed_rows = -(-21 * channels // unit) * unit
    corr_scratch = (
        ext, pltpu.VMEM((PAIR, pairs * slots), BF), pltpu.VMEM((28, channels, LANES), F32),
    )
    corr = call(
        functools.partial(corr_kernel, channels), shape((packed_rows, LANES), BF), conv_flops, 5e6,
        scratch=corr_scratch,
    )

    def reduce(part):
        got = lax.all_to_all(
            part.reshape(count_all, packed_rows // count_all, LANES), axes, split_axis=0, concat_axis=0, tiled=True
        )
        chunk = call(
            chunk_sum_kernel, shape((packed_rows // count_all, LANES), BF), 1e6, 1e6
        )(got)
        return lax.all_gather(chunk, axes, tiled=True)

    first_packed = reduce(corr(field, *field_halo, hg))
    second_packed = reduce(corr(act, *act_halo, outer))

    rows_acc = pltpu.VMEM((slots, row_width), F32)
    back = call(
        grid_grad_kernel, shape((buffers, row_width), BF), 1.5 * conv_flops, 14e6, (pairs,),
        halo_specs + [band_spec, field_spec, by_pair(row_width, PAIR), whole(buffers, slots)],
        whole(buffers, row_width), (ext, rows_acc),
    )(hg, *hg_halo, f1, outer, perm, take)
    returned = lax.all_to_all(
        back.reshape(count_all, cap, row_width), axes, split_axis=0, concat_axis=0, tiled=True
    ).reshape(buffers, row_width)

    block_output = call(
        block_kernel, shape((slots, row_width), BF), 1.5 * conv_flops, 14e6, (pairs,),
        halo_specs + [mask_spec, band_spec, field_spec, by_pair(row_width, PAIR)],
        whole(slots, row_width), (ext, rows_acc),
    )(act, *act_halo, mask, w2, field, perm)

    feature_grads = call(
        functools.partial(collect_kernel, cap, slots), shape((shard_rows, row_width), BF),
        2 * buffers * shard_rows * row_width, 3 * shard_rows * row_width * 2,
    )(route_row, route_col, returned)

    factor = float(1.0 / np.sqrt(np.float32(count_all * shard_rows * depth)))
    unpack = call(functools.partial(unpack_kernel, factor), shape(first_weight.shape, F32), 1e6, 2e6)
    return (
        block_output.reshape(nx, ny, row_width), feature_grads, unpack(first_packed), unpack(second_packed),
    )


def solution(mesh):
    in_specs = (P(("rx", "ry"), None), P(("rx", "ry")), P("rx", "ry", None), P(), P())
    out_specs = (P("rx", "ry", None), P(("rx", "ry"), None), P(), P())
    return jax.shard_map(
        on_device, mesh=mesh, in_specs=in_specs, out_specs=out_specs, check_vma=False
    )
```

time: 644 us -> 425 us (0.66)
  matrix products: 338 us -> 0 us
  blocking collectives: 0 us -> 215 us
  Pallas kernels: 0 us -> 115 us
  waiting for transfers between devices: 115 us -> 13.5 us
  local copies, waits for them, and re-layouts: 95.3 us -> 13 us
  between operations: 15.2 us -> 1.24 us
  other arithmetic: 10.4 us -> 0.97 us
    dot_general x166 -> x0, matrix products: 338 us -> none  [the longest x108 270 us: conv_sum(): jnp.einsum('xyzi,oi->xyzo', piece, weights[9 * a + 3 * b + c], preferred_...]
    all_gather x0 -> x3, blocking collectives: none -> 215 us  [the longest x2 148 us: reduce(): return lax.all_gather(chunk, axes, tiled=True)]
    pallas_call x0 -> x16, Pallas kernels: none -> 115 us  [the longest x1 16.4 us: on_device(): call(grid_grad_kernel, shape((buffers, row_width), BF), 1.5 * conv_flops,...]
    psum x1 -> x0, waiting for transfers between devices: 107 us -> none  [on_device(): lax.psum((first_local, second_local), ('rx', 'ry'))]
    reshape x12 -> x1, local copies, waits for them, and re-layouts: 48.4 us -> 1.38 us  [on_device(): route_col = column_route.reshape(shard_rows, 1)]
    convert_element_type x4 -> x0, local copies, waits for them, and re-layouts: 27.2 us -> none  [the longest x2 15.3 us: on_device(): cot_field = jnp.transpose(cotangent.reshape(region_x, region_y, channels,...]
    transpose x3 -> x0, local copies, waits for them, and re-layouts: 8.89 us -> none  [the longest x1 6.04 us: on_device(): jnp.transpose(region_rows.reshape(region_x, region_y, channels, depth), (...]
    all_to_all x3 -> x4, starting transfers between devices: 22.3 us -> 26.8 us  [the longest x2 11.5 us: reduce(): lax.all_to_all(part.reshape(count_all, packed_rows // count_all, LANES),...]
  transfers between devices with their start and end apart: 20 -> 20, of which waited for: 5 -> 5; matrix products, arithmetic and copies ran while one was open for 34% -> 1% of each run, Pallas kernels for 0% -> 23%
where the time goes in v1:
time: 425 us; the launch traced here: 423 us
  blocking collectives  215 us (51%)
  Pallas kernels  115 us (27%)
  starting transfers between devices  64.4 us (15%)
  waiting for transfers between devices  13.5 us (3%)
  local copies, waits for them, and re-layouts  13 us (3%)
    all_gather x2, blocking collectives, reduce(): return lax.all_gather(chunk, axes, tiled=True)  148 us
    all_gather x1, blocking collectives, on_device(): lax.all_gather(column_route, axes).reshape(count_all, shard_rows)  67.3 us
    pallas_call x1, Pallas kernels, on_device(): call(grid_grad_kernel, shape((buffers, row_width), BF), 1.5 * conv_flops,...  16.4 us
    pallas_call x1, Pallas kernels, on_device(): call(block_kernel, shape((slots, row_width), BF), 1.5 * conv_flops, 14000...  16.1 us
    ppermute x4, starting transfers between devices, exchange(): xlo = lax.ppermute(cut(field, size - ny, size), 'rx', ahead)  14 us
    ppermute x4, starting transfers between devices, exchange(): ylo = lax.ppermute(high, 'ry', ahead)  13.2 us
    pallas_call x1, Pallas kernels, on_device(): call(hidden_kernel, (zeros_like_field, zeros_like_field, shape((2, pairs,...  12.2 us
    all_to_all x2, starting transfers between devices, reduce(): lax.all_to_all(part.reshape(count_all, packed_rows // count_all, LANES),...  11.5 us
  transfers between devices with their start and end apart: 20, of which 5 were waited for; matrix products, arithmetic and copies ran while one was open for 1% of the time, Pallas kernels for 23%

profile of v1, /device:TPU:0, one launch (start us, length us, event | category | flops | bytes accessed | tf_op | source)
XLA Modules:
  0.0 423.3 jit_solution(1277176668533764352)
XLA Ops:
  2.0 2.4 shard_map.139
  4.4 7.3 %all-to-all-start = ((bf16[32,8,1536]{2,1,0:T(8,128)(2,1)}), bf16[32,8,1536]{2,1,0:T(8,128)(2,1)S(1)}, u32[]{:S(2)}, u32[]{:S(2)}) async-start(bf16[32,8,1536]{2,1,0:T(8,128)(2,1)} %bitcast.17), calls=%async_computation | async-start | bytes 1572864 | tf_op jit(solution)/shard_map/all_to_all | solution.py:397
  11.8 8.3 %shard_map.142 = (bf16[8,256,256]{2,1,0:T(8,128)(2,1)}, bf16[8,32,256]{2,1,0:T(8,128)(2,1)}) custom-call(bf16[256,1536]{1,0:T(8,128)(2,1)} %bitcast.19, bf16[8,1536,256]{2,1,0:T(8,128)(2,1)} %constant.32.clone.perm_ref, bf16[32,256]{1,0:T(8,128)(2,1)} %constant.33.clone.face_ref), custom_call_target="tpu_custom_call" | custom-call | flops 1610612736 | bytes 10000000 | tf_op jit(solution)/shard_map/pallas_call | solution.py:421
  22.3 3.0 collective-permute-start.4
  26.2 67.3 %all-gather.1 = s32[32,1,128]{2,1,0:T(1,128)S(1)} all-gather(s32[1,1,128]{2,1,0:T(1,128)S(1)} %bitcast.28), channel_id=2, replica_groups=mesh['rx'=4,'ry'=8] {'rx','ry'}, dimensions={0}, use_global_device_ids=true | all-gather | bytes 16896 | tf_op jit(solution)/shard_map/all_gather | solution.py:392
  94.1 2.7 shard_map.138
  97.7 6.1 %shard_map.141 = (bf16[4608,256]{1,0:T(8,128)(2,1)}, bf16[4608,256]{1,0:T(8,128)(2,1)}, bf16[4608,256]{1,0:T(8,128)(2,1)}, bf16[4608,256]{1,0:T(8,128)(2,1)}) custom-call(bf16[27,96,96]{2,1,0:T(8,128)(2,1)} %first_ref.1, bf16[27,96,96]{2,1,0:T(8,128)(2,1)} %second_ref.1), custom_call_target="tpu_custom_call" | custom-call | flops 1000000000 | bytes 12000000 | tf_op jit(solution)/shard_map/pallas_call | solution.py:430
  107.5 8.7 %shard_map.140 = (bf16[8,256,256]{2,1,0:T(8,128)(2,1)}, bf16[8,32,256]{2,1,0:T(8,128)(2,1)}) custom-call(bf16[256,256]{1,0:T(8,128)(2,1)} %get-tuple-element.20.put_ref, bf16[256,1536]{1,0:T(8,128)(2,1)} %bitcast.16, bf16[8,1536,256]{2,1,0:T(8,128)(2,1)} %constant.32.clone.perm_ref, bf16[32,256]{1,0:T(8,128)(2,1)} %constant.33.clone.face_ref), custom_call_target="tpu_custom_call" | custom-call | flops 1610612736 | bytes 10000000 | tf_op jit(solution)/shard_map/pallas_call | solution.py:452
  119.2 3.0 collective-permute-start
  123.2 4.6 %collective-permute-start.2 = (bf16[8,18,256]{2,1,0:T(8,128)(2,1)S(1)}, bf16[8,18,256]{2,1,0:T(8,128)(2,1)S(1)}, u32[]{:S(2)}, u32[]{:S(2)}) collective-permute-start(bf16[8,18,256]{2,1,0:T(8,128)(2,1)S(1)} %pad_maximum_fusion), channel_id=1, source_target_pairs={{0,1},{1,2},{2,3},{3,4},{4,5},{5,6},{6,7},{8,9},{9,10},{10,11},{11... | collective-permute-start | bytes 221192 | tf_op jit(solution)/shard_map/ppermute | solution.py:355
  129.8 10.4 %shard_map.143 = (f32[8,256,256]{2,1,0:T(8,128)}, bf16[8,256,256]{2,1,0:T(8,128)(2,1)}) custom-call(bf16[8,256,256]{2,1,0:T(8,128)(2,1)} %get-tuple-element.25.f_ref, bf16[8,16,256]{2,1,0:T(8,128)(2,1)} %copy-done.7, bf16[8,16,256]{2,1,0:T(8,128)(2,1)} %copy-done.6, bf16[8,18,256]{2,1,0:T(8,128)(2,1)} %copy-done.20, bf16[8,18,256]{2,1,0:T(8,128)(2,1)} %copy-done.21, ...), custom_call_target="tpu_custom_call" | custom-call | flops 4831838208 | bytes 7000000 | tf_op jit(solution)/shard_map/pallas_call | solution.py:446
  140.9 12.2 %shard_map.144 = (bf16[8,256,256]{2,1,0:T(8,128)(2,1)}, bf16[8,256,256]{2,1,0:T(8,128)(2,1)}, bf16[2,8,32,256]{3,2,1,0:T(8,128)(2,1)}) custom-call(bf16[8,256,256]{2,1,0:T(8,128)(2,1)} %get-tuple-element.21.f_ref.field_ref, bf16[8,16,256]{2,1,0:T(8,128)(2,1)} %copy-done.13, bf16[8,16,256]{2,1,0:T(8,128)(2,1)} %copy-done.10, bf16[8,18,256]{2,1,0:T(8,128)(2,1)} %copy-done.22, ...), custom_call_target="tpu_custom_call" | custom-call | flops 4831838208 | bytes 10000000 | tf_op jit(solution)/shard_map/pallas_call | solution.py:461
  156.3 4.8 %collective-permute-start.8 = (bf16[8,16,256]{2,1,0:T(8,128)(2,1)S(1)}, bf16[8,16,256]{2,1,0:T(8,128)(2,1)S(1)}, u32[]{:S(2)}, u32[]{:S(2)}) collective-permute-start(bf16[8,16,256]{2,1,0:T(8,128)(2,1)S(1)} %get-tuple-element.39), channel_id=1, source_target_pairs={{0,8},{8,16},{16,24},{1,9},{9,17},{17,25},{2,10},{10,18},{18,26},{... | collective-permute-start | bytes 196616 | tf_op jit(solution)/shard_map/ppermute | solution.py:347
  162.0 10.4 %shard_map.148 = bf16[2048,128]{1,0:T(8,128)(2,1)} custom-call(bf16[8,256,256]{2,1,0:T(8,128)(2,1)} %get-tuple-element.21.f_ref.field_ref, bf16[8,16,256]{2,1,0:T(8,128)(2,1)} %copy-done.13, bf16[8,16,256]{2,1,0:T(8,128)(2,1)} %copy-done.10, bf16[8,18,256]{2,1,0:T(8,128)(2,1)} %copy-done.22, bf16[8,18,256]{2,1,0:T(8,128)(2,1)} %copy-done.23, ...), custom_call_target="tpu_custom_call" | custom-call | flops 4831838208 | bytes 5000000 | tf_op jit(solution)/shard_map/pallas_call | solution.py:491
  172.4 6.6 %all-to-all-start.2 = ((bf16[32,64,128]{2,1,0:T(8,128)(2,1)}), bf16[32,64,128]{2,1,0:T(8,128)(2,1)S(1)}, u32[]{:S(2)}, u32[]{:S(2)}) async-start(bf16[32,64,128]{2,1,0:T(8,128)(2,1)} %bitcast.21), calls=%async_computation.2 | async-start | bytes 1048576 | tf_op jit(solution)/shard_map/all_to_all | solution.py:483
  180.3 3.0 collective-permute-start.12
  183.5 3.7 collective-permute-start.10
  190.0 4.6 %collective-permute-done.11.yhi_ref = bf16[8,18,256]{2,1,0:T(8,128)(2,1)S(1)} collective-permute-done((bf16[8,18,256]{2,1,0:T(8,128)(2,1)S(1)}, bf16[8,18,256]{2,1,0:T(8,128)(2,1)S(1)}, u32[]{:S(2)}, u32[]{:S(2)}) %collective-permute-start.11) | collective-permute-done | bytes 73760 | tf_op jit(solution)/shard_map/ppermute | solution.py:356
  195.3 10.4 %shard_map.151 = bf16[2048,128]{1,0:T(8,128)(2,1)} custom-call(bf16[8,256,256]{2,1,0:T(8,128)(2,1)} %get-tuple-element.29.f_ref, bf16[8,16,256]{2,1,0:T(8,128)(2,1)} %copy-done.9, bf16[8,16,256]{2,1,0:T(8,128)(2,1)} %copy-done.8, bf16[8,18,256]{2,1,0:T(8,128)(2,1)} %copy-done.18, bf16[8,18,256]{2,1,0:T(8,128)(2,1)} %copy-done.19, ...), custom_call_target="tpu_custom_call" | custom-call | flops 4831838208 | bytes 5000000 | tf_op jit(solution)/shard_map/pallas_call | solution.py:492
  205.7 4.9 %all-to-all-start.3 = ((bf16[32,64,128]{2,1,0:T(8,128)(2,1)}), bf16[32,64,128]{2,1,0:T(8,128)(2,1)S(1)}, u32[]{:S(2)}, u32[]{:S(2)}) async-start(bf16[32,64,128]{2,1,0:T(8,128)(2,1)} %bitcast.22), calls=%async_computation.3 | async-start | bytes 1048576 | tf_op jit(solution)/shard_map/all_to_all | solution.py:483
  210.6 3.7 collective-permute-start.14
  215.9 3.5 collective-permute-done.14.ylo_ref
  219.4 3.0 collective-permute-done.15.yhi_ref
  223.0 16.4 %shard_map.146 = bf16[256,1536]{1,0:T(8,128)(2,1)} custom-call(bf16[8,256,256]{2,1,0:T(8,128)(2,1)} %get-tuple-element.32.f_ref.g_ref, bf16[8,16,256]{2,1,0:T(8,128)(2,1)} %copy-done.12, bf16[8,16,256]{2,1,0:T(8,128)(2,1)} %copy-done.11, bf16[8,18,256]{2,1,0:T(8,128)(2,1)} %copy-done.24, bf16[8,18,256]{2,1,0:T(8,128)(2,1)} %copy-done.25, ...), custom_call_target="tpu_custom_call" | custom-call | flops 7247757312 | bytes 14000000 | tf_op jit(solution)/shard_map/pallas_call | solution.py:495
  239.4 8.0 %all-to-all-start.1 = ((bf16[32,8,1536]{2,1,0:T(8,128)(2,1)}), bf16[32,8,1536]{2,1,0:T(8,128)(2,1)S(1)}, u32[]{:S(2)}, u32[]{:S(2)}) async-start(bf16[32,8,1536]{2,1,0:T(8,128)(2,1)} %bitcast.20), calls=%async_computation.1 | async-start | bytes 1572864 | tf_op jit(solution)/shard_map/all_to_all | solution.py:500
  247.4 16.1 %shard_map.145 = bf16[256,1536]{1,0:T(8,128)(2,1)} custom-call(bf16[8,256,256]{2,1,0:T(8,128)(2,1)} %get-tuple-element.29.f_ref, bf16[8,16,256]{2,1,0:T(8,128)(2,1)} %copy-done.9, bf16[8,16,256]{2,1,0:T(8,128)(2,1)} %copy-done.8, bf16[8,18,256]{2,1,0:T(8,128)(2,1)} %copy-done.18, bf16[8,18,256]{2,1,0:T(8,128)(2,1)} %copy-done.19, ...), custom_call_target="tpu_custom_call" | custom-call | flops 7247757312 | bytes 14000000 | tf_op jit(solution)/shard_map/pallas_call | solution.py:504
  263.6 1.7 shard_map.149
  265.3 76.4 %all_gather.14.packed_ref = bf16[2048,128]{1,0:T(8,128)(2,1)} all-gather(bf16[64,128]{1,0:T(8,128)(2,1)} %shard_map.149), channel_id=1, replica_groups=mesh['rx'=4,'ry'=8] {'rx','ry'}, dimensions={0}, use_global_device_ids=true | all-gather | bytes 540672 | tf_op jit(solution)/shard_map/all_gather | solution.py:489
  341.8 2.4 shard_map.150
  345.9 71.6 %all_gather.15.packed_ref = bf16[2048,128]{1,0:T(8,128)(2,1)} all-gather(bf16[64,128]{1,0:T(8,128)(2,1)} %shard_map.152), channel_id=1, replica_groups=mesh['rx'=4,'ry'=8] {'rx','ry'}, dimensions={0}, use_global_device_ids=true | all-gather | bytes 540672 | tf_op jit(solution)/shard_map/all_gather | solution.py:489
  417.5 2.4 shard_map.153
  420.9 2.4 shard_map.147
  (108 shorter events, 29.9 us)
Async XLA Ops:
  4.4 102.2 %all-to-all-start = ((bf16[32,8,1536]{2,1,0:T(8,128)(2,1)}), bf16[32,8,1536]{2,1,0:T(8,128)(2,1)S(1)}, u32[]{:S(2)}, u32[]{:S(2)}) async-start(bf16[32,8,1536]{2,1,0:T(8,128)(2,1)} %bitcast.17), calls=%async_computation | async-start | bytes 1572864 | tf_op jit(solution)/shard_map/all_to_all | solution.py:397
  11.7 13.6 %copy-start.14 = (s32[352]{0:T(512)S(1)}, s32[352]{0:T(512)}, u32[]{:S(2)}) copy-start(s32[352]{0:T(512)} %constant.37.clone) | copy-start | bytes 4228
  11.7 13.6 %copy-start.15 = (s32[352]{0:T(512)S(1)}, s32[352]{0:T(512)}, u32[]{:S(2)}) copy-start(s32[352]{0:T(512)} %constant.35.clone) | copy-start | bytes 4228
  11.7 13.6 %copy-start.16 = (s32[352]{0:T(512)S(1)}, s32[352]{0:T(512)}, u32[]{:S(2)}) copy-start(s32[352]{0:T(512)} %constant.34.clone) | copy-start | bytes 4228
  11.7 13.6 %copy-start.17 = (pred[352]{0:T(512)(128)(4,1)S(1)}, pred[352]{0:T(512)(128)(4,1)}, u32[]{:S(2)}) copy-start(pred[352]{0:T(512)(128)(4,1)} %constant.36.clone) | copy-start | bytes 1060
  11.8 14.4 %copy-start.5 = (s32[128]{0:T(128)S(1)}, s32[128]{0:T(128)}, u32[]{:S(2)}) copy-start(s32[128]{0:T(128)} %param.12) | copy-start | bytes 1540
  21.0 82.8 %collective-permute-start.5 = (bf16[8,16,256]{2,1,0:T(8,128)(2,1)S(1)}, bf16[8,16,256]{2,1,0:T(8,128)(2,1)S(1)}, u32[]{:S(2)}, u32[]{:S(2)}) collective-permute-start(bf16[8,16,256]{2,1,0:T(8,128)(2,1)S(1)} %get-tuple-element.40), channel_id=1, source_target_pairs={{8,0},{16,8},{24,16},{9,1},{17,9},{25,17},{10,2},{18,10},{26,18},{... | collective-permute-start | bytes 196616 | tf_op jit(solution)/shard_map/ppermute | solution.py:348
  22.3 81.5 %collective-permute-start.4 = (bf16[8,16,256]{2,1,0:T(8,128)(2,1)S(1)}, bf16[8,16,256]{2,1,0:T(8,128)(2,1)S(1)}, u32[]{:S(2)}, u32[]{:S(2)}) collective-permute-start(bf16[8,16,256]{2,1,0:T(8,128)(2,1)S(1)} %get-tuple-element.41), channel_id=1, source_target_pairs={{0,8},{8,16},{16,24},{1,9},{9,17},{17,25},{2,10},{10,18},{18,26},{... | collective-permute-start | bytes 196616 | tf_op jit(solution)/shard_map/ppermute | solution.py:347
  103.8 12.4 %copy-start.6 = (bf16[8,16,256]{2,1,0:T(8,128)(2,1)}, bf16[8,16,256]{2,1,0:T(8,128)(2,1)S(1)}, u32[]{:S(2)}) copy-start(bf16[8,16,256]{2,1,0:T(8,128)(2,1)S(1)} %collective-permute-done.5.xhi_ref) | copy-start | bytes 196612
  103.8 12.3 %copy-start.7 = (bf16[8,16,256]{2,1,0:T(8,128)(2,1)}, bf16[8,16,256]{2,1,0:T(8,128)(2,1)S(1)}, u32[]{:S(2)}) copy-start(bf16[8,16,256]{2,1,0:T(8,128)(2,1)S(1)} %collective-permute-done.4.xlo_ref) | copy-start | bytes 196612
  103.9 25.2 %collective-permute-start.6 = (bf16[8,18,256]{2,1,0:T(8,128)(2,1)S(1)}, bf16[8,18,256]{2,1,0:T(8,128)(2,1)S(1)}, u32[]{:S(2)}, u32[]{:S(2)}) collective-permute-start(bf16[8,18,256]{2,1,0:T(8,128)(2,1)S(1)} %pad_maximum_fusion.2), channel_id=1, source_target_pairs={{0,1},{1,2},{2,3},{3,4},{4,5},{5,6},{6,7},{8,9},{9,10},{10,11},{11... | collective-permute-start | bytes 221192 | tf_op jit(solution)/shard_map/ppermute | solution.py:355
  105.3 23.9 %collective-permute-start.7 = (bf16[8,18,256]{2,1,0:T(8,128)(2,1)S(1)}, bf16[8,18,256]{2,1,0:T(8,128)(2,1)S(1)}, u32[]{:S(2)}, u32[]{:S(2)}) collective-permute-start(bf16[8,18,256]{2,1,0:T(8,128)(2,1)S(1)} %pad_maximum_fusion.3), channel_id=1, source_target_pairs={{1,0},{2,1},{3,2},{4,3},{5,4},{6,5},{7,6},{9,8},{10,9},{11,10},{12... | collective-permute-start | bytes 221192 | tf_op jit(solution)/shard_map/ppermute | solution.py:356
  117.1 5.2 %collective-permute-start.1 = (bf16[8,16,256]{2,1,0:T(8,128)(2,1)S(1)}, bf16[8,16,256]{2,1,0:T(8,128)(2,1)S(1)}, u32[]{:S(2)}, u32[]{:S(2)}) collective-permute-start(bf16[8,16,256]{2,1,0:T(8,128)(2,1)S(1)} %get-tuple-element.42), channel_id=1, source_target_pairs={{8,0},{16,8},{24,16},{9,1},{17,9},{25,17},{10,2},{18,10},{26,18},{... | collective-permute-start | bytes 196616 | tf_op jit(solution)/shard_map/ppermute | solution.py:348
  119.2 3.9 collective-permute-start
  122.3 17.9 %copy-start.10 = (bf16[8,16,256]{2,1,0:T(8,128)(2,1)}, bf16[8,16,256]{2,1,0:T(8,128)(2,1)S(1)}, u32[]{:S(2)}) copy-start(bf16[8,16,256]{2,1,0:T(8,128)(2,1)S(1)} %collective-permute-done.1.xhi_ref) | copy-start | bytes 196612
  123.2 17.0 %copy-start.13 = (bf16[8,16,256]{2,1,0:T(8,128)(2,1)}, bf16[8,16,256]{2,1,0:T(8,128)(2,1)S(1)}, u32[]{:S(2)}) copy-start(bf16[8,16,256]{2,1,0:T(8,128)(2,1)S(1)} %collective-permute-done.xlo_ref) | copy-start | bytes 196612
  123.2 17.0 %collective-permute-start.2 = (bf16[8,18,256]{2,1,0:T(8,128)(2,1)S(1)}, bf16[8,18,256]{2,1,0:T(8,128)(2,1)S(1)}, u32[]{:S(2)}, u32[]{:S(2)}) collective-permute-start(bf16[8,18,256]{2,1,0:T(8,128)(2,1)S(1)} %pad_maximum_fusion), channel_id=1, source_target_pairs={{0,1},{1,2},{2,3},{3,4},{4,5},{5,6},{6,7},{8,9},{9,10},{10,11},{11... | collective-permute-start | bytes 221192 | tf_op jit(solution)/shard_map/ppermute | solution.py:355
  127.8 12.4 %collective-permute-start.3 = (bf16[8,18,256]{2,1,0:T(8,128)(2,1)S(1)}, bf16[8,18,256]{2,1,0:T(8,128)(2,1)S(1)}, u32[]{:S(2)}, u32[]{:S(2)}) collective-permute-start(bf16[8,18,256]{2,1,0:T(8,128)(2,1)S(1)} %pad_maximum_fusion.1), channel_id=1, source_target_pairs={{1,0},{2,1},{3,2},{4,3},{5,4},{6,5},{7,6},{9,8},{10,9},{11,10},{12... | collective-permute-start | bytes 221192 | tf_op jit(solution)/shard_map/ppermute | solution.py:356
  155.0 28.4 %collective-permute-start.9 = (bf16[8,16,256]{2,1,0:T(8,128)(2,1)S(1)}, bf16[8,16,256]{2,1,0:T(8,128)(2,1)S(1)}, u32[]{:S(2)}, u32[]{:S(2)}) collective-permute-start(bf16[8,16,256]{2,1,0:T(8,128)(2,1)S(1)} %get-tuple-element.38), channel_id=1, source_target_pairs={{8,0},{16,8},{24,16},{9,1},{17,9},{25,17},{10,2},{18,10},{26,18},{... | collective-permute-start | bytes 196616 | tf_op jit(solution)/shard_map/ppermute | solution.py:348
  156.3 27.1 %collective-permute-start.8 = (bf16[8,16,256]{2,1,0:T(8,128)(2,1)S(1)}, bf16[8,16,256]{2,1,0:T(8,128)(2,1)S(1)}, u32[]{:S(2)}, u32[]{:S(2)}) collective-permute-start(bf16[8,16,256]{2,1,0:T(8,128)(2,1)S(1)} %get-tuple-element.39), channel_id=1, source_target_pairs={{0,8},{8,16},{16,24},{1,9},{9,17},{17,25},{2,10},{10,18},{18,26},{... | collective-permute-start | bytes 196616 | tf_op jit(solution)/shard_map/ppermute | solution.py:347
  172.4 33.3 %all-to-all-start.2 = ((bf16[32,64,128]{2,1,0:T(8,128)(2,1)}), bf16[32,64,128]{2,1,0:T(8,128)(2,1)S(1)}, u32[]{:S(2)}, u32[]{:S(2)}) async-start(bf16[32,64,128]{2,1,0:T(8,128)(2,1)} %bitcast.21), calls=%async_computation.2 | async-start | bytes 1048576 | tf_op jit(solution)/shard_map/all_to_all | solution.py:483
  179.0 9.5 %collective-permute-start.13 = (bf16[8,16,256]{2,1,0:T(8,128)(2,1)S(1)}, bf16[8,16,256]{2,1,0:T(8,128)(2,1)S(1)}, u32[]{:S(2)}, u32[]{:S(2)}) collective-permute-start(bf16[8,16,256]{2,1,0:T(8,128)(2,1)S(1)} %get-tuple-element.36), channel_id=1, source_target_pairs={{8,0},{16,8},{24,16},{9,1},{17,9},{25,17},{10,2},{18,10},{26,18},{... | collective-permute-start | bytes 196616 | tf_op jit(solution)/shard_map/ppermute | solution.py:348
  180.3 30.2 %collective-permute-start.12 = (bf16[8,16,256]{2,1,0:T(8,128)(2,1)S(1)}, bf16[8,16,256]{2,1,0:T(8,128)(2,1)S(1)}, u32[]{:S(2)}, u32[]{:S(2)}) collective-permute-start(bf16[8,16,256]{2,1,0:T(8,128)(2,1)S(1)} %get-tuple-element.37), channel_id=1, source_target_pairs={{0,8},{8,16},{16,24},{1,9},{9,17},{17,25},{2,10},{10,18},{18,26},{... | collective-permute-start | bytes 196616 | tf_op jit(solution)/shard_map/ppermute | solution.py:347
  183.5 6.5 %collective-permute-start.10 = (bf16[8,18,256]{2,1,0:T(8,128)(2,1)S(1)}, bf16[8,18,256]{2,1,0:T(8,128)(2,1)S(1)}, u32[]{:S(2)}, u32[]{:S(2)}) collective-permute-start(bf16[8,18,256]{2,1,0:T(8,128)(2,1)S(1)} %pad_maximum_fusion.4), channel_id=1, source_target_pairs={{0,1},{1,2},{2,3},{3,4},{4,5},{5,6},{6,7},{8,9},{9,10},{10,11},{11... | collective-permute-start | bytes 221192 | tf_op jit(solution)/shard_map/ppermute | solution.py:355
  187.2 7.4 %collective-permute-start.11 = (bf16[8,18,256]{2,1,0:T(8,128)(2,1)S(1)}, bf16[8,18,256]{2,1,0:T(8,128)(2,1)S(1)}, u32[]{:S(2)}, u32[]{:S(2)}) collective-permute-start(bf16[8,18,256]{2,1,0:T(8,128)(2,1)S(1)} %pad_maximum_fusion.5), channel_id=1, source_target_pairs={{1,0},{2,1},{3,2},{4,3},{5,4},{6,5},{7,6},{9,8},{10,9},{11,10},{12... | collective-permute-start | bytes 221192 | tf_op jit(solution)/shard_map/ppermute | solution.py:356
  188.6 17.1 %copy-start.11 = (bf16[8,16,256]{2,1,0:T(8,128)(2,1)}, bf16[8,16,256]{2,1,0:T(8,128)(2,1)S(1)}, u32[]{:S(2)}) copy-start(bf16[8,16,256]{2,1,0:T(8,128)(2,1)S(1)} %collective-permute-done.13.xhi_ref) | copy-start | bytes 196612
  205.7 33.7 %copy-start.2 = (bf16[32,64,128]{2,1,0:T(8,128)(2,1)}, bf16[32,64,128]{2,1,0:T(8,128)(2,1)S(1)}, u32[]{:S(2)}) copy-start(bf16[32,64,128]{2,1,0:T(8,128)(2,1)S(1)} %all-to-all-done.2.in_ref) | copy-start | bytes 1572868
  205.7 33.7 %all-to-all-start.3 = ((bf16[32,64,128]{2,1,0:T(8,128)(2,1)}), bf16[32,64,128]{2,1,0:T(8,128)(2,1)S(1)}, u32[]{:S(2)}, u32[]{:S(2)}) async-start(bf16[32,64,128]{2,1,0:T(8,128)(2,1)} %bitcast.22), calls=%async_computation.3 | async-start | bytes 1048576 | tf_op jit(solution)/shard_map/all_to_all | solution.py:483
  210.6 8.7 %collective-permute-start.14 = (bf16[8,18,256]{2,1,0:T(8,128)(2,1)S(1)}, bf16[8,18,256]{2,1,0:T(8,128)(2,1)S(1)}, u32[]{:S(2)}, u32[]{:S(2)}) collective-permute-start(bf16[8,18,256]{2,1,0:T(8,128)(2,1)S(1)} %pad_maximum_fusion.6), channel_id=1, source_target_pairs={{0,1},{1,2},{2,3},{3,4},{4,5},{5,6},{6,7},{8,9},{9,10},{10,11},{11... | collective-permute-start | bytes 221192 | tf_op jit(solution)/shard_map/ppermute | solution.py:355
  214.4 8.0 %collective-permute-start.15 = (bf16[8,18,256]{2,1,0:T(8,128)(2,1)S(1)}, bf16[8,18,256]{2,1,0:T(8,128)(2,1)S(1)}, u32[]{:S(2)}, u32[]{:S(2)}) collective-permute-start(bf16[8,18,256]{2,1,0:T(8,128)(2,1)S(1)} %pad_maximum_fusion.7), channel_id=1, source_target_pairs={{1,0},{2,1},{3,2},{4,3},{5,4},{6,5},{7,6},{9,8},{10,9},{11,10},{12... | collective-permute-start | bytes 221192 | tf_op jit(solution)/shard_map/ppermute | solution.py:356
  239.4 24.2 %copy-start.3 = (bf16[32,64,128]{2,1,0:T(8,128)(2,1)}, bf16[32,64,128]{2,1,0:T(8,128)(2,1)S(1)}, u32[]{:S(2)}) copy-start(bf16[32,64,128]{2,1,0:T(8,128)(2,1)S(1)} %all-to-all-done.3.in_ref) | copy-start | bytes 1572868
  239.4 180.5 %all-to-all-start.1 = ((bf16[32,8,1536]{2,1,0:T(8,128)(2,1)}), bf16[32,8,1536]{2,1,0:T(8,128)(2,1)S(1)}, u32[]{:S(2)}, u32[]{:S(2)}) async-start(bf16[32,8,1536]{2,1,0:T(8,128)(2,1)} %bitcast.20), calls=%async_computation.1 | async-start | bytes 1572864 | tf_op jit(solution)/shard_map/all_to_all | solution.py:500
  (14 other events, 48.4 us)

commit v2 on v1

--- a/solution.py
+++ b/solution.py
@@ -10,12 +10,12 @@
 
 LANES = 128
 PAIR = 256
-VMEM = 56 * 1024 * 1024
+MIB = 1024 * 1024
 BF = jnp.bfloat16
 F32 = jnp.float32
 
 
-def call(body, out_shape, flops, moved, grid=None, in_specs=None, out_specs=None, scratch=()):
+def call(body, out_shape, flops, moved, grid=None, in_specs=None, out_specs=None, scratch=(), room=16):
     extra = {}
     if grid is not None:
         extra = dict(grid=grid, in_specs=in_specs, out_specs=out_specs)
@@ -23,7 +23,7 @@
         body,
         out_shape=out_shape,
         scratch_shapes=list(scratch),
-        compiler_params=pltpu.CompilerParams(vmem_limit_bytes=VMEM),
+        compiler_params=pltpu.CompilerParams(vmem_limit_bytes=room * MIB),
         cost_estimate=pl.CostEstimate(flops=int(flops), bytes_accessed=int(moved), transcendentals=0),
         **extra,
     )
@@ -300,21 +300,33 @@
         out_ref[21 * channels :, :] = jnp.zeros((rest, LANES), BF)
 
 
-def chunk_sum_kernel(in_ref, out_ref):
-    total = in_ref[0].astype(F32)
-    for s in range(1, in_ref.shape[0]):
-        total = total + in_ref[s].astype(F32)
-    out_ref[...] = total.astype(BF)
-
-
-def unpack_kernel(factor, packed_ref, out_ref):
+def chunk_sum_kernel(first_ref, second_ref, out_ref):
+    count = first_ref.shape[0]
+    for i, ref in enumerate((first_ref, second_ref)):
+        total = ref[0].astype(F32)
+        for s in range(1, count):
+            total = total + ref[s].astype(F32)
+        total = total.astype(BF)
+        for s in range(count):
+            out_ref[s, i] = total
+
+
+def unpack_kernel(factor, packed_ref, first_ref, second_ref, flat_ref):
+    count, _, rows, _ = packed_ref.shape
+    for i, out_ref in enumerate((first_ref, second_ref)):
+        for s in range(count):
+            flat_ref[s * rows : (s + 1) * rows, :] = packed_ref[s, i].astype(F32)
+        unpack_taps(factor, flat_ref, out_ref)
+
+
+def unpack_taps(factor, packed_ref, out_ref):
     channels = out_ref.shape[1]
     lane = lax.broadcasted_iota(jnp.int32, (channels, LANES), 1)
     for g in range(7):
         v = []
         for i in range(3):
             start = (3 * g + i) * channels
-            v.append(packed_ref[start : start + channels, :].astype(F32) * factor)
+            v.append(packed_ref[start : start + channels, :] * factor)
         taps = (
             v[0],
             pltpu.roll(jnp.where(lane < 64, v[1], v[0]), 32, 1),
@@ -387,9 +399,12 @@
         face_np[nx + u, u * ny + ny - 1] = 1.0
     face = jnp.asarray(face_np, BF)
 
+    def share(parts):
+        return lax.all_to_all(parts, axes, split_axis=0, concat_axis=0, tiled=True)
+
     route_row = column_route.reshape(1, shard_rows)
     route_col = column_route.reshape(shard_rows, 1)
-    route_all = lax.all_gather(column_route, axes).reshape(count_all, shard_rows)
+    route_all = share(jnp.broadcast_to(route_row, (count_all, shard_rows)))
     outgoing = call(
         functools.partial(send_kernel, cap, slots), shape((buffers, row_width), BF),
         2 * buffers * shard_rows * row_width, 3 * shard_rows * row_width * 2,
@@ -479,17 +494,13 @@
         scratch=corr_scratch,
     )
 
-    def reduce(part):
-        got = lax.all_to_all(
-            part.reshape(count_all, packed_rows // count_all, LANES), axes, split_axis=0, concat_axis=0, tiled=True
-        )
-        chunk = call(
-            chunk_sum_kernel, shape((packed_rows // count_all, LANES), BF), 1e6, 1e6
-        )(got)
-        return lax.all_gather(chunk, axes, tiled=True)
-
-    first_packed = reduce(corr(field, *field_halo, hg))
-    second_packed = reduce(corr(act, *act_halo, outer))
+    chunk = packed_rows // count_all
+
+    def spread(part):
+        return share(part.reshape(count_all, chunk, LANES))
+
+    first_parts = spread(corr(field, *field_halo, hg))
+    second_parts = spread(corr(act, *act_halo, outer))
 
     rows_acc = pltpu.VMEM((slots, row_width), F32)
     back = call(
@@ -513,9 +524,16 @@
     )(route_row, route_col, returned)
 
     factor = float(1.0 / np.sqrt(np.float32(count_all * shard_rows * depth)))
-    unpack = call(functools.partial(unpack_kernel, factor), shape(first_weight.shape, F32), 1e6, 2e6)
+    sums = share(call(
+        chunk_sum_kernel, shape((count_all, 2, chunk, LANES), BF), 1e6, 2e6,
+    )(first_parts, second_parts))
+    grads = shape(first_weight.shape, F32)
+    first_grad, second_grad = call(
+        functools.partial(unpack_kernel, factor), (grads, grads), 1e6, 4e6,
+        scratch=(pltpu.VMEM((packed_rows, LANES), F32),),
+    )(sums)
     return (
-        block_output.reshape(nx, ny, row_width), feature_grads, unpack(first_packed), unpack(second_packed),
+        block_output.reshape(nx, ny, row_width), feature_grads, first_grad, second_grad,
     )
 
 

time: 425 us -> 233 us (0.55)
  blocking collectives: 215 us -> 0 us
  Pallas kernels: 115 us -> 78.1 us
  waiting for transfers between devices: 13.5 us -> 43.5 us
  local copies, waits for them, and re-layouts: 13 us -> 32.1 us
  starting transfers between devices: 64.4 us -> 75.7 us
    all_gather x3 -> x0, blocking collectives: 215 us -> none  [the longest x2 148 us: reduce(): return lax.all_gather(chunk, axes, tiled=True)]
    unnamed x52 -> x66, local copies, waits for them, and re-layouts: 4.41 us -> 30.4 us
    all_to_all x1, waiting for transfers between devices: 0.01 us -> 20.8 us  [on_device(): lax.all_to_all(back.reshape(count_all, cap, row_width), axes, split_axis=...]
    all_to_all x2 -> x4, starting transfers between devices: 11.5 us -> 23.9 us  [share(): return lax.all_to_all(parts, axes, split_axis=0, concat_axis=0, tiled=True)]
    pallas_call x6 -> x4, Pallas kernels: 29 us -> 20.5 us  [the longest x1 8.68 us: on_device(): second_parts = spread(corr(act, *act_halo, outer))]
    all_to_all x2 -> x4, waiting for transfers between devices: 0.01 us -> 7.16 us  [share(): return lax.all_to_all(parts, axes, split_axis=0, concat_axis=0, tiled=True)]
    slice x16, local copies, waits for them, and re-layouts: 5.48 us -> 0.24 us  [cut(): return lax.slice_in_dim(value, start, stop, axis=axis)]
    pallas_call x1, Pallas kernels: 6.11 us -> 1.29 us  [on_device(): call(band_kernel, (band,) * 4, 1000000000.0, 12000000.0)]
  transfers between devices with their start and end apart: 20 -> 22, of which waited for: 5 -> 8; matrix products, arithmetic and copies ran while one was open for 1% -> 0% of each run, Pallas kernels for 23% -> 29%
where the time goes in v2:
time: 233 us; the launch traced here: 231 us
  Pallas kernels  78.1 us (34%)
  starting transfers between devices  75.7 us (32%)
  waiting for transfers between devices  43.5 us (19%)
  local copies, waits for them, and re-layouts  32.1 us (14%)
    unnamed x66, local copies, waits for them, and re-layouts  30.4 us
    all_to_all x4, starting transfers between devices, share(): return lax.all_to_all(parts, axes, split_axis=0, concat_axis=0, tiled=True)  23.9 us
    all_to_all x1, waiting for transfers between devices, on_device(): lax.all_to_all(back.reshape(count_all, cap, row_width), axes, split_axis=...  20.8 us
    ppermute x4, starting transfers between devices, exchange(): ylo = lax.ppermute(high, 'ry', ahead)  13.9 us
    pallas_call x1, Pallas kernels, on_device(): call(grid_grad_kernel, shape((buffers, row_width), BF), 1.5 * conv_flops,...  13.8 us
    pallas_call x1, Pallas kernels, on_device(): call(block_kernel, shape((slots, row_width), BF), 1.5 * conv_flops, 14000...  13.5 us
    ppermute x4, starting transfers between devices, exchange(): xlo = lax.ppermute(cut(field, size - ny, size), 'rx', ahead)  13.5 us
    pallas_call x1, Pallas kernels, on_device(): call(hidden_kernel, (zeros_like_field, zeros_like_field, shape((2, pairs,...  9.16 us
  transfers between devices with their start and end apart: 22, of which 8 were waited for; matrix products, arithmetic and copies ran while one was open for 0% of the time, Pallas kernels for 29%

profile of v2, /device:TPU:0, one launch (start us, length us, event | category | flops | bytes accessed | tf_op | source)
XLA Modules:
  0.0 231.0 jit_solution(1148819303396661538)
XLA Ops:
  1.9 7.3 %all-to-all-start = ((s32[32,1,128]{2,1,0:T(1,128)}), s32[32,1,128]{2,1,0:T(1,128)S(1)}, u32[]{:S(2)}, u32[]{:S(2)}) async-start(s32[32,1,128]{2,1,0:T(1,128)} %broadcast_in_dim.12), calls=%async_computation | async-start | bytes 32768 | tf_op jit(solution)/shard_map/all_to_all | solution.py:403
  9.2 2.8 %copy-done = bf16[8,1536,256]{2,1,0:T(8,128)(2,1)S(1)} copy-done((bf16[8,1536,256]{2,1,0:T(8,128)(2,1)S(1)}, bf16[8,1536,256]{2,1,0:T(8,128)(2,1)}, u32[]{:S(2)}) %copy-start) | copy-done | bytes 6291480
  13.8 4.3 %shard_map.142 = (bf16[8,256,256]{2,1,0:T(8,128)(2,1)S(1)}, bf16[8,32,256]{2,1,0:T(8,128)(2,1)S(1)}) custom-call(bf16[256,1536]{1,0:T(8,128)(2,1)S(1)} %bitcast.17, bf16[8,1536,256]{2,1,0:T(8,128)(2,1)S(1)} %copy-done, bf16[32,256]{1,0:T(8,128)(2,1)S(1)} %copy-done.6), custom_call_target="tpu_custom_call" | custom-call | flops 1610612736 | bytes 10000000 | tf_op jit(solution)/shard_map/pallas_call | solution.py:436
  19.6 5.8 %all-to-all-start.1 = ((bf16[32,8,1536]{2,1,0:T(8,128)(2,1)}), bf16[32,8,1536]{2,1,0:T(8,128)(2,1)S(1)}, u32[]{:S(2)}, u32[]{:S(2)}) async-start(bf16[32,8,1536]{2,1,0:T(8,128)(2,1)} %bitcast.3), calls=%async_computation.1 | async-start | bytes 1572864 | tf_op jit(solution)/shard_map/all_to_all | solution.py:412
  26.8 3.0 %collective-permute-start.4 = (bf16[8,16,256]{2,1,0:T(8,128)(2,1)S(1)}, bf16[8,16,256]{2,1,0:T(8,128)(2,1)S(1)}, u32[]{:S(2)}, u32[]{:S(2)}) collective-permute-start(bf16[8,16,256]{2,1,0:T(8,128)(2,1)S(1)} %get-tuple-element.45), channel_id=1, source_target_pairs={{0,8},{8,16},{16,24},{1,9},{9,17},{17,25},{2,10},{10,18},{18,26},{... | collective-permute-start | bytes 196616 | tf_op jit(solution)/shard_map/ppermute | solution.py:359
  40.4 3.7 %collective-permute-start.6 = (bf16[8,18,256]{2,1,0:T(8,128)(2,1)S(1)}, bf16[8,18,256]{2,1,0:T(8,128)(2,1)S(1)}, u32[]{:S(2)}, u32[]{:S(2)}) collective-permute-start(bf16[8,18,256]{2,1,0:T(8,128)(2,1)S(1)} %pad_maximum_fusion.2), channel_id=1, source_target_pairs={{0,1},{1,2},{2,3},{3,4},{4,5},{5,6},{6,7},{8,9},{9,10},{10,11},{11... | collective-permute-start | bytes 221192 | tf_op jit(solution)/shard_map/ppermute | solution.py:367
  45.4 2.0 all-to-all-done.1
  47.5 2.8 %copy-done.1 = bf16[8,1536,256]{2,1,0:T(8,128)(2,1)S(1)} copy-done((bf16[8,1536,256]{2,1,0:T(8,128)(2,1)S(1)}, bf16[8,1536,256]{2,1,0:T(8,128)(2,1)}, u32[]{:S(2)}) %copy-start.1) | copy-done | bytes 6291480
  50.2 4.6 %shard_map.140 = (bf16[8,256,256]{2,1,0:T(8,128)(2,1)S(1)}, bf16[8,32,256]{2,1,0:T(8,128)(2,1)S(1)}) custom-call(bf16[256,256]{1,0:T(8,128)(2,1)S(1)} %get-tuple-element.22.put_ref, bf16[256,1536]{1,0:T(8,128)(2,1)S(1)} %bitcast.15, bf16[8,1536,256]{2,1,0:T(8,128)(2,1)S(1)} %copy-done.1, bf16[32,256]{1,0:T(8,128)(2,1)S(1)} %copy-done.7), custom_call_target="tpu_custom_call" | custom-call | flops 1610612736 | bytes 10000000 | tf_op jit(solution)/shard_map/pallas_call | solution.py:467
  56.2 3.0 %collective-permute-start = (bf16[8,16,256]{2,1,0:T(8,128)(2,1)S(1)}, bf16[8,16,256]{2,1,0:T(8,128)(2,1)S(1)}, u32[]{:S(2)}, u32[]{:S(2)}) collective-permute-start(bf16[8,16,256]{2,1,0:T(8,128)(2,1)S(1)} %get-tuple-element.47), channel_id=1, source_target_pairs={{0,8},{8,16},{16,24},{1,9},{9,17},{17,25},{2,10},{10,18},{18,26},{... | collective-permute-start | bytes 196616 | tf_op jit(solution)/shard_map/ppermute | solution.py:359
  60.2 2.9 %collective-permute-start.2 = (bf16[8,18,256]{2,1,0:T(8,128)(2,1)S(1)}, bf16[8,18,256]{2,1,0:T(8,128)(2,1)S(1)}, u32[]{:S(2)}, u32[]{:S(2)}) collective-permute-start(bf16[8,18,256]{2,1,0:T(8,128)(2,1)S(1)} %pad_maximum_fusion), channel_id=1, source_target_pairs={{0,1},{1,2},{2,3},{3,4},{4,5},{5,6},{6,7},{8,9},{9,10},{10,11},{11... | collective-permute-start | bytes 221192 | tf_op jit(solution)/shard_map/ppermute | solution.py:367
  64.5 7.3 %shard_map.143 = (f32[8,256,256]{2,1,0:T(8,128)S(1)}, bf16[8,256,256]{2,1,0:T(8,128)(2,1)S(1)}) custom-call(bf16[8,256,256]{2,1,0:T(8,128)(2,1)S(1)} %copy-done.12, bf16[8,16,256]{2,1,0:T(8,128)(2,1)S(1)} %collective-permute-done.4.xlo_ref, bf16[8,16,256]{2,1,0:T(8,128)(2,1)S(1)} %collective-permute-done.5.xhi_ref, ...), custom_call_target="tpu_custom_call" | custom-call | flops 4831838208 | bytes 7000000 | tf_op jit(solution)/shard_map/pallas_call | solution.py:461
  71.8 9.2 %shard_map.144 = (bf16[8,256,256]{2,1,0:T(8,128)(2,1)S(1)}, bf16[8,256,256]{2,1,0:T(8,128)(2,1)S(1)}, bf16[2,8,32,256]{3,2,1,0:T(8,128)(2,1)S(1)}) custom-call(bf16[8,256,256]{2,1,0:T(8,128)(2,1)S(1)} %get-tuple-element.23.f_ref.field_ref, bf16[8,16,256]{2,1,0:T(8,128)(2,1)S(1)} %collective-permute-done.xlo_ref, ...), custom_call_target="tpu_custom_call" | custom-call | flops 4831838208 | bytes 10000000 | tf_op jit(solution)/shard_map/pallas_call | solution.py:476
  82.4 4.4 %collective-permute-start.8 = (bf16[8,16,256]{2,1,0:T(8,128)(2,1)S(1)}, bf16[8,16,256]{2,1,0:T(8,128)(2,1)S(1)}, u32[]{:S(2)}, u32[]{:S(2)}) collective-permute-start(bf16[8,16,256]{2,1,0:T(8,128)(2,1)S(1)} %get-tuple-element.43), channel_id=1, source_target_pairs={{0,8},{8,16},{16,24},{1,9},{9,17},{17,25},{2,10},{10,18},{18,26},{... | collective-permute-start | bytes 196616 | tf_op jit(solution)/shard_map/ppermute | solution.py:359
  86.8 8.7 %shard_map.148 = bf16[2048,128]{1,0:T(8,128)(2,1)} custom-call(bf16[8,256,256]{2,1,0:T(8,128)(2,1)S(1)} %get-tuple-element.23.f_ref.field_ref, bf16[8,16,256]{2,1,0:T(8,128)(2,1)S(1)} %collective-permute-done.xlo_ref, bf16[8,16,256]{2,1,0:T(8,128)(2,1)S(1)} %collective-permute-done.1.xhi_ref, bf16[8,18,256]{2,1,0:T(8,128)(2,1)S(1)} %collective-permute-done.2.ylo_ref, ...), custom_call_target="tpu_custom_call" | custom-call | flops 4831838208 | bytes 5000000 | tf_op jit(solution)/shard_map/pallas_call | solution.py:502
  95.5 9.1 %all-to-all-start.3 = ((bf16[32,64,128]{2,1,0:T(8,128)(2,1)}), bf16[32,64,128]{2,1,0:T(8,128)(2,1)S(1)}, u32[]{:S(2)}, u32[]{:S(2)}) async-start(bf16[32,64,128]{2,1,0:T(8,128)(2,1)} %bitcast.11), calls=%async_computation.3 | async-start | bytes 1048576 | tf_op jit(solution)/shard_map/all_to_all | solution.py:403
  105.9 3.0 %collective-permute-start.12 = (bf16[8,16,256]{2,1,0:T(8,128)(2,1)S(1)}, bf16[8,16,256]{2,1,0:T(8,128)(2,1)S(1)}, u32[]{:S(2)}, u32[]{:S(2)}) collective-permute-start(bf16[8,16,256]{2,1,0:T(8,128)(2,1)S(1)} %get-tuple-element.41), channel_id=1, source_target_pairs={{0,8},{8,16},{16,24},{1,9},{9,17},{17,25},{2,10},{10,18},{18,26},{... | collective-permute-start | bytes 196616 | tf_op jit(solution)/shard_map/ppermute | solution.py:359
  109.1 3.7 %collective-permute-start.10 = (bf16[8,18,256]{2,1,0:T(8,128)(2,1)S(1)}, bf16[8,18,256]{2,1,0:T(8,128)(2,1)S(1)}, u32[]{:S(2)}, u32[]{:S(2)}) collective-permute-start(bf16[8,18,256]{2,1,0:T(8,128)(2,1)S(1)} %pad_maximum_fusion.4), channel_id=1, source_target_pairs={{0,1},{1,2},{2,3},{3,4},{4,5},{5,6},{6,7},{8,9},{9,10},{10,11},{11... | collective-permute-start | bytes 221192 | tf_op jit(solution)/shard_map/ppermute | solution.py:367
  115.6 4.6 %collective-permute-done.11.yhi_ref = bf16[8,18,256]{2,1,0:T(8,128)(2,1)S(1)} collective-permute-done((bf16[8,18,256]{2,1,0:T(8,128)(2,1)S(1)}, bf16[8,18,256]{2,1,0:T(8,128)(2,1)S(1)}, u32[]{:S(2)}, u32[]{:S(2)}) %collective-permute-start.11) | collective-permute-done | bytes 73760 | tf_op jit(solution)/shard_map/ppermute | solution.py:368
  122.7 8.7 %shard_map.149 = bf16[2048,128]{1,0:T(8,128)(2,1)} custom-call(bf16[8,256,256]{2,1,0:T(8,128)(2,1)S(1)} %copy-done.9, bf16[8,16,256]{2,1,0:T(8,128)(2,1)S(1)} %collective-permute-done.8.xlo_ref, bf16[8,16,256]{2,1,0:T(8,128)(2,1)S(1)} %collective-permute-done.9.xhi_ref, bf16[8,18,256]{2,1,0:T(8,128)(2,1)S(1)} %collective-permute-done.10.ylo_ref, ...), custom_call_target="tpu_custom_call" | custom-call | flops 4831838208 | bytes 5000000 | tf_op jit(solution)/shard_map/pallas_call | solution.py:503
  131.4 4.9 %all-to-all-start.4 = ((bf16[32,64,128]{2,1,0:T(8,128)(2,1)}), bf16[32,64,128]{2,1,0:T(8,128)(2,1)S(1)}, u32[]{:S(2)}, u32[]{:S(2)}) async-start(bf16[32,64,128]{2,1,0:T(8,128)(2,1)} %bitcast.12), calls=%async_computation.4 | async-start | bytes 1048576 | tf_op jit(solution)/shard_map/all_to_all | solution.py:403
  136.3 3.7 %collective-permute-start.14 = (bf16[8,18,256]{2,1,0:T(8,128)(2,1)S(1)}, bf16[8,18,256]{2,1,0:T(8,128)(2,1)S(1)}, u32[]{:S(2)}, u32[]{:S(2)}) collective-permute-start(bf16[8,18,256]{2,1,0:T(8,128)(2,1)S(1)} %pad_maximum_fusion.6), channel_id=1, source_target_pairs={{0,1},{1,2},{2,3},{3,4},{4,5},{5,6},{6,7},{8,9},{9,10},{10,11},{11... | collective-permute-start | bytes 221192 | tf_op jit(solution)/shard_map/ppermute | solution.py:367
  141.6 3.5 %collective-permute-done.14.ylo_ref = bf16[8,18,256]{2,1,0:T(8,128)(2,1)S(1)} collective-permute-done((bf16[8,18,256]{2,1,0:T(8,128)(2,1)S(1)}, bf16[8,18,256]{2,1,0:T(8,128)(2,1)S(1)}, u32[]{:S(2)}, u32[]{:S(2)}) %collective-permute-start.14) | collective-permute-done | bytes 73760 | tf_op jit(solution)/shard_map/ppermute | solution.py:367
  145.1 3.0 %collective-permute-done.15.yhi_ref = bf16[8,18,256]{2,1,0:T(8,128)(2,1)S(1)} collective-permute-done((bf16[8,18,256]{2,1,0:T(8,128)(2,1)S(1)}, bf16[8,18,256]{2,1,0:T(8,128)(2,1)S(1)}, u32[]{:S(2)}, u32[]{:S(2)}) %collective-permute-start.15) | collective-permute-done | bytes 73760 | tf_op jit(solution)/shard_map/ppermute | solution.py:368
  148.1 2.8 %copy-done.2 = bf16[8,1536,256]{2,1,0:T(8,128)(2,1)S(1)} copy-done((bf16[8,1536,256]{2,1,0:T(8,128)(2,1)S(1)}, bf16[8,1536,256]{2,1,0:T(8,128)(2,1)}, u32[]{:S(2)}) %copy-start.2) | copy-done | bytes 6291480
  155.0 13.8 %shard_map.146 = bf16[256,1536]{1,0:T(8,128)(2,1)} custom-call(bf16[8,256,256]{2,1,0:T(8,128)(2,1)S(1)} %copy-done.14, bf16[8,16,256]{2,1,0:T(8,128)(2,1)S(1)} %collective-permute-done.12.xlo_ref, bf16[8,16,256]{2,1,0:T(8,128)(2,1)S(1)} %collective-permute-done.13.xhi_ref, bf16[8,18,256]{2,1,0:T(8,128)(2,1)S(1)} %collective-permute-done.14.ylo_ref, ...), custom_call_target="tpu_custom_call" | custom-call | flops 7247757312 | bytes 14000000 | tf_op jit(solution)/shard_map/pallas_call | solution.py:506
  168.8 8.0 %all-to-all-start.2 = ((bf16[32,8,1536]{2,1,0:T(8,128)(2,1)}), bf16[32,8,1536]{2,1,0:T(8,128)(2,1)S(1)}, u32[]{:S(2)}, u32[]{:S(2)}) async-start(bf16[32,8,1536]{2,1,0:T(8,128)(2,1)} %bitcast.9), calls=%async_computation.2 | async-start | bytes 1572864 | tf_op jit(solution)/shard_map/all_to_all | solution.py:511
  178.0 20.8 %all-to-all-done.2 = bf16[32,8,1536]{2,1,0:T(8,128)(2,1)S(1)} async-done(((bf16[32,8,1536]{2,1,0:T(8,128)(2,1)}), bf16[32,8,1536]{2,1,0:T(8,128)(2,1)S(1)}, u32[]{:S(2)}, u32[]{:S(2)}) %all-to-all-start.2) | async-done | bytes 786464 | tf_op jit(solution)/shard_map/all_to_all | solution.py:511
  198.8 2.6 %all-to-all-start.5 = ((bf16[32,2,64,128]{3,2,1,0:T(8,128)(2,1)}), bf16[32,2,64,128]{3,2,1,0:T(8,128)(2,1)S(1)}, u32[]{:S(2)}, u32[]{:S(2)}) async-start(bf16[32,2,64,128]{3,2,1,0:T(8,128)(2,1)} %shard_map.150), calls=%async_computation.5 | async-start | bytes 2097152 | tf_op jit(solution)/shard_map/all_to_all | solution.py:403
  201.5 2.8 %copy-done.3 = bf16[8,1536,256]{2,1,0:T(8,128)(2,1)S(1)} copy-done((bf16[8,1536,256]{2,1,0:T(8,128)(2,1)S(1)}, bf16[8,1536,256]{2,1,0:T(8,128)(2,1)}, u32[]{:S(2)}) %copy-start.3) | copy-done | bytes 6291480
  207.1 13.5 %shard_map.145 = bf16[256,1536]{1,0:T(8,128)(2,1)} custom-call(bf16[8,256,256]{2,1,0:T(8,128)(2,1)S(1)} %copy-done.10, bf16[8,16,256]{2,1,0:T(8,128)(2,1)S(1)} %collective-permute-done.8.xlo_ref, bf16[8,16,256]{2,1,0:T(8,128)(2,1)S(1)} %collective-permute-done.9.xhi_ref, bf16[8,18,256]{2,1,0:T(8,128)(2,1)S(1)} %collective-permute-done.10.ylo_ref, ...), custom_call_target="tpu_custom_call" | custom-call | flops 7247757312 | bytes 14000000 | tf_op jit(solution)/shard_map/pallas_call | solution.py:515
  221.9 7.2 %all-to-all-done.5.packed_ref = bf16[32,2,64,128]{3,2,1,0:T(8,128)(2,1)S(1)} async-done(((bf16[32,2,64,128]{3,2,1,0:T(8,128)(2,1)}), bf16[32,2,64,128]{3,2,1,0:T(8,128)(2,1)S(1)}, u32[]{:S(2)}, u32[]{:S(2)}) %all-to-all-start.5) | async-done | bytes 1048608 | tf_op jit(solution)/shard_map/all_to_all | solution.py:403
  (122 shorter events, 42.2 us)
Async XLA Ops:
  1.9 17.7 %all-to-all-start = ((s32[32,1,128]{2,1,0:T(1,128)}), s32[32,1,128]{2,1,0:T(1,128)S(1)}, u32[]{:S(2)}, u32[]{:S(2)}) async-start(s32[32,1,128]{2,1,0:T(1,128)} %broadcast_in_dim.12), calls=%async_computation | async-start | bytes 32768 | tf_op jit(solution)/shard_map/all_to_all | solution.py:403
  18.1 15.4 %copy-start.11 = (bf16[8,256,256]{2,1,0:T(8,128)(2,1)}, bf16[8,256,256]{2,1,0:T(8,128)(2,1)S(1)}, u32[]{:S(2)}) copy-start(bf16[8,256,256]{2,1,0:T(8,128)(2,1)S(1)} %get-tuple-element.27.f_ref) | copy-start | bytes 3145732
  18.1 11.7 %copy-start.29 = (s32[352]{0:T(512)S(1)}, s32[352]{0:T(512)}, u32[]{:S(2)}) copy-start(s32[352]{0:T(512)} %constant.37.clone) | copy-start | bytes 4228
  18.1 11.7 %copy-start.30 = (s32[352]{0:T(512)S(1)}, s32[352]{0:T(512)}, u32[]{:S(2)}) copy-start(s32[352]{0:T(512)} %constant.35.clone) | copy-start | bytes 4228
  18.1 11.7 %copy-start.31 = (s32[352]{0:T(512)S(1)}, s32[352]{0:T(512)}, u32[]{:S(2)}) copy-start(s32[352]{0:T(512)} %constant.34.clone) | copy-start | bytes 4228
  18.2 11.7 %copy-start.32 = (pred[352]{0:T(512)(128)(4,1)S(1)}, pred[352]{0:T(512)(128)(4,1)}, u32[]{:S(2)}) copy-start(pred[352]{0:T(512)(128)(4,1)} %constant.36.clone) | copy-start | bytes 1060
  19.6 27.8 %all-to-all-start.1 = ((bf16[32,8,1536]{2,1,0:T(8,128)(2,1)}), bf16[32,8,1536]{2,1,0:T(8,128)(2,1)S(1)}, u32[]{:S(2)}, u32[]{:S(2)}) async-start(bf16[32,8,1536]{2,1,0:T(8,128)(2,1)} %bitcast.3), calls=%async_computation.1 | async-start | bytes 1572864 | tf_op jit(solution)/shard_map/all_to_all | solution.py:412
  25.5 14.8 %collective-permute-start.5 = (bf16[8,16,256]{2,1,0:T(8,128)(2,1)S(1)}, bf16[8,16,256]{2,1,0:T(8,128)(2,1)S(1)}, u32[]{:S(2)}, u32[]{:S(2)}) collective-permute-start(bf16[8,16,256]{2,1,0:T(8,128)(2,1)S(1)} %get-tuple-element.44), channel_id=1, source_target_pairs={{8,0},{16,8},{24,16},{9,1},{17,9},{25,17},{10,2},{18,10},{26,18},{... | collective-permute-start | bytes 196616 | tf_op jit(solution)/shard_map/ppermute | solution.py:360
  26.8 13.5 %collective-permute-start.4 = (bf16[8,16,256]{2,1,0:T(8,128)(2,1)S(1)}, bf16[8,16,256]{2,1,0:T(8,128)(2,1)S(1)}, u32[]{:S(2)}, u32[]{:S(2)}) collective-permute-start(bf16[8,16,256]{2,1,0:T(8,128)(2,1)S(1)} %get-tuple-element.45), channel_id=1, source_target_pairs={{0,8},{8,16},{16,24},{1,9},{9,17},{17,25},{2,10},{10,18},{18,26},{... | collective-permute-start | bytes 196616 | tf_op jit(solution)/shard_map/ppermute | solution.py:359
  32.2 15.3 %copy-start.7 = (bf16[32,256]{1,0:T(8,128)(2,1)S(1)}, bf16[32,256]{1,0:T(8,128)(2,1)}, u32[]{:S(2)}) copy-start(bf16[32,256]{1,0:T(8,128)(2,1)} %constant.33.clone.face_ref) | copy-start | bytes 49156
  40.4 24.0 %collective-permute-start.6 = (bf16[8,18,256]{2,1,0:T(8,128)(2,1)S(1)}, bf16[8,18,256]{2,1,0:T(8,128)(2,1)S(1)}, u32[]{:S(2)}, u32[]{:S(2)}) collective-permute-start(bf16[8,18,256]{2,1,0:T(8,128)(2,1)S(1)} %pad_maximum_fusion.2), channel_id=1, source_target_pairs={{0,1},{1,2},{2,3},{3,4},{4,5},{5,6},{6,7},{8,9},{9,10},{10,11},{11... | collective-permute-start | bytes 221192 | tf_op jit(solution)/shard_map/ppermute | solution.py:367
  44.1 20.3 %collective-permute-start.7 = (bf16[8,18,256]{2,1,0:T(8,128)(2,1)S(1)}, bf16[8,18,256]{2,1,0:T(8,128)(2,1)S(1)}, u32[]{:S(2)}, u32[]{:S(2)}) collective-permute-start(bf16[8,18,256]{2,1,0:T(8,128)(2,1)S(1)} %pad_maximum_fusion.3), channel_id=1, source_target_pairs={{1,0},{2,1},{3,2},{4,3},{5,4},{6,5},{7,6},{9,8},{10,9},{11,10},{12... | collective-permute-start | bytes 221192 | tf_op jit(solution)/shard_map/ppermute | solution.py:368
  50.2 14.2 %copy-start.12 = (bf16[8,256,256]{2,1,0:T(8,128)(2,1)S(1)}, bf16[8,256,256]{2,1,0:T(8,128)(2,1)}, u32[]{:S(2)}) copy-start(bf16[8,256,256]{2,1,0:T(8,128)(2,1)} %copy-done.11) | copy-start | bytes 3145732
  50.2 14.2 %copy-start.25 = (bf16[4608,256]{1,0:T(8,128)(2,1)S(1)}, bf16[4608,256]{1,0:T(8,128)(2,1)}, u32[]{:S(2)}) copy-start(bf16[4608,256]{1,0:T(8,128)(2,1)} %copy-done.24) | copy-start | bytes 7077892
  54.9 4.4 %collective-permute-start.1 = (bf16[8,16,256]{2,1,0:T(8,128)(2,1)S(1)}, bf16[8,16,256]{2,1,0:T(8,128)(2,1)S(1)}, u32[]{:S(2)}, u32[]{:S(2)}) collective-permute-start(bf16[8,16,256]{2,1,0:T(8,128)(2,1)S(1)} %get-tuple-element.46), channel_id=1, source_target_pairs={{8,0},{16,8},{24,16},{9,1},{17,9},{25,17},{10,2},{18,10},{26,18},{... | collective-permute-start | bytes 196616 | tf_op jit(solution)/shard_map/ppermute | solution.py:360
  56.2 3.9 %collective-permute-start = (bf16[8,16,256]{2,1,0:T(8,128)(2,1)S(1)}, bf16[8,16,256]{2,1,0:T(8,128)(2,1)S(1)}, u32[]{:S(2)}, u32[]{:S(2)}) collective-permute-start(bf16[8,16,256]{2,1,0:T(8,128)(2,1)S(1)} %get-tuple-element.47), channel_id=1, source_target_pairs={{0,8},{8,16},{16,24},{1,9},{9,17},{17,25},{2,10},{10,18},{18,26},{... | collective-permute-start | bytes 196616 | tf_op jit(solution)/shard_map/ppermute | solution.py:359
  60.2 11.6 %collective-permute-start.2 = (bf16[8,18,256]{2,1,0:T(8,128)(2,1)S(1)}, bf16[8,18,256]{2,1,0:T(8,128)(2,1)S(1)}, u32[]{:S(2)}, u32[]{:S(2)}) collective-permute-start(bf16[8,18,256]{2,1,0:T(8,128)(2,1)S(1)} %pad_maximum_fusion), channel_id=1, source_target_pairs={{0,1},{1,2},{2,3},{3,4},{4,5},{5,6},{6,7},{8,9},{9,10},{10,11},{11... | collective-permute-start | bytes 221192 | tf_op jit(solution)/shard_map/ppermute | solution.py:367
  63.1 8.7 %collective-permute-start.3 = (bf16[8,18,256]{2,1,0:T(8,128)(2,1)S(1)}, bf16[8,18,256]{2,1,0:T(8,128)(2,1)S(1)}, u32[]{:S(2)}, u32[]{:S(2)}) collective-permute-start(bf16[8,18,256]{2,1,0:T(8,128)(2,1)S(1)} %pad_maximum_fusion.1), channel_id=1, source_target_pairs={{1,0},{2,1},{3,2},{4,3},{5,4},{6,5},{7,6},{9,8},{10,9},{11,10},{12... | collective-permute-start | bytes 221192 | tf_op jit(solution)/shard_map/ppermute | solution.py:368
  81.0 14.5 %copy-start.8 = (bf16[8,256,256]{2,1,0:T(8,128)(2,1)}, bf16[8,256,256]{2,1,0:T(8,128)(2,1)S(1)}, u32[]{:S(2)}) copy-start(bf16[8,256,256]{2,1,0:T(8,128)(2,1)S(1)} %get-tuple-element.31.f_ref) | copy-start | bytes 3145732
  81.0 14.5 %copy-start.13 = (bf16[8,256,256]{2,1,0:T(8,128)(2,1)}, bf16[8,256,256]{2,1,0:T(8,128)(2,1)S(1)}, u32[]{:S(2)}) copy-start(bf16[8,256,256]{2,1,0:T(8,128)(2,1)S(1)} %get-tuple-element.34.f_ref.g_ref) | copy-start | bytes 3145732
  81.1 27.9 %collective-permute-start.9 = (bf16[8,16,256]{2,1,0:T(8,128)(2,1)S(1)}, bf16[8,16,256]{2,1,0:T(8,128)(2,1)S(1)}, u32[]{:S(2)}, u32[]{:S(2)}) collective-permute-start(bf16[8,16,256]{2,1,0:T(8,128)(2,1)S(1)} %get-tuple-element.42), channel_id=1, source_target_pairs={{8,0},{16,8},{24,16},{9,1},{17,9},{25,17},{10,2},{18,10},{26,18},{... | collective-permute-start | bytes 196616 | tf_op jit(solution)/shard_map/ppermute | solution.py:360
  82.4 26.6 %collective-permute-start.8 = (bf16[8,16,256]{2,1,0:T(8,128)(2,1)S(1)}, bf16[8,16,256]{2,1,0:T(8,128)(2,1)S(1)}, u32[]{:S(2)}, u32[]{:S(2)}) collective-permute-start(bf16[8,16,256]{2,1,0:T(8,128)(2,1)S(1)} %get-tuple-element.43), channel_id=1, source_target_pairs={{0,8},{8,16},{16,24},{1,9},{9,17},{17,25},{2,10},{10,18},{18,26},{... | collective-permute-start | bytes 196616 | tf_op jit(solution)/shard_map/ppermute | solution.py:359
  95.5 35.9 %all-to-all-start.3 = ((bf16[32,64,128]{2,1,0:T(8,128)(2,1)}), bf16[32,64,128]{2,1,0:T(8,128)(2,1)S(1)}, u32[]{:S(2)}, u32[]{:S(2)}) async-start(bf16[32,64,128]{2,1,0:T(8,128)(2,1)} %bitcast.11), calls=%async_computation.3 | async-start | bytes 1048576 | tf_op jit(solution)/shard_map/all_to_all | solution.py:403
  104.6 9.5 %collective-permute-start.13 = (bf16[8,16,256]{2,1,0:T(8,128)(2,1)S(1)}, bf16[8,16,256]{2,1,0:T(8,128)(2,1)S(1)}, u32[]{:S(2)}, u32[]{:S(2)}) collective-permute-start(bf16[8,16,256]{2,1,0:T(8,128)(2,1)S(1)} %get-tuple-element.40), channel_id=1, source_target_pairs={{8,0},{16,8},{24,16},{9,1},{17,9},{25,17},{10,2},{18,10},{26,18},{... | collective-permute-start | bytes 196616 | tf_op jit(solution)/shard_map/ppermute | solution.py:360
  105.9 30.3 %collective-permute-start.12 = (bf16[8,16,256]{2,1,0:T(8,128)(2,1)S(1)}, bf16[8,16,256]{2,1,0:T(8,128)(2,1)S(1)}, u32[]{:S(2)}, u32[]{:S(2)}) collective-permute-start(bf16[8,16,256]{2,1,0:T(8,128)(2,1)S(1)} %get-tuple-element.41), channel_id=1, source_target_pairs={{0,8},{8,16},{16,24},{1,9},{9,17},{17,25},{2,10},{10,18},{18,26},{... | collective-permute-start | bytes 196616 | tf_op jit(solution)/shard_map/ppermute | solution.py:359
  109.1 6.5 %collective-permute-start.10 = (bf16[8,18,256]{2,1,0:T(8,128)(2,1)S(1)}, bf16[8,18,256]{2,1,0:T(8,128)(2,1)S(1)}, u32[]{:S(2)}, u32[]{:S(2)}) collective-permute-start(bf16[8,18,256]{2,1,0:T(8,128)(2,1)S(1)} %pad_maximum_fusion.4), channel_id=1, source_target_pairs={{0,1},{1,2},{2,3},{3,4},{4,5},{5,6},{6,7},{8,9},{9,10},{10,11},{11... | collective-permute-start | bytes 221192 | tf_op jit(solution)/shard_map/ppermute | solution.py:367
  112.8 7.4 %collective-permute-start.11 = (bf16[8,18,256]{2,1,0:T(8,128)(2,1)S(1)}, bf16[8,18,256]{2,1,0:T(8,128)(2,1)S(1)}, u32[]{:S(2)}, u32[]{:S(2)}) collective-permute-start(bf16[8,18,256]{2,1,0:T(8,128)(2,1)S(1)} %pad_maximum_fusion.5), channel_id=1, source_target_pairs={{1,0},{2,1},{3,2},{4,3},{5,4},{6,5},{7,6},{9,8},{10,9},{11,10},{12... | collective-permute-start | bytes 221192 | tf_op jit(solution)/shard_map/ppermute | solution.py:368
  131.4 37.4 %all-to-all-start.4 = ((bf16[32,64,128]{2,1,0:T(8,128)(2,1)}), bf16[32,64,128]{2,1,0:T(8,128)(2,1)S(1)}, u32[]{:S(2)}, u32[]{:S(2)}) async-start(bf16[32,64,128]{2,1,0:T(8,128)(2,1)} %bitcast.12), calls=%async_computation.4 | async-start | bytes 1048576 | tf_op jit(solution)/shard_map/all_to_all | solution.py:403
  136.3 8.8 %collective-permute-start.14 = (bf16[8,18,256]{2,1,0:T(8,128)(2,1)S(1)}, bf16[8,18,256]{2,1,0:T(8,128)(2,1)S(1)}, u32[]{:S(2)}, u32[]{:S(2)}) collective-permute-start(bf16[8,18,256]{2,1,0:T(8,128)(2,1)S(1)} %pad_maximum_fusion.6), channel_id=1, source_target_pairs={{0,1},{1,2},{2,3},{3,4},{4,5},{5,6},{6,7},{8,9},{9,10},{10,11},{11... | collective-permute-start | bytes 221192 | tf_op jit(solution)/shard_map/ppermute | solution.py:367
  140.1 8.0 %collective-permute-start.15 = (bf16[8,18,256]{2,1,0:T(8,128)(2,1)S(1)}, bf16[8,18,256]{2,1,0:T(8,128)(2,1)S(1)}, u32[]{:S(2)}, u32[]{:S(2)}) collective-permute-start(bf16[8,18,256]{2,1,0:T(8,128)(2,1)S(1)} %pad_maximum_fusion.7), channel_id=1, source_target_pairs={{1,0},{2,1},{3,2},{4,3},{5,4},{6,5},{7,6},{9,8},{10,9},{11,10},{12... | collective-permute-start | bytes 221192 | tf_op jit(solution)/shard_map/ppermute | solution.py:368
  168.8 30.0 %all-to-all-start.2 = ((bf16[32,8,1536]{2,1,0:T(8,128)(2,1)}), bf16[32,8,1536]{2,1,0:T(8,128)(2,1)S(1)}, u32[]{:S(2)}, u32[]{:S(2)}) async-start(bf16[32,8,1536]{2,1,0:T(8,128)(2,1)} %bitcast.9), calls=%async_computation.2 | async-start | bytes 1572864 | tf_op jit(solution)/shard_map/all_to_all | solution.py:511
  198.8 30.2 %all-to-all-start.5 = ((bf16[32,2,64,128]{3,2,1,0:T(8,128)(2,1)}), bf16[32,2,64,128]{3,2,1,0:T(8,128)(2,1)S(1)}, u32[]{:S(2)}, u32[]{:S(2)}) async-start(bf16[32,2,64,128]{3,2,1,0:T(8,128)(2,1)} %shard_map.150), calls=%async_computation.5 | async-start | bytes 2097152 | tf_op jit(solution)/shard_map/all_to_all | solution.py:403
  (23 other events, 55.6 us)

commit v3 on v2

v3 whole, which is shorter than its diff:
```python
import functools

import jax
import jax.numpy as jnp
import numpy as np
from jax import lax
from jax.experimental import pallas as pl
from jax.experimental.pallas import tpu as pltpu
from jax.sharding import PartitionSpec as P

LANES = 128
PAIR = 256
MIB = 1024 * 1024
BF = jnp.bfloat16
F32 = jnp.float32


def call(body, out_shape, flops, moved, scratch=(), room=16, **extra):
    return pl.pallas_call(
        body,
        out_shape=out_shape,
        scratch_shapes=list(scratch),
        compiler_params=pltpu.CompilerParams(vmem_limit_bytes=room * MIB),
        cost_estimate=pl.CostEstimate(flops=int(flops), bytes_accessed=int(moved), transcendentals=0),
        **extra,
    )


def dot(left, right):
    return jnp.dot(left, right, preferred_element_type=F32)


def dot_nt(left, right):
    return lax.dot_general(left, right, (((1,), (1,)), ((), ())), preferred_element_type=F32)


def send_kernel(cap, slots, row_ref, col_ref, feat_ref, out_ref):
    rows = feat_ref.shape[0]
    owner_row = row_ref[...] // slots
    owner_col = col_ref[...] // slots
    first = lax.broadcasted_iota(jnp.int32, (rows, rows), 0)
    second = lax.broadcasted_iota(jnp.int32, (rows, rows), 1)
    same = jnp.where((owner_col == owner_row) & (first < second), 1.0, 0.0)
    rank = jnp.sum(same, axis=0, keepdims=True)
    pos = owner_row.astype(F32) * cap + rank
    place = lax.broadcasted_iota(jnp.int32, (out_ref.shape[0], rows), 0).astype(F32)
    hot = jnp.where(place == pos, 1.0, 0.0).astype(BF)
    out_ref[...] = dot(hot, feat_ref[...]).astype(BF)


def collect_kernel(cap, slots, row_ref, col_ref, back_ref, out_ref):
    rows = out_ref.shape[0]
    owner_row = row_ref[...] // slots
    owner_col = col_ref[...] // slots
    first = lax.broadcasted_iota(jnp.int32, (rows, rows), 0)
    second = lax.broadcasted_iota(jnp.int32, (rows, rows), 1)
    same = jnp.where((owner_col == owner_row) & (second < first), 1.0, 0.0)
    rank = jnp.sum(same, axis=1, keepdims=True)
    pos = owner_col.astype(F32) * cap + rank
    place = lax.broadcasted_iota(jnp.int32, (rows, back_ref.shape[0]), 1).astype(F32)
    hot = jnp.where(place == pos, 1.0, 0.0).astype(BF)
    out_ref[...] = dot(hot, back_ref[...]).astype(BF)


def mask_kernel(cap, slots, route_ref, rel_ref, codes_ref, mask_ref, take_ref, put_ref):
    count, rows = route_ref.shape
    total = mask_ref.shape[0]
    codes = jnp.broadcast_to(codes_ref[...], (total, rows))
    hits = jnp.zeros((total, rows), F32)
    for s in range(count):
        hits = hits + jnp.where(codes == route_ref[s : s + 1, :], 1.0, 0.0)
    mask_ref[...] = jnp.broadcast_to(jnp.sum(hits, axis=1, keepdims=True), (total, LANES))
    rel = rel_ref[...]
    mine = (rel >= 0) & (rel < slots)
    mine_f = jnp.where(mine, 1.0, 0.0)
    slot_f = jnp.where(mine, rel, 0).astype(F32)
    first = lax.broadcasted_iota(jnp.int32, (rows, rows), 0)
    second = lax.broadcasted_iota(jnp.int32, (rows, rows), 1)
    tri = jnp.where(first < second, 1.0, 0.0).astype(BF)
    rank = dot(mine_f.astype(BF), tri)
    lane = lax.broadcasted_iota(jnp.int32, (count, LANES), 1)
    held = jnp.zeros((count, LANES), F32)
    for j in range(cap):
        here = jnp.where(rank == j, mine_f, 0.0)
        number = jnp.sum(here, axis=1, keepdims=True)
        value = jnp.sum(here * slot_f, axis=1, keepdims=True)
        value = value + (1.0 - number) * slots
        held = jnp.where(lane == j, value, held)
    buffers = count * cap
    place = lax.broadcasted_iota(jnp.int32, (buffers, count), 0)
    source = lax.broadcasted_iota(jnp.int32, (buffers, count), 1)
    spread = jnp.where(place // cap == source, 1.0, 0.0).astype(BF)
    wide = dot(spread, held.astype(BF))
    place = lax.broadcasted_iota(jnp.int32, (buffers, LANES), 0)
    lane = lax.broadcasted_iota(jnp.int32, (buffers, LANES), 1)
    slot_col = jnp.sum(jnp.where(place % cap == lane, wide, 0.0), axis=1, keepdims=True)
    slot_id = lax.broadcasted_iota(jnp.int32, (buffers, slots), 1).astype(F32)
    take = jnp.where(slot_col == slot_id, 1.0, 0.0)
    take_ref[...] = take.astype(BF)
    put_ref[...] = take.T.astype(BF)


GROUP = 16
FOLD = LANES // GROUP


def permutation(channels, depth):
    perm = np.zeros((channels // GROUP, PAIR, PAIR), np.float32)
    for i in range(channels // GROUP):
        for j in range(GROUP):
            for z in range(depth):
                perm[i, depth * j + z, LANES * (z // FOLD) + GROUP * ((z + i) % FOLD) + j] = 1.0
    return perm


def lane_group(rows):
    return lax.broadcasted_iota(jnp.int32, (rows, LANES), 1) // GROUP


def spread_pairs(turned_ref, out_ref):
    chunks, rows, _ = turned_ref.shape
    step = 32
    group = lane_group(step)

    def body(t, carry):
        at = pl.ds(pl.multiple_of(t * step, step), step)
        for half in range(2):
            lanes = slice(half * LANES, (half + 1) * LANES)
            parts = [turned_ref[i, at, lanes] for i in range(chunks)]
            parts = parts + [jnp.zeros((step, LANES), F32)] * (FOLD - chunks)
            for bit in (1, 2, 4):
                odd = (group & bit) != 0
                parts = [jnp.where(odd, parts[(i + bit) % FOLD], parts[i]) for i in range(FOLD)]
            for g in range(FOLD):
                value = parts[(-g) % FOLD]
                if g:
                    value = pltpu.roll(value, LANES - GROUP * g, 1)
                z = half * FOLD + g
                out_ref[z // 2, at, (z % 2) * LANES : (z % 2 + 1) * LANES] = value.astype(BF)
        return carry

    lax.fori_loop(0, rows // step, body, 0)


def gather_pairs(in_ref, turned_ref):
    chunks, rows, _ = turned_ref.shape
    step = 32
    group = lane_group(step)

    def body(t, carry):
        at = pl.ds(pl.multiple_of(t * step, step), step)
        for half in range(2):
            turned = []
            for g in range(FOLD):
                z = half * FOLD + g
                value = in_ref[z // 2, at, (z % 2) * LANES : (z % 2 + 1) * LANES].astype(F32)
                turned.append(pltpu.roll(value, GROUP * g, 1) if g else value)
            parts = [turned[(-i) % FOLD] for i in range(FOLD)]
            for bit in (1, 2, 4):
                odd = (group & bit) != 0
                parts = [jnp.where(odd, parts[(i - bit) % FOLD], parts[i]) for i in range(FOLD)]
            for i in range(chunks):
                turned_ref[i, at, half * LANES : (half + 1) * LANES] = parts[i].astype(BF)
        return carry

    lax.fori_loop(0, rows // step, body, 0)


def to_pairs_kernel(rows_ref, perm_ref, out_ref, turned_ref):
    for i in range(perm_ref.shape[0]):
        turned_ref[i] = dot(rows_ref[:, i * PAIR : (i + 1) * PAIR], perm_ref[i])
    spread_pairs(turned_ref, out_ref)


def place_kernel(put_ref, rows_ref, perm_ref, out_ref, turned_ref):
    put = put_ref[...]
    for i in range(perm_ref.shape[0]):
        held = dot(put, rows_ref[:, i * PAIR : (i + 1) * PAIR]).astype(BF)
        turned_ref[i] = dot(held, perm_ref[i])
    spread_pairs(turned_ref, out_ref)


def message_kernel(f_ref, xlo_ref, xhi_ref, pick_ref, low_ref, high_ref):
    pick = pick_ref[...]
    half = low_ref.shape[1]
    for k in range(f_ref.shape[0]):
        rows = jnp.concatenate([xlo_ref[k], f_ref[k], xhi_ref[k]], axis=0)
        sent = dot(pick, rows).astype(BF)
        low_ref[k] = sent[0:half]
        high_ref[k] = sent[half : 2 * half]


def band_kernel(first_ref, second_ref, w1_ref, w2_ref, f1_ref, f2_ref):
    channels = first_ref.shape[1]
    for ref in (w1_ref, w2_ref, f1_ref, f2_ref):
        ref[...] = jnp.zeros_like(ref)
    for a in range(3):
        for b in range(3):
            for c in range(3):
                tap = 9 * a + 3 * b + c
                back = 26 - tap
                parts = (
                    (w1_ref, first_ref[tap].T),
                    (w2_ref, second_ref[tap].T),
                    (f1_ref, first_ref[back]),
                    (f2_ref, second_ref[back]),
                )
                for zo in range(2):
                    row = ((a * 3 + b) * 4 + zo + c) * LANES
                    for ref, value in parts:
                        ref[row : row + channels, zo * LANES : zo * LANES + channels] = value


NX = 16
NY = 16
OUT_MAIN = (NX + 2) * NY
EDGE = 24
OUT_ROWS = OUT_MAIN + 2 * EDGE
MSG = 48
M_XLO = NX * NY
M_XHI = M_XLO + 2 * NY
M_YLO = M_XHI + 2 * NY
M_YHI = M_YLO + MSG
M_LOW = M_YHI + MSG
M_HIGH = M_LOW + MSG
M_EDGE = M_HIGH + MSG
M_ROWS = M_EDGE + 2 * EDGE


def twice(value):
    return jnp.concatenate([value, value], axis=1)


def put_pair(ref, lead, k, tail, value):
    value = value.astype(BF)
    ref[lead + (k,) + tail + (slice(LANES, PAIR),)] = value[:, 0:LANES]
    ref[lead + (k + 1,) + tail + (slice(0, LANES),)] = value[:, LANES:PAIR]


def clear_ends(ref, lead):
    last = ref.shape[len(lead)] - 1
    dims = ref.shape[len(lead) + 1 : -1]
    ref[lead + (0,) + (slice(None),) * len(dims) + (slice(0, LANES),)] = jnp.zeros(dims + (LANES,), BF)
    ref[lead + (last,) + (slice(None),) * len(dims) + (slice(LANES, PAIR),)] = jnp.zeros(dims + (LANES,), BF)


def put_shifted(ext_ref, k, xp, mid, before, after, row):
    ny = mid.shape[0]
    up = jnp.where(row == 0, before, pltpu.roll(mid, 1, 0))
    down = jnp.where(row == ny - 1, after, pltpu.roll(mid, ny - 1, 0))
    for b, value in enumerate((up, mid, down)):
        put_pair(ext_ref, (b,), k, (xp, slice(None)), value)


def widen_two(ext_ref, edge_ref, f_ref, xlo_ref, xhi_ref, ylo_ref, yhi_ref, low_ref, high_ref, mask_ref=None):
    pairs = f_ref.shape[0]
    for b in range(3):
        clear_ends(ext_ref, (b,))
        for a in range(3):
            clear_ends(edge_ref, (a, b))
    row = lax.broadcasted_iota(jnp.int32, (NY, PAIR), 0)

    def read(ref, k, start, size, mask_start):
        value = ref[k, start : start + size, :].astype(F32)
        if mask_ref is None:
            return value
        return value * twice(mask_ref[mask_start + start : mask_start + start + size, :])

    def body(k, carry):
        ylo = read(ylo_ref, k, 0, MSG, M_YLO)
        yhi = read(yhi_ref, k, 0, MSG, M_YHI)
        low = read(low_ref, k, 0, MSG, M_LOW)
        high = read(high_ref, k, 0, MSG, M_HIGH)
        wide = NX + 4
        for xp in range(wide):
            if xp < 2:
                mid = read(xlo_ref, k, xp * NY, NY, M_XLO)
            elif xp >= NX + 2:
                mid = read(xhi_ref, k, (xp - NX - 2) * NY, NY, M_XHI)
            else:
                mid = read(f_ref, k, (xp - 2) * NY, NY, 0)
            put_shifted(ext_ref, k, xp, mid, ylo[wide + xp : wide + xp + 1, :], yhi[xp : xp + 1, :], row)
        first = ((ylo, 0), (ylo, wide), (low, 0))
        second = ((high, wide), (yhi, 0), (yhi, wide))
        for a in range(3):
            for b in range(3):
                sides = []
                for value, start in (first[b], second[b]):
                    turn = start + a
                    if turn:
                        value = pltpu.roll(value, MSG - turn, 0)
                    sides.append(value[0:EDGE])
                put_pair(edge_ref, (a, b), k, (slice(None),), jnp.concatenate(sides, axis=0))
        return carry

    lax.fori_loop(0, pairs, body, 0)


def widen_one(ext_ref, rows_ref):
    pairs = rows_ref.shape[0]
    for b in range(3):
        clear_ends(ext_ref, (b,))
    row = lax.broadcasted_iota(jnp.int32, (NY, PAIR), 0)

    def body(k, carry):
        edges = rows_ref[k, OUT_MAIN:OUT_ROWS, :].astype(F32)
        for xp in range(NX + 2):
            mid = rows_ref[k, xp * NY : (xp + 1) * NY, :].astype(F32)
            put_shifted(ext_ref, k, xp, mid, edges[xp : xp + 1, :], edges[EDGE + xp : EDGE + xp + 1, :], row)
        return carry

    lax.fori_loop(0, pairs, body, 0)


def conv_wide(ext_ref, edge_ref, w_ref, k):
    pieces = []
    for a in range(3):
        for b in range(3):
            for j in range(2):
                main = ext_ref[b, k + j, a : a + NX + 2].reshape(OUT_MAIN, PAIR)
                pieces.append(jnp.concatenate([main, edge_ref[a, b, k + j]], axis=0))
    return dot(jnp.concatenate(pieces, axis=1), w_ref[...])


def conv_inner(ext_ref, w_ref, k):
    pieces = []
    for a in range(3):
        for b in range(3):
            for j in range(2):
                pieces.append(ext_ref[b, k + j, a : a + NX].reshape(NX * NY, PAIR))
    return dot(jnp.concatenate(pieces, axis=1), w_ref[...])


def out_mask(mask_ref):
    return twice(jnp.concatenate([
        mask_ref[M_XLO + NY : M_XLO + 2 * NY, :], mask_ref[0 : NX * NY, :],
        mask_ref[M_XHI : M_XHI + NY, :], mask_ref[M_EDGE:M_ROWS, :],
    ], axis=0))


def outer_kernel(f_ref, xlo_ref, xhi_ref, ylo_ref, yhi_ref, low_ref, high_ref, mask_ref, w_ref,
                 out_ref, outer_ref, ext_ref, edge_ref):
    widen_two(ext_ref, edge_ref, f_ref, xlo_ref, xhi_ref, ylo_ref, yhi_ref, low_ref, high_ref, mask_ref)

    def body(k, carry):
        out_ref[k] = conv_wide(ext_ref, edge_ref, w_ref, k)
        outer_ref[k] = (f_ref[k].astype(F32) * twice(mask_ref[0 : NX * NY, :])).astype(BF)
        return carry

    lax.fori_loop(0, f_ref.shape[0], body, 0)


def correlate(gt_ref, ext_ref, first_x, taps_ref, channels):
    pairs = ext_ref.shape[1] - 1

    def body(ab, carry):
        a = ab // 3
        b = ab % 3
        left = gt_ref[...]
        near = dot(left, ext_ref[b, 0:pairs, pl.ds(a + first_x, NX)].reshape(pairs * NX * NY, PAIR))
        far = dot(left, ext_ref[b, 1 : pairs + 1, pl.ds(a + first_x, NX)].reshape(pairs * NX * NY, PAIR))
        low = slice(0, channels)
        high = slice(LANES, LANES + channels)
        taps_ref[3 * ab] = near[low, 0:LANES] + near[high, LANES:PAIR]
        taps_ref[3 * ab + 1] = near[low, LANES:PAIR] + far[high, 0:LANES]
        taps_ref[3 * ab + 2] = far[low, 0:LANES] + far[high, LANES:PAIR]
        return carry

    lax.fori_loop(0, 9, body, 0)


def pack_taps(taps_ref, packed_ref, channels):
    lane = lax.broadcasted_iota(jnp.int32, (channels, LANES), 1)
    for g in range(7):
        t1 = pltpu.roll(taps_ref[4 * g + 1], 96, 1)
        t2 = pltpu.roll(taps_ref[4 * g + 2], 64, 1)
        t3 = pltpu.roll(taps_ref[4 * g + 3], 32, 1)
        blocks = (
            jnp.where(lane < 96, taps_ref[4 * g], t1),
            jnp.where(lane < 64, t1, t2),
            jnp.where(lane < 32, t2, t3),
        )
        for i, value in enumerate(blocks):
            start = (3 * g + i) * channels
            packed_ref[start : start + channels, :] = value
    rest = packed_ref.shape[0] - 21 * channels
    if rest:
        packed_ref[21 * channels :, :] = jnp.zeros((rest, LANES), F32)


def main_kernel(channels, core_ref, f_ref, xlo_ref, xhi_ref, ylo_ref, yhi_ref, low_ref, high_ref, mask_ref, w_ref,
                grad_ref, outer_ref, hg_ref, wide_ref, keep_ref, give_ref,
                ext_ref, edge_ref, act_ref, gt_ref, taps_ref, packed_ref):
    pairs = f_ref.shape[0]
    inner = NX * NY
    widen_two(ext_ref, edge_ref, f_ref, xlo_ref, xhi_ref, ylo_ref, yhi_ref, low_ref, high_ref)

    def body(k, carry):
        m = out_mask(mask_ref)
        hidden = m * conv_wide(ext_ref, edge_ref, w_ref, k)
        sigma = jax.nn.sigmoid(hidden)
        act_ref[k] = (hidden * sigma).astype(BF)
        hg_ref[k] = (m * grad_ref[k] * sigma * (1.0 + hidden * (1.0 - sigma))).astype(BF)
        return carry

    lax.fori_loop(0, pairs, body, 0)
    half = keep_ref.shape[1]
    mine = pl.ds(pl.multiple_of(core_ref[0] * half, half), half)
    other = pl.ds(pl.multiple_of((1 - core_ref[0]) * half, half), half)
    taps_ref[27] = jnp.zeros((channels, LANES), F32)
    for k in range(pairs):
        gt_ref[:, k * inner : (k + 1) * inner] = hg_ref[k, NY : NY + inner, :].T
    correlate(gt_ref, ext_ref, 1, taps_ref, channels)
    pack_taps(taps_ref, packed_ref, channels)
    keep_ref[0] = packed_ref[mine, :]
    give_ref[0] = packed_ref[other, :]
    widen_one(wide_ref, act_ref)
    for k in range(pairs):
        gt_ref[:, k * inner : (k + 1) * inner] = outer_ref[k].T
    correlate(gt_ref, wide_ref, 0, taps_ref, channels)
    pack_taps(taps_ref, packed_ref, channels)
    keep_ref[1] = packed_ref[mine, :]
    give_ref[1] = packed_ref[other, :]


def grid_grad_kernel(hg_ref, w_ref, outer_ref, perm_ref, take_ref, out_ref, ext_ref, sum_ref, turned_ref):
    widen_one(ext_ref, hg_ref)

    def body(k, carry):
        sum_ref[k] = (outer_ref[k].astype(F32) + conv_inner(ext_ref, w_ref, k)).astype(BF)
        return carry

    lax.fori_loop(0, outer_ref.shape[0], body, 0)
    gather_pairs(sum_ref, turned_ref)
    take = take_ref[...]
    for i in range(perm_ref.shape[0]):
        rows = dot_nt(turned_ref[i], perm_ref[i]).astype(BF)
        out_ref[:, i * PAIR : (i + 1) * PAIR] = dot(take, rows).astype(BF)


def block_kernel(ext_ref, mask_ref, w_ref, field_ref, perm_ref, out_ref, sum_ref, turned_ref):
    def body(k, carry):
        m = twice(mask_ref[0 : NX * NY, :])
        sum_ref[k] = (field_ref[k].astype(F32) + m * conv_inner(ext_ref, w_ref, k)).astype(BF)
        return carry

    lax.fori_loop(0, field_ref.shape[0], body, 0)
    gather_pairs(sum_ref, turned_ref)
    for i in range(perm_ref.shape[0]):
        out_ref[:, i * PAIR : (i + 1) * PAIR] = dot_nt(turned_ref[i], perm_ref[i]).astype(BF)


def pair_sum_kernel(keep_ref, got_ref, out_ref):
    count, _, chunk, _ = out_ref.shape
    for i in range(2):
        for s in range(count):
            rows = slice(s * chunk, (s + 1) * chunk)
            out_ref[s, i] = (keep_ref[i, rows, :] + got_ref[i, rows, :]).astype(BF)


def chunk_sum_kernel(in_ref, out_ref):
    count = in_ref.shape[0]
    for i in range(2):
        total = in_ref[0, i].astype(F32)
        for s in range(1, count):
            total = total + in_ref[s, i].astype(F32)
        total = total.astype(BF)
        for s in range(count):
            out_ref[s, i] = total


def unpack_kernel(factor, core_ref, mine_ref, other_ref, first_ref, second_ref, flat_ref):
    count, _, chunk, _ = mine_ref.shape
    half = count * chunk
    for i, out_ref in enumerate((first_ref, second_ref)):
        for s in range(count):
            start = core_ref[0] * half + s * chunk
            flat_ref[pl.ds(pl.multiple_of(start, chunk), chunk), :] = mine_ref[s, i].astype(F32)
            start = (1 - core_ref[0]) * half + s * chunk
            flat_ref[pl.ds(pl.multiple_of(start, chunk), chunk), :] = other_ref[s, i].astype(F32)
        unpack_taps(factor, flat_ref, out_ref)


def unpack_taps(factor, packed_ref, out_ref):
    channels = out_ref.shape[1]
    lane = lax.broadcasted_iota(jnp.int32, (channels, LANES), 1)
    for g in range(7):
        v = []
        for i in range(3):
            start = (3 * g + i) * channels
            v.append(packed_ref[start : start + channels, :] * factor)
        taps = (
            v[0],
            pltpu.roll(jnp.where(lane < 64, v[1], v[0]), 32, 1),
            pltpu.roll(jnp.where(lane < 32, v[2], v[1]), 64, 1),
            pltpu.roll(v[2], 96, 1),
        )
        for u in range(4):
            if 4 * g + u < 27:
                out_ref[4 * g + u] = taps[u][:, 0:channels]


RX = ("cx", "core")
ALL = ("cx", "core", "ry")
SAME_CORE = ("cx", "ry")


def size_of(axes):
    return int(np.prod([lax.axis_size(a) for a in ((axes,) if isinstance(axes, str) else axes)]))


def share(parts, axes):
    return lax.all_to_all(parts, axes, split_axis=0, concat_axis=0, tiled=True)


def neighbours(axes, upper, lower):
    count = size_of(axes)
    ahead = [(i, i + 1) for i in range(count - 1)]
    behind = [(t, s) for s, t in ahead]
    return lax.ppermute(upper, axes, ahead), lax.ppermute(lower, axes, behind)


def swap_cores(value):
    count = size_of(RX)
    return lax.ppermute(value, RX, [(i, i ^ 1) for i in range(count)])


def message_rows():
    cells = []
    for ys in ((0, 1), (NY - 2, NY - 1)):
        for y in ys:
            cells += [(x, y) for x in range(-2, NX + 2)]
        cells += [None] * (MSG - 2 * (NX + 4))
    return cells


def exchange(field, pick):
    pairs = field.shape[0]
    xlo, xhi = neighbours(RX, field[:, (NX - 2) * NY :, :], field[:, : 2 * NY, :])
    message = jax.ShapeDtypeStruct((pairs, MSG, PAIR), BF)
    low, high = call(message_kernel, (message, message), 5e8, 3e6)(field, xlo, xhi, pick)
    ylo, yhi = neighbours("ry", high, low)
    return xlo, xhi, ylo, yhi, low, high


def mask_cells():
    cells = [(x, y) for x in range(NX) for y in range(NY)]
    cells += [(x, y) for x in (-2, -1) for y in range(NY)]
    cells += [(x, y) for x in (NX, NX + 1) for y in range(NY)]
    for ys in ((-2, -1), (NY, NY + 1), (0, 1), (NY - 2, NY - 1)):
        for y in ys:
            cells += [(x, y) for x in range(-2, NX + 2)]
        cells += [None] * (MSG - 2 * (NX + 4))
    for y in (-1, NY):
        cells += [(x, y) for x in range(-1, NX + 1)]
        cells += [None] * (EDGE - NX - 2)
    return cells


def on_device(column_features, column_route, cotangent, first_weight, second_weight):
    count_x = size_of(RX)
    count_y = size_of("ry")
    count_all = count_x * count_y
    shard_rows, row_width = column_features.shape
    channels = first_weight.shape[1]
    depth = row_width // channels
    slots = NX * NY
    pairs = depth // 2
    chunks = channels // GROUP
    cap = 2 * shard_rows // count_all
    buffers = count_all * cap
    me_x = lax.axis_index(RX)
    me_y = lax.axis_index("ry")
    core = lax.axis_index("core").astype(jnp.int32).reshape(1)
    conv_flops = 2 * slots * pairs * 36 * LANES * PAIR

    shape = jax.ShapeDtypeStruct
    field_shape = shape((pairs, slots, PAIR), BF)
    wide_shape = shape((pairs, OUT_ROWS, PAIR), BF)
    ext = pltpu.VMEM((3, pairs + 1, NX + 4, NY, PAIR), BF)
    edge = pltpu.VMEM((3, 3, pairs + 1, 2 * EDGE, PAIR), BF)
    turned = pltpu.VMEM((chunks, slots, PAIR), F32)
    turned_low = pltpu.VMEM((chunks, slots, PAIR), BF)
    sums = pltpu.VMEM((pairs, slots, PAIR), BF)

    perm = jnp.asarray(permutation(channels, depth), BF)
    pick_np = np.zeros((2 * MSG, (NX + 4) * NY), np.float32)
    for r, cell in enumerate(message_rows()):
        if cell is not None:
            pick_np[r, (cell[0] + 2) * NY + cell[1]] = 1.0
    pick = jnp.asarray(pick_np, BF)

    route_row = column_route.reshape(1, shard_rows)
    route_col = column_route.reshape(shard_rows, 1)
    route_all = share(jnp.broadcast_to(route_row, (count_all, shard_rows)), ALL)
    outgoing = call(
        functools.partial(send_kernel, cap, slots), shape((buffers, row_width), BF),
        2 * buffers * shard_rows * row_width, 3 * shard_rows * row_width * 2,
    )(route_row, route_col, column_features)
    incoming = share(outgoing.reshape(count_all, cap, row_width), ALL).reshape(buffers, row_width)

    cells = mask_cells()
    steps = np.asarray([(0, 0) if c is None else (c[0] // NX, c[1] // NY) for c in cells], np.int32)
    local = np.asarray([-1 if c is None else (c[0] % NX) * NY + c[1] % NY for c in cells], np.int32)
    to_x = me_x + steps[:, 0]
    to_y = me_y + steps[:, 1]
    inside = (to_x >= 0) & (to_x < count_x) & (to_y >= 0) & (to_y < count_y) & (local >= 0)
    codes = jnp.where(inside, (to_x * count_y + to_y) * slots + local, -1).astype(jnp.int32)[:, None]

    cot = call(
        to_pairs_kernel, field_shape, 1e9, 3e6, (turned,),
    )(cotangent.reshape(slots, row_width), perm)
    cot_halo = exchange(cot, pick)

    band = shape((36 * LANES, PAIR), BF)
    w1, w2, f1, f2 = call(band_kernel, (band,) * 4, 1e9, 3e6)(first_weight, second_weight)

    mask, take, put = call(
        functools.partial(mask_kernel, cap, slots),
        (shape((M_ROWS, LANES), F32), shape((buffers, slots), BF), shape((slots, buffers), BF)),
        1e8, 1e6,
    )(route_all, route_all - (me_x * count_y + me_y) * slots, codes)

    act_grad, outer = call(
        outer_kernel, (shape((pairs, OUT_ROWS, PAIR), F32), field_shape),
        1.3 * conv_flops, 7e6, (ext, edge), 20,
    )(cot, *cot_halo, mask, f2)

    field = call(
        place_kernel, field_shape, 1e9, 3e6, (turned,),
    )(put, incoming, perm)
    field_halo = exchange(field, pick)

    unit = 16 * count_all
    packed_rows = -(-21 * channels // unit) * unit
    half = packed_rows // 2
    chunk = packed_rows // count_all
    smem = pl.BlockSpec(memory_space=pltpu.SMEM)
    vmem = pl.BlockSpec(memory_space=pltpu.VMEM)
    half_shape = shape((2, half, LANES), F32)
    hg, act_wide, keep, give = call(
        functools.partial(main_kernel, channels),
        (wide_shape, shape((3, pairs + 1, NX + 2, NY, PAIR), BF), half_shape, half_shape),
        3.3 * conv_flops, 10e6,
        (
            ext, edge, pltpu.VMEM((pairs, OUT_ROWS, PAIR), BF), pltpu.VMEM((PAIR, pairs * slots), BF),
            pltpu.VMEM((28, channels, LANES), F32), pltpu.VMEM((packed_rows, LANES), F32),
        ),
        28, in_specs=[smem] + [vmem] * 11,
    )(core, field, *field_halo, mask, w1, act_grad, outer)

    got = swap_cores(give)
    back = call(
        grid_grad_kernel, shape((buffers, row_width), BF), 1.2 * conv_flops, 6e6,
        (pltpu.VMEM((3, pairs + 1, NX + 2, NY, PAIR), BF), sums, turned_low),
    )(hg, f1, outer, perm, take)
    parts = share(call(
        pair_sum_kernel, shape((count_all // 2, 2, chunk, LANES), BF), 1e6, 2e6,
    )(keep, got), SAME_CORE)
    returned = share(back.reshape(count_all, cap, row_width), ALL).reshape(buffers, row_width)

    totals = share(call(
        chunk_sum_kernel, shape((count_all // 2, 2, chunk, LANES), BF), 1e6, 1e6,
    )(parts), SAME_CORE)
    block_output = call(
        block_kernel, shape((slots, row_width), BF), 1.2 * conv_flops, 8e6, (sums, turned_low),
    )(act_wide, mask, w2, field, perm)

    feature_grads = call(
        functools.partial(collect_kernel, cap, slots), shape((shard_rows, row_width), BF),
        2 * buffers * shard_rows * row_width, 3 * shard_rows * row_width * 2,
    )(route_row, route_col, returned)

    factor = float(1.0 / np.sqrt(np.float32(count_all * shard_rows * depth)))
    grads = shape(first_weight.shape, F32)
    first_grad, second_grad = call(
        functools.partial(unpack_kernel, factor), (grads, grads), 1e6, 4e6,
        (pltpu.VMEM((packed_rows, LANES), F32),), in_specs=[smem, vmem, vmem],
    )(core, totals, swap_cores(totals))
    return (block_output.reshape(cotangent.shape), feature_grads, first_grad, second_grad)


def solution(mesh):
    count_x = mesh.shape["rx"]
    fine = jax.sharding.Mesh(mesh.devices.reshape(count_x // 2, 2, mesh.shape["ry"]), ALL)
    in_specs = (P(ALL, None), P(ALL), P(RX, "ry", None), P(), P())
    out_specs = (P(RX, "ry", None), P(ALL, None), P(), P())
    return jax.shard_map(
        on_device, mesh=fine, in_specs=in_specs, out_specs=out_specs, check_vma=False
    )
```

time: 233 us -> 172 us (0.74)
  starting transfers between devices: 75.7 us -> 39.7 us
  waiting for transfers between devices: 43.5 us -> 21.6 us
  blocking collectives: 0 us -> 19.9 us
  Pallas kernels: 78.1 us -> 65.4 us
  local copies, waits for them, and re-layouts: 32.1 us -> 23.2 us
    all_to_all x2 -> x0, waiting for transfers between devices: 22.8 us -> none  [the longest x1 20.8 us: on_device(): lax.all_to_all(back.reshape(count_all, cap, row_width), axes, split_axis=...]
    all_to_all x0 -> x1, blocking collectives: none -> 19.9 us  [share(): return lax.all_to_all(parts, axes, split_axis=0, concat_axis=0, tiled=True)]
    ppermute x16 -> x10, starting transfers between devices: 38 us -> 20.5 us  [the longest x8 18.8 us: neighbours(): return (lax.ppermute(upper, axes, ahead), lax.ppermute(lower, axes, behind))]
    all_to_all x2 -> x0, starting transfers between devices: 13.8 us -> none  [the longest x1 7.97 us: on_device(): lax.all_to_all(back.reshape(count_all, cap, row_width), axes, split_axis=...]
    pallas_call x11 -> x12, Pallas kernels: 73.5 us -> 60.7 us  [the longest x1 24.8 us: on_device(): call(functools.partial(main_kernel, channels), (wide_shape, shape((3, pai...]
    all_to_all x4, waiting for transfers between devices: 7.16 us -> 19.3 us  [share(): return lax.all_to_all(parts, axes, split_axis=0, concat_axis=0, tiled=True)]
    ppermute x16 -> x10, waiting for transfers between devices: 13.5 us -> 2.31 us  [the longest x2 2.29 us: swap_cores(): return lax.ppermute(value, RX, [(i, i ^ 1) for i in range(count)])]
    unnamed x66 -> x68, local copies, waits for them, and re-layouts: 30.4 us -> 21 us
  transfers between devices with their start and end apart: 22 -> 14, of which waited for: 8 -> 5; matrix products, arithmetic and copies ran while one was open for 0% -> 1% of each run, Pallas kernels for 29% -> 22%
where the time goes in v3:
time: 172 us; the launch traced here: 171 us
  Pallas kernels  65.4 us (38%)
  starting transfers between devices  39.7 us (23%)
  local copies, waits for them, and re-layouts  23.2 us (13%)
  waiting for transfers between devices  21.6 us (13%)
  blocking collectives  19.9 us (12%)
    pallas_call x1, Pallas kernels, on_device(): call(functools.partial(main_kernel, channels), (wide_shape, shape((3, pai...  24.8 us
    unnamed x68, local copies, waits for them, and re-layouts  21 us
    all_to_all x1, blocking collectives, share(): return lax.all_to_all(parts, axes, split_axis=0, concat_axis=0, tiled=True)  19.9 us
    all_to_all x4, waiting for transfers between devices, share(): return lax.all_to_all(parts, axes, split_axis=0, concat_axis=0, tiled=True)  19.3 us
    all_to_all x4, starting transfers between devices, share(): return lax.all_to_all(parts, axes, split_axis=0, concat_axis=0, tiled=True)  19.1 us
    ppermute x8, starting transfers between devices, neighbours(): return (lax.ppermute(upper, axes, ahead), lax.ppermute(lower, axes, behind))  18.8 us
    pallas_call x1, Pallas kernels, on_device(): call(outer_kernel, (shape((pairs, OUT_ROWS, PAIR), F32), field_shape), 1....  10.3 us
    pallas_call x1, Pallas kernels, on_device(): call(grid_grad_kernel, shape((buffers, row_width), BF), 1.2 * conv_flops,...  9.83 us
  transfers between devices with their start and end apart: 14, of which 5 were waited for; matrix products, arithmetic and copies ran while one was open for 1% of the time, Pallas kernels for 22%

profile of v3, /device:TPU:0, one launch (start us, length us, event | category | flops | bytes accessed | tf_op | source)
XLA Modules:
  0.0 170.9 jit_solution(13700842030110904885)
XLA Ops:
  1.9 7.3 %all-to-all-start = ((s32[32,1,128]{2,1,0:T(1,128)}), s32[32,1,128]{2,1,0:T(1,128)S(1)}, u32[]{:S(2)}, u32[]{:S(2)}) async-start(s32[32,1,128]{2,1,0:T(1,128)} %broadcast_in_dim.12), calls=%async_computation | async-start | bytes 32768 | tf_op jit(solution)/shard_map/all_to_all | solution.py:513
  11.6 1.3 shard_map.139
  13.0 3.3 %all-to-all-done = s32[32,1,128]{2,1,0:T(1,128)S(1)} async-done(((s32[32,1,128]{2,1,0:T(1,128)}), s32[32,1,128]{2,1,0:T(1,128)S(1)}, u32[]{:S(2)}, u32[]{:S(2)}) %all-to-all-start) | async-done | bytes 16416 | tf_op jit(solution)/shard_map/all_to_all | solution.py:513
  16.2 2.6 %all-to-all-start.1 = ((bf16[32,8,1536]{2,1,0:T(8,128)(2,1)}), bf16[32,8,1536]{2,1,0:T(8,128)(2,1)S(1)}, u32[]{:S(2)}, u32[]{:S(2)}) async-start(bf16[32,8,1536]{2,1,0:T(8,128)(2,1)} %bitcast.4), calls=%async_computation.1 | async-start | bytes 1572864 | tf_op jit(solution)/shard_map/all_to_all | solution.py:513
  21.3 1.3 collective-permute-start.5
  22.6 3.0 %collective-permute-start.4 = (bf16[8,32,256]{2,1,0:T(8,128)(2,1)S(1)}, bf16[8,32,256]{2,1,0:T(8,128)(2,1)S(1)}, u32[]{:S(2)}, u32[]{:S(2)}) collective-permute-start(bf16[8,32,256]{2,1,0:T(8,128)(2,1)S(1)} %get-tuple-element.43), channel_id=1, source_target_pairs={{0,8},{8,16},{16,24},{1,9},{9,17},{17,25},{2,10},{10,18},{18,26},{... | collective-permute-start | bytes 393224 | tf_op jit(solution)/shard_map/ppermute | solution.py:520
  25.9 1.3 shard_map.138
  27.7 4.3 %collective-permute-start.6 = (bf16[8,48,256]{2,1,0:T(8,128)(2,1)S(1)}, bf16[8,48,256]{2,1,0:T(8,128)(2,1)}, u32[]{:S(2)}, u32[]{:S(2)}) collective-permute-start(bf16[8,48,256]{2,1,0:T(8,128)(2,1)S(1)} %get-tuple-element.28.high_ref), channel_id=1, source_target_pairs={{0,1},{1,2},{2,3},{3,4},{4,5},{5,6},{6,7},{8,9},{9,10},{10,11},{11... | collective-permute-start | bytes 589832 | tf_op jit(solution)/shard_map/ppermute | solution.py:520
  33.3 7.6 %all-to-all-done.1 = bf16[32,8,1536]{2,1,0:T(8,128)(2,1)S(1)} async-done(((bf16[32,8,1536]{2,1,0:T(8,128)(2,1)}), bf16[32,8,1536]{2,1,0:T(8,128)(2,1)S(1)}, u32[]{:S(2)}, u32[]{:S(2)}) %all-to-all-start.1) | async-done | bytes 786464 | tf_op jit(solution)/shard_map/all_to_all | solution.py:513
  42.9 1.5 shard_map.140.f_ref.field_ref
  44.5 1.3 collective-permute-start.1
  45.8 3.0 %collective-permute-start = (bf16[8,32,256]{2,1,0:T(8,128)(2,1)S(1)}, bf16[8,32,256]{2,1,0:T(8,128)(2,1)S(1)}, u32[]{:S(2)}, u32[]{:S(2)}) collective-permute-start(bf16[8,32,256]{2,1,0:T(8,128)(2,1)S(1)} %get-tuple-element.45), channel_id=1, source_target_pairs={{0,8},{8,16},{16,24},{1,9},{9,17},{17,25},{2,10},{10,18},{18,26},{... | collective-permute-start | bytes 393224 | tf_op jit(solution)/shard_map/ppermute | solution.py:520
  51.0 1.3 shard_map.142
  52.3 1.4 copy-done.20
  53.7 1.5 copy-done.22
  55.7 3.3 %collective-permute-start.2 = (bf16[8,48,256]{2,1,0:T(8,128)(2,1)S(1)}, bf16[8,48,256]{2,1,0:T(8,128)(2,1)S(1)}, u32[]{:S(2)}, u32[]{:S(2)}) collective-permute-start(bf16[8,48,256]{2,1,0:T(8,128)(2,1)S(1)} %get-tuple-element.24.high_ref), channel_id=1, source_target_pairs={{0,1},{1,2},{2,3},{3,4},{4,5},{5,6},{6,7},{8,9},{9,10},{10,11},{11... | collective-permute-start | bytes 589832 | tf_op jit(solution)/shard_map/ppermute | solution.py:520
  60.3 10.3 %shard_map.145 = (f32[8,336,256]{2,1,0:T(8,128)S(1)}, bf16[8,256,256]{2,1,0:T(8,128)(2,1)S(1)}) custom-call(bf16[8,256,256]{2,1,0:T(8,128)(2,1)S(1)} %shard_map.143.f_ref, bf16[8,32,256]{2,1,0:T(8,128)(2,1)S(1)} %copy-done.7, bf16[8,32,256]{2,1,0:T(8,128)(2,1)S(1)} %collective-permute-done.5.xhi_ref, bf16[8,48,256]{2,1,0:T(8,128)(2,1)} %collective-permute-done.6.ylo_ref, ...), custom_call_target="tpu_custom_call" | custom-call | flops 6281389568 | bytes 7000000 | tf_op jit(solution)/shard_map/pallas_call | solution.py:624
  70.6 24.8 %shard_map.146 = (bf16[8,336,256]{2,1,0:T(8,128)(2,1)S(1)}, bf16[3,9,18,16,256]{4,3,2,1,0:T(8,128)(2,1)S(1)}, f32[2,1024,128]{2,1,0:T(8,128)S(1)}, f32[2,1024,128]{2,1,0:T(8,128)S(1)}) custom-call(s32[1]{0:T(128)} %bitcast.core_ref, bf16[8,256,256]{2,1,0:T(8,128)(2,1)S(1)} %shard_map.140.f_ref.field_ref, ...), custom_call_target="tpu_custom_call" | custom-call | flops 15945066496 | bytes 10000000 | tf_op jit(solution)/shard_map/pallas_call | solution.py:641
  95.4 1.9 %copy-done.24 = bf16[3,9,18,16,256]{4,3,2,1,0:T(8,128)(2,1)} copy-done((bf16[3,9,18,16,256]{4,3,2,1,0:T(8,128)(2,1)}, bf16[3,9,18,16,256]{4,3,2,1,0:T(8,128)(2,1)S(1)}, u32[]{:S(2)}) %copy-start.24) | copy-done | bytes 3981336
  97.3 1.5 collective-permute-start.8
  98.8 2.3 %collective-permute-done.8.got_ref = f32[2,1024,128]{2,1,0:T(8,128)S(1)} collective-permute-done((f32[2,1024,128]{2,1,0:T(8,128)S(1)}, f32[2,1024,128]{2,1,0:T(8,128)S(1)}, u32[]{:S(2)}, u32[]{:S(2)}) %collective-permute-start.8) | collective-permute-done | bytes 1048608 | tf_op jit(solution)/shard_map/ppermute | solution.py:525
  101.3 19.9 %all_to_all.28.in_ref = bf16[16,2,64,128]{3,2,1,0:T(8,128)(2,1)S(1)} all-to-all(bf16[16,2,64,128]{3,2,1,0:T(8,128)(2,1)S(1)} %shard_map.150), channel_id=1, replica_groups=mesh['cx'=2,'core'=2,'ry'=8] {'cx','ry'}, dimensions={0} | all-to-all | bytes 1048576 | tf_op jit(solution)/shard_map/all_to_all | solution.py:513
  122.1 3.8 %all-to-all-start.4 = ((bf16[16,2,64,128]{3,2,1,0:T(8,128)(2,1)}), bf16[16,2,64,128]{3,2,1,0:T(8,128)(2,1)S(1)}, u32[]{:S(2)}, u32[]{:S(2)}) async-start(bf16[16,2,64,128]{3,2,1,0:T(8,128)(2,1)} %shard_map.151), calls=%async_computation.4 | async-start | bytes 1048576 | tf_op jit(solution)/shard_map/all_to_all | solution.py:513
  125.9 1.7 copy-done.23
  127.5 1.3 copy-done.27
  130.1 9.8 %shard_map.148 = bf16[256,1536]{1,0:T(8,128)(2,1)} custom-call(bf16[8,336,256]{2,1,0:T(8,128)(2,1)S(1)} %copy-done.27, bf16[4608,256]{1,0:T(8,128)(2,1)S(1)} %copy-done.23, bf16[8,256,256]{2,1,0:T(8,128)(2,1)S(1)} %copy-done.29, bf16[6,256,256]{2,1,0:T(8,128)(2,1)S(1)} %copy-done.10, bf16[256,256]{1,0:T(8,128)(2,1)S(1)} %copy-done.17), custom_call_target="tpu_custom_call" | custom-call | flops 5798205952 | bytes 6000000 | tf_op jit(solution)/shard_map/pallas_call | solution.py:653
  140.1 5.5 %all-to-all-start.2 = ((bf16[32,8,1536]{2,1,0:T(8,128)(2,1)}), bf16[32,8,1536]{2,1,0:T(8,128)(2,1)S(1)}, u32[]{:S(2)}, u32[]{:S(2)}) async-start(bf16[32,8,1536]{2,1,0:T(8,128)(2,1)} %bitcast.8), calls=%async_computation.2 | async-start | bytes 1572864 | tf_op jit(solution)/shard_map/all_to_all | solution.py:513
  147.1 1.7 copy-done.21
  148.7 2.1 %copy-done.25 = bf16[3,9,18,16,256]{4,3,2,1,0:T(8,128)(2,1)S(1)} copy-done((bf16[3,9,18,16,256]{4,3,2,1,0:T(8,128)(2,1)S(1)}, bf16[3,9,18,16,256]{4,3,2,1,0:T(8,128)(2,1)}, u32[]{:S(2)}) %copy-start.25) | copy-done | bytes 3981336
  150.8 8.5 %shard_map.147 = bf16[256,1536]{1,0:T(8,128)(2,1)} custom-call(bf16[3,9,18,16,256]{4,3,2,1,0:T(8,128)(2,1)S(1)} %copy-done.25, f32[560,128]{1,0:T(8,128)S(1)} %copy-done.15, bf16[4608,256]{1,0:T(8,128)(2,1)S(1)} %copy-done.21, bf16[8,256,256]{2,1,0:T(8,128)(2,1)S(1)} %shard_map.140.f_ref.field_ref, bf16[6,256,256]{2,1,0:T(8,128)(2,1)S(1)} %copy-done.11), custom_call_target="tpu_custom_call" | custom-call | flops 5798205952 | bytes 8000000 | tf_op jit(solution)/shard_map/pallas_call | solution.py:665
  159.3 8.2 %all-to-all-done.2 = bf16[32,8,1536]{2,1,0:T(8,128)(2,1)S(1)} async-done(((bf16[32,8,1536]{2,1,0:T(8,128)(2,1)}), bf16[32,8,1536]{2,1,0:T(8,128)(2,1)S(1)}, u32[]{:S(2)}, u32[]{:S(2)}) %all-to-all-start.2) | async-done | bytes 786464 | tf_op jit(solution)/shard_map/all_to_all | solution.py:513
  168.8 2.1 %shard_map.152 = (f32[27,96,96]{2,1,0:T(8,128)}, f32[27,96,96]{2,1,0:T(8,128)}) custom-call(s32[1]{0:T(128)} %bitcast.core_ref, bf16[16,2,64,128]{3,2,1,0:T(8,128)(2,1)S(1)} %all-to-all-done.4.mine_ref, bf16[16,2,64,128]{3,2,1,0:T(8,128)(2,1)S(1)} %collective-permute-done.9.other_ref), custom_call_target="tpu_custom_call" | custom-call | flops 1000000 | bytes 4000000 | tf_op jit(solution)/shard_map/pallas_call | solution.py:676
  (87 shorter events, 19.1 us)
Async XLA Ops:
  1.9 14.3 %all-to-all-start = ((s32[32,1,128]{2,1,0:T(1,128)}), s32[32,1,128]{2,1,0:T(1,128)S(1)}, u32[]{:S(2)}, u32[]{:S(2)}) async-start(s32[32,1,128]{2,1,0:T(1,128)} %broadcast_in_dim.12), calls=%async_computation | async-start | bytes 32768 | tf_op jit(solution)/shard_map/all_to_all | solution.py:513
  11.6 7.3 %copy-start.3 = (bf16[16,16,1536]{2,1,0:T(8,128)(2,1)S(1)}, bf16[16,16,1536]{2,1,0:T(8,128)(2,1)}, u32[]{:S(2)}) copy-start(bf16[16,16,1536]{2,1,0:T(8,128)(2,1)} %param.13) | copy-start | bytes 2359300
  16.2 24.6 %all-to-all-start.1 = ((bf16[32,8,1536]{2,1,0:T(8,128)(2,1)}), bf16[32,8,1536]{2,1,0:T(8,128)(2,1)S(1)}, u32[]{:S(2)}, u32[]{:S(2)}) async-start(bf16[32,8,1536]{2,1,0:T(8,128)(2,1)} %bitcast.4), calls=%async_computation.1 | async-start | bytes 1572864 | tf_op jit(solution)/shard_map/all_to_all | solution.py:513
  18.9 6.8 %copy-start.33 = (pred[560]{0:T(1024)(128)(4,1)S(1)}, pred[560]{0:T(1024)(128)(4,1)}, u32[]{:S(2)}) copy-start(pred[560]{0:T(1024)(128)(4,1)} %constant.43.clone) | copy-start | bytes 1684
  20.0 5.6 %copy-start.30 = (s32[560]{0:T(1024)S(1)}, s32[560]{0:T(1024)}, u32[]{:S(2)}) copy-start(s32[560]{0:T(1024)} %constant.44.clone) | copy-start | bytes 6724
  20.0 5.7 %copy-start.31 = (s32[560]{0:T(1024)S(1)}, s32[560]{0:T(1024)}, u32[]{:S(2)}) copy-start(s32[560]{0:T(1024)} %constant.42.clone) | copy-start | bytes 6724
  20.0 5.7 %copy-start.32 = (s32[560]{0:T(1024)S(1)}, s32[560]{0:T(1024)}, u32[]{:S(2)}) copy-start(s32[560]{0:T(1024)} %constant.41.clone) | copy-start | bytes 6724
  20.0 7.2 %copy-start.12 = (bf16[96,320]{1,0:T(8,128)(2,1)S(1)}, bf16[96,320]{1,0:T(8,128)(2,1)}, u32[]{:S(2)}) copy-start(bf16[96,320]{1,0:T(8,128)(2,1)} %constant.40.clone.pick_ref) | copy-start | bytes 184324
  21.3 5.9 %collective-permute-start.5 = (bf16[8,32,256]{2,1,0:T(8,128)(2,1)S(1)}, bf16[8,32,256]{2,1,0:T(8,128)(2,1)S(1)}, u32[]{:S(2)}, u32[]{:S(2)}) collective-permute-start(bf16[8,32,256]{2,1,0:T(8,128)(2,1)S(1)} %get-tuple-element.42), channel_id=1, source_target_pairs={{8,0},{16,8},{24,16},{9,1},{17,9},{25,17},{10,2},{18,10},{26,18},{... | collective-permute-start | bytes 393224 | tf_op jit(solution)/shard_map/ppermute | solution.py:520
  22.6 4.6 %collective-permute-start.4 = (bf16[8,32,256]{2,1,0:T(8,128)(2,1)S(1)}, bf16[8,32,256]{2,1,0:T(8,128)(2,1)S(1)}, u32[]{:S(2)}, u32[]{:S(2)}) collective-permute-start(bf16[8,32,256]{2,1,0:T(8,128)(2,1)S(1)} %get-tuple-element.43), channel_id=1, source_target_pairs={{0,8},{8,16},{16,24},{1,9},{9,17},{17,25},{2,10},{10,18},{18,26},{... | collective-permute-start | bytes 393224 | tf_op jit(solution)/shard_map/ppermute | solution.py:520
  27.2 4.8 %copy-start.13 = (f32[560,128]{1,0:T(8,128)}, f32[560,128]{1,0:T(8,128)S(1)}, u32[]{:S(2)}) copy-start(f32[560,128]{1,0:T(8,128)S(1)} %get-tuple-element.26.mask_ref) | copy-start | bytes 860164
  27.2 4.8 %copy-start.16 = (bf16[256,256]{1,0:T(8,128)(2,1)}, bf16[256,256]{1,0:T(8,128)(2,1)S(1)}, u32[]{:S(2)}) copy-start(bf16[256,256]{1,0:T(8,128)(2,1)S(1)} %get-tuple-element.37.take_ref) | copy-start | bytes 393220
  27.2 13.6 %copy-start.18 = (bf16[256,256]{1,0:T(8,128)(2,1)}, bf16[256,256]{1,0:T(8,128)(2,1)S(1)}, u32[]{:S(2)}) copy-start(bf16[256,256]{1,0:T(8,128)(2,1)S(1)} %get-tuple-element.23.put_ref) | copy-start | bytes 393220
  27.3 13.6 %copy-start.6 = (bf16[8,32,256]{2,1,0:T(8,128)(2,1)}, bf16[8,32,256]{2,1,0:T(8,128)(2,1)S(1)}, u32[]{:S(2)}) copy-start(bf16[8,32,256]{2,1,0:T(8,128)(2,1)S(1)} %collective-permute-done.4.xlo_ref) | copy-start | bytes 393220
  27.7 32.5 %collective-permute-start.6 = (bf16[8,48,256]{2,1,0:T(8,128)(2,1)S(1)}, bf16[8,48,256]{2,1,0:T(8,128)(2,1)}, u32[]{:S(2)}, u32[]{:S(2)}) collective-permute-start(bf16[8,48,256]{2,1,0:T(8,128)(2,1)S(1)} %get-tuple-element.28.high_ref), channel_id=1, source_target_pairs={{0,1},{1,2},{2,3},{3,4},{4,5},{5,6},{6,7},{8,9},{9,10},{10,11},{11... | collective-permute-start | bytes 589832 | tf_op jit(solution)/shard_map/ppermute | solution.py:520
  32.0 28.3 %collective-permute-start.7 = (bf16[8,48,256]{2,1,0:T(8,128)(2,1)S(1)}, bf16[8,48,256]{2,1,0:T(8,128)(2,1)}, u32[]{:S(2)}, u32[]{:S(2)}) collective-permute-start(bf16[8,48,256]{2,1,0:T(8,128)(2,1)S(1)} %get-tuple-element.29.low_ref), channel_id=1, source_target_pairs={{1,0},{2,1},{3,2},{4,3},{5,4},{6,5},{7,6},{9,8},{10,9},{11,10},{12... | collective-permute-start | bytes 589832 | tf_op jit(solution)/shard_map/ppermute | solution.py:520
  44.5 10.8 %collective-permute-start.1 = (bf16[8,32,256]{2,1,0:T(8,128)(2,1)S(1)}, bf16[8,32,256]{2,1,0:T(8,128)(2,1)S(1)}, u32[]{:S(2)}, u32[]{:S(2)}) collective-permute-start(bf16[8,32,256]{2,1,0:T(8,128)(2,1)S(1)} %get-tuple-element.44), channel_id=1, source_target_pairs={{8,0},{16,8},{24,16},{9,1},{17,9},{25,17},{10,2},{18,10},{26,18},{... | collective-permute-start | bytes 393224 | tf_op jit(solution)/shard_map/ppermute | solution.py:520
  45.8 9.5 %collective-permute-start = (bf16[8,32,256]{2,1,0:T(8,128)(2,1)S(1)}, bf16[8,32,256]{2,1,0:T(8,128)(2,1)S(1)}, u32[]{:S(2)}, u32[]{:S(2)}) collective-permute-start(bf16[8,32,256]{2,1,0:T(8,128)(2,1)S(1)} %get-tuple-element.45), channel_id=1, source_target_pairs={{0,8},{8,16},{16,24},{1,9},{9,17},{17,25},{2,10},{10,18},{18,26},{... | collective-permute-start | bytes 393224 | tf_op jit(solution)/shard_map/ppermute | solution.py:520
  51.0 9.2 %copy-start.7 = (bf16[8,32,256]{2,1,0:T(8,128)(2,1)S(1)}, bf16[8,32,256]{2,1,0:T(8,128)(2,1)}, u32[]{:S(2)}) copy-start(bf16[8,32,256]{2,1,0:T(8,128)(2,1)} %copy-done.6) | copy-start | bytes 393220
  51.0 9.3 %copy-start.14 = (f32[560,128]{1,0:T(8,128)S(1)}, f32[560,128]{1,0:T(8,128)}, u32[]{:S(2)}) copy-start(f32[560,128]{1,0:T(8,128)} %copy-done.13) | copy-start | bytes 860164
  55.7 14.9 %collective-permute-start.2 = (bf16[8,48,256]{2,1,0:T(8,128)(2,1)S(1)}, bf16[8,48,256]{2,1,0:T(8,128)(2,1)S(1)}, u32[]{:S(2)}, u32[]{:S(2)}) collective-permute-start(bf16[8,48,256]{2,1,0:T(8,128)(2,1)S(1)} %get-tuple-element.24.high_ref), channel_id=1, source_target_pairs={{0,1},{1,2},{2,3},{3,4},{4,5},{5,6},{6,7},{8,9},{9,10},{10,11},{11... | collective-permute-start | bytes 589832 | tf_op jit(solution)/shard_map/ppermute | solution.py:520
  58.9 11.6 %collective-permute-start.3 = (bf16[8,48,256]{2,1,0:T(8,128)(2,1)S(1)}, bf16[8,48,256]{2,1,0:T(8,128)(2,1)S(1)}, u32[]{:S(2)}, u32[]{:S(2)}) collective-permute-start(bf16[8,48,256]{2,1,0:T(8,128)(2,1)S(1)} %get-tuple-element.25.low_ref), channel_id=1, source_target_pairs={{1,0},{2,1},{3,2},{4,3},{5,4},{6,5},{7,6},{9,8},{10,9},{11,10},{12... | collective-permute-start | bytes 589832 | tf_op jit(solution)/shard_map/ppermute | solution.py:520
  70.5 24.9 %copy-start.28 = (bf16[8,256,256]{2,1,0:T(8,128)(2,1)}, bf16[8,256,256]{2,1,0:T(8,128)(2,1)S(1)}, u32[]{:S(2)}) copy-start(bf16[8,256,256]{2,1,0:T(8,128)(2,1)S(1)} %get-tuple-element.32.outer_ref) | copy-start | bytes 3145732
  97.3 23.8 %copy-start.26 = (bf16[8,336,256]{2,1,0:T(8,128)(2,1)}, bf16[8,336,256]{2,1,0:T(8,128)(2,1)S(1)}, u32[]{:S(2)}) copy-start(bf16[8,336,256]{2,1,0:T(8,128)(2,1)S(1)} %get-tuple-element.35.hg_ref) | copy-start | bytes 4128772
  97.3 3.7 %collective-permute-start.8 = (f32[2,1024,128]{2,1,0:T(8,128)S(1)}, f32[2,1024,128]{2,1,0:T(8,128)S(1)}, u32[]{:S(2)}, u32[]{:S(2)}) collective-permute-start(f32[2,1024,128]{2,1,0:T(8,128)S(1)} %get-tuple-element.39), channel_id=1, source_target_pairs={{0,8},{8,0},{16,24},{24,16},{1,9},{9,1},{17,25},{25,17},{2,10},{10... | collective-permute-start | bytes 3145736 | tf_op jit(solution)/shard_map/ppermute | solution.py:525
  101.1 24.7 %copy-start.10 = (bf16[6,256,256]{2,1,0:T(8,128)(2,1)S(1)}, bf16[6,256,256]{2,1,0:T(8,128)(2,1)}, u32[]{:S(2)}) copy-start(bf16[6,256,256]{2,1,0:T(8,128)(2,1)} %constant.39.clone.perm_ref) | copy-start | bytes 2359300
  101.1 24.7 %copy-start.17 = (bf16[256,256]{1,0:T(8,128)(2,1)S(1)}, bf16[256,256]{1,0:T(8,128)(2,1)}, u32[]{:S(2)}) copy-start(bf16[256,256]{1,0:T(8,128)(2,1)} %copy-done.16) | copy-start | bytes 393220
  122.1 18.1 %all-to-all-start.4 = ((bf16[16,2,64,128]{3,2,1,0:T(8,128)(2,1)}), bf16[16,2,64,128]{3,2,1,0:T(8,128)(2,1)S(1)}, u32[]{:S(2)}, u32[]{:S(2)}) async-start(bf16[16,2,64,128]{3,2,1,0:T(8,128)(2,1)} %shard_map.151), calls=%async_computation.4 | async-start | bytes 1048576 | tf_op jit(solution)/shard_map/all_to_all | solution.py:513
  130.1 15.8 %copy-start.15 = (f32[560,128]{1,0:T(8,128)S(1)}, f32[560,128]{1,0:T(8,128)}, u32[]{:S(2)}) copy-start(f32[560,128]{1,0:T(8,128)} %copy-done.13) | copy-start | bytes 860164
  140.1 27.4 %all-to-all-start.2 = ((bf16[32,8,1536]{2,1,0:T(8,128)(2,1)}), bf16[32,8,1536]{2,1,0:T(8,128)(2,1)S(1)}, u32[]{:S(2)}, u32[]{:S(2)}) async-start(bf16[32,8,1536]{2,1,0:T(8,128)(2,1)} %bitcast.8), calls=%async_computation.2 | async-start | bytes 1572864 | tf_op jit(solution)/shard_map/all_to_all | solution.py:513
  145.6 23.2 %collective-permute-start.9 = (bf16[16,2,64,128]{3,2,1,0:T(8,128)(2,1)S(1)}, bf16[16,2,64,128]{3,2,1,0:T(8,128)(2,1)S(1)}, u32[]{:S(2)}, u32[]{:S(2)}) collective-permute-start(bf16[16,2,64,128]{3,2,1,0:T(8,128)(2,1)S(1)} %all-to-all-done.4.mine_ref), channel_id=1, source_target_pairs={{0,8},{8,0},{16,24},{24,16},{1,9},{9,1},{17,25},{25,17},{2,10},{10... | collective-permute-start | bytes 1572872 | tf_op jit(solution)/shard_map/ppermute | solution.py:525
  150.8 16.7 %copy-start.2 = (s32[128]{0:T(128)S(1)}, s32[128]{0:T(128)}, u32[]{:S(2)}) copy-start(s32[128]{0:T(128)} %param.12) | copy-start | bytes 1540
  (16 other events, 21.0 us)

commit v4 on v3

--- a/solution.py
+++ b/solution.py
@@ -11,11 +11,12 @@
 LANES = 128
 PAIR = 256
 MIB = 1024 * 1024
+ROOM_WIDE, ROOM_NEAR, ROOM_CORR, ROOM_SMALL = 16, 12, 14, 5
 BF = jnp.bfloat16
 F32 = jnp.float32
 
 
-def call(body, out_shape, flops, moved, scratch=(), room=16, **extra):
+def call(body, out_shape, flops, moved, scratch=(), room=ROOM_SMALL, **extra):
     return pl.pallas_call(
         body,
         out_shape=out_shape,
@@ -190,25 +191,14 @@
         high_ref[k] = sent[half : 2 * half]
 
 
-def band_kernel(first_ref, second_ref, w1_ref, w2_ref, f1_ref, f2_ref):
-    channels = first_ref.shape[1]
-    for ref in (w1_ref, w2_ref, f1_ref, f2_ref):
-        ref[...] = jnp.zeros_like(ref)
-    for a in range(3):
-        for b in range(3):
-            for c in range(3):
-                tap = 9 * a + 3 * b + c
-                back = 26 - tap
-                parts = (
-                    (w1_ref, first_ref[tap].T),
-                    (w2_ref, second_ref[tap].T),
-                    (f1_ref, first_ref[back]),
-                    (f2_ref, second_ref[back]),
-                )
-                for zo in range(2):
-                    row = ((a * 3 + b) * 4 + zo + c) * LANES
-                    for ref, value in parts:
-                        ref[row : row + channels, zo * LANES : zo * LANES + channels] = value
+def build_band(band_ref, raw_ref, backward):
+    channels = raw_ref.shape[1]
+    band_ref[...] = jnp.zeros_like(band_ref)
+    for tap in range(27):
+        value = raw_ref[26 - tap] if backward else raw_ref[tap].T
+        for zo in range(2):
+            row = ((tap // 3) * 4 + zo + tap % 3) * LANES
+            band_ref[row : row + channels, zo * LANES : zo * LANES + channels] = value
 
 
 NX = 16
@@ -296,6 +286,28 @@
     lax.fori_loop(0, pairs, body, 0)
 
 
+def widen_near(ext_ref, f_ref, xlo_ref, xhi_ref, ylo_ref, yhi_ref):
+    for b in range(3):
+        clear_ends(ext_ref, (b,))
+    row = lax.broadcasted_iota(jnp.int32, (NY, PAIR), 0)
+    wide = NX + 4
+
+    def body(k, carry):
+        ylo = ylo_ref[k].astype(F32)
+        yhi = yhi_ref[k].astype(F32)
+        for xp in range(NX + 2):
+            if xp == 0:
+                mid = xlo_ref[k, NY : 2 * NY, :].astype(F32)
+            elif xp == NX + 1:
+                mid = xhi_ref[k, 0:NY, :].astype(F32)
+            else:
+                mid = f_ref[k, (xp - 1) * NY : xp * NY, :].astype(F32)
+            put_shifted(ext_ref, k, xp, mid, ylo[wide + xp + 1 : wide + xp + 2, :], yhi[xp + 1 : xp + 2, :], row)
+        return carry
+
+    lax.fori_loop(0, f_ref.shape[0], body, 0)
+
+
 def widen_one(ext_ref, rows_ref):
     pairs = rows_ref.shape[0]
     for b in range(3):
@@ -338,8 +350,9 @@
     ], axis=0))
 
 
-def outer_kernel(f_ref, xlo_ref, xhi_ref, ylo_ref, yhi_ref, low_ref, high_ref, mask_ref, w_ref,
-                 out_ref, outer_ref, ext_ref, edge_ref):
+def outer_kernel(f_ref, xlo_ref, xhi_ref, ylo_ref, yhi_ref, low_ref, high_ref, mask_ref, raw_ref,
+                 out_ref, outer_ref, ext_ref, edge_ref, w_ref):
+    build_band(w_ref, raw_ref, True)
     widen_two(ext_ref, edge_ref, f_ref, xlo_ref, xhi_ref, ylo_ref, yhi_ref, low_ref, high_ref, mask_ref)
 
     def body(k, carry):
@@ -360,7 +373,7 @@
         near = dot(left, ext_ref[b, 0:pairs, pl.ds(a + first_x, NX)].reshape(pairs * NX * NY, PAIR))
         far = dot(left, ext_ref[b, 1 : pairs + 1, pl.ds(a + first_x, NX)].reshape(pairs * NX * NY, PAIR))
         low = slice(0, channels)
-        high = slice(LANES, LANES + channels)
+        high = slice(channels, 2 * channels)
         taps_ref[3 * ab] = near[low, 0:LANES] + near[high, LANES:PAIR]
         taps_ref[3 * ab + 1] = near[low, LANES:PAIR] + far[high, 0:LANES]
         taps_ref[3 * ab + 2] = far[low, 0:LANES] + far[high, LANES:PAIR]
@@ -388,11 +401,9 @@
         packed_ref[21 * channels :, :] = jnp.zeros((rest, LANES), F32)
 
 
-def main_kernel(channels, core_ref, f_ref, xlo_ref, xhi_ref, ylo_ref, yhi_ref, low_ref, high_ref, mask_ref, w_ref,
-                grad_ref, outer_ref, hg_ref, wide_ref, keep_ref, give_ref,
-                ext_ref, edge_ref, act_ref, gt_ref, taps_ref, packed_ref):
-    pairs = f_ref.shape[0]
-    inner = NX * NY
+def hidden_kernel(f_ref, xlo_ref, xhi_ref, ylo_ref, yhi_ref, low_ref, high_ref, mask_ref, raw_ref, grad_ref,
+                  act_ref, hg_ref, ext_ref, edge_ref, w_ref):
+    build_band(w_ref, raw_ref, False)
     widen_two(ext_ref, edge_ref, f_ref, xlo_ref, xhi_ref, ylo_ref, yhi_ref, low_ref, high_ref)
 
     def body(k, carry):
@@ -403,27 +414,38 @@
         hg_ref[k] = (m * grad_ref[k] * sigma * (1.0 + hidden * (1.0 - sigma))).astype(BF)
         return carry
 
-    lax.fori_loop(0, pairs, body, 0)
+    lax.fori_loop(0, f_ref.shape[0], body, 0)
+
+
+def turn(gt_ref, g_ref, start, channels):
+    inner = NX * NY
+    for k in range(g_ref.shape[0]):
+        value = g_ref[k, start : start + inner, :].T
+        gt_ref[0:channels, k * inner : (k + 1) * inner] = value[0:channels]
+        gt_ref[channels : 2 * channels, k * inner : (k + 1) * inner] = value[LANES : LANES + channels]
+
+
+def corr_kernel(channels, core_ref, f_ref, xlo_ref, xhi_ref, ylo_ref, yhi_ref, hg_ref, act_ref, outer_ref,
+                keep_ref, give_ref, ext_ref, gt_ref, taps_ref, packed_ref):
     half = keep_ref.shape[1]
     mine = pl.ds(pl.multiple_of(core_ref[0] * half, half), half)
     other = pl.ds(pl.multiple_of((1 - core_ref[0]) * half, half), half)
     taps_ref[27] = jnp.zeros((channels, LANES), F32)
-    for k in range(pairs):
-        gt_ref[:, k * inner : (k + 1) * inner] = hg_ref[k, NY : NY + inner, :].T
-    correlate(gt_ref, ext_ref, 1, taps_ref, channels)
-    pack_taps(taps_ref, packed_ref, channels)
-    keep_ref[0] = packed_ref[mine, :]
-    give_ref[0] = packed_ref[other, :]
-    widen_one(wide_ref, act_ref)
-    for k in range(pairs):
-        gt_ref[:, k * inner : (k + 1) * inner] = outer_ref[k].T
-    correlate(gt_ref, wide_ref, 0, taps_ref, channels)
-    pack_taps(taps_ref, packed_ref, channels)
-    keep_ref[1] = packed_ref[mine, :]
-    give_ref[1] = packed_ref[other, :]
-
-
-def grid_grad_kernel(hg_ref, w_ref, outer_ref, perm_ref, take_ref, out_ref, ext_ref, sum_ref, turned_ref):
+    for i in range(2):
+        if i == 0:
+            widen_near(ext_ref, f_ref, xlo_ref, xhi_ref, ylo_ref, yhi_ref)
+            turn(gt_ref, hg_ref, NY, channels)
+        else:
+            widen_one(ext_ref, act_ref)
+            turn(gt_ref, outer_ref, 0, channels)
+        correlate(gt_ref, ext_ref, 0, taps_ref, channels)
+        pack_taps(taps_ref, packed_ref, channels)
+        keep_ref[i] = packed_ref[mine, :]
+        give_ref[i] = packed_ref[other, :]
+
+
+def grid_grad_kernel(hg_ref, raw_ref, outer_ref, perm_ref, take_ref, out_ref, ext_ref, sum_ref, turned_ref, w_ref):
+    build_band(w_ref, raw_ref, True)
     widen_one(ext_ref, hg_ref)
 
     def body(k, carry):
@@ -438,7 +460,10 @@
         out_ref[:, i * PAIR : (i + 1) * PAIR] = dot(take, rows).astype(BF)
 
 
-def block_kernel(ext_ref, mask_ref, w_ref, field_ref, perm_ref, out_ref, sum_ref, turned_ref):
+def block_kernel(act_ref, mask_ref, raw_ref, field_ref, perm_ref, out_ref, ext_ref, sum_ref, turned_ref, w_ref):
+    build_band(w_ref, raw_ref, False)
+    widen_one(ext_ref, act_ref)
+
     def body(k, carry):
         m = twice(mask_ref[0 : NX * NY, :])
         sum_ref[k] = (field_ref[k].astype(F32) + m * conv_inner(ext_ref, w_ref, k)).astype(BF)
@@ -612,20 +637,20 @@
     )(cotangent.reshape(slots, row_width), perm)
     cot_halo = exchange(cot, pick)
 
-    band = shape((36 * LANES, PAIR), BF)
-    w1, w2, f1, f2 = call(band_kernel, (band,) * 4, 1e9, 3e6)(first_weight, second_weight)
-
     mask, take, put = call(
         functools.partial(mask_kernel, cap, slots),
         (shape((M_ROWS, LANES), F32), shape((buffers, slots), BF), shape((slots, buffers), BF)),
         1e8, 1e6,
     )(route_all, route_all - (me_x * count_y + me_y) * slots, codes)
 
+    band = pltpu.VMEM((36 * LANES, PAIR), BF)
+    ext_near = pltpu.VMEM((3, pairs + 1, NX + 2, NY, PAIR), BF)
     act_grad, outer = call(
         outer_kernel, (shape((pairs, OUT_ROWS, PAIR), F32), field_shape),
-        1.3 * conv_flops, 7e6, (ext, edge), 20,
-    )(cot, *cot_halo, mask, f2)
-
+        1.3 * conv_flops, 7e6, (ext, edge, band), ROOM_WIDE,
+    )(cot, *cot_halo, mask, second_weight)
+
+    incoming, act_grad = lax.optimization_barrier((incoming, act_grad))
     field = call(
         place_kernel, field_shape, 1e9, 3e6, (turned,),
     )(put, incoming, perm)
@@ -638,33 +663,41 @@
     smem = pl.BlockSpec(memory_space=pltpu.SMEM)
     vmem = pl.BlockSpec(memory_space=pltpu.VMEM)
     half_shape = shape((2, half, LANES), F32)
-    hg, act_wide, keep, give = call(
-        functools.partial(main_kernel, channels),
-        (wide_shape, shape((3, pairs + 1, NX + 2, NY, PAIR), BF), half_shape, half_shape),
-        3.3 * conv_flops, 10e6,
+    act, hg = call(
+        hidden_kernel, (wide_shape, wide_shape), 1.3 * conv_flops, 8e6, (ext, edge, band), ROOM_WIDE,
+    )(field, *field_halo, mask, first_weight, act_grad)
+
+    back = call(
+        grid_grad_kernel, shape((buffers, row_width), BF), 1.2 * conv_flops, 6e6,
+        (ext_near, sums, turned_low, band), ROOM_NEAR,
+    )(hg, first_weight, outer, perm, take)
+    returned = share(back.reshape(count_all, cap, row_width), ALL).reshape(buffers, row_width)
+
+    act, back = lax.optimization_barrier((act, back))
+    keep, give = call(
+        functools.partial(corr_kernel, channels), (half_shape, half_shape), 2 * conv_flops, 10e6,
         (
-            ext, edge, pltpu.VMEM((pairs, OUT_ROWS, PAIR), BF), pltpu.VMEM((PAIR, pairs * slots), BF),
+            ext_near, pltpu.VMEM((2 * channels, pairs * slots), BF),
             pltpu.VMEM((28, channels, LANES), F32), pltpu.VMEM((packed_rows, LANES), F32),
         ),
-        28, in_specs=[smem] + [vmem] * 11,
-    )(core, field, *field_halo, mask, w1, act_grad, outer)
-
+        ROOM_CORR, in_specs=[smem] + [vmem] * 8,
+    )(core, field, *field_halo[:4], hg, act, outer)
     got = swap_cores(give)
-    back = call(
-        grid_grad_kernel, shape((buffers, row_width), BF), 1.2 * conv_flops, 6e6,
-        (pltpu.VMEM((3, pairs + 1, NX + 2, NY, PAIR), BF), sums, turned_low),
-    )(hg, f1, outer, perm, take)
-    parts = share(call(
+    got, returned = lax.optimization_barrier((got, returned))
+    sent = call(
         pair_sum_kernel, shape((count_all // 2, 2, chunk, LANES), BF), 1e6, 2e6,
-    )(keep, got), SAME_CORE)
-    returned = share(back.reshape(count_all, cap, row_width), ALL).reshape(buffers, row_width)
-
+    )(keep, got)
+    parts = share(sent, SAME_CORE)
+    act, sent = lax.optimization_barrier((act, sent))
+    block_output = call(
+        block_kernel, shape((slots, row_width), BF), 1.2 * conv_flops, 8e6,
+        (ext_near, sums, turned_low, band), ROOM_NEAR,
+    )(act, mask, second_weight, field, perm)
+
+    parts, block_output = lax.optimization_barrier((parts, block_output))
     totals = share(call(
         chunk_sum_kernel, shape((count_all // 2, 2, chunk, LANES), BF), 1e6, 1e6,
     )(parts), SAME_CORE)
-    block_output = call(
-        block_kernel, shape((slots, row_width), BF), 1.2 * conv_flops, 8e6, (sums, turned_low),
-    )(act_wide, mask, w2, field, perm)
 
     feature_grads = call(
         functools.partial(collect_kernel, cap, slots), shape((shard_rows, row_width), BF),

time: 172 us -> 176 us (1.023)
  starting transfers between devices: 39.7 us -> 47.1 us
  local copies, waits for them, and re-layouts: 23.2 us -> 20.7 us
  Pallas kernels: 65.4 us -> 63.5 us
    all_to_all x4, waiting for transfers between devices: 19.3 us -> 4.98 us  [share(): return lax.all_to_all(parts, axes, split_axis=0, concat_axis=0, tiled=True)]
    ppermute x8, waiting for transfers between devices: 0.02 us -> 14.1 us  [neighbours(): return (lax.ppermute(upper, axes, ahead), lax.ppermute(lower, axes, behind))]
    all_to_all x4, starting transfers between devices: 19.1 us -> 24 us  [share(): return lax.all_to_all(parts, axes, split_axis=0, concat_axis=0, tiled=True)]
    ppermute x8, starting transfers between devices: 18.8 us -> 22.8 us  [neighbours(): return (lax.ppermute(upper, axes, ahead), lax.ppermute(lower, axes, behind))]
    pallas_call x2, Pallas kernels: 26.1 us -> 23.6 us  [the longest x1 13.8 us: on_device(): call(functools.partial(corr_kernel, channels), (half_shape, half_shape),...]
    unnamed x68, local copies, waits for them, and re-layouts: 21 us -> 18.5 us
  transfers between devices with their start and end apart: 14 -> 14, of which waited for: 5 -> 11; matrix products, arithmetic and copies ran while one was open for 1% -> 1% of each run, Pallas kernels for 22% -> 22%
where the time goes in v4:
time: 176 us; the launch traced here: 175 us
  Pallas kernels  63.5 us (36%)
  starting transfers between devices  47.1 us (27%)
  waiting for transfers between devices  22.2 us (13%)
  local copies, waits for them, and re-layouts  20.7 us (12%)
  blocking collectives  20.7 us (12%)
    all_to_all x4, starting transfers between devices, share(): return lax.all_to_all(parts, axes, split_axis=0, concat_axis=0, tiled=True)  24 us
    ppermute x8, starting transfers between devices, neighbours(): return (lax.ppermute(upper, axes, ahead), lax.ppermute(lower, axes, behind))  22.8 us
    all_to_all x1, blocking collectives, share(): return lax.all_to_all(parts, axes, split_axis=0, concat_axis=0, tiled=True)  20.7 us
    unnamed x68, local copies, waits for them, and re-layouts  18.5 us
    ppermute x8, waiting for transfers between devices, neighbours(): return (lax.ppermute(upper, axes, ahead), lax.ppermute(lower, axes, behind))  14.1 us
    pallas_call x1, Pallas kernels, on_device(): call(functools.partial(corr_kernel, channels), (half_shape, half_shape),...  13.8 us
    pallas_call x1, Pallas kernels, on_device(): call(grid_grad_kernel, shape((buffers, row_width), BF), 1.2 * conv_flops,...  10.2 us
    pallas_call x1, Pallas kernels, on_device(): call(hidden_kernel, (wide_shape, wide_shape), 1.3 * conv_flops, 8000000.0...  9.82 us
  transfers between devices with their start and end apart: 14, of which 11 were waited for; matrix products, arithmetic and copies ran while one was open for 1% of the time, Pallas kernels for 22%

profile of v4, /device:TPU:0, one launch (start us, length us, event | category | flops | bytes accessed | tf_op | source)
XLA Modules:
  0.0 175.2 jit_solution(3235627154464553892)
XLA Ops:
  0.6 1.3 broadcast_in_dim.12
  1.9 7.3 %all-to-all-start = ((s32[32,1,128]{2,1,0:T(1,128)}), s32[32,1,128]{2,1,0:T(1,128)S(1)}, u32[]{:S(2)}, u32[]{:S(2)}) async-start(s32[32,1,128]{2,1,0:T(1,128)} %broadcast_in_dim.12), calls=%async_computation | async-start | bytes 32768 | tf_op jit(solution)/shard_map/all_to_all | solution.py:538
  11.6 1.3 shard_map.139
  13.0 3.3 %all-to-all-done = s32[32,1,128]{2,1,0:T(1,128)S(1)} async-done(((s32[32,1,128]{2,1,0:T(1,128)}), s32[32,1,128]{2,1,0:T(1,128)S(1)}, u32[]{:S(2)}, u32[]{:S(2)}) %all-to-all-start) | async-done | bytes 16416 | tf_op jit(solution)/shard_map/all_to_all | solution.py:538
  16.2 2.6 %all-to-all-start.1 = ((bf16[32,8,1536]{2,1,0:T(8,128)(2,1)}), bf16[32,8,1536]{2,1,0:T(8,128)(2,1)S(1)}, u32[]{:S(2)}, u32[]{:S(2)}) async-start(bf16[32,8,1536]{2,1,0:T(8,128)(2,1)} %bitcast.4), calls=%async_computation.1 | async-start | bytes 1572864 | tf_op jit(solution)/shard_map/all_to_all | solution.py:538
  22.5 1.4 collective-permute-start.1
  23.9 3.0 %collective-permute-start = (bf16[8,32,256]{2,1,0:T(8,128)(2,1)S(1)}, bf16[8,32,256]{2,1,0:T(8,128)(2,1)S(1)}, u32[]{:S(2)}, u32[]{:S(2)}) collective-permute-start(bf16[8,32,256]{2,1,0:T(8,128)(2,1)S(1)} %get-tuple-element.53), channel_id=1, source_target_pairs={{0,8},{8,16},{16,24},{1,9},{9,17},{17,25},{2,10},{10,18},{18,26},{... | collective-permute-start | bytes 393224 | tf_op jit(solution)/shard_map/ppermute | solution.py:545
  28.3 3.6 %collective-permute-start.2 = (bf16[8,48,256]{2,1,0:T(8,128)(2,1)S(1)}, bf16[8,48,256]{2,1,0:T(8,128)(2,1)S(1)}, u32[]{:S(2)}, u32[]{:S(2)}) collective-permute-start(bf16[8,48,256]{2,1,0:T(8,128)(2,1)S(1)} %get-tuple-element.28.high_ref), channel_id=1, source_target_pairs={{0,1},{1,2},{2,3},{3,4},{4,5},{5,6},{6,7},{8,9},{9,10},{10,11},{11... | collective-permute-start | bytes 589832 | tf_op jit(solution)/shard_map/ppermute | solution.py:545
  31.9 1.3 collective-permute-start.3
  33.2 1.3 shard_map.138
  35.7 4.0 %collective-permute-done.3.yhi_ref = bf16[8,48,256]{2,1,0:T(8,128)(2,1)S(1)} collective-permute-done((bf16[8,48,256]{2,1,0:T(8,128)(2,1)S(1)}, bf16[8,48,256]{2,1,0:T(8,128)(2,1)S(1)}, u32[]{:S(2)}, u32[]{:S(2)}) %collective-permute-start.3) | collective-permute-done | bytes 196640 | tf_op jit(solution)/shard_map/ppermute | solution.py:545
  39.7 9.5 %shard_map.142 = (f32[8,336,256]{2,1,0:T(8,128)S(1)}, bf16[8,256,256]{2,1,0:T(8,128)(2,1)S(1)}) custom-call(bf16[8,256,256]{2,1,0:T(8,128)(2,1)S(1)} %shard_map.140.f_ref, bf16[8,32,256]{2,1,0:T(8,128)(2,1)S(1)} %collective-permute-done.xlo_ref, bf16[8,32,256]{2,1,0:T(8,128)(2,1)S(1)} %collective-permute-done.1.xhi_ref, ...), custom_call_target="tpu_custom_call" | custom-call | flops 6281389568 | bytes 7000000 | tf_op jit(solution)/shard_map/pallas_call | solution.py:648
  50.0 1.5 copy-done.20
  53.6 1.5 shard_map.143.f_ref.field_ref
  55.2 1.4 collective-permute-start.5
  56.6 6.5 %collective-permute-start.4 = (bf16[8,32,256]{2,1,0:T(8,128)(2,1)S(1)}, bf16[8,32,256]{2,1,0:T(8,128)(2,1)S(1)}, u32[]{:S(2)}, u32[]{:S(2)}) collective-permute-start(bf16[8,32,256]{2,1,0:T(8,128)(2,1)S(1)} %get-tuple-element.51), channel_id=1, source_target_pairs={{0,8},{8,16},{16,24},{1,9},{9,17},{17,25},{2,10},{10,18},{18,26},{... | collective-permute-start | bytes 393224 | tf_op jit(solution)/shard_map/ppermute | solution.py:545
  64.5 4.1 %collective-permute-start.6 = (bf16[8,48,256]{2,1,0:T(8,128)(2,1)S(1)}, bf16[8,48,256]{2,1,0:T(8,128)(2,1)S(1)}, u32[]{:S(2)}, u32[]{:S(2)}) collective-permute-start(bf16[8,48,256]{2,1,0:T(8,128)(2,1)S(1)} %get-tuple-element.33.high_ref), channel_id=1, source_target_pairs={{0,1},{1,2},{2,3},{3,4},{4,5},{5,6},{6,7},{8,9},{9,10},{10,11},{11... | collective-permute-start | bytes 589832 | tf_op jit(solution)/shard_map/ppermute | solution.py:545
  68.6 1.4 collective-permute-start.7
  70.1 1.7 collective-permute-done.6.ylo_ref
  71.8 6.2 %collective-permute-done.7.yhi_ref = bf16[8,48,256]{2,1,0:T(8,128)(2,1)S(1)} collective-permute-done((bf16[8,48,256]{2,1,0:T(8,128)(2,1)S(1)}, bf16[8,48,256]{2,1,0:T(8,128)(2,1)S(1)}, u32[]{:S(2)}, u32[]{:S(2)}) %collective-permute-start.7) | collective-permute-done | bytes 196640 | tf_op jit(solution)/shard_map/ppermute | solution.py:545
  78.0 9.8 %shard_map.145 = (bf16[8,336,256]{2,1,0:T(8,128)(2,1)S(1)}, bf16[8,336,256]{2,1,0:T(8,128)(2,1)S(1)}) custom-call(bf16[8,256,256]{2,1,0:T(8,128)(2,1)S(1)} %shard_map.143.f_ref.field_ref, bf16[8,32,256]{2,1,0:T(8,128)(2,1)S(1)} %collective-permute-done.4.xlo_ref, bf16[8,32,256]{2,1,0:T(8,128)(2,1)S(1)} %collective-permute-done.5.xhi_ref, ...), custom_call_target="tpu_custom_call" | custom-call | flops 6281389568 | bytes 8000000 | tf_op jit(solution)/shard_map/pallas_call | solution.py:666
  87.9 10.2 %shard_map.146 = bf16[256,1536]{1,0:T(8,128)(2,1)} custom-call(bf16[8,336,256]{2,1,0:T(8,128)(2,1)S(1)} %get-tuple-element.36.hg_ref, bf16[27,96,96]{2,1,0:T(8,128)(2,1)S(1)} %copy-done.6, bf16[8,256,256]{2,1,0:T(8,128)(2,1)S(1)} %copy-done.28, bf16[6,256,256]{2,1,0:T(8,128)(2,1)S(1)} %copy-done.12, bf16[256,256]{1,0:T(8,128)(2,1)S(1)} %copy-done.19), custom_call_target="tpu_custom_call" | custom-call | flops 5798205952 | bytes 6000000 | tf_op jit(solution)/shard_map/pallas_call | solution.py:670
  98.0 7.8 %all-to-all-start.2 = ((bf16[32,8,1536]{2,1,0:T(8,128)(2,1)}), bf16[32,8,1536]{2,1,0:T(8,128)(2,1)S(1)}, u32[]{:S(2)}, u32[]{:S(2)}) async-start(bf16[32,8,1536]{2,1,0:T(8,128)(2,1)} %bitcast.7), calls=%async_computation.2 | async-start | bytes 1572864 | tf_op jit(solution)/shard_map/all_to_all | solution.py:538
  106.8 1.3 copy-done.23
  108.1 1.3 copy-done.26
  110.7 13.8 %shard_map.147 = (f32[2,1024,128]{2,1,0:T(8,128)S(1)}, f32[2,1024,128]{2,1,0:T(8,128)S(1)}) custom-call(s32[1]{0:T(128)} %bitcast.core_ref, bf16[8,256,256]{2,1,0:T(8,128)(2,1)S(1)} %shard_map.143.f_ref.field_ref, bf16[8,32,256]{2,1,0:T(8,128)(2,1)S(1)} %copy-done.10, bf16[8,32,256]{2,1,0:T(8,128)(2,1)S(1)} %collective-permute-done.5.xhi_ref, ...), custom_call_target="tpu_custom_call" | custom-call | flops 9663676416 | bytes 10000000 | tf_op jit(solution)/shard_map/pallas_call | solution.py:677
  124.8 2.4 %collective-permute-done.8.got_ref = f32[2,1024,128]{2,1,0:T(8,128)S(1)} collective-permute-done((f32[2,1024,128]{2,1,0:T(8,128)S(1)}, f32[2,1024,128]{2,1,0:T(8,128)S(1)}, u32[]{:S(2)}, u32[]{:S(2)}) %collective-permute-start.8) | collective-permute-done | bytes 1048608 | tf_op jit(solution)/shard_map/ppermute | solution.py:550
  128.7 6.3 %all-to-all-start.3 = ((bf16[16,2,64,128]{3,2,1,0:T(8,128)(2,1)}), bf16[16,2,64,128]{3,2,1,0:T(8,128)(2,1)S(1)}, u32[]{:S(2)}, u32[]{:S(2)}) async-start(bf16[16,2,64,128]{3,2,1,0:T(8,128)(2,1)} %shard_map.148), calls=%async_computation.3 | async-start | bytes 1048576 | tf_op jit(solution)/shard_map/all_to_all | solution.py:538
  138.4 1.3 copy-done.24
  139.8 9.6 %shard_map.149 = bf16[256,1536]{1,0:T(8,128)(2,1)} custom-call(bf16[8,336,256]{2,1,0:T(8,128)(2,1)S(1)} %copy-done.24, f32[560,128]{1,0:T(8,128)S(1)} %copy-done.17, bf16[27,96,96]{2,1,0:T(8,128)(2,1)S(1)} %copy-done.8, bf16[8,256,256]{2,1,0:T(8,128)(2,1)S(1)} %copy-done.2, bf16[6,256,256]{2,1,0:T(8,128)(2,1)S(1)} %copy-done.13), custom_call_target="tpu_custom_call" | custom-call | flops 5798205952 | bytes 8000000 | tf_op jit(solution)/shard_map/pallas_call | solution.py:692
  150.6 20.7 %all_to_all.28.mine_ref = bf16[16,2,64,128]{3,2,1,0:T(8,128)(2,1)S(1)} all-to-all(bf16[16,2,64,128]{3,2,1,0:T(8,128)(2,1)S(1)} %shard_map.151), channel_id=1, replica_groups=mesh['cx'=2,'core'=2,'ry'=8] {'cx','ry'}, dimensions={0} | all-to-all | bytes 1048576 | tf_op jit(solution)/shard_map/all_to_all | solution.py:538
  173.1 2.1 %shard_map.152 = (f32[27,96,96]{2,1,0:T(8,128)}, f32[27,96,96]{2,1,0:T(8,128)}) custom-call(s32[1]{0:T(128)} %bitcast.core_ref, bf16[16,2,64,128]{3,2,1,0:T(8,128)(2,1)S(1)} %all_to_all.28.mine_ref, bf16[16,2,64,128]{3,2,1,0:T(8,128)(2,1)S(1)} %collective-permute-done.9.other_ref), custom_call_target="tpu_custom_call" | custom-call | flops 1000000 | bytes 4000000 | tf_op jit(solution)/shard_map/pallas_call | solution.py:709
  (87 shorter events, 23.1 us)
Async XLA Ops:
  1.9 14.3 %all-to-all-start = ((s32[32,1,128]{2,1,0:T(1,128)}), s32[32,1,128]{2,1,0:T(1,128)S(1)}, u32[]{:S(2)}, u32[]{:S(2)}) async-start(s32[32,1,128]{2,1,0:T(1,128)} %broadcast_in_dim.12), calls=%async_computation | async-start | bytes 32768 | tf_op jit(solution)/shard_map/all_to_all | solution.py:538
  16.2 36.2 %all-to-all-start.1 = ((bf16[32,8,1536]{2,1,0:T(8,128)(2,1)}), bf16[32,8,1536]{2,1,0:T(8,128)(2,1)S(1)}, u32[]{:S(2)}, u32[]{:S(2)}) async-start(bf16[32,8,1536]{2,1,0:T(8,128)(2,1)} %bitcast.4), calls=%async_computation.1 | async-start | bytes 1572864 | tf_op jit(solution)/shard_map/all_to_all | solution.py:538
  21.2 5.8 %copy-start.30 = (s32[560]{0:T(1024)S(1)}, s32[560]{0:T(1024)}, u32[]{:S(2)}) copy-start(s32[560]{0:T(1024)} %constant.44.clone) | copy-start | bytes 6724
  21.2 5.8 %copy-start.31 = (s32[560]{0:T(1024)S(1)}, s32[560]{0:T(1024)}, u32[]{:S(2)}) copy-start(s32[560]{0:T(1024)} %constant.42.clone) | copy-start | bytes 6724
  21.2 5.8 %copy-start.32 = (s32[560]{0:T(1024)S(1)}, s32[560]{0:T(1024)}, u32[]{:S(2)}) copy-start(s32[560]{0:T(1024)} %constant.41.clone) | copy-start | bytes 6724
  21.2 5.8 %copy-start.33 = (pred[560]{0:T(1024)(128)(4,1)S(1)}, pred[560]{0:T(1024)(128)(4,1)}, u32[]{:S(2)}) copy-start(pred[560]{0:T(1024)(128)(4,1)} %constant.43.clone) | copy-start | bytes 1684
  21.2 6.7 %copy-start.14 = (bf16[96,320]{1,0:T(8,128)(2,1)S(1)}, bf16[96,320]{1,0:T(8,128)(2,1)}, u32[]{:S(2)}) copy-start(bf16[96,320]{1,0:T(8,128)(2,1)} %constant.40.clone.pick_ref) | copy-start | bytes 184324
  22.4 17.3 %copy-start.7 = (bf16[27,96,96]{2,1,0:T(8,128)(2,1)S(1)}, bf16[27,96,96]{2,1,0:T(8,128)(2,1)}, u32[]{:S(2)}) copy-start(bf16[27,96,96]{2,1,0:T(8,128)(2,1)} %raw_ref.7) | copy-start | bytes 1492996
  22.5 4.7 %collective-permute-start.1 = (bf16[8,32,256]{2,1,0:T(8,128)(2,1)S(1)}, bf16[8,32,256]{2,1,0:T(8,128)(2,1)S(1)}, u32[]{:S(2)}, u32[]{:S(2)}) collective-permute-start(bf16[8,32,256]{2,1,0:T(8,128)(2,1)S(1)} %get-tuple-element.52), channel_id=1, source_target_pairs={{8,0},{16,8},{24,16},{9,1},{17,9},{25,17},{10,2},{18,10},{26,18},{... | collective-permute-start | bytes 393224 | tf_op jit(solution)/shard_map/ppermute | solution.py:545
  23.9 4.0 %collective-permute-start = (bf16[8,32,256]{2,1,0:T(8,128)(2,1)S(1)}, bf16[8,32,256]{2,1,0:T(8,128)(2,1)S(1)}, u32[]{:S(2)}, u32[]{:S(2)}) collective-permute-start(bf16[8,32,256]{2,1,0:T(8,128)(2,1)S(1)} %get-tuple-element.53), channel_id=1, source_target_pairs={{0,8},{8,16},{16,24},{1,9},{9,17},{17,25},{2,10},{10,18},{18,26},{... | collective-permute-start | bytes 393224 | tf_op jit(solution)/shard_map/ppermute | solution.py:545
  28.3 7.4 %collective-permute-start.2 = (bf16[8,48,256]{2,1,0:T(8,128)(2,1)S(1)}, bf16[8,48,256]{2,1,0:T(8,128)(2,1)S(1)}, u32[]{:S(2)}, u32[]{:S(2)}) collective-permute-start(bf16[8,48,256]{2,1,0:T(8,128)(2,1)S(1)} %get-tuple-element.28.high_ref), channel_id=1, source_target_pairs={{0,1},{1,2},{2,3},{3,4},{4,5},{5,6},{6,7},{8,9},{9,10},{10,11},{11... | collective-permute-start | bytes 589832 | tf_op jit(solution)/shard_map/ppermute | solution.py:545
  31.9 7.8 %collective-permute-start.3 = (bf16[8,48,256]{2,1,0:T(8,128)(2,1)S(1)}, bf16[8,48,256]{2,1,0:T(8,128)(2,1)S(1)}, u32[]{:S(2)}, u32[]{:S(2)}) collective-permute-start(bf16[8,48,256]{2,1,0:T(8,128)(2,1)S(1)} %get-tuple-element.29.low_ref), channel_id=1, source_target_pairs={{1,0},{2,1},{3,2},{4,3},{5,4},{6,5},{7,6},{9,8},{10,9},{11,10},{12... | collective-permute-start | bytes 589832 | tf_op jit(solution)/shard_map/ppermute | solution.py:545
  50.0 1.5 copy-start.20
  53.6 24.4 %copy-start.21 = (f32[8,336,256]{2,1,0:T(8,128)S(1)}, f32[8,336,256]{2,1,0:T(8,128)}, u32[]{:S(2)}) copy-start(f32[8,336,256]{2,1,0:T(8,128)} %copy-done.20) | copy-start | bytes 8257540
  55.1 50.7 %copy-start.1 = (bf16[8,256,256]{2,1,0:T(8,128)(2,1)}, bf16[8,256,256]{2,1,0:T(8,128)(2,1)S(1)}, u32[]{:S(2)}) copy-start(bf16[8,256,256]{2,1,0:T(8,128)(2,1)S(1)} %shard_map.143.f_ref.field_ref) | copy-start | bytes 3145732
  55.1 22.8 %copy-start.6 = (bf16[27,96,96]{2,1,0:T(8,128)(2,1)S(1)}, bf16[27,96,96]{2,1,0:T(8,128)(2,1)}, u32[]{:S(2)}) copy-start(bf16[27,96,96]{2,1,0:T(8,128)(2,1)} %raw_ref.6) | copy-start | bytes 1492996
  55.2 22.8 %copy-start.16 = (f32[560,128]{1,0:T(8,128)S(1)}, f32[560,128]{1,0:T(8,128)}, u32[]{:S(2)}) copy-start(f32[560,128]{1,0:T(8,128)} %copy-done.15) | copy-start | bytes 860164
  55.2 7.9 %collective-permute-start.5 = (bf16[8,32,256]{2,1,0:T(8,128)(2,1)S(1)}, bf16[8,32,256]{2,1,0:T(8,128)(2,1)S(1)}, u32[]{:S(2)}, u32[]{:S(2)}) collective-permute-start(bf16[8,32,256]{2,1,0:T(8,128)(2,1)S(1)} %get-tuple-element.50), channel_id=1, source_target_pairs={{8,0},{16,8},{24,16},{9,1},{17,9},{25,17},{10,2},{18,10},{26,18},{... | collective-permute-start | bytes 393224 | tf_op jit(solution)/shard_map/ppermute | solution.py:545
  56.6 7.4 %collective-permute-start.4 = (bf16[8,32,256]{2,1,0:T(8,128)(2,1)S(1)}, bf16[8,32,256]{2,1,0:T(8,128)(2,1)S(1)}, u32[]{:S(2)}, u32[]{:S(2)}) collective-permute-start(bf16[8,32,256]{2,1,0:T(8,128)(2,1)S(1)} %get-tuple-element.51), channel_id=1, source_target_pairs={{0,8},{8,16},{16,24},{1,9},{9,17},{17,25},{2,10},{10,18},{18,26},{... | collective-permute-start | bytes 393224 | tf_op jit(solution)/shard_map/ppermute | solution.py:545
  64.1 23.7 %copy-start.9 = (bf16[8,32,256]{2,1,0:T(8,128)(2,1)}, bf16[8,32,256]{2,1,0:T(8,128)(2,1)S(1)}, u32[]{:S(2)}) copy-start(bf16[8,32,256]{2,1,0:T(8,128)(2,1)S(1)} %collective-permute-done.4.xlo_ref) | copy-start | bytes 393220
  64.5 7.3 %collective-permute-start.6 = (bf16[8,48,256]{2,1,0:T(8,128)(2,1)S(1)}, bf16[8,48,256]{2,1,0:T(8,128)(2,1)S(1)}, u32[]{:S(2)}, u32[]{:S(2)}) collective-permute-start(bf16[8,48,256]{2,1,0:T(8,128)(2,1)S(1)} %get-tuple-element.33.high_ref), channel_id=1, source_target_pairs={{0,1},{1,2},{2,3},{3,4},{4,5},{5,6},{6,7},{8,9},{9,10},{10,11},{11... | collective-permute-start | bytes 589832 | tf_op jit(solution)/shard_map/ppermute | solution.py:545
  68.6 19.2 %copy-start.19 = (bf16[256,256]{1,0:T(8,128)(2,1)S(1)}, bf16[256,256]{1,0:T(8,128)(2,1)}, u32[]{:S(2)}) copy-start(bf16[256,256]{1,0:T(8,128)(2,1)} %copy-done.18) | copy-start | bytes 393220
  68.6 19.2 %copy-start.28 = (bf16[8,256,256]{2,1,0:T(8,128)(2,1)S(1)}, bf16[8,256,256]{2,1,0:T(8,128)(2,1)}, u32[]{:S(2)}) copy-start(bf16[8,256,256]{2,1,0:T(8,128)(2,1)} %copy-done.27) | copy-start | bytes 3145732
  68.6 9.3 %collective-permute-start.7 = (bf16[8,48,256]{2,1,0:T(8,128)(2,1)S(1)}, bf16[8,48,256]{2,1,0:T(8,128)(2,1)S(1)}, u32[]{:S(2)}, u32[]{:S(2)}) collective-permute-start(bf16[8,48,256]{2,1,0:T(8,128)(2,1)S(1)} %get-tuple-element.34.low_ref), channel_id=1, source_target_pairs={{1,0},{2,1},{3,2},{4,3},{5,4},{6,5},{7,6},{9,8},{10,9},{11,10},{12... | collective-permute-start | bytes 589832 | tf_op jit(solution)/shard_map/ppermute | solution.py:545
  87.8 10.2 %copy-start.22 = (bf16[8,336,256]{2,1,0:T(8,128)(2,1)}, bf16[8,336,256]{2,1,0:T(8,128)(2,1)S(1)}, u32[]{:S(2)}) copy-start(bf16[8,336,256]{2,1,0:T(8,128)(2,1)S(1)} %get-tuple-element.44.act_ref) | copy-start | bytes 4128772
  87.8 10.2 %copy-start.25 = (bf16[8,336,256]{2,1,0:T(8,128)(2,1)}, bf16[8,336,256]{2,1,0:T(8,128)(2,1)S(1)}, u32[]{:S(2)}) copy-start(bf16[8,336,256]{2,1,0:T(8,128)(2,1)S(1)} %get-tuple-element.36.hg_ref) | copy-start | bytes 4128772
  98.0 29.8 %all-to-all-start.2 = ((bf16[32,8,1536]{2,1,0:T(8,128)(2,1)}), bf16[32,8,1536]{2,1,0:T(8,128)(2,1)S(1)}, u32[]{:S(2)}, u32[]{:S(2)}) async-start(bf16[32,8,1536]{2,1,0:T(8,128)(2,1)} %bitcast.7), calls=%async_computation.2 | async-start | bytes 1572864 | tf_op jit(solution)/shard_map/all_to_all | solution.py:538
  124.5 2.7 %collective-permute-start.8 = (f32[2,1024,128]{2,1,0:T(8,128)S(1)}, f32[2,1024,128]{2,1,0:T(8,128)S(1)}, u32[]{:S(2)}, u32[]{:S(2)}) collective-permute-start(f32[2,1024,128]{2,1,0:T(8,128)S(1)} %get-tuple-element.42), channel_id=1, source_target_pairs={{0,8},{8,0},{16,24},{24,16},{1,9},{9,1},{17,25},{25,17},{2,10},{10... | collective-permute-start | bytes 3145736 | tf_op jit(solution)/shard_map/ppermute | solution.py:550
  127.8 7.1 %copy-start.17 = (f32[560,128]{1,0:T(8,128)S(1)}, f32[560,128]{1,0:T(8,128)}, u32[]{:S(2)}) copy-start(f32[560,128]{1,0:T(8,128)} %copy-done.15) | copy-start | bytes 860164
  128.7 21.8 %all-to-all-start.3 = ((bf16[16,2,64,128]{3,2,1,0:T(8,128)(2,1)}), bf16[16,2,64,128]{3,2,1,0:T(8,128)(2,1)S(1)}, u32[]{:S(2)}, u32[]{:S(2)}) async-start(bf16[16,2,64,128]{3,2,1,0:T(8,128)(2,1)} %shard_map.148), calls=%async_computation.3 | async-start | bytes 1048576 | tf_op jit(solution)/shard_map/all_to_all | solution.py:538
  149.4 21.8 %copy-start.4 = (s32[128]{0:T(128)S(1)}, s32[128]{0:T(128)}, u32[]{:S(2)}) copy-start(s32[128]{0:T(128)} %param.12) | copy-start | bytes 1540
  171.2 1.9 %collective-permute-start.9 = (bf16[16,2,64,128]{3,2,1,0:T(8,128)(2,1)S(1)}, bf16[16,2,64,128]{3,2,1,0:T(8,128)(2,1)S(1)}, u32[]{:S(2)}, u32[]{:S(2)}) collective-permute-start(bf16[16,2,64,128]{3,2,1,0:T(8,128)(2,1)S(1)} %all_to_all.28.mine_ref), channel_id=1, source_target_pairs={{0,8},{8,0},{16,24},{24,16},{1,9},{9,1},{17,25},{25,17},{2,10},{10... | collective-permute-start | bytes 1572872 | tf_op jit(solution)/shard_map/ppermute | solution.py:550
  (16 other events, 17.0 us)

commit v5 on v4

--- a/solution.py
+++ b/solution.py
@@ -36,7 +36,8 @@
 
 
 def send_kernel(cap, slots, row_ref, col_ref, feat_ref, out_ref):
-    rows = feat_ref.shape[0]
+    rows, width = feat_ref.shape
+    buffers = out_ref.shape[0]
     owner_row = row_ref[...] // slots
     owner_col = col_ref[...] // slots
     first = lax.broadcasted_iota(jnp.int32, (rows, rows), 0)
@@ -44,9 +45,22 @@
     same = jnp.where((owner_col == owner_row) & (first < second), 1.0, 0.0)
     rank = jnp.sum(same, axis=0, keepdims=True)
     pos = owner_row.astype(F32) * cap + rank
-    place = lax.broadcasted_iota(jnp.int32, (out_ref.shape[0], rows), 0).astype(F32)
-    hot = jnp.where(place == pos, 1.0, 0.0).astype(BF)
-    out_ref[...] = dot(hot, feat_ref[...]).astype(BF)
+    place = lax.broadcasted_iota(jnp.int32, (buffers, rows), 0)
+    hot = jnp.where(place.astype(F32) == pos, 1.0, 0.0).astype(BF)
+    out_ref[:, 0:width] = dot(hot, feat_ref[...]).astype(BF)
+    slot_row = (row_ref[...] % slots).astype(F32)
+    kind = place % cap
+    told = jnp.where(kind == 0, owner_row.astype(F32), jnp.where(kind == 1, slot_row, 0.0))
+    out_ref[:, width : width + rows] = told.astype(BF)
+
+
+def told_rows(cap, in_ref, which):
+    buffers, width = in_ref.shape
+    count = buffers // cap
+    source = lax.broadcasted_iota(jnp.int32, (count, buffers), 0)
+    place = lax.broadcasted_iota(jnp.int32, (count, buffers), 1)
+    pick = jnp.where(place == source * cap + which, 1.0, 0.0).astype(BF)
+    return dot(pick, in_ref[:, width - LANES : width])
 
 
 def collect_kernel(cap, slots, row_ref, col_ref, back_ref, out_ref):
@@ -63,20 +77,23 @@
     out_ref[...] = dot(hot, back_ref[...]).astype(BF)
 
 
-def mask_kernel(cap, slots, route_ref, rel_ref, codes_ref, mask_ref, take_ref, put_ref):
-    count, rows = route_ref.shape
+def mask_kernel(cap, slots, in_ref, codes_ref, mask_ref, route_ref):
     total = mask_ref.shape[0]
-    codes = jnp.broadcast_to(codes_ref[...], (total, rows))
-    hits = jnp.zeros((total, rows), F32)
-    for s in range(count):
+    route_ref[...] = told_rows(cap, in_ref, 0) * slots + told_rows(cap, in_ref, 1)
+    codes = jnp.broadcast_to(codes_ref[...], (total, LANES))
+    hits = jnp.zeros((total, LANES), F32)
+    for s in range(route_ref.shape[0]):
         hits = hits + jnp.where(codes == route_ref[s : s + 1, :], 1.0, 0.0)
     mask_ref[...] = jnp.broadcast_to(jnp.sum(hits, axis=1, keepdims=True), (total, LANES))
-    rel = rel_ref[...]
-    mine = (rel >= 0) & (rel < slots)
-    mine_f = jnp.where(mine, 1.0, 0.0)
-    slot_f = jnp.where(mine, rel, 0).astype(F32)
-    first = lax.broadcasted_iota(jnp.int32, (rows, rows), 0)
-    second = lax.broadcasted_iota(jnp.int32, (rows, rows), 1)
+
+
+def slot_table(cap, slots, me, in_ref):
+    buffers = in_ref.shape[0]
+    count = buffers // cap
+    mine_f = jnp.where(told_rows(cap, in_ref, 0) == me.astype(F32), 1.0, 0.0)
+    slot_f = told_rows(cap, in_ref, 1)
+    first = lax.broadcasted_iota(jnp.int32, (LANES, LANES), 0)
+    second = lax.broadcasted_iota(jnp.int32, (LANES, LANES), 1)
     tri = jnp.where(first < second, 1.0, 0.0).astype(BF)
     rank = dot(mine_f.astype(BF), tri)
     lane = lax.broadcasted_iota(jnp.int32, (count, LANES), 1)
@@ -87,7 +104,6 @@
         value = jnp.sum(here * slot_f, axis=1, keepdims=True)
         value = value + (1.0 - number) * slots
         held = jnp.where(lane == j, value, held)
-    buffers = count * cap
     place = lax.broadcasted_iota(jnp.int32, (buffers, count), 0)
     source = lax.broadcasted_iota(jnp.int32, (buffers, count), 1)
     spread = jnp.where(place // cap == source, 1.0, 0.0).astype(BF)
@@ -96,9 +112,7 @@
     lane = lax.broadcasted_iota(jnp.int32, (buffers, LANES), 1)
     slot_col = jnp.sum(jnp.where(place % cap == lane, wide, 0.0), axis=1, keepdims=True)
     slot_id = lax.broadcasted_iota(jnp.int32, (buffers, slots), 1).astype(F32)
-    take = jnp.where(slot_col == slot_id, 1.0, 0.0)
-    take_ref[...] = take.astype(BF)
-    put_ref[...] = take.T.astype(BF)
+    return jnp.where(slot_col == slot_id, 1.0, 0.0)
 
 
 GROUP = 16
@@ -173,8 +187,10 @@
     spread_pairs(turned_ref, out_ref)
 
 
-def place_kernel(put_ref, rows_ref, perm_ref, out_ref, turned_ref):
-    put = put_ref[...]
+def place_kernel(cap, slots, me_ref, rows_ref, perm_ref, out_ref, take_ref, turned_ref):
+    take = slot_table(cap, slots, me_ref[0], rows_ref)
+    take_ref[...] = take.astype(BF)
+    put = take.T.astype(BF)
     for i in range(perm_ref.shape[0]):
         held = dot(put, rows_ref[:, i * PAIR : (i + 1) * PAIR]).astype(BF)
         turned_ref[i] = dot(held, perm_ref[i])
@@ -617,12 +633,12 @@
 
     route_row = column_route.reshape(1, shard_rows)
     route_col = column_route.reshape(shard_rows, 1)
-    route_all = share(jnp.broadcast_to(route_row, (count_all, shard_rows)), ALL)
+    told_width = row_width + LANES
     outgoing = call(
-        functools.partial(send_kernel, cap, slots), shape((buffers, row_width), BF),
+        functools.partial(send_kernel, cap, slots), shape((buffers, told_width), BF),
         2 * buffers * shard_rows * row_width, 3 * shard_rows * row_width * 2,
     )(route_row, route_col, column_features)
-    incoming = share(outgoing.reshape(count_all, cap, row_width), ALL).reshape(buffers, row_width)
+    incoming = share(outgoing.reshape(count_all, cap, told_width), ALL).reshape(buffers, told_width)
 
     cells = mask_cells()
     steps = np.asarray([(0, 0) if c is None else (c[0] // NX, c[1] // NY) for c in cells], np.int32)
@@ -630,19 +646,26 @@
     to_x = me_x + steps[:, 0]
     to_y = me_y + steps[:, 1]
     inside = (to_x >= 0) & (to_x < count_x) & (to_y >= 0) & (to_y < count_y) & (local >= 0)
-    codes = jnp.where(inside, (to_x * count_y + to_y) * slots + local, -1).astype(jnp.int32)[:, None]
+    codes = jnp.where(inside, (to_x * count_y + to_y) * slots + local, -1).astype(F32)[:, None]
+    me = (me_x * count_y + me_y).astype(jnp.int32).reshape(1)
 
     cot = call(
         to_pairs_kernel, field_shape, 1e9, 3e6, (turned,),
     )(cotangent.reshape(slots, row_width), perm)
     cot_halo = exchange(cot, pick)
 
-    mask, take, put = call(
-        functools.partial(mask_kernel, cap, slots),
-        (shape((M_ROWS, LANES), F32), shape((buffers, slots), BF), shape((slots, buffers), BF)),
-        1e8, 1e6,
-    )(route_all, route_all - (me_x * count_y + me_y) * slots, codes)
-
+    smem = pl.BlockSpec(memory_space=pltpu.SMEM)
+    vmem = pl.BlockSpec(memory_space=pltpu.VMEM)
+    field, take = call(
+        functools.partial(place_kernel, cap, slots), (field_shape, shape((buffers, slots), BF)), 1e9, 3e6,
+        (turned,), in_specs=[smem, vmem, vmem],
+    )(me, incoming, perm)
+    field_halo = exchange(field, pick)
+
+    mask = call(
+        functools.partial(mask_kernel, cap, slots), shape((M_ROWS, LANES), F32), 1e8, 1e6,
+        (pltpu.VMEM((count_all, LANES), F32),),
+    )(incoming, codes)
     band = pltpu.VMEM((36 * LANES, PAIR), BF)
     ext_near = pltpu.VMEM((3, pairs + 1, NX + 2, NY, PAIR), BF)
     act_grad, outer = call(
@@ -650,18 +673,10 @@
         1.3 * conv_flops, 7e6, (ext, edge, band), ROOM_WIDE,
     )(cot, *cot_halo, mask, second_weight)
 
-    incoming, act_grad = lax.optimization_barrier((incoming, act_grad))
-    field = call(
-        place_kernel, field_shape, 1e9, 3e6, (turned,),
-    )(put, incoming, perm)
-    field_halo = exchange(field, pick)
-
     unit = 16 * count_all
     packed_rows = -(-21 * channels // unit) * unit
     half = packed_rows // 2
     chunk = packed_rows // count_all
-    smem = pl.BlockSpec(memory_space=pltpu.SMEM)
-    vmem = pl.BlockSpec(memory_space=pltpu.VMEM)
     half_shape = shape((2, half, LANES), F32)
     act, hg = call(
         hidden_kernel, (wide_shape, wide_shape), 1.3 * conv_flops, 8e6, (ext, edge, band), ROOM_WIDE,

time: 176 us -> 160 us (0.909)
  waiting for transfers between devices: 22.2 us -> 14.7 us
  starting transfers between devices: 47.1 us -> 40.7 us
  local copies, waits for them, and re-layouts: 20.7 us -> 16.4 us
    ppermute x8, waiting for transfers between devices: 14.1 us -> 0.95 us  [neighbours(): return (lax.ppermute(upper, axes, ahead), lax.ppermute(lower, axes, behind))]
    all_to_all x4 -> x3, waiting for transfers between devices: 4.98 us -> 10.7 us  [share(): return lax.all_to_all(parts, axes, split_axis=0, concat_axis=0, tiled=True)]
    ppermute x8, starting transfers between devices: 22.8 us -> 18.9 us  [neighbours(): return (lax.ppermute(upper, axes, ahead), lax.ppermute(lower, axes, behind))]
    unnamed x68 -> x76, local copies, waits for them, and re-layouts: 18.5 us -> 15.4 us
    all_to_all x4 -> x3, starting transfers between devices: 24 us -> 21.5 us  [share(): return lax.all_to_all(parts, axes, split_axis=0, concat_axis=0, tiled=True)]
  transfers between devices with their start and end apart: 14 -> 13, of which waited for: 11 -> 5; matrix products, arithmetic and copies ran while one was open for 1% -> 0% of each run, Pallas kernels for 22% -> 26%
where the time goes in v5:
time: 160 us; the launch traced here: 159 us
  Pallas kernels  65 us (41%)
  starting transfers between devices  40.7 us (25%)
  blocking collectives  20.7 us (13%)
  local copies, waits for them, and re-layouts  16.4 us (10%)
  waiting for transfers between devices  14.7 us (9%)
    all_to_all x3, starting transfers between devices, share(): return lax.all_to_all(parts, axes, split_axis=0, concat_axis=0, tiled=True)  21.5 us
    all_to_all x1, blocking collectives, share(): return lax.all_to_all(parts, axes, split_axis=0, concat_axis=0, tiled=True)  20.7 us
    ppermute x8, starting transfers between devices, neighbours(): return (lax.ppermute(upper, axes, ahead), lax.ppermute(lower, axes, behind))  18.9 us
    unnamed x76, local copies, waits for them, and re-layouts  15.4 us
    pallas_call x1, Pallas kernels, on_device(): call(functools.partial(corr_kernel, channels), (half_shape, half_shape),...  13.8 us
    all_to_all x3, waiting for transfers between devices, share(): return lax.all_to_all(parts, axes, split_axis=0, concat_axis=0, tiled=True)  10.7 us
    pallas_call x1, Pallas kernels, on_device(): call(outer_kernel, (shape((pairs, OUT_ROWS, PAIR), F32), field_shape), 1....  10.6 us
    pallas_call x1, Pallas kernels, on_device(): call(grid_grad_kernel, shape((buffers, row_width), BF), 1.2 * conv_flops,...  10.2 us
  transfers between devices with their start and end apart: 13, of which 5 were waited for; matrix products, arithmetic and copies ran while one was open for 0% of the time, Pallas kernels for 26%

profile of v5, /device:TPU:0, one launch (start us, length us, event | category | flops | bytes accessed | tf_op | source)
XLA Modules:
  0.0 158.6 jit_solution(16165922849596840294)
XLA Ops:
  3.0 1.4 shard_map.138
  4.4 7.3 %all-to-all-start = ((bf16[32,8,1664]{2,1,0:T(8,128)(2,1)}), bf16[32,8,1664]{2,1,0:T(8,128)(2,1)S(1)}, u32[]{:S(2)}, u32[]{:S(2)}) async-start(bf16[32,8,1664]{2,1,0:T(8,128)(2,1)} %bitcast.4), calls=%async_computation | async-start | bytes 1703936 | tf_op jit(solution)/shard_map/all_to_all | solution.py:554
  11.7 1.1 copy-done.22
  12.9 1.2 shard_map.142.f_ref
  14.1 1.3 collective-permute-start.5
  15.4 3.0 %collective-permute-start.4 = (bf16[8,32,256]{2,1,0:T(8,128)(2,1)S(1)}, bf16[8,32,256]{2,1,0:T(8,128)(2,1)S(1)}, u32[]{:S(2)}, u32[]{:S(2)}) collective-permute-start(bf16[8,32,256]{2,1,0:T(8,128)(2,1)S(1)} %get-tuple-element.45), channel_id=1, source_target_pairs={{0,8},{8,16},{16,24},{1,9},{9,17},{17,25},{2,10},{10,18},{18,26},{... | collective-permute-start | bytes 393224 | tf_op jit(solution)/shard_map/ppermute | solution.py:561
  19.9 4.4 %collective-permute-start.6 = (bf16[8,48,256]{2,1,0:T(8,128)(2,1)S(1)}, bf16[8,48,256]{2,1,0:T(8,128)(2,1)}, u32[]{:S(2)}, u32[]{:S(2)}) collective-permute-start(bf16[8,48,256]{2,1,0:T(8,128)(2,1)S(1)} %get-tuple-element.27.high_ref), channel_id=1, source_target_pairs={{0,1},{1,2},{2,3},{3,4},{4,5},{5,6},{6,7},{8,9},{9,10},{10,11},{11... | collective-permute-start | bytes 589832 | tf_op jit(solution)/shard_map/ppermute | solution.py:561
  24.2 1.3 collective-permute-start.7
  25.5 9.6 %all-to-all-done = bf16[32,8,1664]{2,1,0:T(8,128)(2,1)S(1)} async-done(((bf16[32,8,1664]{2,1,0:T(8,128)(2,1)}), bf16[32,8,1664]{2,1,0:T(8,128)(2,1)S(1)}, u32[]{:S(2)}, u32[]{:S(2)}) %all-to-all-start) | async-done | bytes 852000 | tf_op jit(solution)/shard_map/all_to_all | solution.py:554
  35.1 1.1 copy-done.23
  36.2 2.2 %shard_map.139 = (bf16[8,256,256]{2,1,0:T(8,128)(2,1)S(1)}, bf16[256,256]{1,0:T(8,128)(2,1)S(1)}) custom-call(s32[1]{0:T(128)} %bitcast.1.me_ref, bf16[256,1664]{1,0:T(8,128)(2,1)S(1)} %bitcast.10, bf16[6,256,256]{2,1,0:T(8,128)(2,1)S(1)} %copy-done.23), custom_call_target="tpu_custom_call" | custom-call | flops 1000000000 | bytes 3000000 | tf_op jit(solution)/shard_map/pallas_call | solution.py:659
  38.5 1.3 collective-permute-start.1
  39.8 3.0 %collective-permute-start = (bf16[8,32,256]{2,1,0:T(8,128)(2,1)S(1)}, bf16[8,32,256]{2,1,0:T(8,128)(2,1)S(1)}, u32[]{:S(2)}, u32[]{:S(2)}) collective-permute-start(bf16[8,32,256]{2,1,0:T(8,128)(2,1)S(1)} %get-tuple-element.47), channel_id=1, source_target_pairs={{0,8},{8,16},{16,24},{1,9},{9,17},{17,25},{2,10},{10,18},{18,26},{... | collective-permute-start | bytes 393224 | tf_op jit(solution)/shard_map/ppermute | solution.py:561
  44.6 3.2 %collective-permute-start.2 = (bf16[8,48,256]{2,1,0:T(8,128)(2,1)S(1)}, bf16[8,48,256]{2,1,0:T(8,128)(2,1)S(1)}, u32[]{:S(2)}, u32[]{:S(2)}) collective-permute-start(bf16[8,48,256]{2,1,0:T(8,128)(2,1)S(1)} %get-tuple-element.25.high_ref), channel_id=1, source_target_pairs={{0,1},{1,2},{2,3},{3,4},{4,5},{5,6},{6,7},{8,9},{9,10},{10,11},{11... | collective-permute-start | bytes 589832 | tf_op jit(solution)/shard_map/ppermute | solution.py:561
  47.8 1.4 collective-permute-start.3
  49.3 10.6 %shard_map.144 = (f32[8,336,256]{2,1,0:T(8,128)S(1)}, bf16[8,256,256]{2,1,0:T(8,128)(2,1)S(1)}) custom-call(bf16[8,256,256]{2,1,0:T(8,128)(2,1)S(1)} %shard_map.142.f_ref, bf16[8,32,256]{2,1,0:T(8,128)(2,1)S(1)} %copy-done.17, bf16[8,32,256]{2,1,0:T(8,128)(2,1)S(1)} %copy-done.15, bf16[8,48,256]{2,1,0:T(8,128)(2,1)} %collective-permute-done.6.ylo_ref, ...), custom_call_target="tpu_custom_call" | custom-call | flops 6281389568 | bytes 7000000 | tf_op jit(solution)/shard_map/pallas_call | solution.py:671
  60.0 9.8 %shard_map.145 = (bf16[8,336,256]{2,1,0:T(8,128)(2,1)S(1)}, bf16[8,336,256]{2,1,0:T(8,128)(2,1)S(1)}) custom-call(bf16[8,256,256]{2,1,0:T(8,128)(2,1)S(1)} %get-tuple-element.24.f_ref.field_ref, bf16[8,32,256]{2,1,0:T(8,128)(2,1)S(1)} %collective-permute-done.xlo_ref, bf16[8,32,256]{2,1,0:T(8,128)(2,1)S(1)} %collective-permute-done.1.xhi_ref, ...), custom_call_target="tpu_custom_call" | custom-call | flops 6281389568 | bytes 8000000 | tf_op jit(solution)/shard_map/pallas_call | solution.py:681
  69.9 10.2 %shard_map.146 = bf16[256,1536]{1,0:T(8,128)(2,1)} custom-call(bf16[8,336,256]{2,1,0:T(8,128)(2,1)S(1)} %get-tuple-element.30.hg_ref, bf16[27,96,96]{2,1,0:T(8,128)(2,1)S(1)} %copy-done.7, bf16[8,256,256]{2,1,0:T(8,128)(2,1)S(1)} %get-tuple-element.32.outer_ref, bf16[6,256,256]{2,1,0:T(8,128)(2,1)S(1)} %copy-done.24, ...), custom_call_target="tpu_custom_call" | custom-call | flops 5798205952 | bytes 6000000 | tf_op jit(solution)/shard_map/pallas_call | solution.py:685
  80.0 7.3 %all-to-all-start.1 = ((bf16[32,8,1536]{2,1,0:T(8,128)(2,1)}), bf16[32,8,1536]{2,1,0:T(8,128)(2,1)S(1)}, u32[]{:S(2)}, u32[]{:S(2)}) async-start(bf16[32,8,1536]{2,1,0:T(8,128)(2,1)} %bitcast.7), calls=%async_computation.1 | async-start | bytes 1572864 | tf_op jit(solution)/shard_map/all_to_all | solution.py:554
  90.1 1.3 copy-done.28
  91.4 1.3 copy-done.31
  92.8 1.2 copy-done.33
  94.0 13.8 %shard_map.147 = (f32[2,1024,128]{2,1,0:T(8,128)S(1)}, f32[2,1024,128]{2,1,0:T(8,128)S(1)}) custom-call(s32[1]{0:T(128)} %bitcast.core_ref, bf16[8,256,256]{2,1,0:T(8,128)(2,1)S(1)} %copy-done.2, bf16[8,32,256]{2,1,0:T(8,128)(2,1)S(1)} %copy-done.21, bf16[8,32,256]{2,1,0:T(8,128)(2,1)S(1)} %copy-done.19, bf16[8,48,256]{2,1,0:T(8,128)(2,1)S(1)} %copy-done.11, ...), custom_call_target="tpu_custom_call" | custom-call | flops 9663676416 | bytes 10000000 | tf_op jit(solution)/shard_map/pallas_call | solution.py:692
  108.1 2.4 %collective-permute-done.8.got_ref = f32[2,1024,128]{2,1,0:T(8,128)S(1)} collective-permute-done((f32[2,1024,128]{2,1,0:T(8,128)S(1)}, f32[2,1024,128]{2,1,0:T(8,128)S(1)}, u32[]{:S(2)}, u32[]{:S(2)}) %collective-permute-start.8) | collective-permute-done | bytes 1048608 | tf_op jit(solution)/shard_map/ppermute | solution.py:566
  111.4 6.9 %all-to-all-start.2 = ((bf16[16,2,64,128]{3,2,1,0:T(8,128)(2,1)}), bf16[16,2,64,128]{3,2,1,0:T(8,128)(2,1)S(1)}, u32[]{:S(2)}, u32[]{:S(2)}) async-start(bf16[16,2,64,128]{3,2,1,0:T(8,128)(2,1)} %shard_map.148), calls=%async_computation.2 | async-start | bytes 1048576 | tf_op jit(solution)/shard_map/all_to_all | solution.py:554
  118.3 1.2 copy-done.3
  120.6 1.1 copy-done.25
  121.8 1.3 copy-done.29
  123.1 9.6 %shard_map.149 = bf16[256,1536]{1,0:T(8,128)(2,1)} custom-call(bf16[8,336,256]{2,1,0:T(8,128)(2,1)S(1)} %copy-done.29, f32[560,128]{1,0:T(8,128)S(1)} %shard_map.141.mask_ref, bf16[27,96,96]{2,1,0:T(8,128)(2,1)S(1)} %copy-done.9, bf16[8,256,256]{2,1,0:T(8,128)(2,1)S(1)} %copy-done.3, bf16[6,256,256]{2,1,0:T(8,128)(2,1)S(1)} %copy-done.25), custom_call_target="tpu_custom_call" | custom-call | flops 5798205952 | bytes 8000000 | tf_op jit(solution)/shard_map/pallas_call | solution.py:707
  133.9 20.7 %all_to_all.20.mine_ref = bf16[16,2,64,128]{3,2,1,0:T(8,128)(2,1)S(1)} all-to-all(bf16[16,2,64,128]{3,2,1,0:T(8,128)(2,1)S(1)} %shard_map.151), channel_id=1, replica_groups=mesh['cx'=2,'core'=2,'ry'=8] {'cx','ry'}, dimensions={0} | all-to-all | bytes 1048576 | tf_op jit(solution)/shard_map/all_to_all | solution.py:554
  154.6 1.2 shard_map.150
  156.5 2.1 %shard_map.152 = (f32[27,96,96]{2,1,0:T(8,128)}, f32[27,96,96]{2,1,0:T(8,128)}) custom-call(s32[1]{0:T(128)} %bitcast.core_ref, bf16[16,2,64,128]{3,2,1,0:T(8,128)(2,1)S(1)} %all_to_all.20.mine_ref, bf16[16,2,64,128]{3,2,1,0:T(8,128)(2,1)S(1)} %collective-permute-done.9.other_ref), custom_call_target="tpu_custom_call" | custom-call | flops 1000000 | bytes 4000000 | tf_op jit(solution)/shard_map/pallas_call | solution.py:724
  (91 shorter events, 12.5 us)
Async XLA Ops:
  3.0 8.7 %copy-start.6 = (bf16[16,16,1536]{2,1,0:T(8,128)(2,1)S(1)}, bf16[16,16,1536]{2,1,0:T(8,128)(2,1)}, u32[]{:S(2)}) copy-start(bf16[16,16,1536]{2,1,0:T(8,128)(2,1)} %param.13) | copy-start | bytes 2359300
  4.4 30.7 %all-to-all-start = ((bf16[32,8,1664]{2,1,0:T(8,128)(2,1)}), bf16[32,8,1664]{2,1,0:T(8,128)(2,1)S(1)}, u32[]{:S(2)}, u32[]{:S(2)}) async-start(bf16[32,8,1664]{2,1,0:T(8,128)(2,1)} %bitcast.4), calls=%async_computation | async-start | bytes 1703936 | tf_op jit(solution)/shard_map/all_to_all | solution.py:554
  14.1 4.4 %collective-permute-start.5 = (bf16[8,32,256]{2,1,0:T(8,128)(2,1)S(1)}, bf16[8,32,256]{2,1,0:T(8,128)(2,1)S(1)}, u32[]{:S(2)}, u32[]{:S(2)}) collective-permute-start(bf16[8,32,256]{2,1,0:T(8,128)(2,1)S(1)} %get-tuple-element.44), channel_id=1, source_target_pairs={{8,0},{16,8},{24,16},{9,1},{17,9},{25,17},{10,2},{18,10},{26,18},{... | collective-permute-start | bytes 393224 | tf_op jit(solution)/shard_map/ppermute | solution.py:561
  15.4 4.0 %collective-permute-start.4 = (bf16[8,32,256]{2,1,0:T(8,128)(2,1)S(1)}, bf16[8,32,256]{2,1,0:T(8,128)(2,1)S(1)}, u32[]{:S(2)}, u32[]{:S(2)}) collective-permute-start(bf16[8,32,256]{2,1,0:T(8,128)(2,1)S(1)} %get-tuple-element.45), channel_id=1, source_target_pairs={{0,8},{8,16},{16,24},{1,9},{9,17},{17,25},{2,10},{10,18},{18,26},{... | collective-permute-start | bytes 393224 | tf_op jit(solution)/shard_map/ppermute | solution.py:561
  18.5 19.9 %copy-start.14 = (bf16[8,32,256]{2,1,0:T(8,128)(2,1)}, bf16[8,32,256]{2,1,0:T(8,128)(2,1)S(1)}, u32[]{:S(2)}) copy-start(bf16[8,32,256]{2,1,0:T(8,128)(2,1)S(1)} %collective-permute-done.5.xhi_ref) | copy-start | bytes 393220
  19.4 19.0 %copy-start.16 = (bf16[8,32,256]{2,1,0:T(8,128)(2,1)}, bf16[8,32,256]{2,1,0:T(8,128)(2,1)S(1)}, u32[]{:S(2)}) copy-start(bf16[8,32,256]{2,1,0:T(8,128)(2,1)S(1)} %collective-permute-done.4.xlo_ref) | copy-start | bytes 393220
  19.9 29.4 %collective-permute-start.6 = (bf16[8,48,256]{2,1,0:T(8,128)(2,1)S(1)}, bf16[8,48,256]{2,1,0:T(8,128)(2,1)}, u32[]{:S(2)}, u32[]{:S(2)}) collective-permute-start(bf16[8,48,256]{2,1,0:T(8,128)(2,1)S(1)} %get-tuple-element.27.high_ref), channel_id=1, source_target_pairs={{0,1},{1,2},{2,3},{3,4},{4,5},{5,6},{6,7},{8,9},{9,10},{10,11},{11... | collective-permute-start | bytes 589832 | tf_op jit(solution)/shard_map/ppermute | solution.py:561
  24.2 25.1 %collective-permute-start.7 = (bf16[8,48,256]{2,1,0:T(8,128)(2,1)S(1)}, bf16[8,48,256]{2,1,0:T(8,128)(2,1)}, u32[]{:S(2)}, u32[]{:S(2)}) collective-permute-start(bf16[8,48,256]{2,1,0:T(8,128)(2,1)S(1)} %get-tuple-element.28.low_ref), channel_id=1, source_target_pairs={{1,0},{2,1},{3,2},{4,3},{5,4},{6,5},{7,6},{9,8},{10,9},{11,10},{12... | collective-permute-start | bytes 589832 | tf_op jit(solution)/shard_map/ppermute | solution.py:561
  36.2 6.6 %copy-start.35 = (s32[560]{0:T(1024)S(1)}, s32[560]{0:T(1024)}, u32[]{:S(2)}) copy-start(s32[560]{0:T(1024)} %constant.41.clone) | copy-start | bytes 6724
  36.2 6.6 %copy-start.36 = (s32[560]{0:T(1024)S(1)}, s32[560]{0:T(1024)}, u32[]{:S(2)}) copy-start(s32[560]{0:T(1024)} %constant.40.clone) | copy-start | bytes 6724
  36.2 6.6 %copy-start.37 = (pred[560]{0:T(1024)(128)(4,1)S(1)}, pred[560]{0:T(1024)(128)(4,1)}, u32[]{:S(2)}) copy-start(pred[560]{0:T(1024)(128)(4,1)} %constant.42.clone) | copy-start | bytes 1684
  38.4 21.5 %copy-start.1 = (bf16[8,256,256]{2,1,0:T(8,128)(2,1)}, bf16[8,256,256]{2,1,0:T(8,128)(2,1)S(1)}, u32[]{:S(2)}) copy-start(bf16[8,256,256]{2,1,0:T(8,128)(2,1)S(1)} %get-tuple-element.24.f_ref.field_ref) | copy-start | bytes 3145732
  38.5 5.7 %collective-permute-start.1 = (bf16[8,32,256]{2,1,0:T(8,128)(2,1)S(1)}, bf16[8,32,256]{2,1,0:T(8,128)(2,1)S(1)}, u32[]{:S(2)}, u32[]{:S(2)}) collective-permute-start(bf16[8,32,256]{2,1,0:T(8,128)(2,1)S(1)} %get-tuple-element.46), channel_id=1, source_target_pairs={{8,0},{16,8},{24,16},{9,1},{17,9},{25,17},{10,2},{18,10},{26,18},{... | collective-permute-start | bytes 393224 | tf_op jit(solution)/shard_map/ppermute | solution.py:561
  39.8 4.4 %collective-permute-start = (bf16[8,32,256]{2,1,0:T(8,128)(2,1)S(1)}, bf16[8,32,256]{2,1,0:T(8,128)(2,1)S(1)}, u32[]{:S(2)}, u32[]{:S(2)}) collective-permute-start(bf16[8,32,256]{2,1,0:T(8,128)(2,1)S(1)} %get-tuple-element.47), channel_id=1, source_target_pairs={{0,8},{8,16},{16,24},{1,9},{9,17},{17,25},{2,10},{10,18},{18,26},{... | collective-permute-start | bytes 393224 | tf_op jit(solution)/shard_map/ppermute | solution.py:561
  44.2 15.8 %copy-start.18 = (bf16[8,32,256]{2,1,0:T(8,128)(2,1)}, bf16[8,32,256]{2,1,0:T(8,128)(2,1)S(1)}, u32[]{:S(2)}) copy-start(bf16[8,32,256]{2,1,0:T(8,128)(2,1)S(1)} %collective-permute-done.1.xhi_ref) | copy-start | bytes 393220
  44.2 15.8 %copy-start.20 = (bf16[8,32,256]{2,1,0:T(8,128)(2,1)}, bf16[8,32,256]{2,1,0:T(8,128)(2,1)S(1)}, u32[]{:S(2)}) copy-start(bf16[8,32,256]{2,1,0:T(8,128)(2,1)S(1)} %collective-permute-done.xlo_ref) | copy-start | bytes 393220
  44.6 15.3 %collective-permute-start.2 = (bf16[8,48,256]{2,1,0:T(8,128)(2,1)S(1)}, bf16[8,48,256]{2,1,0:T(8,128)(2,1)S(1)}, u32[]{:S(2)}, u32[]{:S(2)}) collective-permute-start(bf16[8,48,256]{2,1,0:T(8,128)(2,1)S(1)} %get-tuple-element.25.high_ref), channel_id=1, source_target_pairs={{0,1},{1,2},{2,3},{3,4},{4,5},{5,6},{6,7},{8,9},{9,10},{10,11},{11... | collective-permute-start | bytes 589832 | tf_op jit(solution)/shard_map/ppermute | solution.py:561
  47.8 12.2 %copy-start.7 = (bf16[27,96,96]{2,1,0:T(8,128)(2,1)S(1)}, bf16[27,96,96]{2,1,0:T(8,128)(2,1)}, u32[]{:S(2)}) copy-start(bf16[27,96,96]{2,1,0:T(8,128)(2,1)} %raw_ref.6) | copy-start | bytes 1492996
  47.8 12.1 %collective-permute-start.3 = (bf16[8,48,256]{2,1,0:T(8,128)(2,1)S(1)}, bf16[8,48,256]{2,1,0:T(8,128)(2,1)S(1)}, u32[]{:S(2)}, u32[]{:S(2)}) collective-permute-start(bf16[8,48,256]{2,1,0:T(8,128)(2,1)S(1)} %get-tuple-element.26.low_ref), channel_id=1, source_target_pairs={{1,0},{2,1},{3,2},{4,3},{5,4},{6,5},{7,6},{9,8},{10,9},{11,10},{12... | collective-permute-start | bytes 589832 | tf_op jit(solution)/shard_map/ppermute | solution.py:561
  59.9 10.0 %copy-start.32 = (bf16[8,256,256]{2,1,0:T(8,128)(2,1)}, bf16[8,256,256]{2,1,0:T(8,128)(2,1)S(1)}, u32[]{:S(2)}) copy-start(bf16[8,256,256]{2,1,0:T(8,128)(2,1)S(1)} %get-tuple-element.32.outer_ref) | copy-start | bytes 3145732
  59.9 9.9 %copy-start.10 = (bf16[8,48,256]{2,1,0:T(8,128)(2,1)}, bf16[8,48,256]{2,1,0:T(8,128)(2,1)S(1)}, u32[]{:S(2)}) copy-start(bf16[8,48,256]{2,1,0:T(8,128)(2,1)S(1)} %collective-permute-done.2.ylo_ref) | copy-start | bytes 589828
  59.9 9.9 %copy-start.12 = (bf16[8,48,256]{2,1,0:T(8,128)(2,1)}, bf16[8,48,256]{2,1,0:T(8,128)(2,1)S(1)}, u32[]{:S(2)}) copy-start(bf16[8,48,256]{2,1,0:T(8,128)(2,1)S(1)} %collective-permute-done.3.yhi_ref) | copy-start | bytes 589828
  60.0 9.9 %copy-start.24 = (bf16[6,256,256]{2,1,0:T(8,128)(2,1)S(1)}, bf16[6,256,256]{2,1,0:T(8,128)(2,1)}, u32[]{:S(2)}) copy-start(bf16[6,256,256]{2,1,0:T(8,128)(2,1)} %constant.38.clone.perm_ref) | copy-start | bytes 2359300
  69.8 10.2 %copy-start.27 = (bf16[8,336,256]{2,1,0:T(8,128)(2,1)}, bf16[8,336,256]{2,1,0:T(8,128)(2,1)S(1)}, u32[]{:S(2)}) copy-start(bf16[8,336,256]{2,1,0:T(8,128)(2,1)S(1)} %get-tuple-element.38.act_ref) | copy-start | bytes 4128772
  69.8 10.2 %copy-start.30 = (bf16[8,336,256]{2,1,0:T(8,128)(2,1)}, bf16[8,336,256]{2,1,0:T(8,128)(2,1)S(1)}, u32[]{:S(2)}) copy-start(bf16[8,336,256]{2,1,0:T(8,128)(2,1)S(1)} %get-tuple-element.30.hg_ref) | copy-start | bytes 4128772
  80.0 7.3 %copy-start.2 = (bf16[8,256,256]{2,1,0:T(8,128)(2,1)S(1)}, bf16[8,256,256]{2,1,0:T(8,128)(2,1)}, u32[]{:S(2)}) copy-start(bf16[8,256,256]{2,1,0:T(8,128)(2,1)} %copy-done.1) | copy-start | bytes 3145732
  80.0 7.3 %copy-start.11 = (bf16[8,48,256]{2,1,0:T(8,128)(2,1)S(1)}, bf16[8,48,256]{2,1,0:T(8,128)(2,1)}, u32[]{:S(2)}) copy-start(bf16[8,48,256]{2,1,0:T(8,128)(2,1)} %copy-done.10) | copy-start | bytes 589828
  80.0 30.5 %all-to-all-start.1 = ((bf16[32,8,1536]{2,1,0:T(8,128)(2,1)}), bf16[32,8,1536]{2,1,0:T(8,128)(2,1)S(1)}, u32[]{:S(2)}, u32[]{:S(2)}) async-start(bf16[32,8,1536]{2,1,0:T(8,128)(2,1)} %bitcast.7), calls=%async_computation.1 | async-start | bytes 1572864 | tf_op jit(solution)/shard_map/all_to_all | solution.py:554
  107.8 2.7 %collective-permute-start.8 = (f32[2,1024,128]{2,1,0:T(8,128)S(1)}, f32[2,1024,128]{2,1,0:T(8,128)S(1)}, u32[]{:S(2)}, u32[]{:S(2)}) collective-permute-start(f32[2,1024,128]{2,1,0:T(8,128)S(1)} %get-tuple-element.36), channel_id=1, source_target_pairs={{0,8},{8,0},{16,24},{24,16},{1,9},{9,1},{17,25},{25,17},{2,10},{10... | collective-permute-start | bytes 3145736 | tf_op jit(solution)/shard_map/ppermute | solution.py:566
  111.4 22.4 %all-to-all-start.2 = ((bf16[16,2,64,128]{3,2,1,0:T(8,128)(2,1)}), bf16[16,2,64,128]{3,2,1,0:T(8,128)(2,1)S(1)}, u32[]{:S(2)}, u32[]{:S(2)}) async-start(bf16[16,2,64,128]{3,2,1,0:T(8,128)(2,1)} %shard_map.148), calls=%async_computation.2 | async-start | bytes 1048576 | tf_op jit(solution)/shard_map/all_to_all | solution.py:554
  132.7 21.9 %copy-start.5 = (s32[128]{0:T(128)S(1)}, s32[128]{0:T(128)}, u32[]{:S(2)}) copy-start(s32[128]{0:T(128)} %param.12) | copy-start | bytes 1540
  154.6 1.9 %collective-permute-start.9 = (bf16[16,2,64,128]{3,2,1,0:T(8,128)(2,1)S(1)}, bf16[16,2,64,128]{3,2,1,0:T(8,128)(2,1)S(1)}, u32[]{:S(2)}, u32[]{:S(2)}) collective-permute-start(bf16[16,2,64,128]{3,2,1,0:T(8,128)(2,1)S(1)} %all_to_all.20.mine_ref), channel_id=1, source_target_pairs={{0,8},{8,0},{16,24},{24,16},{1,9},{9,1},{17,25},{25,17},{2,10},{10... | collective-permute-start | bytes 1572872 | tf_op jit(solution)/shard_map/ppermute | solution.py:566
  (19 other events, 47.3 us)

commit v6 on v5

--- a/solution.py
+++ b/solution.py
@@ -11,7 +11,7 @@
 LANES = 128
 PAIR = 256
 MIB = 1024 * 1024
-ROOM_WIDE, ROOM_NEAR, ROOM_CORR, ROOM_SMALL = 16, 12, 14, 5
+ROOM_WIDE, ROOM_NEAR, ROOM_CORR, ROOM_SMALL = 20, 14, 16, 5
 BF = jnp.bfloat16
 F32 = jnp.float32
 
@@ -340,13 +340,19 @@
     lax.fori_loop(0, pairs, body, 0)
 
 
+STEP = 2
+
+
 def conv_wide(ext_ref, edge_ref, w_ref, k):
     pieces = []
     for a in range(3):
         for b in range(3):
             for j in range(2):
-                main = ext_ref[b, k + j, a : a + NX + 2].reshape(OUT_MAIN, PAIR)
-                pieces.append(jnp.concatenate([main, edge_ref[a, b, k + j]], axis=0))
+                parts = []
+                for i in range(STEP):
+                    parts.append(ext_ref[b, k + i + j, a : a + NX + 2].reshape(OUT_MAIN, PAIR))
+                    parts.append(edge_ref[a, b, k + i + j])
+                pieces.append(jnp.concatenate(parts, axis=0))
     return dot(jnp.concatenate(pieces, axis=1), w_ref[...])
 
 
@@ -355,8 +361,16 @@
     for a in range(3):
         for b in range(3):
             for j in range(2):
-                pieces.append(ext_ref[b, k + j, a : a + NX].reshape(NX * NY, PAIR))
+                pieces.append(ext_ref[b, pl.ds(k + j, STEP), a : a + NX].reshape(STEP * NX * NY, PAIR))
     return dot(jnp.concatenate(pieces, axis=1), w_ref[...])
+
+
+def each_step(pairs, body):
+    def step(t, carry):
+        body(t * STEP)
+        return carry
+
+    lax.fori_loop(0, pairs // STEP, step, 0)
 
 
 def out_mask(mask_ref):
@@ -371,23 +385,24 @@
     build_band(w_ref, raw_ref, True)
     widen_two(ext_ref, edge_ref, f_ref, xlo_ref, xhi_ref, ylo_ref, yhi_ref, low_ref, high_ref, mask_ref)
 
-    def body(k, carry):
-        out_ref[k] = conv_wide(ext_ref, edge_ref, w_ref, k)
-        outer_ref[k] = (f_ref[k].astype(F32) * twice(mask_ref[0 : NX * NY, :])).astype(BF)
-        return carry
-
-    lax.fori_loop(0, f_ref.shape[0], body, 0)
-
-
-def correlate(gt_ref, ext_ref, first_x, taps_ref, channels):
-    pairs = ext_ref.shape[1] - 1
+    def body(k):
+        total = conv_wide(ext_ref, edge_ref, w_ref, k)
+        for i in range(STEP):
+            out_ref[k + i] = total[i * OUT_ROWS : (i + 1) * OUT_ROWS]
+            outer_ref[k + i] = (f_ref[k + i].astype(F32) * twice(mask_ref[0 : NX * NY, :])).astype(BF)
+
+    each_step(f_ref.shape[0], body)
+
+
+def correlate(gt_ref, ext_ref, taps_ref, channels):
+    blocks = ext_ref.shape[1]
 
     def body(ab, carry):
         a = ab // 3
         b = ab % 3
-        left = gt_ref[...]
-        near = dot(left, ext_ref[b, 0:pairs, pl.ds(a + first_x, NX)].reshape(pairs * NX * NY, PAIR))
-        far = dot(left, ext_ref[b, 1 : pairs + 1, pl.ds(a + first_x, NX)].reshape(pairs * NX * NY, PAIR))
+        both = dot(gt_ref[...], ext_ref[b, :, pl.ds(a, NX)].reshape(blocks * NX * NY, PAIR))
+        near = both[0 : 2 * channels]
+        far = both[2 * channels : 4 * channels]
         low = slice(0, channels)
         high = slice(channels, 2 * channels)
         taps_ref[3 * ab] = near[low, 0:LANES] + near[high, LANES:PAIR]
@@ -422,23 +437,31 @@
     build_band(w_ref, raw_ref, False)
     widen_two(ext_ref, edge_ref, f_ref, xlo_ref, xhi_ref, ylo_ref, yhi_ref, low_ref, high_ref)
 
-    def body(k, carry):
+    def body(k):
+        total = conv_wide(ext_ref, edge_ref, w_ref, k)
         m = out_mask(mask_ref)
-        hidden = m * conv_wide(ext_ref, edge_ref, w_ref, k)
-        sigma = jax.nn.sigmoid(hidden)
-        act_ref[k] = (hidden * sigma).astype(BF)
-        hg_ref[k] = (m * grad_ref[k] * sigma * (1.0 + hidden * (1.0 - sigma))).astype(BF)
-        return carry
-
-    lax.fori_loop(0, f_ref.shape[0], body, 0)
+        for i in range(STEP):
+            hidden = m * total[i * OUT_ROWS : (i + 1) * OUT_ROWS]
+            sigma = jax.nn.sigmoid(hidden)
+            act_ref[k + i] = (hidden * sigma).astype(BF)
+            hg_ref[k + i] = (m * grad_ref[k + i] * sigma * (1.0 + hidden * (1.0 - sigma))).astype(BF)
+
+    each_step(f_ref.shape[0], body)
 
 
 def turn(gt_ref, g_ref, start, channels):
     inner = NX * NY
-    for k in range(g_ref.shape[0]):
+    pairs = g_ref.shape[0]
+    two = 2 * channels
+    gt_ref[0:two, pairs * inner :] = jnp.zeros((two, inner), BF)
+    gt_ref[two : 2 * two, 0:inner] = jnp.zeros((two, inner), BF)
+    for k in range(pairs):
         value = g_ref[k, start : start + inner, :].T
-        gt_ref[0:channels, k * inner : (k + 1) * inner] = value[0:channels]
-        gt_ref[channels : 2 * channels, k * inner : (k + 1) * inner] = value[LANES : LANES + channels]
+        for i in range(2):
+            half = value[i * LANES : i * LANES + channels]
+            at = i * channels
+            gt_ref[at : at + channels, k * inner : (k + 1) * inner] = half
+            gt_ref[two + at : two + at + channels, (k + 1) * inner : (k + 2) * inner] = half
 
 
 def corr_kernel(channels, core_ref, f_ref, xlo_ref, xhi_ref, ylo_ref, yhi_ref, hg_ref, act_ref, outer_ref,
@@ -454,7 +477,7 @@
         else:
             widen_one(ext_ref, act_ref)
             turn(gt_ref, outer_ref, 0, channels)
-        correlate(gt_ref, ext_ref, 0, taps_ref, channels)
+        correlate(gt_ref, ext_ref, taps_ref, channels)
         pack_taps(taps_ref, packed_ref, channels)
         keep_ref[i] = packed_ref[mine, :]
         give_ref[i] = packed_ref[other, :]
@@ -464,11 +487,13 @@
     build_band(w_ref, raw_ref, True)
     widen_one(ext_ref, hg_ref)
 
-    def body(k, carry):
-        sum_ref[k] = (outer_ref[k].astype(F32) + conv_inner(ext_ref, w_ref, k)).astype(BF)
-        return carry
-
-    lax.fori_loop(0, outer_ref.shape[0], body, 0)
+    def body(k):
+        total = conv_inner(ext_ref, w_ref, k)
+        rows = NX * NY
+        for i in range(STEP):
+            sum_ref[k + i] = (outer_ref[k + i].astype(F32) + total[i * rows : (i + 1) * rows]).astype(BF)
+
+    each_step(outer_ref.shape[0], body)
     gather_pairs(sum_ref, turned_ref)
     take = take_ref[...]
     for i in range(perm_ref.shape[0]):
@@ -480,12 +505,14 @@
     build_band(w_ref, raw_ref, False)
     widen_one(ext_ref, act_ref)
 
-    def body(k, carry):
+    def body(k):
+        total = conv_inner(ext_ref, w_ref, k)
         m = twice(mask_ref[0 : NX * NY, :])
-        sum_ref[k] = (field_ref[k].astype(F32) + m * conv_inner(ext_ref, w_ref, k)).astype(BF)
-        return carry
-
-    lax.fori_loop(0, field_ref.shape[0], body, 0)
+        rows = NX * NY
+        for i in range(STEP):
+            sum_ref[k + i] = (field_ref[k + i].astype(F32) + m * total[i * rows : (i + 1) * rows]).astype(BF)
+
+    each_step(field_ref.shape[0], body)
     gather_pairs(sum_ref, turned_ref)
     for i in range(perm_ref.shape[0]):
         out_ref[:, i * PAIR : (i + 1) * PAIR] = dot_nt(turned_ref[i], perm_ref[i]).astype(BF)
@@ -692,7 +719,7 @@
     keep, give = call(
         functools.partial(corr_kernel, channels), (half_shape, half_shape), 2 * conv_flops, 10e6,
         (
-            ext_near, pltpu.VMEM((2 * channels, pairs * slots), BF),
+            ext_near, pltpu.VMEM((4 * channels, (pairs + 1) * slots), BF),
             pltpu.VMEM((28, channels, LANES), F32), pltpu.VMEM((packed_rows, LANES), F32),
         ),
         ROOM_CORR, in_specs=[smem] + [vmem] * 8,

time: 160 us -> 158 us (0.988)
  Pallas kernels: 65 us -> 63.1 us
where the time goes in v6:
time: 158 us; the launch traced here: 157 us
  Pallas kernels  63.1 us (40%)
  starting transfers between devices  40.5 us (26%)
  blocking collectives  20 us (13%)
  local copies, waits for them, and re-layouts  16.4 us (10%)
  waiting for transfers between devices  15.6 us (10%)
    all_to_all x3, starting transfers between devices, share(): return lax.all_to_all(parts, axes, split_axis=0, concat_axis=0, tiled=True)  21.5 us
    all_to_all x1, blocking collectives, share(): return lax.all_to_all(parts, axes, split_axis=0, concat_axis=0, tiled=True)  20 us
    ppermute x8, starting transfers between devices, neighbours(): return (lax.ppermute(upper, axes, ahead), lax.ppermute(lower, axes, behind))  18.9 us
    unnamed x76, local copies, waits for them, and re-layouts  15.4 us
    pallas_call x1, Pallas kernels, on_device(): call(functools.partial(corr_kernel, channels), (half_shape, half_shape),...  14.6 us
    all_to_all x3, waiting for transfers between devices, share(): return lax.all_to_all(parts, axes, split_axis=0, concat_axis=0, tiled=True)  11.3 us
    pallas_call x1, Pallas kernels, on_device(): call(outer_kernel, (shape((pairs, OUT_ROWS, PAIR), F32), field_shape), 1....  9.9 us
    pallas_call x1, Pallas kernels, on_device(): call(grid_grad_kernel, shape((buffers, row_width), BF), 1.2 * conv_flops,...  9.47 us
  transfers between devices with their start and end apart: 13, of which 5 were waited for; matrix products, arithmetic and copies ran while one was open for 0% of the time, Pallas kernels for 26%

profile of v6, /device:TPU:0, one launch (start us, length us, event | category | flops | bytes accessed | tf_op | source)
XLA Modules:
  0.0 156.7 jit_solution(17794130664090394667)
XLA Ops:
  3.0 1.4 shard_map.138
  4.4 7.3 %all-to-all-start = ((bf16[32,8,1664]{2,1,0:T(8,128)(2,1)}), bf16[32,8,1664]{2,1,0:T(8,128)(2,1)S(1)}, u32[]{:S(2)}, u32[]{:S(2)}) async-start(bf16[32,8,1664]{2,1,0:T(8,128)(2,1)} %bitcast.4), calls=%async_computation | async-start | bytes 1703936 | tf_op jit(solution)/shard_map/all_to_all | solution.py:581
  12.9 1.2 shard_map.142.f_ref
  14.1 1.3 collective-permute-start.5
  15.4 3.0 %collective-permute-start.4 = (bf16[8,32,256]{2,1,0:T(8,128)(2,1)S(1)}, bf16[8,32,256]{2,1,0:T(8,128)(2,1)S(1)}, u32[]{:S(2)}, u32[]{:S(2)}) collective-permute-start(bf16[8,32,256]{2,1,0:T(8,128)(2,1)S(1)} %get-tuple-element.45), channel_id=1, source_target_pairs={{0,8},{8,16},{16,24},{1,9},{9,17},{17,25},{2,10},{10,18},{18,26},{... | collective-permute-start | bytes 393224 | tf_op jit(solution)/shard_map/ppermute | solution.py:588
  19.9 4.4 %collective-permute-start.6 = (bf16[8,48,256]{2,1,0:T(8,128)(2,1)S(1)}, bf16[8,48,256]{2,1,0:T(8,128)(2,1)}, u32[]{:S(2)}, u32[]{:S(2)}) collective-permute-start(bf16[8,48,256]{2,1,0:T(8,128)(2,1)S(1)} %get-tuple-element.27.high_ref), channel_id=1, source_target_pairs={{0,1},{1,2},{2,3},{3,4},{4,5},{5,6},{6,7},{8,9},{9,10},{10,11},{11... | collective-permute-start | bytes 589832 | tf_op jit(solution)/shard_map/ppermute | solution.py:588
  24.2 1.3 collective-permute-start.7
  25.5 9.6 %all-to-all-done = bf16[32,8,1664]{2,1,0:T(8,128)(2,1)S(1)} async-done(((bf16[32,8,1664]{2,1,0:T(8,128)(2,1)}), bf16[32,8,1664]{2,1,0:T(8,128)(2,1)S(1)}, u32[]{:S(2)}, u32[]{:S(2)}) %all-to-all-start) | async-done | bytes 852000 | tf_op jit(solution)/shard_map/all_to_all | solution.py:581
  35.1 1.1 copy-done.23
  36.2 2.2 %shard_map.139 = (bf16[8,256,256]{2,1,0:T(8,128)(2,1)S(1)}, bf16[256,256]{1,0:T(8,128)(2,1)S(1)}) custom-call(s32[1]{0:T(128)} %bitcast.1.me_ref, bf16[256,1664]{1,0:T(8,128)(2,1)S(1)} %bitcast.10, bf16[6,256,256]{2,1,0:T(8,128)(2,1)S(1)} %copy-done.23), custom_call_target="tpu_custom_call" | custom-call | flops 1000000000 | bytes 3000000 | tf_op jit(solution)/shard_map/pallas_call | solution.py:686
  38.5 1.3 collective-permute-start.1
  39.8 3.0 %collective-permute-start = (bf16[8,32,256]{2,1,0:T(8,128)(2,1)S(1)}, bf16[8,32,256]{2,1,0:T(8,128)(2,1)S(1)}, u32[]{:S(2)}, u32[]{:S(2)}) collective-permute-start(bf16[8,32,256]{2,1,0:T(8,128)(2,1)S(1)} %get-tuple-element.47), channel_id=1, source_target_pairs={{0,8},{8,16},{16,24},{1,9},{9,17},{17,25},{2,10},{10,18},{18,26},{... | collective-permute-start | bytes 393224 | tf_op jit(solution)/shard_map/ppermute | solution.py:588
  44.6 3.2 %collective-permute-start.2 = (bf16[8,48,256]{2,1,0:T(8,128)(2,1)S(1)}, bf16[8,48,256]{2,1,0:T(8,128)(2,1)S(1)}, u32[]{:S(2)}, u32[]{:S(2)}) collective-permute-start(bf16[8,48,256]{2,1,0:T(8,128)(2,1)S(1)} %get-tuple-element.25.high_ref), channel_id=1, source_target_pairs={{0,1},{1,2},{2,3},{3,4},{4,5},{5,6},{6,7},{8,9},{9,10},{10,11},{11... | collective-permute-start | bytes 589832 | tf_op jit(solution)/shard_map/ppermute | solution.py:588
  47.8 1.4 collective-permute-start.3
  49.3 9.9 %shard_map.144 = (f32[8,336,256]{2,1,0:T(8,128)S(1)}, bf16[8,256,256]{2,1,0:T(8,128)(2,1)S(1)}) custom-call(bf16[8,256,256]{2,1,0:T(8,128)(2,1)S(1)} %shard_map.142.f_ref, bf16[8,32,256]{2,1,0:T(8,128)(2,1)S(1)} %copy-done.17, bf16[8,32,256]{2,1,0:T(8,128)(2,1)S(1)} %copy-done.15, bf16[8,48,256]{2,1,0:T(8,128)(2,1)} %collective-permute-done.6.ylo_ref, ...), custom_call_target="tpu_custom_call" | custom-call | flops 6281389568 | bytes 7000000 | tf_op jit(solution)/shard_map/pallas_call | solution.py:698
  59.3 9.1 %shard_map.145 = (bf16[8,336,256]{2,1,0:T(8,128)(2,1)S(1)}, bf16[8,336,256]{2,1,0:T(8,128)(2,1)S(1)}) custom-call(bf16[8,256,256]{2,1,0:T(8,128)(2,1)S(1)} %get-tuple-element.24.f_ref.field_ref, bf16[8,32,256]{2,1,0:T(8,128)(2,1)S(1)} %collective-permute-done.xlo_ref, bf16[8,32,256]{2,1,0:T(8,128)(2,1)S(1)} %collective-permute-done.1.xhi_ref, ...), custom_call_target="tpu_custom_call" | custom-call | flops 6281389568 | bytes 8000000 | tf_op jit(solution)/shard_map/pallas_call | solution.py:708
  68.5 9.5 %shard_map.146 = bf16[256,1536]{1,0:T(8,128)(2,1)} custom-call(bf16[8,336,256]{2,1,0:T(8,128)(2,1)S(1)} %get-tuple-element.30.hg_ref, bf16[27,96,96]{2,1,0:T(8,128)(2,1)S(1)} %copy-done.7, bf16[8,256,256]{2,1,0:T(8,128)(2,1)S(1)} %get-tuple-element.32.outer_ref, bf16[6,256,256]{2,1,0:T(8,128)(2,1)S(1)} %copy-done.24, ...), custom_call_target="tpu_custom_call" | custom-call | flops 5798205952 | bytes 6000000 | tf_op jit(solution)/shard_map/pallas_call | solution.py:712
  78.0 7.5 %all-to-all-start.1 = ((bf16[32,8,1536]{2,1,0:T(8,128)(2,1)}), bf16[32,8,1536]{2,1,0:T(8,128)(2,1)S(1)}, u32[]{:S(2)}, u32[]{:S(2)}) async-start(bf16[32,8,1536]{2,1,0:T(8,128)(2,1)} %bitcast.7), calls=%async_computation.1 | async-start | bytes 1572864 | tf_op jit(solution)/shard_map/all_to_all | solution.py:581
  88.2 1.3 copy-done.28
  89.6 1.3 copy-done.31
  90.9 1.2 copy-done.33
  92.1 14.6 %shard_map.147 = (f32[2,1024,128]{2,1,0:T(8,128)S(1)}, f32[2,1024,128]{2,1,0:T(8,128)S(1)}) custom-call(s32[1]{0:T(128)} %bitcast.core_ref, bf16[8,256,256]{2,1,0:T(8,128)(2,1)S(1)} %copy-done.2, bf16[8,32,256]{2,1,0:T(8,128)(2,1)S(1)} %copy-done.21, bf16[8,32,256]{2,1,0:T(8,128)(2,1)S(1)} %copy-done.19, bf16[8,48,256]{2,1,0:T(8,128)(2,1)S(1)} %copy-done.11, ...), custom_call_target="tpu_custom_call" | custom-call | flops 9663676416 | bytes 10000000 | tf_op jit(solution)/shard_map/pallas_call | solution.py:719
  106.9 2.6 %collective-permute-done.8.got_ref = f32[2,1024,128]{2,1,0:T(8,128)S(1)} collective-permute-done((f32[2,1024,128]{2,1,0:T(8,128)S(1)}, f32[2,1024,128]{2,1,0:T(8,128)S(1)}, u32[]{:S(2)}, u32[]{:S(2)}) %collective-permute-start.8) | collective-permute-done | bytes 1048608 | tf_op jit(solution)/shard_map/ppermute | solution.py:593
  110.4 6.7 %all-to-all-start.2 = ((bf16[16,2,64,128]{3,2,1,0:T(8,128)(2,1)}), bf16[16,2,64,128]{3,2,1,0:T(8,128)(2,1)S(1)}, u32[]{:S(2)}, u32[]{:S(2)}) async-start(bf16[16,2,64,128]{3,2,1,0:T(8,128)(2,1)} %shard_map.148), calls=%async_computation.2 | async-start | bytes 1048576 | tf_op jit(solution)/shard_map/all_to_all | solution.py:581
  117.1 1.2 copy-done.3
  119.4 1.1 copy-done.25
  120.5 1.3 copy-done.29
  121.9 8.9 %shard_map.149 = bf16[256,1536]{1,0:T(8,128)(2,1)} custom-call(bf16[8,336,256]{2,1,0:T(8,128)(2,1)S(1)} %copy-done.29, f32[560,128]{1,0:T(8,128)S(1)} %shard_map.141.mask_ref, bf16[27,96,96]{2,1,0:T(8,128)(2,1)S(1)} %copy-done.9, bf16[8,256,256]{2,1,0:T(8,128)(2,1)S(1)} %copy-done.3, bf16[6,256,256]{2,1,0:T(8,128)(2,1)S(1)} %copy-done.25), custom_call_target="tpu_custom_call" | custom-call | flops 5798205952 | bytes 8000000 | tf_op jit(solution)/shard_map/pallas_call | solution.py:734
  130.8 1.8 %all-to-all-done.2.in_ref = bf16[16,2,64,128]{3,2,1,0:T(8,128)(2,1)S(1)} async-done(((bf16[16,2,64,128]{3,2,1,0:T(8,128)(2,1)}), bf16[16,2,64,128]{3,2,1,0:T(8,128)(2,1)S(1)}, u32[]{:S(2)}, u32[]{:S(2)}) %all-to-all-start.2) | async-done | bytes 524320 | tf_op jit(solution)/shard_map/all_to_all | solution.py:581
  132.7 20.0 %all_to_all.20.mine_ref = bf16[16,2,64,128]{3,2,1,0:T(8,128)(2,1)S(1)} all-to-all(bf16[16,2,64,128]{3,2,1,0:T(8,128)(2,1)S(1)} %shard_map.151), channel_id=1, replica_groups=mesh['cx'=2,'core'=2,'ry'=8] {'cx','ry'}, dimensions={0} | all-to-all | bytes 1048576 | tf_op jit(solution)/shard_map/all_to_all | solution.py:581
  152.7 1.2 shard_map.150
  154.6 2.1 %shard_map.152 = (f32[27,96,96]{2,1,0:T(8,128)}, f32[27,96,96]{2,1,0:T(8,128)}) custom-call(s32[1]{0:T(128)} %bitcast.core_ref, bf16[16,2,64,128]{3,2,1,0:T(8,128)(2,1)S(1)} %all_to_all.20.mine_ref, bf16[16,2,64,128]{3,2,1,0:T(8,128)(2,1)S(1)} %collective-permute-done.9.other_ref), custom_call_target="tpu_custom_call" | custom-call | flops 1000000 | bytes 4000000 | tf_op jit(solution)/shard_map/pallas_call | solution.py:751
  (91 shorter events, 12.4 us)
Async XLA Ops:
  3.0 8.7 %copy-start.6 = (bf16[16,16,1536]{2,1,0:T(8,128)(2,1)S(1)}, bf16[16,16,1536]{2,1,0:T(8,128)(2,1)}, u32[]{:S(2)}) copy-start(bf16[16,16,1536]{2,1,0:T(8,128)(2,1)} %param.13) | copy-start | bytes 2359300
  4.4 30.7 %all-to-all-start = ((bf16[32,8,1664]{2,1,0:T(8,128)(2,1)}), bf16[32,8,1664]{2,1,0:T(8,128)(2,1)S(1)}, u32[]{:S(2)}, u32[]{:S(2)}) async-start(bf16[32,8,1664]{2,1,0:T(8,128)(2,1)} %bitcast.4), calls=%async_computation | async-start | bytes 1703936 | tf_op jit(solution)/shard_map/all_to_all | solution.py:581
  14.1 4.4 %collective-permute-start.5 = (bf16[8,32,256]{2,1,0:T(8,128)(2,1)S(1)}, bf16[8,32,256]{2,1,0:T(8,128)(2,1)S(1)}, u32[]{:S(2)}, u32[]{:S(2)}) collective-permute-start(bf16[8,32,256]{2,1,0:T(8,128)(2,1)S(1)} %get-tuple-element.44), channel_id=1, source_target_pairs={{8,0},{16,8},{24,16},{9,1},{17,9},{25,17},{10,2},{18,10},{26,18},{... | collective-permute-start | bytes 393224 | tf_op jit(solution)/shard_map/ppermute | solution.py:588
  15.4 4.0 %collective-permute-start.4 = (bf16[8,32,256]{2,1,0:T(8,128)(2,1)S(1)}, bf16[8,32,256]{2,1,0:T(8,128)(2,1)S(1)}, u32[]{:S(2)}, u32[]{:S(2)}) collective-permute-start(bf16[8,32,256]{2,1,0:T(8,128)(2,1)S(1)} %get-tuple-element.45), channel_id=1, source_target_pairs={{0,8},{8,16},{16,24},{1,9},{9,17},{17,25},{2,10},{10,18},{18,26},{... | collective-permute-start | bytes 393224 | tf_op jit(solution)/shard_map/ppermute | solution.py:588
  18.5 19.9 %copy-start.14 = (bf16[8,32,256]{2,1,0:T(8,128)(2,1)}, bf16[8,32,256]{2,1,0:T(8,128)(2,1)S(1)}, u32[]{:S(2)}) copy-start(bf16[8,32,256]{2,1,0:T(8,128)(2,1)S(1)} %collective-permute-done.5.xhi_ref) | copy-start | bytes 393220
  19.4 19.0 %copy-start.16 = (bf16[8,32,256]{2,1,0:T(8,128)(2,1)}, bf16[8,32,256]{2,1,0:T(8,128)(2,1)S(1)}, u32[]{:S(2)}) copy-start(bf16[8,32,256]{2,1,0:T(8,128)(2,1)S(1)} %collective-permute-done.4.xlo_ref) | copy-start | bytes 393220
  19.9 29.4 %collective-permute-start.6 = (bf16[8,48,256]{2,1,0:T(8,128)(2,1)S(1)}, bf16[8,48,256]{2,1,0:T(8,128)(2,1)}, u32[]{:S(2)}, u32[]{:S(2)}) collective-permute-start(bf16[8,48,256]{2,1,0:T(8,128)(2,1)S(1)} %get-tuple-element.27.high_ref), channel_id=1, source_target_pairs={{0,1},{1,2},{2,3},{3,4},{4,5},{5,6},{6,7},{8,9},{9,10},{10,11},{11... | collective-permute-start | bytes 589832 | tf_op jit(solution)/shard_map/ppermute | solution.py:588
  24.2 25.1 %collective-permute-start.7 = (bf16[8,48,256]{2,1,0:T(8,128)(2,1)S(1)}, bf16[8,48,256]{2,1,0:T(8,128)(2,1)}, u32[]{:S(2)}, u32[]{:S(2)}) collective-permute-start(bf16[8,48,256]{2,1,0:T(8,128)(2,1)S(1)} %get-tuple-element.28.low_ref), channel_id=1, source_target_pairs={{1,0},{2,1},{3,2},{4,3},{5,4},{6,5},{7,6},{9,8},{10,9},{11,10},{12... | collective-permute-start | bytes 589832 | tf_op jit(solution)/shard_map/ppermute | solution.py:588
  36.2 6.6 %copy-start.35 = (s32[560]{0:T(1024)S(1)}, s32[560]{0:T(1024)}, u32[]{:S(2)}) copy-start(s32[560]{0:T(1024)} %constant.41.clone) | copy-start | bytes 6724
  36.2 6.6 %copy-start.36 = (s32[560]{0:T(1024)S(1)}, s32[560]{0:T(1024)}, u32[]{:S(2)}) copy-start(s32[560]{0:T(1024)} %constant.40.clone) | copy-start | bytes 6724
  36.2 6.6 %copy-start.37 = (pred[560]{0:T(1024)(128)(4,1)S(1)}, pred[560]{0:T(1024)(128)(4,1)}, u32[]{:S(2)}) copy-start(pred[560]{0:T(1024)(128)(4,1)} %constant.42.clone) | copy-start | bytes 1684
  38.4 20.8 %copy-start.1 = (bf16[8,256,256]{2,1,0:T(8,128)(2,1)}, bf16[8,256,256]{2,1,0:T(8,128)(2,1)S(1)}, u32[]{:S(2)}) copy-start(bf16[8,256,256]{2,1,0:T(8,128)(2,1)S(1)} %get-tuple-element.24.f_ref.field_ref) | copy-start | bytes 3145732
  38.5 5.7 %collective-permute-start.1 = (bf16[8,32,256]{2,1,0:T(8,128)(2,1)S(1)}, bf16[8,32,256]{2,1,0:T(8,128)(2,1)S(1)}, u32[]{:S(2)}, u32[]{:S(2)}) collective-permute-start(bf16[8,32,256]{2,1,0:T(8,128)(2,1)S(1)} %get-tuple-element.46), channel_id=1, source_target_pairs={{8,0},{16,8},{24,16},{9,1},{17,9},{25,17},{10,2},{18,10},{26,18},{... | collective-permute-start | bytes 393224 | tf_op jit(solution)/shard_map/ppermute | solution.py:588
  39.8 4.4 %collective-permute-start = (bf16[8,32,256]{2,1,0:T(8,128)(2,1)S(1)}, bf16[8,32,256]{2,1,0:T(8,128)(2,1)S(1)}, u32[]{:S(2)}, u32[]{:S(2)}) collective-permute-start(bf16[8,32,256]{2,1,0:T(8,128)(2,1)S(1)} %get-tuple-element.47), channel_id=1, source_target_pairs={{0,8},{8,16},{16,24},{1,9},{9,17},{17,25},{2,10},{10,18},{18,26},{... | collective-permute-start | bytes 393224 | tf_op jit(solution)/shard_map/ppermute | solution.py:588
  44.2 15.1 %copy-start.18 = (bf16[8,32,256]{2,1,0:T(8,128)(2,1)}, bf16[8,32,256]{2,1,0:T(8,128)(2,1)S(1)}, u32[]{:S(2)}) copy-start(bf16[8,32,256]{2,1,0:T(8,128)(2,1)S(1)} %collective-permute-done.1.xhi_ref) | copy-start | bytes 393220
  44.2 15.1 %copy-start.20 = (bf16[8,32,256]{2,1,0:T(8,128)(2,1)}, bf16[8,32,256]{2,1,0:T(8,128)(2,1)S(1)}, u32[]{:S(2)}) copy-start(bf16[8,32,256]{2,1,0:T(8,128)(2,1)S(1)} %collective-permute-done.xlo_ref) | copy-start | bytes 393220
  44.6 14.6 %collective-permute-start.2 = (bf16[8,48,256]{2,1,0:T(8,128)(2,1)S(1)}, bf16[8,48,256]{2,1,0:T(8,128)(2,1)S(1)}, u32[]{:S(2)}, u32[]{:S(2)}) collective-permute-start(bf16[8,48,256]{2,1,0:T(8,128)(2,1)S(1)} %get-tuple-element.25.high_ref), channel_id=1, source_target_pairs={{0,1},{1,2},{2,3},{3,4},{4,5},{5,6},{6,7},{8,9},{9,10},{10,11},{11... | collective-permute-start | bytes 589832 | tf_op jit(solution)/shard_map/ppermute | solution.py:588
  47.8 11.5 %copy-start.7 = (bf16[27,96,96]{2,1,0:T(8,128)(2,1)S(1)}, bf16[27,96,96]{2,1,0:T(8,128)(2,1)}, u32[]{:S(2)}) copy-start(bf16[27,96,96]{2,1,0:T(8,128)(2,1)} %raw_ref.6) | copy-start | bytes 1492996
  47.8 11.4 %collective-permute-start.3 = (bf16[8,48,256]{2,1,0:T(8,128)(2,1)S(1)}, bf16[8,48,256]{2,1,0:T(8,128)(2,1)S(1)}, u32[]{:S(2)}, u32[]{:S(2)}) collective-permute-start(bf16[8,48,256]{2,1,0:T(8,128)(2,1)S(1)} %get-tuple-element.26.low_ref), channel_id=1, source_target_pairs={{1,0},{2,1},{3,2},{4,3},{5,4},{6,5},{7,6},{9,8},{10,9},{11,10},{12... | collective-permute-start | bytes 589832 | tf_op jit(solution)/shard_map/ppermute | solution.py:588
  59.2 9.3 %copy-start.32 = (bf16[8,256,256]{2,1,0:T(8,128)(2,1)}, bf16[8,256,256]{2,1,0:T(8,128)(2,1)S(1)}, u32[]{:S(2)}) copy-start(bf16[8,256,256]{2,1,0:T(8,128)(2,1)S(1)} %get-tuple-element.32.outer_ref) | copy-start | bytes 3145732
  59.2 9.2 %copy-start.10 = (bf16[8,48,256]{2,1,0:T(8,128)(2,1)}, bf16[8,48,256]{2,1,0:T(8,128)(2,1)S(1)}, u32[]{:S(2)}) copy-start(bf16[8,48,256]{2,1,0:T(8,128)(2,1)S(1)} %collective-permute-done.2.ylo_ref) | copy-start | bytes 589828
  59.3 9.2 %copy-start.12 = (bf16[8,48,256]{2,1,0:T(8,128)(2,1)}, bf16[8,48,256]{2,1,0:T(8,128)(2,1)S(1)}, u32[]{:S(2)}) copy-start(bf16[8,48,256]{2,1,0:T(8,128)(2,1)S(1)} %collective-permute-done.3.yhi_ref) | copy-start | bytes 589828
  59.3 9.2 %copy-start.24 = (bf16[6,256,256]{2,1,0:T(8,128)(2,1)S(1)}, bf16[6,256,256]{2,1,0:T(8,128)(2,1)}, u32[]{:S(2)}) copy-start(bf16[6,256,256]{2,1,0:T(8,128)(2,1)} %constant.38.clone.perm_ref) | copy-start | bytes 2359300
  68.5 9.5 %copy-start.27 = (bf16[8,336,256]{2,1,0:T(8,128)(2,1)}, bf16[8,336,256]{2,1,0:T(8,128)(2,1)S(1)}, u32[]{:S(2)}) copy-start(bf16[8,336,256]{2,1,0:T(8,128)(2,1)S(1)} %get-tuple-element.38.act_ref) | copy-start | bytes 4128772
  68.5 9.5 %copy-start.30 = (bf16[8,336,256]{2,1,0:T(8,128)(2,1)}, bf16[8,336,256]{2,1,0:T(8,128)(2,1)S(1)}, u32[]{:S(2)}) copy-start(bf16[8,336,256]{2,1,0:T(8,128)(2,1)S(1)} %get-tuple-element.30.hg_ref) | copy-start | bytes 4128772
  78.0 7.5 %copy-start.2 = (bf16[8,256,256]{2,1,0:T(8,128)(2,1)S(1)}, bf16[8,256,256]{2,1,0:T(8,128)(2,1)}, u32[]{:S(2)}) copy-start(bf16[8,256,256]{2,1,0:T(8,128)(2,1)} %copy-done.1) | copy-start | bytes 3145732
  78.0 7.5 %copy-start.11 = (bf16[8,48,256]{2,1,0:T(8,128)(2,1)S(1)}, bf16[8,48,256]{2,1,0:T(8,128)(2,1)}, u32[]{:S(2)}) copy-start(bf16[8,48,256]{2,1,0:T(8,128)(2,1)} %copy-done.10) | copy-start | bytes 589828
  78.0 31.5 %all-to-all-start.1 = ((bf16[32,8,1536]{2,1,0:T(8,128)(2,1)}), bf16[32,8,1536]{2,1,0:T(8,128)(2,1)S(1)}, u32[]{:S(2)}, u32[]{:S(2)}) async-start(bf16[32,8,1536]{2,1,0:T(8,128)(2,1)} %bitcast.7), calls=%async_computation.1 | async-start | bytes 1572864 | tf_op jit(solution)/shard_map/all_to_all | solution.py:581
  106.8 2.7 %collective-permute-start.8 = (f32[2,1024,128]{2,1,0:T(8,128)S(1)}, f32[2,1024,128]{2,1,0:T(8,128)S(1)}, u32[]{:S(2)}, u32[]{:S(2)}) collective-permute-start(f32[2,1024,128]{2,1,0:T(8,128)S(1)} %get-tuple-element.36), channel_id=1, source_target_pairs={{0,8},{8,0},{16,24},{24,16},{1,9},{9,1},{17,25},{25,17},{2,10},{10... | collective-permute-start | bytes 3145736 | tf_op jit(solution)/shard_map/ppermute | solution.py:593
  110.4 22.2 %all-to-all-start.2 = ((bf16[16,2,64,128]{3,2,1,0:T(8,128)(2,1)}), bf16[16,2,64,128]{3,2,1,0:T(8,128)(2,1)S(1)}, u32[]{:S(2)}, u32[]{:S(2)}) async-start(bf16[16,2,64,128]{3,2,1,0:T(8,128)(2,1)} %shard_map.148), calls=%async_computation.2 | async-start | bytes 1048576 | tf_op jit(solution)/shard_map/all_to_all | solution.py:581
  130.8 21.8 %copy-start.5 = (s32[128]{0:T(128)S(1)}, s32[128]{0:T(128)}, u32[]{:S(2)}) copy-start(s32[128]{0:T(128)} %param.12) | copy-start | bytes 1540
  152.7 1.9 %collective-permute-start.9 = (bf16[16,2,64,128]{3,2,1,0:T(8,128)(2,1)S(1)}, bf16[16,2,64,128]{3,2,1,0:T(8,128)(2,1)S(1)}, u32[]{:S(2)}, u32[]{:S(2)}) collective-permute-start(bf16[16,2,64,128]{3,2,1,0:T(8,128)(2,1)S(1)} %all_to_all.20.mine_ref), channel_id=1, source_target_pairs={{0,8},{8,0},{16,24},{24,16},{1,9},{9,1},{17,25},{25,17},{2,10},{10... | collective-permute-start | bytes 1572872 | tf_op jit(solution)/shard_map/ppermute | solution.py:593
  (19 other events, 47.3 us)

commit v7 on v6

--- a/solution.py
+++ b/solution.py
@@ -74,7 +74,7 @@
     pos = owner_col.astype(F32) * cap + rank
     place = lax.broadcasted_iota(jnp.int32, (rows, back_ref.shape[0]), 1).astype(F32)
     hot = jnp.where(place == pos, 1.0, 0.0).astype(BF)
-    out_ref[...] = dot(hot, back_ref[...]).astype(BF)
+    out_ref[...] = dot(hot, back_ref[:, 0 : out_ref.shape[1]]).astype(BF)
 
 
 def mask_kernel(cap, slots, in_ref, codes_ref, mask_ref, route_ref):
@@ -394,15 +394,15 @@
     each_step(f_ref.shape[0], body)
 
 
-def correlate(gt_ref, ext_ref, taps_ref, channels):
-    blocks = ext_ref.shape[1]
+def correlate(gt_ref, ext_ref, first_x, taps_ref, channels):
+    pairs = ext_ref.shape[1] - 1
 
     def body(ab, carry):
         a = ab // 3
         b = ab % 3
-        both = dot(gt_ref[...], ext_ref[b, :, pl.ds(a, NX)].reshape(blocks * NX * NY, PAIR))
-        near = both[0 : 2 * channels]
-        far = both[2 * channels : 4 * channels]
+        left = gt_ref[...]
+        near = dot(left, ext_ref[b, 0:pairs, pl.ds(a + first_x, NX)].reshape(pairs * NX * NY, PAIR))
+        far = dot(left, ext_ref[b, 1 : pairs + 1, pl.ds(a + first_x, NX)].reshape(pairs * NX * NY, PAIR))
         low = slice(0, channels)
         high = slice(channels, 2 * channels)
         taps_ref[3 * ab] = near[low, 0:LANES] + near[high, LANES:PAIR]
@@ -451,24 +451,17 @@
 
 def turn(gt_ref, g_ref, start, channels):
     inner = NX * NY
-    pairs = g_ref.shape[0]
-    two = 2 * channels
-    gt_ref[0:two, pairs * inner :] = jnp.zeros((two, inner), BF)
-    gt_ref[two : 2 * two, 0:inner] = jnp.zeros((two, inner), BF)
-    for k in range(pairs):
+    for k in range(g_ref.shape[0]):
         value = g_ref[k, start : start + inner, :].T
-        for i in range(2):
-            half = value[i * LANES : i * LANES + channels]
-            at = i * channels
-            gt_ref[at : at + channels, k * inner : (k + 1) * inner] = half
-            gt_ref[two + at : two + at + channels, (k + 1) * inner : (k + 2) * inner] = half
-
-
-def corr_kernel(channels, core_ref, f_ref, xlo_ref, xhi_ref, ylo_ref, yhi_ref, hg_ref, act_ref, outer_ref,
+        gt_ref[0:channels, k * inner : (k + 1) * inner] = value[0:channels]
+        gt_ref[channels : 2 * channels, k * inner : (k + 1) * inner] = value[LANES : LANES + channels]
+
+
+def corr_kernel(channels, run, core_ref, f_ref, xlo_ref, xhi_ref, ylo_ref, yhi_ref, hg_ref, act_ref, outer_ref,
                 keep_ref, give_ref, ext_ref, gt_ref, taps_ref, packed_ref):
-    half = keep_ref.shape[1]
-    mine = pl.ds(pl.multiple_of(core_ref[0] * half, half), half)
-    other = pl.ds(pl.multiple_of((1 - core_ref[0]) * half, half), half)
+    runs = keep_ref.shape[0] // run
+    block = 2 * runs * run
+    blocks = packed_ref.shape[0] // block
     taps_ref[27] = jnp.zeros((channels, LANES), F32)
     for i in range(2):
         if i == 0:
@@ -477,10 +470,17 @@
         else:
             widen_one(ext_ref, act_ref)
             turn(gt_ref, outer_ref, 0, channels)
-        correlate(gt_ref, ext_ref, taps_ref, channels)
+        correlate(gt_ref, ext_ref, 0, taps_ref, channels)
         pack_taps(taps_ref, packed_ref, channels)
-        keep_ref[i] = packed_ref[mine, :]
-        give_ref[i] = packed_ref[other, :]
+        for l in range(blocks):
+            lanes = slice((i * blocks + l) * LANES, (i * blocks + l + 1) * LANES)
+            for x in range(runs):
+                base = l * block + 2 * x * run
+                rows = slice(x * run, (x + 1) * run)
+                mine = pl.multiple_of(base + core_ref[0] * run, run)
+                other = pl.multiple_of(base + (1 - core_ref[0]) * run, run)
+                keep_ref[rows, lanes] = packed_ref[pl.ds(mine, run), :]
+                give_ref[rows, lanes] = packed_ref[pl.ds(other, run), :]
 
 
 def grid_grad_kernel(hg_ref, raw_ref, outer_ref, perm_ref, take_ref, out_ref, ext_ref, sum_ref, turned_ref, w_ref):
@@ -519,33 +519,33 @@
 
 
 def pair_sum_kernel(keep_ref, got_ref, out_ref):
-    count, _, chunk, _ = out_ref.shape
+    out_ref[...] = (keep_ref[...] + got_ref[...]).astype(BF)
+
+
+def assemble_kernel(cap, run, back_ref, parts_ref, out_ref):
+    buffers, width = back_ref.shape
+    senders, lanes = parts_ref.shape
+    half = lanes // 2
+    out_ref[:, 0:width] = back_ref[...]
+    row = lax.broadcasted_iota(jnp.int32, (buffers, senders), 0)
+    col = lax.broadcasted_iota(jnp.int32, (buffers, senders), 1)
+    same = row % cap == col % cap
+    core = (row // run) % 2
+    total = jnp.zeros((buffers, half), F32)
     for i in range(2):
-        for s in range(count):
-            rows = slice(s * chunk, (s + 1) * chunk)
-            out_ref[s, i] = (keep_ref[i, rows, :] + got_ref[i, rows, :]).astype(BF)
-
-
-def chunk_sum_kernel(in_ref, out_ref):
-    count = in_ref.shape[0]
-    for i in range(2):
-        total = in_ref[0, i].astype(F32)
-        for s in range(1, count):
-            total = total + in_ref[s, i].astype(F32)
-        total = total.astype(BF)
-        for s in range(count):
-            out_ref[s, i] = total
+        add = jnp.where(same & (core == i), 1.0, 0.0).astype(BF)
+        total = total + dot(add, parts_ref[:, i * half : (i + 1) * half])
+    out_ref[:, width : width + half] = total.astype(BF)
 
 
 def unpack_kernel(factor, core_ref, mine_ref, other_ref, first_ref, second_ref, flat_ref):
-    count, _, chunk, _ = mine_ref.shape
-    half = count * chunk
+    rows, lanes = mine_ref.shape
     for i, out_ref in enumerate((first_ref, second_ref)):
-        for s in range(count):
-            start = core_ref[0] * half + s * chunk
-            flat_ref[pl.ds(pl.multiple_of(start, chunk), chunk), :] = mine_ref[s, i].astype(F32)
-            start = (1 - core_ref[0]) * half + s * chunk
-            flat_ref[pl.ds(pl.multiple_of(start, chunk), chunk), :] = other_ref[s, i].astype(F32)
+        own = core_ref[0] == i
+        for l in range(lanes // LANES):
+            at = slice(l * LANES, (l + 1) * LANES)
+            value = jnp.where(own, mine_ref[:, at].astype(F32), other_ref[:, at].astype(F32))
+            flat_ref[l * rows : (l + 1) * rows, :] = value
         unpack_taps(factor, flat_ref, out_ref)
 
 
@@ -700,47 +700,46 @@
         1.3 * conv_flops, 7e6, (ext, edge, band), ROOM_WIDE,
     )(cot, *cot_halo, mask, second_weight)
 
-    unit = 16 * count_all
-    packed_rows = -(-21 * channels // unit) * unit
-    half = packed_rows // 2
-    chunk = packed_rows // count_all
-    half_shape = shape((2, half, LANES), F32)
     act, hg = call(
         hidden_kernel, (wide_shape, wide_shape), 1.3 * conv_flops, 8e6, (ext, edge, band), ROOM_WIDE,
     )(field, *field_halo, mask, first_weight, act_grad)
 
-    back = call(
-        grid_grad_kernel, shape((buffers, row_width), BF), 1.2 * conv_flops, 6e6,
-        (ext_near, sums, turned_low, band), ROOM_NEAR,
-    )(hg, first_weight, outer, perm, take)
-    returned = share(back.reshape(count_all, cap, row_width), ALL).reshape(buffers, row_width)
-
-    act, back = lax.optimization_barrier((act, back))
+    packed_rows = -(-21 * channels // buffers) * buffers
+    run = count_y * cap
+    grad_lanes = 2 * packed_rows // buffers * LANES
+    half_shape = shape((buffers // 2, grad_lanes), F32)
     keep, give = call(
-        functools.partial(corr_kernel, channels), (half_shape, half_shape), 2 * conv_flops, 10e6,
+        functools.partial(corr_kernel, channels, run), (half_shape, half_shape), 2 * conv_flops, 10e6,
         (
-            ext_near, pltpu.VMEM((4 * channels, (pairs + 1) * slots), BF),
+            ext_near, pltpu.VMEM((2 * channels, pairs * slots), BF),
             pltpu.VMEM((28, channels, LANES), F32), pltpu.VMEM((packed_rows, LANES), F32),
         ),
         ROOM_CORR, in_specs=[smem] + [vmem] * 8,
     )(core, field, *field_halo[:4], hg, act, outer)
     got = swap_cores(give)
-    got, returned = lax.optimization_barrier((got, returned))
     sent = call(
-        pair_sum_kernel, shape((count_all // 2, 2, chunk, LANES), BF), 1e6, 2e6,
+        pair_sum_kernel, shape((buffers // 2, grad_lanes), BF), 1e6, 2e6,
     )(keep, got)
-    parts = share(sent, SAME_CORE)
-    act, sent = lax.optimization_barrier((act, sent))
+    parts = share(sent.reshape(count_all // 2, cap, grad_lanes), SAME_CORE).reshape(buffers // 2, grad_lanes)
+
+    hg, sent = lax.optimization_barrier((hg, sent))
+    back = call(
+        grid_grad_kernel, shape((buffers, row_width), BF), 1.2 * conv_flops, 6e6,
+        (ext_near, sums, turned_low, band), ROOM_NEAR,
+    )(hg, first_weight, outer, perm, take)
+    back_width = row_width + grad_lanes // 2
+    mixed = call(
+        functools.partial(assemble_kernel, cap, run), shape((buffers, back_width), BF), 2e8, 3e6,
+    )(back, parts)
+    returned = share(mixed.reshape(count_all, cap, back_width), ALL).reshape(buffers, back_width)
+
+    act, mixed = lax.optimization_barrier((act, mixed))
     block_output = call(
         block_kernel, shape((slots, row_width), BF), 1.2 * conv_flops, 8e6,
         (ext_near, sums, turned_low, band), ROOM_NEAR,
     )(act, mask, second_weight, field, perm)
 
-    parts, block_output = lax.optimization_barrier((parts, block_output))
-    totals = share(call(
-        chunk_sum_kernel, shape((count_all // 2, 2, chunk, LANES), BF), 1e6, 1e6,
-    )(parts), SAME_CORE)
-
+    mine = returned[:, row_width:]
     feature_grads = call(
         functools.partial(collect_kernel, cap, slots), shape((shard_rows, row_width), BF),
         2 * buffers * shard_rows * row_width, 3 * shard_rows * row_width * 2,
@@ -751,7 +750,7 @@
     first_grad, second_grad = call(
         functools.partial(unpack_kernel, factor), (grads, grads), 1e6, 4e6,
         (pltpu.VMEM((packed_rows, LANES), F32),), in_specs=[smem, vmem, vmem],
-    )(core, totals, swap_cores(totals))
+    )(core, mine, swap_cores(mine))
     return (block_output.reshape(cotangent.shape), feature_grads, first_grad, second_grad)
 
 

time: 158 us -> 163 us (1.032)
  waiting for transfers between devices: 15.6 us -> 49.2 us
  blocking collectives: 20 us -> 0 us
  local copies, waits for them, and re-layouts: 16.4 us -> 11.1 us
  starting transfers between devices: 40.5 us -> 37.8 us
    all_to_all x3, waiting for transfers between devices: 11.3 us -> 45.9 us  [share(): return lax.all_to_all(parts, axes, split_axis=0, concat_axis=0, tiled=True)]
    all_to_all x1 -> x0, blocking collectives: 20 us -> none  [share(): return lax.all_to_all(parts, axes, split_axis=0, concat_axis=0, tiled=True)]
    unnamed x76 -> x56, local copies, waits for them, and re-layouts: 15.4 us -> 10.2 us
    all_to_all x3, starting transfers between devices: 21.5 us -> 16.8 us  [share(): return lax.all_to_all(parts, axes, split_axis=0, concat_axis=0, tiled=True)]
    ppermute x2, starting transfers between devices: 0.14 us -> 2.15 us  [swap_cores(): return lax.ppermute(value, RX, [(i, i ^ 1) for i in range(count)])]
  transfers between devices with their start and end apart: 13 -> 13, of which waited for: 5 -> 5; matrix products, arithmetic and copies ran while one was open for 0% -> 0% of each run, Pallas kernels for 26% -> 21%
where the time goes in v7:
time: 163 us; the launch traced here: 162 us
  Pallas kernels  62.7 us (38%)
  waiting for transfers between devices  49.2 us (30%)
  starting transfers between devices  37.8 us (23%)
  local copies, waits for them, and re-layouts  11.1 us (7%)
    all_to_all x3, waiting for transfers between devices, share(): return lax.all_to_all(parts, axes, split_axis=0, concat_axis=0, tiled=True)  45.9 us
    ppermute x8, starting transfers between devices, neighbours(): return (lax.ppermute(upper, axes, ahead), lax.ppermute(lower, axes, behind))  18.9 us
    all_to_all x3, starting transfers between devices, share(): return lax.all_to_all(parts, axes, split_axis=0, concat_axis=0, tiled=True)  16.8 us
    pallas_call x1, Pallas kernels, on_device(): call(functools.partial(corr_kernel, channels, run), (half_shape, half_sha...  13.9 us
    unnamed x56, local copies, waits for them, and re-layouts  10.2 us
    pallas_call x1, Pallas kernels, on_device(): call(outer_kernel, (shape((pairs, OUT_ROWS, PAIR), F32), field_shape), 1....  9.9 us
    pallas_call x1, Pallas kernels, on_device(): call(hidden_kernel, (wide_shape, wide_shape), 1.3 * conv_flops, 8000000.0...  9.11 us
    pallas_call x1, Pallas kernels, on_device(): call(block_kernel, shape((slots, row_width), BF), 1.2 * conv_flops, 80000...  8.93 us
  transfers between devices with their start and end apart: 13, of which 5 were waited for; matrix products, arithmetic and copies ran while one was open for 0% of the time, Pallas kernels for 21%

profile of v7, /device:TPU:0, one launch (start us, length us, event | category | flops | bytes accessed | tf_op | source)
XLA Modules:
  0.0 162.0 jit_solution(9515769019637809924)
XLA Ops:
  3.0 1.4 shard_map.138
  4.4 7.3 %all-to-all-start = ((bf16[32,8,1664]{2,1,0:T(8,128)(2,1)}), bf16[32,8,1664]{2,1,0:T(8,128)(2,1)S(1)}, u32[]{:S(2)}, u32[]{:S(2)}) async-start(bf16[32,8,1664]{2,1,0:T(8,128)(2,1)} %bitcast.3), calls=%async_computation | async-start | bytes 1703936 | tf_op jit(solution)/shard_map/all_to_all | solution.py:581
  11.7 1.1 copy-done.11
  12.9 1.2 shard_map.142.f_ref
  14.1 1.3 collective-permute-start.5
  15.4 3.0 %collective-permute-start.4 = (bf16[8,32,256]{2,1,0:T(8,128)(2,1)S(1)}, bf16[8,32,256]{2,1,0:T(8,128)(2,1)S(1)}, u32[]{:S(2)}, u32[]{:S(2)}) collective-permute-start(bf16[8,32,256]{2,1,0:T(8,128)(2,1)S(1)} %get-tuple-element.37), channel_id=1, source_target_pairs={{0,8},{8,16},{16,24},{1,9},{9,17},{17,25},{2,10},{10,18},{18,26},{... | collective-permute-start | bytes 393224 | tf_op jit(solution)/shard_map/ppermute | solution.py:588
  19.9 4.4 %collective-permute-start.6 = (bf16[8,48,256]{2,1,0:T(8,128)(2,1)S(1)}, bf16[8,48,256]{2,1,0:T(8,128)(2,1)}, u32[]{:S(2)}, u32[]{:S(2)}) collective-permute-start(bf16[8,48,256]{2,1,0:T(8,128)(2,1)S(1)} %get-tuple-element.23.high_ref), channel_id=1, source_target_pairs={{0,1},{1,2},{2,3},{3,4},{4,5},{5,6},{6,7},{8,9},{9,10},{10,11},{11... | collective-permute-start | bytes 589832 | tf_op jit(solution)/shard_map/ppermute | solution.py:588
  24.2 1.3 collective-permute-start.7
  25.5 9.6 %all-to-all-done = bf16[32,8,1664]{2,1,0:T(8,128)(2,1)S(1)} async-done(((bf16[32,8,1664]{2,1,0:T(8,128)(2,1)}), bf16[32,8,1664]{2,1,0:T(8,128)(2,1)S(1)}, u32[]{:S(2)}, u32[]{:S(2)}) %all-to-all-start) | async-done | bytes 852000 | tf_op jit(solution)/shard_map/all_to_all | solution.py:581
  35.1 1.1 copy-done.12
  36.2 2.2 %shard_map.139 = (bf16[8,256,256]{2,1,0:T(8,128)(2,1)S(1)}, bf16[256,256]{1,0:T(8,128)(2,1)S(1)}) custom-call(s32[1]{0:T(128)} %bitcast.me_ref, bf16[256,1664]{1,0:T(8,128)(2,1)S(1)} %bitcast.14, bf16[6,256,256]{2,1,0:T(8,128)(2,1)S(1)} %copy-done.12), custom_call_target="tpu_custom_call" | custom-call | flops 1000000000 | bytes 3000000 | tf_op jit(solution)/shard_map/pallas_call | solution.py:686
  38.5 1.3 collective-permute-start.1
  39.8 3.0 %collective-permute-start = (bf16[8,32,256]{2,1,0:T(8,128)(2,1)S(1)}, bf16[8,32,256]{2,1,0:T(8,128)(2,1)S(1)}, u32[]{:S(2)}, u32[]{:S(2)}) collective-permute-start(bf16[8,32,256]{2,1,0:T(8,128)(2,1)S(1)} %get-tuple-element.39), channel_id=1, source_target_pairs={{0,8},{8,16},{16,24},{1,9},{9,17},{17,25},{2,10},{10,18},{18,26},{... | collective-permute-start | bytes 393224 | tf_op jit(solution)/shard_map/ppermute | solution.py:588
  44.6 3.2 %collective-permute-start.2 = (bf16[8,48,256]{2,1,0:T(8,128)(2,1)S(1)}, bf16[8,48,256]{2,1,0:T(8,128)(2,1)S(1)}, u32[]{:S(2)}, u32[]{:S(2)}) collective-permute-start(bf16[8,48,256]{2,1,0:T(8,128)(2,1)S(1)} %get-tuple-element.21.high_ref), channel_id=1, source_target_pairs={{0,1},{1,2},{2,3},{3,4},{4,5},{5,6},{6,7},{8,9},{9,10},{10,11},{11... | collective-permute-start | bytes 589832 | tf_op jit(solution)/shard_map/ppermute | solution.py:588
  47.8 1.4 collective-permute-start.3
  49.3 9.9 %shard_map.144 = (f32[8,336,256]{2,1,0:T(8,128)S(1)}, bf16[8,256,256]{2,1,0:T(8,128)(2,1)S(1)}) custom-call(bf16[8,256,256]{2,1,0:T(8,128)(2,1)S(1)} %copy-done.2, bf16[8,32,256]{2,1,0:T(8,128)(2,1)S(1)} %copy-done.10, bf16[8,32,256]{2,1,0:T(8,128)(2,1)S(1)} %collective-permute-done.5.xhi_ref, bf16[8,48,256]{2,1,0:T(8,128)(2,1)} %collective-permute-done.6.ylo_ref, ...), custom_call_target="tpu_custom_call" | custom-call | flops 6281389568 | bytes 7000000 | tf_op jit(solution)/shard_map/pallas_call | solution.py:698
  59.2 9.1 %shard_map.145 = (bf16[8,336,256]{2,1,0:T(8,128)(2,1)S(1)}, bf16[8,336,256]{2,1,0:T(8,128)(2,1)S(1)}) custom-call(bf16[8,256,256]{2,1,0:T(8,128)(2,1)S(1)} %get-tuple-element.20.f_ref.field_ref, bf16[8,32,256]{2,1,0:T(8,128)(2,1)S(1)} %collective-permute-done.xlo_ref, bf16[8,32,256]{2,1,0:T(8,128)(2,1)S(1)} %collective-permute-done.1.xhi_ref, ...), custom_call_target="tpu_custom_call" | custom-call | flops 6281389568 | bytes 8000000 | tf_op jit(solution)/shard_map/pallas_call | solution.py:703
  68.4 13.9 %shard_map.146 = (f32[128,2048]{1,0:T(8,128)S(1)}, f32[128,2048]{1,0:T(8,128)S(1)}) custom-call(s32[1]{0:T(128)} %bitcast.6.core_ref, bf16[8,256,256]{2,1,0:T(8,128)(2,1)S(1)} %get-tuple-element.20.f_ref.field_ref, bf16[8,32,256]{2,1,0:T(8,128)(2,1)S(1)} %collective-permute-done.xlo_ref, bf16[8,32,256]{2,1,0:T(8,128)(2,1)S(1)} %collective-permute-done.1.xhi_ref, ...), custom_call_target="tpu_custom_call" | custom-call | flops 9663676416 | bytes 10000000 | tf_op jit(solution)/shard_map/pallas_call | solution.py:711
  82.3 2.1 %collective-permute-start.8 = (f32[128,2048]{1,0:T(8,128)S(1)}, f32[128,2048]{1,0:T(8,128)S(1)}, u32[]{:S(2)}, u32[]{:S(2)}) collective-permute-start(f32[128,2048]{1,0:T(8,128)S(1)} %get-tuple-element.30), channel_id=1, source_target_pairs={{0,8},{8,0},{16,24},{24,16},{1,9},{9,1},{17,25},{25,17},{2,10},{10... | collective-permute-start | bytes 3145736 | tf_op jit(solution)/shard_map/ppermute | solution.py:593
  84.4 2.3 %collective-permute-done.8.got_ref = f32[128,2048]{1,0:T(8,128)S(1)} collective-permute-done((f32[128,2048]{1,0:T(8,128)S(1)}, f32[128,2048]{1,0:T(8,128)S(1)}, u32[]{:S(2)}, u32[]{:S(2)}) %collective-permute-start.8) | collective-permute-done | bytes 1048608 | tf_op jit(solution)/shard_map/ppermute | solution.py:593
  87.5 6.7 %all-to-all-start.1 = ((bf16[16,8,2048]{2,1,0:T(8,128)(2,1)}), bf16[16,8,2048]{2,1,0:T(8,128)(2,1)S(1)}, u32[]{:S(2)}, u32[]{:S(2)}) async-start(bf16[16,8,2048]{2,1,0:T(8,128)(2,1)} %bitcast.7), calls=%async_computation.1 | async-start | bytes 1048576 | tf_op jit(solution)/shard_map/all_to_all | solution.py:581
  95.4 1.3 copy-done.21
  96.7 1.2 copy-done.23
  97.9 8.6 %shard_map.148.back_ref = bf16[256,1536]{1,0:T(8,128)(2,1)S(1)} custom-call(bf16[8,336,256]{2,1,0:T(8,128)(2,1)S(1)} %copy-done.21, bf16[27,96,96]{2,1,0:T(8,128)(2,1)S(1)} %copy-done.6, bf16[8,256,256]{2,1,0:T(8,128)(2,1)S(1)} %copy-done.23, bf16[6,256,256]{2,1,0:T(8,128)(2,1)S(1)} %copy-done.13, bf16[256,256]{1,0:T(8,128)(2,1)S(1)} %copy-done.17), custom_call_target="tpu_custom_call" | custom-call | flops 5798205952 | bytes 6000000 | tf_op jit(solution)/shard_map/pallas_call | solution.py:726
  106.5 3.2 %all-to-all-done.1 = bf16[16,8,2048]{2,1,0:T(8,128)(2,1)S(1)} async-done(((bf16[16,8,2048]{2,1,0:T(8,128)(2,1)}), bf16[16,8,2048]{2,1,0:T(8,128)(2,1)S(1)}, u32[]{:S(2)}, u32[]{:S(2)}) %all-to-all-start.1) | async-done | bytes 524320 | tf_op jit(solution)/shard_map/all_to_all | solution.py:581
  109.7 1.5 shard_map.149
  111.2 2.8 %all-to-all-start.2 = ((bf16[32,8,2560]{2,1,0:T(8,128)(2,1)}), bf16[32,8,2560]{2,1,0:T(8,128)(2,1)S(1)}, u32[]{:S(2)}, u32[]{:S(2)}) async-start(bf16[32,8,2560]{2,1,0:T(8,128)(2,1)} %bitcast.10), calls=%async_computation.2 | async-start | bytes 2621440 | tf_op jit(solution)/shard_map/all_to_all | solution.py:581
  114.0 33.2 %all-to-all-done.2 = bf16[32,8,2560]{2,1,0:T(8,128)(2,1)S(1)} async-done(((bf16[32,8,2560]{2,1,0:T(8,128)(2,1)}), bf16[32,8,2560]{2,1,0:T(8,128)(2,1)S(1)}, u32[]{:S(2)}, u32[]{:S(2)}) %all-to-all-start.2) | async-done | bytes 1310752 | tf_op jit(solution)/shard_map/all_to_all | solution.py:581
  148.5 1.3 copy-done.19
  149.8 8.9 %shard_map.150 = bf16[256,1536]{1,0:T(8,128)(2,1)} custom-call(bf16[8,336,256]{2,1,0:T(8,128)(2,1)S(1)} %copy-done.19, f32[560,128]{1,0:T(8,128)S(1)} %shard_map.141.mask_ref, bf16[27,96,96]{2,1,0:T(8,128)(2,1)S(1)} %copy-done.8, bf16[8,256,256]{2,1,0:T(8,128)(2,1)S(1)} %get-tuple-element.20.f_ref.field_ref, bf16[6,256,256]{2,1,0:T(8,128)(2,1)S(1)} %copy-done.14), custom_call_target="tpu_custom_call" | custom-call | flops 5798205952 | bytes 8000000 | tf_op jit(solution)/shard_map/pallas_call | solution.py:737
  158.8 1.2 shard_map.151
  160.0 2.0 %shard_map.152 = (f32[27,96,96]{2,1,0:T(8,128)}, f32[27,96,96]{2,1,0:T(8,128)}) custom-call(s32[1]{0:T(128)} %bitcast.6.core_ref, bf16[256,1024]{1,0:T(8,128)(2,1)S(1)} %slice.22.mine_ref, bf16[256,1024]{1,0:T(8,128)(2,1)S(1)} %collective-permute-done.9.other_ref), custom_call_target="tpu_custom_call" | custom-call | flops 1000000 | bytes 4000000 | tf_op jit(solution)/shard_map/pallas_call | solution.py:750
  (71 shorter events, 8.9 us)
Async XLA Ops:
  3.0 8.7 %copy-start.5 = (bf16[16,16,1536]{2,1,0:T(8,128)(2,1)S(1)}, bf16[16,16,1536]{2,1,0:T(8,128)(2,1)}, u32[]{:S(2)}) copy-start(bf16[16,16,1536]{2,1,0:T(8,128)(2,1)} %param.13) | copy-start | bytes 2359300
  4.4 30.7 %all-to-all-start = ((bf16[32,8,1664]{2,1,0:T(8,128)(2,1)}), bf16[32,8,1664]{2,1,0:T(8,128)(2,1)S(1)}, u32[]{:S(2)}, u32[]{:S(2)}) async-start(bf16[32,8,1664]{2,1,0:T(8,128)(2,1)} %bitcast.3), calls=%async_computation | async-start | bytes 1703936 | tf_op jit(solution)/shard_map/all_to_all | solution.py:581
  12.9 6.6 %copy-start.15 = (bf16[96,320]{1,0:T(8,128)(2,1)S(1)}, bf16[96,320]{1,0:T(8,128)(2,1)}, u32[]{:S(2)}) copy-start(bf16[96,320]{1,0:T(8,128)(2,1)} %constant.39.clone.pick_ref) | copy-start | bytes 184324
  14.1 21.0 %copy-start.1 = (bf16[8,256,256]{2,1,0:T(8,128)(2,1)}, bf16[8,256,256]{2,1,0:T(8,128)(2,1)S(1)}, u32[]{:S(2)}) copy-start(bf16[8,256,256]{2,1,0:T(8,128)(2,1)S(1)} %shard_map.142.f_ref) | copy-start | bytes 3145732
  14.1 4.4 %collective-permute-start.5 = (bf16[8,32,256]{2,1,0:T(8,128)(2,1)S(1)}, bf16[8,32,256]{2,1,0:T(8,128)(2,1)S(1)}, u32[]{:S(2)}, u32[]{:S(2)}) collective-permute-start(bf16[8,32,256]{2,1,0:T(8,128)(2,1)S(1)} %get-tuple-element.36), channel_id=1, source_target_pairs={{8,0},{16,8},{24,16},{9,1},{17,9},{25,17},{10,2},{18,10},{26,18},{... | collective-permute-start | bytes 393224 | tf_op jit(solution)/shard_map/ppermute | solution.py:588
  15.4 4.0 %collective-permute-start.4 = (bf16[8,32,256]{2,1,0:T(8,128)(2,1)S(1)}, bf16[8,32,256]{2,1,0:T(8,128)(2,1)S(1)}, u32[]{:S(2)}, u32[]{:S(2)}) collective-permute-start(bf16[8,32,256]{2,1,0:T(8,128)(2,1)S(1)} %get-tuple-element.37), channel_id=1, source_target_pairs={{0,8},{8,16},{16,24},{1,9},{9,17},{17,25},{2,10},{10,18},{18,26},{... | collective-permute-start | bytes 393224 | tf_op jit(solution)/shard_map/ppermute | solution.py:588
  19.4 15.6 %copy-start.9 = (bf16[8,32,256]{2,1,0:T(8,128)(2,1)}, bf16[8,32,256]{2,1,0:T(8,128)(2,1)S(1)}, u32[]{:S(2)}) copy-start(bf16[8,32,256]{2,1,0:T(8,128)(2,1)S(1)} %collective-permute-done.4.xlo_ref) | copy-start | bytes 393220
  19.9 29.4 %collective-permute-start.6 = (bf16[8,48,256]{2,1,0:T(8,128)(2,1)S(1)}, bf16[8,48,256]{2,1,0:T(8,128)(2,1)}, u32[]{:S(2)}, u32[]{:S(2)}) collective-permute-start(bf16[8,48,256]{2,1,0:T(8,128)(2,1)S(1)} %get-tuple-element.23.high_ref), channel_id=1, source_target_pairs={{0,1},{1,2},{2,3},{3,4},{4,5},{5,6},{6,7},{8,9},{9,10},{10,11},{11... | collective-permute-start | bytes 589832 | tf_op jit(solution)/shard_map/ppermute | solution.py:588
  24.2 25.0 %collective-permute-start.7 = (bf16[8,48,256]{2,1,0:T(8,128)(2,1)S(1)}, bf16[8,48,256]{2,1,0:T(8,128)(2,1)}, u32[]{:S(2)}, u32[]{:S(2)}) collective-permute-start(bf16[8,48,256]{2,1,0:T(8,128)(2,1)S(1)} %get-tuple-element.24.low_ref), channel_id=1, source_target_pairs={{1,0},{2,1},{3,2},{4,3},{5,4},{6,5},{7,6},{9,8},{10,9},{11,10},{12... | collective-permute-start | bytes 589832 | tf_op jit(solution)/shard_map/ppermute | solution.py:588
  36.2 6.6 %copy-start.24 = (s32[560]{0:T(1024)S(1)}, s32[560]{0:T(1024)}, u32[]{:S(2)}) copy-start(s32[560]{0:T(1024)} %constant.43.clone) | copy-start | bytes 6724
  36.2 6.6 %copy-start.25 = (s32[560]{0:T(1024)S(1)}, s32[560]{0:T(1024)}, u32[]{:S(2)}) copy-start(s32[560]{0:T(1024)} %constant.41.clone) | copy-start | bytes 6724
  36.2 6.6 %copy-start.26 = (s32[560]{0:T(1024)S(1)}, s32[560]{0:T(1024)}, u32[]{:S(2)}) copy-start(s32[560]{0:T(1024)} %constant.40.clone) | copy-start | bytes 6724
  36.2 6.6 %copy-start.27 = (pred[560]{0:T(1024)(128)(4,1)S(1)}, pred[560]{0:T(1024)(128)(4,1)}, u32[]{:S(2)}) copy-start(pred[560]{0:T(1024)(128)(4,1)} %constant.42.clone) | copy-start | bytes 1684
  38.4 4.4 %copy-start.16 = (bf16[256,256]{1,0:T(8,128)(2,1)}, bf16[256,256]{1,0:T(8,128)(2,1)S(1)}, u32[]{:S(2)}) copy-start(bf16[256,256]{1,0:T(8,128)(2,1)S(1)} %get-tuple-element.32.take_ref) | copy-start | bytes 393220
  38.5 5.7 %collective-permute-start.1 = (bf16[8,32,256]{2,1,0:T(8,128)(2,1)S(1)}, bf16[8,32,256]{2,1,0:T(8,128)(2,1)S(1)}, u32[]{:S(2)}, u32[]{:S(2)}) collective-permute-start(bf16[8,32,256]{2,1,0:T(8,128)(2,1)S(1)} %get-tuple-element.38), channel_id=1, source_target_pairs={{8,0},{16,8},{24,16},{9,1},{17,9},{25,17},{10,2},{18,10},{26,18},{... | collective-permute-start | bytes 393224 | tf_op jit(solution)/shard_map/ppermute | solution.py:588
  39.8 4.4 %collective-permute-start = (bf16[8,32,256]{2,1,0:T(8,128)(2,1)S(1)}, bf16[8,32,256]{2,1,0:T(8,128)(2,1)S(1)}, u32[]{:S(2)}, u32[]{:S(2)}) collective-permute-start(bf16[8,32,256]{2,1,0:T(8,128)(2,1)S(1)} %get-tuple-element.39), channel_id=1, source_target_pairs={{0,8},{8,16},{16,24},{1,9},{9,17},{17,25},{2,10},{10,18},{18,26},{... | collective-permute-start | bytes 393224 | tf_op jit(solution)/shard_map/ppermute | solution.py:588
  43.0 6.2 %copy-start.2 = (bf16[8,256,256]{2,1,0:T(8,128)(2,1)S(1)}, bf16[8,256,256]{2,1,0:T(8,128)(2,1)}, u32[]{:S(2)}) copy-start(bf16[8,256,256]{2,1,0:T(8,128)(2,1)} %copy-done.1) | copy-start | bytes 3145732
  43.0 6.2 %copy-start.7 = (bf16[27,96,96]{2,1,0:T(8,128)(2,1)S(1)}, bf16[27,96,96]{2,1,0:T(8,128)(2,1)}, u32[]{:S(2)}) copy-start(bf16[27,96,96]{2,1,0:T(8,128)(2,1)} %raw_ref.7) | copy-start | bytes 1492996
  43.0 6.2 %copy-start.10 = (bf16[8,32,256]{2,1,0:T(8,128)(2,1)S(1)}, bf16[8,32,256]{2,1,0:T(8,128)(2,1)}, u32[]{:S(2)}) copy-start(bf16[8,32,256]{2,1,0:T(8,128)(2,1)} %copy-done.9) | copy-start | bytes 393220
  44.6 14.6 %collective-permute-start.2 = (bf16[8,48,256]{2,1,0:T(8,128)(2,1)S(1)}, bf16[8,48,256]{2,1,0:T(8,128)(2,1)S(1)}, u32[]{:S(2)}, u32[]{:S(2)}) collective-permute-start(bf16[8,48,256]{2,1,0:T(8,128)(2,1)S(1)} %get-tuple-element.21.high_ref), channel_id=1, source_target_pairs={{0,1},{1,2},{2,3},{3,4},{4,5},{5,6},{6,7},{8,9},{9,10},{10,11},{11... | collective-permute-start | bytes 589832 | tf_op jit(solution)/shard_map/ppermute | solution.py:588
  47.8 11.4 %copy-start.6 = (bf16[27,96,96]{2,1,0:T(8,128)(2,1)S(1)}, bf16[27,96,96]{2,1,0:T(8,128)(2,1)}, u32[]{:S(2)}) copy-start(bf16[27,96,96]{2,1,0:T(8,128)(2,1)} %raw_ref.6) | copy-start | bytes 1492996
  47.8 11.4 %collective-permute-start.3 = (bf16[8,48,256]{2,1,0:T(8,128)(2,1)S(1)}, bf16[8,48,256]{2,1,0:T(8,128)(2,1)S(1)}, u32[]{:S(2)}, u32[]{:S(2)}) collective-permute-start(bf16[8,48,256]{2,1,0:T(8,128)(2,1)S(1)} %get-tuple-element.22.low_ref), channel_id=1, source_target_pairs={{1,0},{2,1},{3,2},{4,3},{5,4},{6,5},{7,6},{9,8},{10,9},{11,10},{12... | collective-permute-start | bytes 589832 | tf_op jit(solution)/shard_map/ppermute | solution.py:588
  59.2 9.2 %copy-start.22 = (bf16[8,256,256]{2,1,0:T(8,128)(2,1)}, bf16[8,256,256]{2,1,0:T(8,128)(2,1)S(1)}, u32[]{:S(2)}) copy-start(bf16[8,256,256]{2,1,0:T(8,128)(2,1)S(1)} %get-tuple-element.28.outer_ref) | copy-start | bytes 3145732
  68.3 13.9 %copy-start.18 = (bf16[8,336,256]{2,1,0:T(8,128)(2,1)}, bf16[8,336,256]{2,1,0:T(8,128)(2,1)S(1)}, u32[]{:S(2)}) copy-start(bf16[8,336,256]{2,1,0:T(8,128)(2,1)S(1)} %get-tuple-element.33.act_ref) | copy-start | bytes 4128772
  68.4 13.9 %copy-start.20 = (bf16[8,336,256]{2,1,0:T(8,128)(2,1)}, bf16[8,336,256]{2,1,0:T(8,128)(2,1)S(1)}, u32[]{:S(2)}) copy-start(bf16[8,336,256]{2,1,0:T(8,128)(2,1)S(1)} %get-tuple-element.31.hg_ref) | copy-start | bytes 4128772
  82.3 4.4 %collective-permute-start.8 = (f32[128,2048]{1,0:T(8,128)S(1)}, f32[128,2048]{1,0:T(8,128)S(1)}, u32[]{:S(2)}, u32[]{:S(2)}) collective-permute-start(f32[128,2048]{1,0:T(8,128)S(1)} %get-tuple-element.30), channel_id=1, source_target_pairs={{0,8},{8,0},{16,24},{24,16},{1,9},{9,1},{17,25},{25,17},{2,10},{10... | collective-permute-start | bytes 3145736 | tf_op jit(solution)/shard_map/ppermute | solution.py:593
  86.6 7.6 %copy-start.17 = (bf16[256,256]{1,0:T(8,128)(2,1)S(1)}, bf16[256,256]{1,0:T(8,128)(2,1)}, u32[]{:S(2)}) copy-start(bf16[256,256]{1,0:T(8,128)(2,1)} %copy-done.16) | copy-start | bytes 393220
  87.5 22.2 %all-to-all-start.1 = ((bf16[16,8,2048]{2,1,0:T(8,128)(2,1)}), bf16[16,8,2048]{2,1,0:T(8,128)(2,1)S(1)}, u32[]{:S(2)}, u32[]{:S(2)}) async-start(bf16[16,8,2048]{2,1,0:T(8,128)(2,1)} %bitcast.7), calls=%async_computation.1 | async-start | bytes 1048576 | tf_op jit(solution)/shard_map/all_to_all | solution.py:581
  111.2 36.2 %copy-start.8 = (bf16[27,96,96]{2,1,0:T(8,128)(2,1)S(1)}, bf16[27,96,96]{2,1,0:T(8,128)(2,1)}, u32[]{:S(2)}) copy-start(bf16[27,96,96]{2,1,0:T(8,128)(2,1)} %raw_ref.7) | copy-start | bytes 1492996
  111.2 36.0 %all-to-all-start.2 = ((bf16[32,8,2560]{2,1,0:T(8,128)(2,1)}), bf16[32,8,2560]{2,1,0:T(8,128)(2,1)S(1)}, u32[]{:S(2)}, u32[]{:S(2)}) async-start(bf16[32,8,2560]{2,1,0:T(8,128)(2,1)} %bitcast.10), calls=%async_computation.2 | async-start | bytes 2621440 | tf_op jit(solution)/shard_map/all_to_all | solution.py:581
  147.3 11.5 %copy-start.4 = (s32[128]{0:T(128)S(1)}, s32[128]{0:T(128)}, u32[]{:S(2)}) copy-start(s32[128]{0:T(128)} %param.12) | copy-start | bytes 1540
  147.3 12.7 %collective-permute-start.9 = (bf16[256,1024]{1,0:T(8,128)(2,1)S(1)}, bf16[256,1024]{1,0:T(8,128)(2,1)S(1)}, u32[]{:S(2)}, u32[]{:S(2)}) collective-permute-start(bf16[256,1024]{1,0:T(8,128)(2,1)S(1)} %slice.22.mine_ref), channel_id=1, source_target_pairs={{0,8},{8,0},{16,24},{24,16},{1,9},{9,1},{17,25},{25,17},{2,10},{10... | collective-permute-start | bytes 1572872 | tf_op jit(solution)/shard_map/ppermute | solution.py:593
  (9 other events, 10.1 us)

commit v8 on v7

--- a/solution.py
+++ b/solution.py
@@ -394,23 +394,26 @@
     each_step(f_ref.shape[0], body)
 
 
-def correlate(gt_ref, ext_ref, first_x, taps_ref, channels):
-    pairs = ext_ref.shape[1] - 1
-
-    def body(ab, carry):
-        a = ab // 3
-        b = ab % 3
-        left = gt_ref[...]
-        near = dot(left, ext_ref[b, 0:pairs, pl.ds(a + first_x, NX)].reshape(pairs * NX * NY, PAIR))
-        far = dot(left, ext_ref[b, 1 : pairs + 1, pl.ds(a + first_x, NX)].reshape(pairs * NX * NY, PAIR))
-        low = slice(0, channels)
-        high = slice(channels, 2 * channels)
-        taps_ref[3 * ab] = near[low, 0:LANES] + near[high, LANES:PAIR]
-        taps_ref[3 * ab + 1] = near[low, LANES:PAIR] + far[high, 0:LANES]
-        taps_ref[3 * ab + 2] = far[low, 0:LANES] + far[high, LANES:PAIR]
+def correlate(gt_ref, ext_ref, taps_ref):
+    depth = 2 * (ext_ref.shape[1] - 1)
+
+    def body(b, carry):
+        rows = []
+        for z in range(depth):
+            parts = []
+            for a in range(3):
+                for c in range(3):
+                    half = (z + c) % 2 * LANES
+                    part = ext_ref[b, (z + c) // 2, a : a + NX, :, half : half + LANES]
+                    parts.append(part.reshape(NX * NY, LANES))
+            rows.append(jnp.concatenate(parts, axis=1))
+        sums = dot(gt_ref[...], jnp.concatenate(rows, axis=0))
+        for a in range(3):
+            for c in range(3):
+                taps_ref[9 * a + 3 * b + c] = sums[:, (3 * a + c) * LANES : (3 * a + c + 1) * LANES]
         return carry
 
-    lax.fori_loop(0, 9, body, 0)
+    lax.fori_loop(0, 3, body, 0)
 
 
 def pack_taps(taps_ref, packed_ref, channels):
@@ -453,8 +456,9 @@
     inner = NX * NY
     for k in range(g_ref.shape[0]):
         value = g_ref[k, start : start + inner, :].T
-        gt_ref[0:channels, k * inner : (k + 1) * inner] = value[0:channels]
-        gt_ref[channels : 2 * channels, k * inner : (k + 1) * inner] = value[LANES : LANES + channels]
+        for i in range(2):
+            z = 2 * k + i
+            gt_ref[:, z * inner : (z + 1) * inner] = value[i * LANES : i * LANES + channels]
 
 
 def corr_kernel(channels, run, core_ref, f_ref, xlo_ref, xhi_ref, ylo_ref, yhi_ref, hg_ref, act_ref, outer_ref,
@@ -470,7 +474,7 @@
         else:
             widen_one(ext_ref, act_ref)
             turn(gt_ref, outer_ref, 0, channels)
-        correlate(gt_ref, ext_ref, 0, taps_ref, channels)
+        correlate(gt_ref, ext_ref, taps_ref)
         pack_taps(taps_ref, packed_ref, channels)
         for l in range(blocks):
             lanes = slice((i * blocks + l) * LANES, (i * blocks + l + 1) * LANES)
@@ -711,7 +715,7 @@
     keep, give = call(
         functools.partial(corr_kernel, channels, run), (half_shape, half_shape), 2 * conv_flops, 10e6,
         (
-            ext_near, pltpu.VMEM((2 * channels, pairs * slots), BF),
+            ext_near, pltpu.VMEM((channels, depth * slots), BF),
             pltpu.VMEM((28, channels, LANES), F32), pltpu.VMEM((packed_rows, LANES), F32),
         ),
         ROOM_CORR, in_specs=[smem] + [vmem] * 8,
@@ -739,6 +743,7 @@
         (ext_near, sums, turned_low, band), ROOM_NEAR,
     )(act, mask, second_weight, field, perm)
 
+    returned, block_output = lax.optimization_barrier((returned, block_output))
     mine = returned[:, row_width:]
     feature_grads = call(
         functools.partial(collect_kernel, cap, slots), shape((shard_rows, row_width), BF),

time: 163 us -> 152 us (0.933)
  waiting for transfers between devices: 49.2 us -> 39.6 us
    all_to_all x3, waiting for transfers between devices: 45.9 us -> 35.7 us  [share(): return lax.all_to_all(parts, axes, split_axis=0, concat_axis=0, tiled=True)]
    unnamed x56 -> x58, local copies, waits for them, and re-layouts: 10.2 us -> 9.65 us
  transfers between devices with their start and end apart: 13 -> 13, of which waited for: 5 -> 6; matrix products, arithmetic and copies ran while one was open for 0% -> 0% of each run, Pallas kernels for 21% -> 22%
where the time goes in v8:
time: 152 us; the launch traced here: 151 us
  Pallas kernels  62 us (41%)
  waiting for transfers between devices  39.6 us (26%)
  starting transfers between devices  38 us (25%)
  local copies, waits for them, and re-layouts  10.6 us (7%)
    all_to_all x3, waiting for transfers between devices, share(): return lax.all_to_all(parts, axes, split_axis=0, concat_axis=0, tiled=True)  35.7 us
    ppermute x8, starting transfers between devices, neighbours(): return (lax.ppermute(upper, axes, ahead), lax.ppermute(lower, axes, behind))  19 us
    all_to_all x3, starting transfers between devices, share(): return lax.all_to_all(parts, axes, split_axis=0, concat_axis=0, tiled=True)  16.8 us
    pallas_call x1, Pallas kernels, on_device(): call(functools.partial(corr_kernel, channels, run), (half_shape, half_sha...  13.2 us
    pallas_call x1, Pallas kernels, on_device(): call(outer_kernel, (shape((pairs, OUT_ROWS, PAIR), F32), field_shape), 1....  9.9 us
    unnamed x58, local copies, waits for them, and re-layouts  9.65 us
    pallas_call x1, Pallas kernels, on_device(): call(hidden_kernel, (wide_shape, wide_shape), 1.3 * conv_flops, 8000000.0...  9.11 us
    pallas_call x1, Pallas kernels, on_device(): call(block_kernel, shape((slots, row_width), BF), 1.2 * conv_flops, 80000...  8.93 us
  transfers between devices with their start and end apart: 13, of which 6 were waited for; matrix products, arithmetic and copies ran while one was open for 0% of the time, Pallas kernels for 22%

profile of v8, /device:TPU:0, one launch (start us, length us, event | category | flops | bytes accessed | tf_op | source)
XLA Modules:
  0.0 151.3 jit_solution(15659735714986780064)
XLA Ops:
  3.0 1.4 shard_map.138
  4.4 7.3 %all-to-all-start = ((bf16[32,8,1664]{2,1,0:T(8,128)(2,1)}), bf16[32,8,1664]{2,1,0:T(8,128)(2,1)S(1)}, u32[]{:S(2)}, u32[]{:S(2)}) async-start(bf16[32,8,1664]{2,1,0:T(8,128)(2,1)} %bitcast.3), calls=%async_computation | async-start | bytes 1703936 | tf_op jit(solution)/shard_map/all_to_all | solution.py:585
  12.9 1.2 shard_map.142.f_ref
  14.1 1.3 collective-permute-start.5
  15.4 3.0 %collective-permute-start.4 = (bf16[8,32,256]{2,1,0:T(8,128)(2,1)S(1)}, bf16[8,32,256]{2,1,0:T(8,128)(2,1)S(1)}, u32[]{:S(2)}, u32[]{:S(2)}) collective-permute-start(bf16[8,32,256]{2,1,0:T(8,128)(2,1)S(1)} %get-tuple-element.41), channel_id=1, source_target_pairs={{0,8},{8,16},{16,24},{1,9},{9,17},{17,25},{2,10},{10,18},{18,26},{... | collective-permute-start | bytes 393224 | tf_op jit(solution)/shard_map/ppermute | solution.py:592
  19.9 4.3 %collective-permute-start.6 = (bf16[8,48,256]{2,1,0:T(8,128)(2,1)S(1)}, bf16[8,48,256]{2,1,0:T(8,128)(2,1)}, u32[]{:S(2)}, u32[]{:S(2)}) collective-permute-start(bf16[8,48,256]{2,1,0:T(8,128)(2,1)S(1)} %get-tuple-element.25.high_ref), channel_id=1, source_target_pairs={{0,1},{1,2},{2,3},{3,4},{4,5},{5,6},{6,7},{8,9},{9,10},{10,11},{11... | collective-permute-start | bytes 589832 | tf_op jit(solution)/shard_map/ppermute | solution.py:592
  24.2 1.3 collective-permute-start.7
  25.5 9.6 %all-to-all-done = bf16[32,8,1664]{2,1,0:T(8,128)(2,1)S(1)} async-done(((bf16[32,8,1664]{2,1,0:T(8,128)(2,1)}), bf16[32,8,1664]{2,1,0:T(8,128)(2,1)S(1)}, u32[]{:S(2)}, u32[]{:S(2)}) %all-to-all-start) | async-done | bytes 852000 | tf_op jit(solution)/shard_map/all_to_all | solution.py:585
  35.1 1.1 copy-done.12
  36.2 2.2 %shard_map.139 = (bf16[8,256,256]{2,1,0:T(8,128)(2,1)S(1)}, bf16[256,256]{1,0:T(8,128)(2,1)S(1)}) custom-call(s32[1]{0:T(128)} %bitcast.me_ref, bf16[256,1664]{1,0:T(8,128)(2,1)S(1)} %bitcast.14, bf16[6,256,256]{2,1,0:T(8,128)(2,1)S(1)} %copy-done.12), custom_call_target="tpu_custom_call" | custom-call | flops 1000000000 | bytes 3000000 | tf_op jit(solution)/shard_map/pallas_call | solution.py:690
  39.1 1.4 collective-permute-start.1
  40.5 3.0 %collective-permute-start = (bf16[8,32,256]{2,1,0:T(8,128)(2,1)S(1)}, bf16[8,32,256]{2,1,0:T(8,128)(2,1)S(1)}, u32[]{:S(2)}, u32[]{:S(2)}) collective-permute-start(bf16[8,32,256]{2,1,0:T(8,128)(2,1)S(1)} %get-tuple-element.43), channel_id=1, source_target_pairs={{0,8},{8,16},{16,24},{1,9},{9,17},{17,25},{2,10},{10,18},{18,26},{... | collective-permute-start | bytes 393224 | tf_op jit(solution)/shard_map/ppermute | solution.py:592
  45.4 3.2 %collective-permute-start.2 = (bf16[8,48,256]{2,1,0:T(8,128)(2,1)S(1)}, bf16[8,48,256]{2,1,0:T(8,128)(2,1)S(1)}, u32[]{:S(2)}, u32[]{:S(2)}) collective-permute-start(bf16[8,48,256]{2,1,0:T(8,128)(2,1)S(1)} %get-tuple-element.23.high_ref), channel_id=1, source_target_pairs={{0,1},{1,2},{2,3},{3,4},{4,5},{5,6},{6,7},{8,9},{9,10},{10,11},{11... | collective-permute-start | bytes 589832 | tf_op jit(solution)/shard_map/ppermute | solution.py:592
  48.5 1.4 collective-permute-start.3
  50.0 9.9 %shard_map.144 = (f32[8,336,256]{2,1,0:T(8,128)S(1)}, bf16[8,256,256]{2,1,0:T(8,128)(2,1)S(1)}) custom-call(bf16[8,256,256]{2,1,0:T(8,128)(2,1)S(1)} %shard_map.142.f_ref, bf16[8,32,256]{2,1,0:T(8,128)(2,1)S(1)} %copy-done.10, bf16[8,32,256]{2,1,0:T(8,128)(2,1)S(1)} %collective-permute-done.5.xhi_ref, bf16[8,48,256]{2,1,0:T(8,128)(2,1)} %collective-permute-done.6.ylo_ref, ...), custom_call_target="tpu_custom_call" | custom-call | flops 6281389568 | bytes 7000000 | tf_op jit(solution)/shard_map/pallas_call | solution.py:702
  60.0 9.1 %shard_map.145 = (bf16[8,336,256]{2,1,0:T(8,128)(2,1)S(1)}, bf16[8,336,256]{2,1,0:T(8,128)(2,1)S(1)}) custom-call(bf16[8,256,256]{2,1,0:T(8,128)(2,1)S(1)} %get-tuple-element.22.f_ref.field_ref, bf16[8,32,256]{2,1,0:T(8,128)(2,1)S(1)} %collective-permute-done.xlo_ref, bf16[8,32,256]{2,1,0:T(8,128)(2,1)S(1)} %collective-permute-done.1.xhi_ref, ...), custom_call_target="tpu_custom_call" | custom-call | flops 6281389568 | bytes 8000000 | tf_op jit(solution)/shard_map/pallas_call | solution.py:707
  69.1 13.2 %shard_map.146 = (f32[128,2048]{1,0:T(8,128)S(1)}, f32[128,2048]{1,0:T(8,128)S(1)}) custom-call(s32[1]{0:T(128)} %bitcast.6.core_ref, bf16[8,256,256]{2,1,0:T(8,128)(2,1)S(1)} %get-tuple-element.22.f_ref.field_ref, bf16[8,32,256]{2,1,0:T(8,128)(2,1)S(1)} %collective-permute-done.xlo_ref, bf16[8,32,256]{2,1,0:T(8,128)(2,1)S(1)} %collective-permute-done.1.xhi_ref, ...), custom_call_target="tpu_custom_call" | custom-call | flops 9663676416 | bytes 10000000 | tf_op jit(solution)/shard_map/pallas_call | solution.py:715
  82.3 2.1 %collective-permute-start.8 = (f32[128,2048]{1,0:T(8,128)S(1)}, f32[128,2048]{1,0:T(8,128)S(1)}, u32[]{:S(2)}, u32[]{:S(2)}) collective-permute-start(f32[128,2048]{1,0:T(8,128)S(1)} %get-tuple-element.32), channel_id=1, source_target_pairs={{0,8},{8,0},{16,24},{24,16},{1,9},{9,1},{17,25},{25,17},{2,10},{10... | collective-permute-start | bytes 3145736 | tf_op jit(solution)/shard_map/ppermute | solution.py:597
  84.4 2.3 %collective-permute-done.8.got_ref = f32[128,2048]{1,0:T(8,128)S(1)} collective-permute-done((f32[128,2048]{1,0:T(8,128)S(1)}, f32[128,2048]{1,0:T(8,128)S(1)}, u32[]{:S(2)}, u32[]{:S(2)}) %collective-permute-start.8) | collective-permute-done | bytes 1048608 | tf_op jit(solution)/shard_map/ppermute | solution.py:597
  87.6 6.7 %all-to-all-start.1 = ((bf16[16,8,2048]{2,1,0:T(8,128)(2,1)}), bf16[16,8,2048]{2,1,0:T(8,128)(2,1)S(1)}, u32[]{:S(2)}, u32[]{:S(2)}) async-start(bf16[16,8,2048]{2,1,0:T(8,128)(2,1)} %bitcast.7), calls=%async_computation.1 | async-start | bytes 1048576 | tf_op jit(solution)/shard_map/all_to_all | solution.py:585
  94.3 1.3 copy-done.22
  95.7 1.2 copy-done.24
  96.9 8.6 %shard_map.148.back_ref = bf16[256,1536]{1,0:T(8,128)(2,1)S(1)} custom-call(bf16[8,336,256]{2,1,0:T(8,128)(2,1)S(1)} %copy-done.22, bf16[27,96,96]{2,1,0:T(8,128)(2,1)S(1)} %copy-done.6, bf16[8,256,256]{2,1,0:T(8,128)(2,1)S(1)} %copy-done.24, bf16[6,256,256]{2,1,0:T(8,128)(2,1)S(1)} %copy-done.13, bf16[256,256]{1,0:T(8,128)(2,1)S(1)} %copy-done.18), custom_call_target="tpu_custom_call" | custom-call | flops 5798205952 | bytes 6000000 | tf_op jit(solution)/shard_map/pallas_call | solution.py:730
  105.5 4.3 %all-to-all-done.1 = bf16[16,8,2048]{2,1,0:T(8,128)(2,1)S(1)} async-done(((bf16[16,8,2048]{2,1,0:T(8,128)(2,1)}), bf16[16,8,2048]{2,1,0:T(8,128)(2,1)S(1)}, u32[]{:S(2)}, u32[]{:S(2)}) %all-to-all-start.1) | async-done | bytes 524320 | tf_op jit(solution)/shard_map/all_to_all | solution.py:585
  109.8 1.5 shard_map.149
  111.3 2.8 %all-to-all-start.2 = ((bf16[32,8,2560]{2,1,0:T(8,128)(2,1)}), bf16[32,8,2560]{2,1,0:T(8,128)(2,1)S(1)}, u32[]{:S(2)}, u32[]{:S(2)}) async-start(bf16[32,8,2560]{2,1,0:T(8,128)(2,1)} %bitcast.9), calls=%async_computation.2 | async-start | bytes 2621440 | tf_op jit(solution)/shard_map/all_to_all | solution.py:585
  114.1 1.1 copy-done.14
  115.2 1.3 copy-done.20
  116.6 8.9 %shard_map.150 = bf16[256,1536]{1,0:T(8,128)(2,1)} custom-call(bf16[8,336,256]{2,1,0:T(8,128)(2,1)S(1)} %copy-done.20, f32[560,128]{1,0:T(8,128)S(1)} %shard_map.141.mask_ref, bf16[27,96,96]{2,1,0:T(8,128)(2,1)S(1)} %copy-done.8, bf16[8,256,256]{2,1,0:T(8,128)(2,1)S(1)} %copy-done.2, bf16[6,256,256]{2,1,0:T(8,128)(2,1)S(1)} %copy-done.14), custom_call_target="tpu_custom_call" | custom-call | flops 5798205952 | bytes 8000000 | tf_op jit(solution)/shard_map/pallas_call | solution.py:741
  125.5 21.8 %all-to-all-done.2 = bf16[32,8,2560]{2,1,0:T(8,128)(2,1)S(1)} async-done(((bf16[32,8,2560]{2,1,0:T(8,128)(2,1)}), bf16[32,8,2560]{2,1,0:T(8,128)(2,1)S(1)}, u32[]{:S(2)}, u32[]{:S(2)}) %all-to-all-start.2) | async-done | bytes 1310752 | tf_op jit(solution)/shard_map/all_to_all | solution.py:585
  147.4 1.2 shard_map.151
  149.3 2.0 %shard_map.152 = (f32[27,96,96]{2,1,0:T(8,128)}, f32[27,96,96]{2,1,0:T(8,128)}) custom-call(s32[1]{0:T(128)} %bitcast.6.core_ref, bf16[256,1024]{1,0:T(8,128)(2,1)S(1)} %slice.19.mine_ref, bf16[256,1024]{1,0:T(8,128)(2,1)S(1)} %collective-permute-done.9.other_ref), custom_call_target="tpu_custom_call" | custom-call | flops 1000000 | bytes 4000000 | tf_op jit(solution)/shard_map/pallas_call | solution.py:755
  (73 shorter events, 9.0 us)
Async XLA Ops:
  3.0 8.7 %copy-start.5 = (bf16[16,16,1536]{2,1,0:T(8,128)(2,1)S(1)}, bf16[16,16,1536]{2,1,0:T(8,128)(2,1)}, u32[]{:S(2)}) copy-start(bf16[16,16,1536]{2,1,0:T(8,128)(2,1)} %param.13) | copy-start | bytes 2359300
  4.4 30.7 %all-to-all-start = ((bf16[32,8,1664]{2,1,0:T(8,128)(2,1)}), bf16[32,8,1664]{2,1,0:T(8,128)(2,1)S(1)}, u32[]{:S(2)}, u32[]{:S(2)}) async-start(bf16[32,8,1664]{2,1,0:T(8,128)(2,1)} %bitcast.3), calls=%async_computation | async-start | bytes 1703936 | tf_op jit(solution)/shard_map/all_to_all | solution.py:585
  12.9 6.6 %copy-start.15 = (bf16[96,320]{1,0:T(8,128)(2,1)S(1)}, bf16[96,320]{1,0:T(8,128)(2,1)}, u32[]{:S(2)}) copy-start(bf16[96,320]{1,0:T(8,128)(2,1)} %constant.39.clone.pick_ref) | copy-start | bytes 184324
  14.1 4.4 %collective-permute-start.5 = (bf16[8,32,256]{2,1,0:T(8,128)(2,1)S(1)}, bf16[8,32,256]{2,1,0:T(8,128)(2,1)S(1)}, u32[]{:S(2)}, u32[]{:S(2)}) collective-permute-start(bf16[8,32,256]{2,1,0:T(8,128)(2,1)S(1)} %get-tuple-element.40), channel_id=1, source_target_pairs={{8,0},{16,8},{24,16},{9,1},{17,9},{25,17},{10,2},{18,10},{26,18},{... | collective-permute-start | bytes 393224 | tf_op jit(solution)/shard_map/ppermute | solution.py:592
  15.4 4.0 %collective-permute-start.4 = (bf16[8,32,256]{2,1,0:T(8,128)(2,1)S(1)}, bf16[8,32,256]{2,1,0:T(8,128)(2,1)S(1)}, u32[]{:S(2)}, u32[]{:S(2)}) collective-permute-start(bf16[8,32,256]{2,1,0:T(8,128)(2,1)S(1)} %get-tuple-element.41), channel_id=1, source_target_pairs={{0,8},{8,16},{16,24},{1,9},{9,17},{17,25},{2,10},{10,18},{18,26},{... | collective-permute-start | bytes 393224 | tf_op jit(solution)/shard_map/ppermute | solution.py:592
  19.4 19.0 %copy-start.9 = (bf16[8,32,256]{2,1,0:T(8,128)(2,1)}, bf16[8,32,256]{2,1,0:T(8,128)(2,1)S(1)}, u32[]{:S(2)}) copy-start(bf16[8,32,256]{2,1,0:T(8,128)(2,1)S(1)} %collective-permute-done.4.xlo_ref) | copy-start | bytes 393220
  19.9 30.1 %collective-permute-start.6 = (bf16[8,48,256]{2,1,0:T(8,128)(2,1)S(1)}, bf16[8,48,256]{2,1,0:T(8,128)(2,1)}, u32[]{:S(2)}, u32[]{:S(2)}) collective-permute-start(bf16[8,48,256]{2,1,0:T(8,128)(2,1)S(1)} %get-tuple-element.25.high_ref), channel_id=1, source_target_pairs={{0,1},{1,2},{2,3},{3,4},{4,5},{5,6},{6,7},{8,9},{9,10},{10,11},{11... | collective-permute-start | bytes 589832 | tf_op jit(solution)/shard_map/ppermute | solution.py:592
  24.2 25.8 %collective-permute-start.7 = (bf16[8,48,256]{2,1,0:T(8,128)(2,1)S(1)}, bf16[8,48,256]{2,1,0:T(8,128)(2,1)}, u32[]{:S(2)}, u32[]{:S(2)}) collective-permute-start(bf16[8,48,256]{2,1,0:T(8,128)(2,1)S(1)} %get-tuple-element.26.low_ref), channel_id=1, source_target_pairs={{1,0},{2,1},{3,2},{4,3},{5,4},{6,5},{7,6},{9,8},{10,9},{11,10},{12... | collective-permute-start | bytes 589832 | tf_op jit(solution)/shard_map/ppermute | solution.py:592
  36.2 7.4 %copy-start.25 = (s32[560]{0:T(1024)S(1)}, s32[560]{0:T(1024)}, u32[]{:S(2)}) copy-start(s32[560]{0:T(1024)} %constant.43.clone) | copy-start | bytes 6724
  36.2 7.4 %copy-start.26 = (s32[560]{0:T(1024)S(1)}, s32[560]{0:T(1024)}, u32[]{:S(2)}) copy-start(s32[560]{0:T(1024)} %constant.41.clone) | copy-start | bytes 6724
  36.2 7.4 %copy-start.27 = (s32[560]{0:T(1024)S(1)}, s32[560]{0:T(1024)}, u32[]{:S(2)}) copy-start(s32[560]{0:T(1024)} %constant.40.clone) | copy-start | bytes 6724
  36.2 7.4 %copy-start.28 = (pred[560]{0:T(1024)(128)(4,1)S(1)}, pred[560]{0:T(1024)(128)(4,1)}, u32[]{:S(2)}) copy-start(pred[560]{0:T(1024)(128)(4,1)} %constant.42.clone) | copy-start | bytes 1684
  39.1 30.0 %copy-start.1 = (bf16[8,256,256]{2,1,0:T(8,128)(2,1)}, bf16[8,256,256]{2,1,0:T(8,128)(2,1)S(1)}, u32[]{:S(2)}) copy-start(bf16[8,256,256]{2,1,0:T(8,128)(2,1)S(1)} %get-tuple-element.22.f_ref.field_ref) | copy-start | bytes 3145732
  39.1 5.8 %copy-start.16 = (bf16[96,320]{1,0:T(8,128)(2,1)S(1)}, bf16[96,320]{1,0:T(8,128)(2,1)}, u32[]{:S(2)}) copy-start(bf16[96,320]{1,0:T(8,128)(2,1)} %constant.39.clone.pick_ref) | copy-start | bytes 184324
  39.1 5.8 %collective-permute-start.1 = (bf16[8,32,256]{2,1,0:T(8,128)(2,1)S(1)}, bf16[8,32,256]{2,1,0:T(8,128)(2,1)S(1)}, u32[]{:S(2)}, u32[]{:S(2)}) collective-permute-start(bf16[8,32,256]{2,1,0:T(8,128)(2,1)S(1)} %get-tuple-element.42), channel_id=1, source_target_pairs={{8,0},{16,8},{24,16},{9,1},{17,9},{25,17},{10,2},{18,10},{26,18},{... | collective-permute-start | bytes 393224 | tf_op jit(solution)/shard_map/ppermute | solution.py:592
  40.5 4.4 %collective-permute-start = (bf16[8,32,256]{2,1,0:T(8,128)(2,1)S(1)}, bf16[8,32,256]{2,1,0:T(8,128)(2,1)S(1)}, u32[]{:S(2)}, u32[]{:S(2)}) collective-permute-start(bf16[8,32,256]{2,1,0:T(8,128)(2,1)S(1)} %get-tuple-element.43), channel_id=1, source_target_pairs={{0,8},{8,16},{16,24},{1,9},{9,17},{17,25},{2,10},{10,18},{18,26},{... | collective-permute-start | bytes 393224 | tf_op jit(solution)/shard_map/ppermute | solution.py:592
  43.8 6.2 %copy-start.7 = (bf16[27,96,96]{2,1,0:T(8,128)(2,1)S(1)}, bf16[27,96,96]{2,1,0:T(8,128)(2,1)}, u32[]{:S(2)}) copy-start(bf16[27,96,96]{2,1,0:T(8,128)(2,1)} %raw_ref.7) | copy-start | bytes 1492996
  43.8 6.2 %copy-start.10 = (bf16[8,32,256]{2,1,0:T(8,128)(2,1)S(1)}, bf16[8,32,256]{2,1,0:T(8,128)(2,1)}, u32[]{:S(2)}) copy-start(bf16[8,32,256]{2,1,0:T(8,128)(2,1)} %copy-done.9) | copy-start | bytes 393220
  45.4 14.6 %collective-permute-start.2 = (bf16[8,48,256]{2,1,0:T(8,128)(2,1)S(1)}, bf16[8,48,256]{2,1,0:T(8,128)(2,1)S(1)}, u32[]{:S(2)}, u32[]{:S(2)}) collective-permute-start(bf16[8,48,256]{2,1,0:T(8,128)(2,1)S(1)} %get-tuple-element.23.high_ref), channel_id=1, source_target_pairs={{0,1},{1,2},{2,3},{3,4},{4,5},{5,6},{6,7},{8,9},{9,10},{10,11},{11... | collective-permute-start | bytes 589832 | tf_op jit(solution)/shard_map/ppermute | solution.py:592
  48.5 11.4 %copy-start.6 = (bf16[27,96,96]{2,1,0:T(8,128)(2,1)S(1)}, bf16[27,96,96]{2,1,0:T(8,128)(2,1)}, u32[]{:S(2)}) copy-start(bf16[27,96,96]{2,1,0:T(8,128)(2,1)} %raw_ref.6) | copy-start | bytes 1492996
  48.5 11.4 %collective-permute-start.3 = (bf16[8,48,256]{2,1,0:T(8,128)(2,1)S(1)}, bf16[8,48,256]{2,1,0:T(8,128)(2,1)S(1)}, u32[]{:S(2)}, u32[]{:S(2)}) collective-permute-start(bf16[8,48,256]{2,1,0:T(8,128)(2,1)S(1)} %get-tuple-element.24.low_ref), channel_id=1, source_target_pairs={{1,0},{2,1},{3,2},{4,3},{5,4},{6,5},{7,6},{9,8},{10,9},{11,10},{12... | collective-permute-start | bytes 589832 | tf_op jit(solution)/shard_map/ppermute | solution.py:592
  59.9 9.2 %copy-start.23 = (bf16[8,256,256]{2,1,0:T(8,128)(2,1)}, bf16[8,256,256]{2,1,0:T(8,128)(2,1)S(1)}, u32[]{:S(2)}) copy-start(bf16[8,256,256]{2,1,0:T(8,128)(2,1)S(1)} %get-tuple-element.30.outer_ref) | copy-start | bytes 3145732
  69.1 13.2 %copy-start.19 = (bf16[8,336,256]{2,1,0:T(8,128)(2,1)}, bf16[8,336,256]{2,1,0:T(8,128)(2,1)S(1)}, u32[]{:S(2)}) copy-start(bf16[8,336,256]{2,1,0:T(8,128)(2,1)S(1)} %get-tuple-element.35.act_ref) | copy-start | bytes 4128772
  69.1 13.2 %copy-start.21 = (bf16[8,336,256]{2,1,0:T(8,128)(2,1)}, bf16[8,336,256]{2,1,0:T(8,128)(2,1)S(1)}, u32[]{:S(2)}) copy-start(bf16[8,336,256]{2,1,0:T(8,128)(2,1)S(1)} %get-tuple-element.33.hg_ref) | copy-start | bytes 4128772
  82.3 4.4 %collective-permute-start.8 = (f32[128,2048]{1,0:T(8,128)S(1)}, f32[128,2048]{1,0:T(8,128)S(1)}, u32[]{:S(2)}, u32[]{:S(2)}) collective-permute-start(f32[128,2048]{1,0:T(8,128)S(1)} %get-tuple-element.32), channel_id=1, source_target_pairs={{0,8},{8,0},{16,24},{24,16},{1,9},{9,1},{17,25},{25,17},{2,10},{10... | collective-permute-start | bytes 3145736 | tf_op jit(solution)/shard_map/ppermute | solution.py:597
  86.7 7.6 %copy-start.13 = (bf16[6,256,256]{2,1,0:T(8,128)(2,1)S(1)}, bf16[6,256,256]{2,1,0:T(8,128)(2,1)}, u32[]{:S(2)}) copy-start(bf16[6,256,256]{2,1,0:T(8,128)(2,1)} %constant.38.clone.perm_ref) | copy-start | bytes 2359300
  86.7 7.6 %copy-start.18 = (bf16[256,256]{1,0:T(8,128)(2,1)S(1)}, bf16[256,256]{1,0:T(8,128)(2,1)}, u32[]{:S(2)}) copy-start(bf16[256,256]{1,0:T(8,128)(2,1)} %copy-done.17) | copy-start | bytes 393220
  87.6 22.2 %all-to-all-start.1 = ((bf16[16,8,2048]{2,1,0:T(8,128)(2,1)}), bf16[16,8,2048]{2,1,0:T(8,128)(2,1)S(1)}, u32[]{:S(2)}, u32[]{:S(2)}) async-start(bf16[16,8,2048]{2,1,0:T(8,128)(2,1)} %bitcast.7), calls=%async_computation.1 | async-start | bytes 1048576 | tf_op jit(solution)/shard_map/all_to_all | solution.py:585
  111.3 2.8 %copy-start.8 = (bf16[27,96,96]{2,1,0:T(8,128)(2,1)S(1)}, bf16[27,96,96]{2,1,0:T(8,128)(2,1)}, u32[]{:S(2)}) copy-start(bf16[27,96,96]{2,1,0:T(8,128)(2,1)} %raw_ref.7) | copy-start | bytes 1492996
  111.3 36.0 %all-to-all-start.2 = ((bf16[32,8,2560]{2,1,0:T(8,128)(2,1)}), bf16[32,8,2560]{2,1,0:T(8,128)(2,1)S(1)}, u32[]{:S(2)}, u32[]{:S(2)}) async-start(bf16[32,8,2560]{2,1,0:T(8,128)(2,1)} %bitcast.9), calls=%async_computation.2 | async-start | bytes 2621440 | tf_op jit(solution)/shard_map/all_to_all | solution.py:585
  116.6 30.8 %copy-start.4 = (s32[128]{0:T(128)S(1)}, s32[128]{0:T(128)}, u32[]{:S(2)}) copy-start(s32[128]{0:T(128)} %param.12) | copy-start | bytes 1540
  147.3 2.0 %collective-permute-start.9 = (bf16[256,1024]{1,0:T(8,128)(2,1)S(1)}, bf16[256,1024]{1,0:T(8,128)(2,1)S(1)}, u32[]{:S(2)}, u32[]{:S(2)}) collective-permute-start(bf16[256,1024]{1,0:T(8,128)(2,1)S(1)} %slice.19.mine_ref), channel_id=1, source_target_pairs={{0,8},{8,0},{16,24},{24,16},{1,9},{9,1},{17,25},{25,17},{2,10},{10... | collective-permute-start | bytes 1572872 | tf_op jit(solution)/shard_map/ppermute | solution.py:597
  (10 other events, 12.4 us)

commit v9 on v8

--- a/solution.py
+++ b/solution.py
@@ -11,7 +11,7 @@
 LANES = 128
 PAIR = 256
 MIB = 1024 * 1024
-ROOM_WIDE, ROOM_NEAR, ROOM_CORR, ROOM_SMALL = 20, 14, 16, 5
+ROOM_WIDE, ROOM_NEAR, ROOM_CORR, ROOM_SMALL = 22, 14, 14, 5
 BF = jnp.bfloat16
 F32 = jnp.float32
 
@@ -35,23 +35,43 @@
     return lax.dot_general(left, right, (((1,), (1,)), ((), ())), preferred_element_type=F32)
 
 
-def send_kernel(cap, slots, row_ref, col_ref, feat_ref, out_ref):
+def as_column(row):
+    return jnp.broadcast_to(row, (row.shape[1], row.shape[1])).T
+
+
+def send_kernel(cap, slots, row_ref, feat_hbm, out_ref, feat_ref, sem):
+    fetch = pltpu.make_async_copy(feat_hbm, feat_ref, sem)
+    fetch.start()
     rows, width = feat_ref.shape
     buffers = out_ref.shape[0]
-    owner_row = row_ref[...] // slots
-    owner_col = col_ref[...] // slots
+    owner_row = (row_ref[...] // slots).astype(F32)
+    owner_col = as_column(owner_row)
     first = lax.broadcasted_iota(jnp.int32, (rows, rows), 0)
     second = lax.broadcasted_iota(jnp.int32, (rows, rows), 1)
     same = jnp.where((owner_col == owner_row) & (first < second), 1.0, 0.0)
     rank = jnp.sum(same, axis=0, keepdims=True)
-    pos = owner_row.astype(F32) * cap + rank
+    pos = owner_row * cap + rank
     place = lax.broadcasted_iota(jnp.int32, (buffers, rows), 0)
     hot = jnp.where(place.astype(F32) == pos, 1.0, 0.0).astype(BF)
-    out_ref[:, 0:width] = dot(hot, feat_ref[...]).astype(BF)
     slot_row = (row_ref[...] % slots).astype(F32)
     kind = place % cap
-    told = jnp.where(kind == 0, owner_row.astype(F32), jnp.where(kind == 1, slot_row, 0.0))
+    told = jnp.where(kind == 0, owner_row, jnp.where(kind == 1, slot_row, 0.0))
     out_ref[:, width : width + rows] = told.astype(BF)
+    fetch.wait()
+    out_ref[:, 0:width] = dot(hot, feat_ref[...]).astype(BF)
+
+
+def collect_kernel(cap, slots, row_ref, back_ref, out_ref):
+    rows, width = out_ref.shape
+    owner_row = (row_ref[...] // slots).astype(F32)
+    owner_col = as_column(owner_row)
+    first = lax.broadcasted_iota(jnp.int32, (rows, rows), 0)
+    second = lax.broadcasted_iota(jnp.int32, (rows, rows), 1)
+    same = jnp.where((owner_col == owner_row) & (second < first), 1.0, 0.0)
+    pos = owner_col[:, 0:1] * cap + jnp.sum(same, axis=1, keepdims=True)
+    place = lax.broadcasted_iota(jnp.int32, (rows, back_ref.shape[0]), 1).astype(F32)
+    hot = jnp.where(place == pos, 1.0, 0.0).astype(BF)
+    out_ref[...] = dot(hot, back_ref[:, 0:width]).astype(BF)
 
 
 def told_rows(cap, in_ref, which):
@@ -61,20 +81,6 @@
     place = lax.broadcasted_iota(jnp.int32, (count, buffers), 1)
     pick = jnp.where(place == source * cap + which, 1.0, 0.0).astype(BF)
     return dot(pick, in_ref[:, width - LANES : width])
-
-
-def collect_kernel(cap, slots, row_ref, col_ref, back_ref, out_ref):
-    rows = out_ref.shape[0]
-    owner_row = row_ref[...] // slots
-    owner_col = col_ref[...] // slots
-    first = lax.broadcasted_iota(jnp.int32, (rows, rows), 0)
-    second = lax.broadcasted_iota(jnp.int32, (rows, rows), 1)
-    same = jnp.where((owner_col == owner_row) & (second < first), 1.0, 0.0)
-    rank = jnp.sum(same, axis=1, keepdims=True)
-    pos = owner_col.astype(F32) * cap + rank
-    place = lax.broadcasted_iota(jnp.int32, (rows, back_ref.shape[0]), 1).astype(F32)
-    hot = jnp.where(place == pos, 1.0, 0.0).astype(BF)
-    out_ref[...] = dot(hot, back_ref[:, 0 : out_ref.shape[1]]).astype(BF)
 
 
 def mask_kernel(cap, slots, in_ref, codes_ref, mask_ref, route_ref):
@@ -187,10 +193,13 @@
     spread_pairs(turned_ref, out_ref)
 
 
-def place_kernel(cap, slots, me_ref, rows_ref, perm_ref, out_ref, take_ref, turned_ref):
+def place_kernel(cap, slots, me_ref, rows_ref, perm_hbm, out_ref, take_ref, turned_ref, perm_ref, sem):
+    fetch = pltpu.make_async_copy(perm_hbm, perm_ref, sem)
+    fetch.start()
     take = slot_table(cap, slots, me_ref[0], rows_ref)
     take_ref[...] = take.astype(BF)
     put = take.T.astype(BF)
+    fetch.wait()
     for i in range(perm_ref.shape[0]):
         held = dot(put, rows_ref[:, i * PAIR : (i + 1) * PAIR]).astype(BF)
         turned_ref[i] = dot(held, perm_ref[i])
@@ -302,28 +311,6 @@
     lax.fori_loop(0, pairs, body, 0)
 
 
-def widen_near(ext_ref, f_ref, xlo_ref, xhi_ref, ylo_ref, yhi_ref):
-    for b in range(3):
-        clear_ends(ext_ref, (b,))
-    row = lax.broadcasted_iota(jnp.int32, (NY, PAIR), 0)
-    wide = NX + 4
-
-    def body(k, carry):
-        ylo = ylo_ref[k].astype(F32)
-        yhi = yhi_ref[k].astype(F32)
-        for xp in range(NX + 2):
-            if xp == 0:
-                mid = xlo_ref[k, NY : 2 * NY, :].astype(F32)
-            elif xp == NX + 1:
-                mid = xhi_ref[k, 0:NY, :].astype(F32)
-            else:
-                mid = f_ref[k, (xp - 1) * NY : xp * NY, :].astype(F32)
-            put_shifted(ext_ref, k, xp, mid, ylo[wide + xp + 1 : wide + xp + 2, :], yhi[xp + 1 : xp + 2, :], row)
-        return carry
-
-    lax.fori_loop(0, f_ref.shape[0], body, 0)
-
-
 def widen_one(ext_ref, rows_ref):
     pairs = rows_ref.shape[0]
     for b in range(3):
@@ -394,7 +381,7 @@
     each_step(f_ref.shape[0], body)
 
 
-def correlate(gt_ref, ext_ref, taps_ref):
+def correlate(gt_ref, ext_ref, first_x, taps_ref):
     depth = 2 * (ext_ref.shape[1] - 1)
 
     def body(b, carry):
@@ -404,7 +391,7 @@
             for a in range(3):
                 for c in range(3):
                     half = (z + c) % 2 * LANES
-                    part = ext_ref[b, (z + c) // 2, a : a + NX, :, half : half + LANES]
+                    part = ext_ref[b, (z + c) // 2, first_x + a : first_x + a + NX, :, half : half + LANES]
                     parts.append(part.reshape(NX * NY, LANES))
             rows.append(jnp.concatenate(parts, axis=1))
         sums = dot(gt_ref[...], jnp.concatenate(rows, axis=0))
@@ -435,8 +422,9 @@
         packed_ref[21 * channels :, :] = jnp.zeros((rest, LANES), F32)
 
 
-def hidden_kernel(f_ref, xlo_ref, xhi_ref, ylo_ref, yhi_ref, low_ref, high_ref, mask_ref, raw_ref, grad_ref,
-                  act_ref, hg_ref, ext_ref, edge_ref, w_ref):
+def hidden_kernel(channels, run, core_ref, f_ref, xlo_ref, xhi_ref, ylo_ref, yhi_ref, low_ref, high_ref, mask_ref,
+                  raw_ref, grad_ref, act_ref, hg_ref, keep_ref, give_ref,
+                  ext_ref, edge_ref, w_ref, gt_ref, taps_ref, packed_ref):
     build_band(w_ref, raw_ref, False)
     widen_two(ext_ref, edge_ref, f_ref, xlo_ref, xhi_ref, ylo_ref, yhi_ref, low_ref, high_ref)
 
@@ -450,6 +438,9 @@
             hg_ref[k + i] = (m * grad_ref[k + i] * sigma * (1.0 + hidden * (1.0 - sigma))).astype(BF)
 
     each_step(f_ref.shape[0], body)
+    turn(gt_ref, hg_ref, NY, channels)
+    correlate(gt_ref, ext_ref, 1, taps_ref)
+    hand_out(channels, run, core_ref, taps_ref, packed_ref, keep_ref, give_ref)
 
 
 def turn(gt_ref, g_ref, start, channels):
@@ -461,30 +452,27 @@
             gt_ref[:, z * inner : (z + 1) * inner] = value[i * LANES : i * LANES + channels]
 
 
-def corr_kernel(channels, run, core_ref, f_ref, xlo_ref, xhi_ref, ylo_ref, yhi_ref, hg_ref, act_ref, outer_ref,
-                keep_ref, give_ref, ext_ref, gt_ref, taps_ref, packed_ref):
+def hand_out(channels, run, core_ref, taps_ref, packed_ref, keep_ref, give_ref):
     runs = keep_ref.shape[0] // run
     block = 2 * runs * run
-    blocks = packed_ref.shape[0] // block
     taps_ref[27] = jnp.zeros((channels, LANES), F32)
-    for i in range(2):
-        if i == 0:
-            widen_near(ext_ref, f_ref, xlo_ref, xhi_ref, ylo_ref, yhi_ref)
-            turn(gt_ref, hg_ref, NY, channels)
-        else:
-            widen_one(ext_ref, act_ref)
-            turn(gt_ref, outer_ref, 0, channels)
-        correlate(gt_ref, ext_ref, taps_ref)
-        pack_taps(taps_ref, packed_ref, channels)
-        for l in range(blocks):
-            lanes = slice((i * blocks + l) * LANES, (i * blocks + l + 1) * LANES)
-            for x in range(runs):
-                base = l * block + 2 * x * run
-                rows = slice(x * run, (x + 1) * run)
-                mine = pl.multiple_of(base + core_ref[0] * run, run)
-                other = pl.multiple_of(base + (1 - core_ref[0]) * run, run)
-                keep_ref[rows, lanes] = packed_ref[pl.ds(mine, run), :]
-                give_ref[rows, lanes] = packed_ref[pl.ds(other, run), :]
+    pack_taps(taps_ref, packed_ref, channels)
+    for l in range(packed_ref.shape[0] // block):
+        lanes = slice(l * LANES, (l + 1) * LANES)
+        for x in range(runs):
+            base = l * block + 2 * x * run
+            rows = slice(x * run, (x + 1) * run)
+            mine = pl.multiple_of(base + core_ref[0] * run, run)
+            other = pl.multiple_of(base + (1 - core_ref[0]) * run, run)
+            keep_ref[rows, lanes] = packed_ref[pl.ds(mine, run), :]
+            give_ref[rows, lanes] = packed_ref[pl.ds(other, run), :]
+
+
+def corr_kernel(channels, run, core_ref, act_ref, outer_ref, keep_ref, give_ref, ext_ref, gt_ref, taps_ref, packed_ref):
+    widen_one(ext_ref, act_ref)
+    turn(gt_ref, outer_ref, 0, channels)
+    correlate(gt_ref, ext_ref, 0, taps_ref)
+    hand_out(channels, run, core_ref, taps_ref, packed_ref, keep_ref, give_ref)
 
 
 def grid_grad_kernel(hg_ref, raw_ref, outer_ref, perm_ref, take_ref, out_ref, ext_ref, sum_ref, turned_ref, w_ref):
@@ -522,15 +510,15 @@
         out_ref[:, i * PAIR : (i + 1) * PAIR] = dot_nt(turned_ref[i], perm_ref[i]).astype(BF)
 
 
-def pair_sum_kernel(keep_ref, got_ref, out_ref):
-    out_ref[...] = (keep_ref[...] + got_ref[...]).astype(BF)
-
-
-def assemble_kernel(cap, run, back_ref, parts_ref, out_ref):
-    buffers, width = back_ref.shape
-    senders, lanes = parts_ref.shape
-    half = lanes // 2
-    out_ref[:, 0:width] = back_ref[...]
+def pair_sum_kernel(keep0_ref, got0_ref, keep1_ref, got1_ref, out_ref):
+    half = keep0_ref.shape[1]
+    out_ref[:, 0:half] = (keep0_ref[...] + got0_ref[...]).astype(BF)
+    out_ref[:, half : 2 * half] = (keep1_ref[...] + got1_ref[...]).astype(BF)
+
+
+def assemble_kernel(cap, run, back_hbm, parts_ref, out_hbm, total_ref, sem):
+    buffers, half = total_ref.shape
+    senders = parts_ref.shape[0]
     row = lax.broadcasted_iota(jnp.int32, (buffers, senders), 0)
     col = lax.broadcasted_iota(jnp.int32, (buffers, senders), 1)
     same = row % cap == col % cap
@@ -539,7 +527,11 @@
     for i in range(2):
         add = jnp.where(same & (core == i), 1.0, 0.0).astype(BF)
         total = total + dot(add, parts_ref[:, i * half : (i + 1) * half])
-    out_ref[:, width : width + half] = total.astype(BF)
+    total_ref[...] = total.astype(BF)
+    width = out_hbm.shape[1] - half
+    store = pltpu.make_async_copy(total_ref, out_hbm.at[:, width : width + half], sem)
+    store.start()
+    store.wait()
 
 
 def unpack_kernel(factor, core_ref, mine_ref, other_ref, first_ref, second_ref, flat_ref):
@@ -646,6 +638,9 @@
     core = lax.axis_index("core").astype(jnp.int32).reshape(1)
     conv_flops = 2 * slots * pairs * 36 * LANES * PAIR
 
+    smem = pl.BlockSpec(memory_space=pltpu.SMEM)
+    vmem = pl.BlockSpec(memory_space=pltpu.VMEM)
+    hbm = pl.BlockSpec(memory_space=pltpu.HBM)
     shape = jax.ShapeDtypeStruct
     field_shape = shape((pairs, slots, PAIR), BF)
     wide_shape = shape((pairs, OUT_ROWS, PAIR), BF)
@@ -663,12 +658,12 @@
     pick = jnp.asarray(pick_np, BF)
 
     route_row = column_route.reshape(1, shard_rows)
-    route_col = column_route.reshape(shard_rows, 1)
     told_width = row_width + LANES
     outgoing = call(
         functools.partial(send_kernel, cap, slots), shape((buffers, told_width), BF),
         2 * buffers * shard_rows * row_width, 3 * shard_rows * row_width * 2,
-    )(route_row, route_col, column_features)
+        (pltpu.VMEM((shard_rows, row_width), BF), pltpu.SemaphoreType.DMA), in_specs=[vmem, hbm],
+    )(route_row, column_features)
     incoming = share(outgoing.reshape(count_all, cap, told_width), ALL).reshape(buffers, told_width)
 
     cells = mask_cells()
@@ -685,11 +680,9 @@
     )(cotangent.reshape(slots, row_width), perm)
     cot_halo = exchange(cot, pick)
 
-    smem = pl.BlockSpec(memory_space=pltpu.SMEM)
-    vmem = pl.BlockSpec(memory_space=pltpu.VMEM)
     field, take = call(
         functools.partial(place_kernel, cap, slots), (field_shape, shape((buffers, slots), BF)), 1e9, 3e6,
-        (turned,), in_specs=[smem, vmem, vmem],
+        (turned, pltpu.VMEM(perm.shape, BF), pltpu.SemaphoreType.DMA), in_specs=[smem, vmem, hbm],
     )(me, incoming, perm)
     field_halo = exchange(field, pick)
 
@@ -704,36 +697,38 @@
         1.3 * conv_flops, 7e6, (ext, edge, band), ROOM_WIDE,
     )(cot, *cot_halo, mask, second_weight)
 
-    act, hg = call(
-        hidden_kernel, (wide_shape, wide_shape), 1.3 * conv_flops, 8e6, (ext, edge, band), ROOM_WIDE,
-    )(field, *field_halo, mask, first_weight, act_grad)
-
     packed_rows = -(-21 * channels // buffers) * buffers
     run = count_y * cap
     grad_lanes = 2 * packed_rows // buffers * LANES
-    half_shape = shape((buffers // 2, grad_lanes), F32)
-    keep, give = call(
-        functools.partial(corr_kernel, channels, run), (half_shape, half_shape), 2 * conv_flops, 10e6,
-        (
-            ext_near, pltpu.VMEM((channels, depth * slots), BF),
-            pltpu.VMEM((28, channels, LANES), F32), pltpu.VMEM((packed_rows, LANES), F32),
-        ),
-        ROOM_CORR, in_specs=[smem] + [vmem] * 8,
-    )(core, field, *field_halo[:4], hg, act, outer)
-    got = swap_cores(give)
+    half_shape = shape((buffers // 2, grad_lanes // 2), F32)
+    corr_scratch = (
+        pltpu.VMEM((channels, depth * slots), BF),
+        pltpu.VMEM((28, channels, LANES), F32), pltpu.VMEM((packed_rows, LANES), F32),
+    )
+    act, hg, keep0, give0 = call(
+        functools.partial(hidden_kernel, channels, run), (wide_shape, wide_shape, half_shape, half_shape),
+        2.3 * conv_flops, 9e6, (ext, edge, band) + corr_scratch, ROOM_WIDE, in_specs=[smem] + [vmem] * 10,
+    )(core, field, *field_halo, mask, first_weight, act_grad)
+    got0 = swap_cores(give0)
+    keep1, give1 = call(
+        functools.partial(corr_kernel, channels, run), (half_shape, half_shape), conv_flops, 5e6,
+        (ext_near,) + corr_scratch, ROOM_CORR, in_specs=[smem, vmem, vmem],
+    )(core, act, outer)
     sent = call(
         pair_sum_kernel, shape((buffers // 2, grad_lanes), BF), 1e6, 2e6,
-    )(keep, got)
+    )(keep0, got0, keep1, swap_cores(give1))
     parts = share(sent.reshape(count_all // 2, cap, grad_lanes), SAME_CORE).reshape(buffers // 2, grad_lanes)
 
     hg, sent = lax.optimization_barrier((hg, sent))
+    back_width = row_width + grad_lanes // 2
     back = call(
-        grid_grad_kernel, shape((buffers, row_width), BF), 1.2 * conv_flops, 6e6,
+        grid_grad_kernel, shape((buffers, back_width), BF), 1.2 * conv_flops, 6e6,
         (ext_near, sums, turned_low, band), ROOM_NEAR,
     )(hg, first_weight, outer, perm, take)
-    back_width = row_width + grad_lanes // 2
     mixed = call(
         functools.partial(assemble_kernel, cap, run), shape((buffers, back_width), BF), 2e8, 3e6,
+        (pltpu.VMEM((buffers, grad_lanes // 2), BF), pltpu.SemaphoreType.DMA),
+        in_specs=[hbm, vmem], out_specs=hbm, input_output_aliases={0: 0},
     )(back, parts)
     returned = share(mixed.reshape(count_all, cap, back_width), ALL).reshape(buffers, back_width)
 
@@ -748,7 +743,7 @@
     feature_grads = call(
         functools.partial(collect_kernel, cap, slots), shape((shard_rows, row_width), BF),
         2 * buffers * shard_rows * row_width, 3 * shard_rows * row_width * 2,
-    )(route_row, route_col, returned)
+    )(route_row, returned)
 
     factor = float(1.0 / np.sqrt(np.float32(count_all * shard_rows * depth)))
     grads = shape(first_weight.shape, F32)

time: 152 us -> 151 us (level)
  waiting for transfers between devices: 39.6 us -> 36.7 us
    pallas_call x2, Pallas kernels: 17.7 us -> 24.6 us  [the longest x1 14.9 us: on_device(): call(functools.partial(hidden_kernel, channels, run), (wide_shape, wide_s...]
    pallas_call x1, Pallas kernels: 13.2 us -> 6.59 us  [on_device(): call(functools.partial(corr_kernel, channels, run), (half_shape, half_sha...]
    all_to_all x3, waiting for transfers between devices: 35.7 us -> 33.2 us  [share(): return lax.all_to_all(parts, axes, split_axis=0, concat_axis=0, tiled=True)]
    unnamed x58 -> x60, local copies, waits for them, and re-layouts: 9.65 us -> 9.92 us
  transfers between devices with their start and end apart: 13 -> 14, of which waited for: 6 -> 6; matrix products, arithmetic and copies ran while one was open for 0% -> 0% of each run, Pallas kernels for 22% -> 28%
where the time goes in v9:
time: 151 us; the launch traced here: 150 us
  Pallas kernels  63.2 us (42%)
  starting transfers between devices  38.6 us (26%)
  waiting for transfers between devices  36.7 us (24%)
  local copies, waits for them, and re-layouts  10.1 us (7%)
    all_to_all x3, waiting for transfers between devices, share(): return lax.all_to_all(parts, axes, split_axis=0, concat_axis=0, tiled=True)  33.2 us
    ppermute x8, starting transfers between devices, neighbours(): return (lax.ppermute(upper, axes, ahead), lax.ppermute(lower, axes, behind))  19.1 us
    all_to_all x3, starting transfers between devices, share(): return lax.all_to_all(parts, axes, split_axis=0, concat_axis=0, tiled=True)  17.3 us
    pallas_call x1, Pallas kernels, on_device(): call(functools.partial(hidden_kernel, channels, run), (wide_shape, wide_s...  14.9 us
    pallas_call x1, Pallas kernels, on_device(): call(outer_kernel, (shape((pairs, OUT_ROWS, PAIR), F32), field_shape), 1....  9.99 us
    unnamed x60, local copies, waits for them, and re-layouts  9.92 us
    pallas_call x1, Pallas kernels, on_device(): call(grid_grad_kernel, shape((buffers, back_width), BF), 1.2 * conv_flops...  9.65 us
    pallas_call x1, Pallas kernels, on_device(): call(block_kernel, shape((slots, row_width), BF), 1.2 * conv_flops, 80000...  8.93 us
  transfers between devices with their start and end apart: 14, of which 6 were waited for; matrix products, arithmetic and copies ran while one was open for 0% of the time, Pallas kernels for 28%

profile of v9, /device:TPU:0, one launch (start us, length us, event | category | flops | bytes accessed | tf_op | source)
XLA Modules:
  0.0 149.8 jit_solution(9454857231088888215)
XLA Ops:
  2.3 1.6 %shard_map.138 = bf16[256,1664]{1,0:T(8,128)(2,1)} custom-call(s32[1,128]{1,0:T(1,128)S(1)} %bitcast.16, bf16[128,1536]{1,0:T(8,128)(2,1)S(1)} %copy-done), custom_call_target="tpu_custom_call" | custom-call | flops 100663296 | bytes 1179648 | tf_op jit(solution)/shard_map/pallas_call | solution.py:662
  3.9 7.3 %all-to-all-start = ((bf16[32,8,1664]{2,1,0:T(8,128)(2,1)}), bf16[32,8,1664]{2,1,0:T(8,128)(2,1)S(1)}, u32[]{:S(2)}, u32[]{:S(2)}) async-start(bf16[32,8,1664]{2,1,0:T(8,128)(2,1)} %bitcast.3), calls=%async_computation | async-start | bytes 1703936 | tf_op jit(solution)/shard_map/all_to_all | solution.py:577
  11.2 1.2 shard_map.142.f_ref
  12.5 1.3 collective-permute-start.5
  13.8 3.0 %collective-permute-start.4 = (bf16[8,32,256]{2,1,0:T(8,128)(2,1)S(1)}, bf16[8,32,256]{2,1,0:T(8,128)(2,1)S(1)}, u32[]{:S(2)}, u32[]{:S(2)}) collective-permute-start(bf16[8,32,256]{2,1,0:T(8,128)(2,1)S(1)} %get-tuple-element.45), channel_id=1, source_target_pairs={{0,8},{8,16},{16,24},{1,9},{9,17},{17,25},{2,10},{10,18},{18,26},{... | collective-permute-start | bytes 393224 | tf_op jit(solution)/shard_map/ppermute | solution.py:584
  19.8 4.3 %collective-permute-start.6 = (bf16[8,48,256]{2,1,0:T(8,128)(2,1)}, bf16[8,48,256]{2,1,0:T(8,128)(2,1)}, u32[]{:S(2)}, u32[]{:S(2)}) collective-permute-start(bf16[8,48,256]{2,1,0:T(8,128)(2,1)} %get-tuple-element.27.high_ref), channel_id=1, source_target_pairs={{0,1},{1,2},{2,3},{3,4},{4,5},{5,6},{6,7},{8,9},{9,10},{10,11},{11... | collective-permute-start | bytes 589832 | tf_op jit(solution)/shard_map/ppermute | solution.py:584
  24.1 1.3 collective-permute-start.7
  25.4 9.1 %all-to-all-done = bf16[32,8,1664]{2,1,0:T(8,128)(2,1)S(1)} async-done(((bf16[32,8,1664]{2,1,0:T(8,128)(2,1)}), bf16[32,8,1664]{2,1,0:T(8,128)(2,1)S(1)}, u32[]{:S(2)}, u32[]{:S(2)}) %all-to-all-start) | async-done | bytes 852000 | tf_op jit(solution)/shard_map/all_to_all | solution.py:577
  35.7 2.3 %shard_map.139 = (bf16[8,256,256]{2,1,0:T(8,128)(2,1)S(1)}, bf16[256,256]{1,0:T(8,128)(2,1)S(1)}) custom-call(s32[1]{0:T(128)} %bitcast.1.me_ref, bf16[256,1664]{1,0:T(8,128)(2,1)S(1)} %bitcast.13, bf16[6,256,256]{2,1,0:T(8,128)(2,1)S(1)} %copy-done.13), custom_call_target="tpu_custom_call" | custom-call | flops 1000000000 | bytes 3000000 | tf_op jit(solution)/shard_map/pallas_call | solution.py:683
  38.1 1.4 collective-permute-start.1
  39.5 3.0 %collective-permute-start = (bf16[8,32,256]{2,1,0:T(8,128)(2,1)S(1)}, bf16[8,32,256]{2,1,0:T(8,128)(2,1)S(1)}, u32[]{:S(2)}, u32[]{:S(2)}) collective-permute-start(bf16[8,32,256]{2,1,0:T(8,128)(2,1)S(1)} %get-tuple-element.47), channel_id=1, source_target_pairs={{0,8},{8,16},{16,24},{1,9},{9,17},{17,25},{2,10},{10,18},{18,26},{... | collective-permute-start | bytes 393224 | tf_op jit(solution)/shard_map/ppermute | solution.py:584
  44.4 3.3 %collective-permute-start.2 = (bf16[8,48,256]{2,1,0:T(8,128)(2,1)S(1)}, bf16[8,48,256]{2,1,0:T(8,128)(2,1)S(1)}, u32[]{:S(2)}, u32[]{:S(2)}) collective-permute-start(bf16[8,48,256]{2,1,0:T(8,128)(2,1)S(1)} %get-tuple-element.25.high_ref), channel_id=1, source_target_pairs={{0,1},{1,2},{2,3},{3,4},{4,5},{5,6},{6,7},{8,9},{9,10},{10,11},{11... | collective-permute-start | bytes 589832 | tf_op jit(solution)/shard_map/ppermute | solution.py:584
  47.7 1.4 collective-permute-start.3
  49.1 10.0 %shard_map.144 = (f32[8,336,256]{2,1,0:T(8,128)S(1)}, bf16[8,256,256]{2,1,0:T(8,128)(2,1)S(1)}) custom-call(bf16[8,256,256]{2,1,0:T(8,128)(2,1)S(1)} %copy-done.2, bf16[8,32,256]{2,1,0:T(8,128)(2,1)S(1)} %copy-done.11, bf16[8,32,256]{2,1,0:T(8,128)(2,1)S(1)} %copy-done.9, bf16[8,48,256]{2,1,0:T(8,128)(2,1)} %collective-permute-done.6.ylo_ref, ...), custom_call_target="tpu_custom_call" | custom-call | flops 6281389568 | bytes 7000000 | tf_op jit(solution)/shard_map/pallas_call | solution.py:695
  59.2 14.9 %shard_map.145 = (bf16[8,336,256]{2,1,0:T(8,128)(2,1)S(1)}, bf16[8,336,256]{2,1,0:T(8,128)(2,1)S(1)}, f32[128,1024]{1,0:T(8,128)S(1)}, f32[128,1024]{1,0:T(8,128)S(1)}) custom-call(s32[1]{0:T(128)} %bitcast.core_ref, bf16[8,256,256]{2,1,0:T(8,128)(2,1)S(1)} %get-tuple-element.24.f_ref.field_ref, bf16[8,32,256]{2,1,0:T(8,128)(2,1)S(1)} %collective-permute-done.xlo_ref, ...), custom_call_target="tpu_custom_call" | custom-call | flops 11113228288 | bytes 9000000 | tf_op jit(solution)/shard_map/pallas_call | solution.py:708
  74.1 2.1 %collective-permute-start.8 = (f32[128,1024]{1,0:T(8,128)S(1)}, f32[128,1024]{1,0:T(8,128)S(1)}, u32[]{:S(2)}, u32[]{:S(2)}) collective-permute-start(f32[128,1024]{1,0:T(8,128)S(1)} %get-tuple-element.32), channel_id=1, source_target_pairs={{0,8},{8,0},{16,24},{24,16},{1,9},{9,1},{17,25},{25,17},{2,10},{10... | collective-permute-start | bytes 1572872 | tf_op jit(solution)/shard_map/ppermute | solution.py:589
  76.2 6.6 %shard_map.146 = (f32[128,1024]{1,0:T(8,128)S(1)}, f32[128,1024]{1,0:T(8,128)S(1)}) custom-call(s32[1]{0:T(128)} %bitcast.core_ref, bf16[8,336,256]{2,1,0:T(8,128)(2,1)S(1)} %get-tuple-element.39.act_ref, bf16[8,256,256]{2,1,0:T(8,128)(2,1)S(1)} %get-tuple-element.34.outer_ref), custom_call_target="tpu_custom_call" | custom-call | flops 4831838208 | bytes 5000000 | tf_op jit(solution)/shard_map/pallas_call | solution.py:713
  82.9 1.9 %collective-permute-done.9.got1_ref = f32[128,1024]{1,0:T(8,128)S(1)} collective-permute-done((f32[128,1024]{1,0:T(8,128)S(1)}, f32[128,1024]{1,0:T(8,128)S(1)}, u32[]{:S(2)}, u32[]{:S(2)}) %collective-permute-start.9) | collective-permute-done | bytes 524320 | tf_op jit(solution)/shard_map/ppermute | solution.py:589
  85.7 6.4 %all-to-all-start.1 = ((bf16[16,8,2048]{2,1,0:T(8,128)(2,1)}), bf16[16,8,2048]{2,1,0:T(8,128)(2,1)S(1)}, u32[]{:S(2)}, u32[]{:S(2)}) async-start(bf16[16,8,2048]{2,1,0:T(8,128)(2,1)} %bitcast.6), calls=%async_computation.1 | async-start | bytes 1048576 | tf_op jit(solution)/shard_map/all_to_all | solution.py:577
  92.1 1.1 copy-done.14
  93.2 1.3 copy-done.23
  94.5 1.2 copy-done.25
  95.8 9.6 %shard_map.148.back_hbm = bf16[256,2560]{1,0:T(8,128)(2,1)} custom-call(bf16[8,336,256]{2,1,0:T(8,128)(2,1)S(1)} %copy-done.23, bf16[27,96,96]{2,1,0:T(8,128)(2,1)S(1)} %copy-done.6, bf16[8,256,256]{2,1,0:T(8,128)(2,1)S(1)} %copy-done.25, bf16[6,256,256]{2,1,0:T(8,128)(2,1)S(1)} %copy-done.14, bf16[256,256]{1,0:T(8,128)(2,1)S(1)} %copy-done.19), custom_call_target="tpu_custom_call" | custom-call | flops 5798205952 | bytes 6000000 | tf_op jit(solution)/shard_map/pallas_call | solution.py:724
  105.4 2.3 %all-to-all-done.1 = bf16[16,8,2048]{2,1,0:T(8,128)(2,1)S(1)} async-done(((bf16[16,8,2048]{2,1,0:T(8,128)(2,1)}), bf16[16,8,2048]{2,1,0:T(8,128)(2,1)S(1)}, u32[]{:S(2)}, u32[]{:S(2)}) %all-to-all-start.1) | async-done | bytes 524320 | tf_op jit(solution)/shard_map/all_to_all | solution.py:577
  107.7 1.2 shard_map.149
  108.9 3.6 %all-to-all-start.2 = ((bf16[32,8,2560]{2,1,0:T(8,128)(2,1)}), bf16[32,8,2560]{2,1,0:T(8,128)(2,1)S(1)}, u32[]{:S(2)}, u32[]{:S(2)}) async-start(bf16[32,8,2560]{2,1,0:T(8,128)(2,1)} %bitcast.8), calls=%async_computation.2 | async-start | bytes 2621440 | tf_op jit(solution)/shard_map/all_to_all | solution.py:577
  112.5 1.1 copy-done.15
  113.7 1.3 copy-done.21
  115.0 8.9 %shard_map.150 = bf16[256,1536]{1,0:T(8,128)(2,1)} custom-call(bf16[8,336,256]{2,1,0:T(8,128)(2,1)S(1)} %copy-done.21, f32[560,128]{1,0:T(8,128)S(1)} %shard_map.141.mask_ref, bf16[27,96,96]{2,1,0:T(8,128)(2,1)S(1)} %copy-done.7, bf16[8,256,256]{2,1,0:T(8,128)(2,1)S(1)} %get-tuple-element.24.f_ref.field_ref, bf16[6,256,256]{2,1,0:T(8,128)(2,1)S(1)} %copy-done.15), custom_call_target="tpu_custom_call" | custom-call | flops 5798205952 | bytes 8000000 | tf_op jit(solution)/shard_map/pallas_call | solution.py:736
  123.9 21.8 %all-to-all-done.2 = bf16[32,8,2560]{2,1,0:T(8,128)(2,1)S(1)} async-done(((bf16[32,8,2560]{2,1,0:T(8,128)(2,1)}), bf16[32,8,2560]{2,1,0:T(8,128)(2,1)S(1)}, u32[]{:S(2)}, u32[]{:S(2)}) %all-to-all-start.2) | async-done | bytes 1310752 | tf_op jit(solution)/shard_map/all_to_all | solution.py:577
  145.9 1.2 shard_map.151
  147.8 2.0 %shard_map.152 = (f32[27,96,96]{2,1,0:T(8,128)}, f32[27,96,96]{2,1,0:T(8,128)}) custom-call(s32[1]{0:T(128)} %bitcast.core_ref, bf16[256,1024]{1,0:T(8,128)(2,1)S(1)} %slice.19.mine_ref, bf16[256,1024]{1,0:T(8,128)(2,1)S(1)} %collective-permute-done.10.other_ref), custom_call_target="tpu_custom_call" | custom-call | flops 1000000 | bytes 4000000 | tf_op jit(solution)/shard_map/pallas_call | solution.py:750
  (76 shorter events, 9.3 us)
Async XLA Ops:
  2.3 8.9 %copy-start.5 = (bf16[16,16,1536]{2,1,0:T(8,128)(2,1)S(1)}, bf16[16,16,1536]{2,1,0:T(8,128)(2,1)}, u32[]{:S(2)}) copy-start(bf16[16,16,1536]{2,1,0:T(8,128)(2,1)} %param.13) | copy-start | bytes 2359300
  2.3 8.9 %copy-start.12 = (bf16[6,256,256]{2,1,0:T(8,128)(2,1)S(1)}, bf16[6,256,256]{2,1,0:T(8,128)(2,1)}, u32[]{:S(2)}) copy-start(bf16[6,256,256]{2,1,0:T(8,128)(2,1)} %constant.38.clone.perm_hbm.perm_ref) | copy-start | bytes 2359300
  3.9 30.7 %all-to-all-start = ((bf16[32,8,1664]{2,1,0:T(8,128)(2,1)}), bf16[32,8,1664]{2,1,0:T(8,128)(2,1)S(1)}, u32[]{:S(2)}, u32[]{:S(2)}) async-start(bf16[32,8,1664]{2,1,0:T(8,128)(2,1)} %bitcast.3), calls=%async_computation | async-start | bytes 1703936 | tf_op jit(solution)/shard_map/all_to_all | solution.py:577
  12.4 22.1 %copy-start.1 = (bf16[8,256,256]{2,1,0:T(8,128)(2,1)}, bf16[8,256,256]{2,1,0:T(8,128)(2,1)S(1)}, u32[]{:S(2)}) copy-start(bf16[8,256,256]{2,1,0:T(8,128)(2,1)S(1)} %shard_map.142.f_ref) | copy-start | bytes 3145732
  12.5 4.4 %collective-permute-start.5 = (bf16[8,32,256]{2,1,0:T(8,128)(2,1)S(1)}, bf16[8,32,256]{2,1,0:T(8,128)(2,1)S(1)}, u32[]{:S(2)}, u32[]{:S(2)}) collective-permute-start(bf16[8,32,256]{2,1,0:T(8,128)(2,1)S(1)} %get-tuple-element.44), channel_id=1, source_target_pairs={{8,0},{16,8},{24,16},{9,1},{17,9},{25,17},{10,2},{18,10},{26,18},{... | collective-permute-start | bytes 393224 | tf_op jit(solution)/shard_map/ppermute | solution.py:584
  13.8 4.0 %collective-permute-start.4 = (bf16[8,32,256]{2,1,0:T(8,128)(2,1)S(1)}, bf16[8,32,256]{2,1,0:T(8,128)(2,1)S(1)}, u32[]{:S(2)}, u32[]{:S(2)}) collective-permute-start(bf16[8,32,256]{2,1,0:T(8,128)(2,1)S(1)} %get-tuple-element.45), channel_id=1, source_target_pairs={{0,8},{8,16},{16,24},{1,9},{9,17},{17,25},{2,10},{10,18},{18,26},{... | collective-permute-start | bytes 393224 | tf_op jit(solution)/shard_map/ppermute | solution.py:584
  16.8 17.7 %copy-start.8 = (bf16[8,32,256]{2,1,0:T(8,128)(2,1)}, bf16[8,32,256]{2,1,0:T(8,128)(2,1)S(1)}, u32[]{:S(2)}) copy-start(bf16[8,32,256]{2,1,0:T(8,128)(2,1)S(1)} %collective-permute-done.5.xhi_ref) | copy-start | bytes 393220
  18.7 15.9 %copy-start.10 = (bf16[8,32,256]{2,1,0:T(8,128)(2,1)}, bf16[8,32,256]{2,1,0:T(8,128)(2,1)S(1)}, u32[]{:S(2)}) copy-start(bf16[8,32,256]{2,1,0:T(8,128)(2,1)S(1)} %collective-permute-done.4.xlo_ref) | copy-start | bytes 393220
  19.8 29.3 %collective-permute-start.6 = (bf16[8,48,256]{2,1,0:T(8,128)(2,1)}, bf16[8,48,256]{2,1,0:T(8,128)(2,1)}, u32[]{:S(2)}, u32[]{:S(2)}) collective-permute-start(bf16[8,48,256]{2,1,0:T(8,128)(2,1)} %get-tuple-element.27.high_ref), channel_id=1, source_target_pairs={{0,1},{1,2},{2,3},{3,4},{4,5},{5,6},{6,7},{8,9},{9,10},{10,11},{11... | collective-permute-start | bytes 589832 | tf_op jit(solution)/shard_map/ppermute | solution.py:584
  24.1 25.0 %collective-permute-start.7 = (bf16[8,48,256]{2,1,0:T(8,128)(2,1)S(1)}, bf16[8,48,256]{2,1,0:T(8,128)(2,1)}, u32[]{:S(2)}, u32[]{:S(2)}) collective-permute-start(bf16[8,48,256]{2,1,0:T(8,128)(2,1)S(1)} %get-tuple-element.28.low_ref), channel_id=1, source_target_pairs={{1,0},{2,1},{3,2},{4,3},{5,4},{6,5},{7,6},{9,8},{10,9},{11,10},{12... | collective-permute-start | bytes 589832 | tf_op jit(solution)/shard_map/ppermute | solution.py:584
  35.7 6.9 %copy-start.26 = (s32[560]{0:T(1024)S(1)}, s32[560]{0:T(1024)}, u32[]{:S(2)}) copy-start(s32[560]{0:T(1024)} %constant.43.clone) | copy-start | bytes 6724
  35.7 6.9 %copy-start.27 = (s32[560]{0:T(1024)S(1)}, s32[560]{0:T(1024)}, u32[]{:S(2)}) copy-start(s32[560]{0:T(1024)} %constant.41.clone) | copy-start | bytes 6724
  35.7 6.9 %copy-start.28 = (s32[560]{0:T(1024)S(1)}, s32[560]{0:T(1024)}, u32[]{:S(2)}) copy-start(s32[560]{0:T(1024)} %constant.40.clone) | copy-start | bytes 6724
  35.7 6.9 %copy-start.29 = (pred[560]{0:T(1024)(128)(4,1)S(1)}, pred[560]{0:T(1024)(128)(4,1)}, u32[]{:S(2)}) copy-start(pred[560]{0:T(1024)(128)(4,1)} %constant.42.clone) | copy-start | bytes 1684
  38.1 5.8 %collective-permute-start.1 = (bf16[8,32,256]{2,1,0:T(8,128)(2,1)S(1)}, bf16[8,32,256]{2,1,0:T(8,128)(2,1)S(1)}, u32[]{:S(2)}, u32[]{:S(2)}) collective-permute-start(bf16[8,32,256]{2,1,0:T(8,128)(2,1)S(1)} %get-tuple-element.46), channel_id=1, source_target_pairs={{8,0},{16,8},{24,16},{9,1},{17,9},{25,17},{10,2},{18,10},{26,18},{... | collective-permute-start | bytes 393224 | tf_op jit(solution)/shard_map/ppermute | solution.py:584
  39.5 4.4 %collective-permute-start = (bf16[8,32,256]{2,1,0:T(8,128)(2,1)S(1)}, bf16[8,32,256]{2,1,0:T(8,128)(2,1)S(1)}, u32[]{:S(2)}, u32[]{:S(2)}) collective-permute-start(bf16[8,32,256]{2,1,0:T(8,128)(2,1)S(1)} %get-tuple-element.47), channel_id=1, source_target_pairs={{0,8},{8,16},{16,24},{1,9},{9,17},{17,25},{2,10},{10,18},{18,26},{... | collective-permute-start | bytes 393224 | tf_op jit(solution)/shard_map/ppermute | solution.py:584
  42.8 6.3 %copy-start.2 = (bf16[8,256,256]{2,1,0:T(8,128)(2,1)S(1)}, bf16[8,256,256]{2,1,0:T(8,128)(2,1)}, u32[]{:S(2)}) copy-start(bf16[8,256,256]{2,1,0:T(8,128)(2,1)} %copy-done.1) | copy-start | bytes 3145732
  42.8 6.3 %copy-start.7 = (bf16[27,96,96]{2,1,0:T(8,128)(2,1)S(1)}, bf16[27,96,96]{2,1,0:T(8,128)(2,1)}, u32[]{:S(2)}) copy-start(bf16[27,96,96]{2,1,0:T(8,128)(2,1)} %raw_ref.7) | copy-start | bytes 1492996
  42.8 6.3 %copy-start.9 = (bf16[8,32,256]{2,1,0:T(8,128)(2,1)S(1)}, bf16[8,32,256]{2,1,0:T(8,128)(2,1)}, u32[]{:S(2)}) copy-start(bf16[8,32,256]{2,1,0:T(8,128)(2,1)} %copy-done.8) | copy-start | bytes 393220
  44.4 14.8 %collective-permute-start.2 = (bf16[8,48,256]{2,1,0:T(8,128)(2,1)S(1)}, bf16[8,48,256]{2,1,0:T(8,128)(2,1)S(1)}, u32[]{:S(2)}, u32[]{:S(2)}) collective-permute-start(bf16[8,48,256]{2,1,0:T(8,128)(2,1)S(1)} %get-tuple-element.25.high_ref), channel_id=1, source_target_pairs={{0,1},{1,2},{2,3},{3,4},{4,5},{5,6},{6,7},{8,9},{9,10},{10,11},{11... | collective-permute-start | bytes 589832 | tf_op jit(solution)/shard_map/ppermute | solution.py:584
  47.6 11.5 %copy-start.6 = (bf16[27,96,96]{2,1,0:T(8,128)(2,1)S(1)}, bf16[27,96,96]{2,1,0:T(8,128)(2,1)}, u32[]{:S(2)}) copy-start(bf16[27,96,96]{2,1,0:T(8,128)(2,1)} %raw_ref.6) | copy-start | bytes 1492996
  47.7 11.5 %collective-permute-start.3 = (bf16[8,48,256]{2,1,0:T(8,128)(2,1)S(1)}, bf16[8,48,256]{2,1,0:T(8,128)(2,1)S(1)}, u32[]{:S(2)}, u32[]{:S(2)}) collective-permute-start(bf16[8,48,256]{2,1,0:T(8,128)(2,1)S(1)} %get-tuple-element.26.low_ref), channel_id=1, source_target_pairs={{1,0},{2,1},{3,2},{4,3},{5,4},{6,5},{7,6},{9,8},{10,9},{11,10},{12... | collective-permute-start | bytes 589832 | tf_op jit(solution)/shard_map/ppermute | solution.py:584
  59.1 17.1 %copy-start.24 = (bf16[8,256,256]{2,1,0:T(8,128)(2,1)}, bf16[8,256,256]{2,1,0:T(8,128)(2,1)S(1)}, u32[]{:S(2)}) copy-start(bf16[8,256,256]{2,1,0:T(8,128)(2,1)S(1)} %get-tuple-element.34.outer_ref) | copy-start | bytes 3145732
  74.1 8.7 %copy-start.20 = (bf16[8,336,256]{2,1,0:T(8,128)(2,1)}, bf16[8,336,256]{2,1,0:T(8,128)(2,1)S(1)}, u32[]{:S(2)}) copy-start(bf16[8,336,256]{2,1,0:T(8,128)(2,1)S(1)} %get-tuple-element.39.act_ref) | copy-start | bytes 4128772
  74.1 8.7 %copy-start.22 = (bf16[8,336,256]{2,1,0:T(8,128)(2,1)}, bf16[8,336,256]{2,1,0:T(8,128)(2,1)S(1)}, u32[]{:S(2)}) copy-start(bf16[8,336,256]{2,1,0:T(8,128)(2,1)S(1)} %get-tuple-element.37.hg_ref) | copy-start | bytes 4128772
  74.1 8.8 %collective-permute-start.8 = (f32[128,1024]{1,0:T(8,128)S(1)}, f32[128,1024]{1,0:T(8,128)S(1)}, u32[]{:S(2)}, u32[]{:S(2)}) collective-permute-start(f32[128,1024]{1,0:T(8,128)S(1)} %get-tuple-element.32), channel_id=1, source_target_pairs={{0,8},{8,0},{16,24},{24,16},{1,9},{9,1},{17,25},{25,17},{2,10},{10... | collective-permute-start | bytes 1572872 | tf_op jit(solution)/shard_map/ppermute | solution.py:589
  82.8 2.0 %collective-permute-start.9 = (f32[128,1024]{1,0:T(8,128)S(1)}, f32[128,1024]{1,0:T(8,128)S(1)}, u32[]{:S(2)}, u32[]{:S(2)}) collective-permute-start(f32[128,1024]{1,0:T(8,128)S(1)} %get-tuple-element.36), channel_id=1, source_target_pairs={{0,8},{8,0},{16,24},{24,16},{1,9},{9,1},{17,25},{25,17},{2,10},{10... | collective-permute-start | bytes 1572872 | tf_op jit(solution)/shard_map/ppermute | solution.py:589
  84.8 7.3 %copy-start.19 = (bf16[256,256]{1,0:T(8,128)(2,1)S(1)}, bf16[256,256]{1,0:T(8,128)(2,1)}, u32[]{:S(2)}) copy-start(bf16[256,256]{1,0:T(8,128)(2,1)} %copy-done.18) | copy-start | bytes 393220
  85.7 22.0 %all-to-all-start.1 = ((bf16[16,8,2048]{2,1,0:T(8,128)(2,1)}), bf16[16,8,2048]{2,1,0:T(8,128)(2,1)S(1)}, u32[]{:S(2)}, u32[]{:S(2)}) async-start(bf16[16,8,2048]{2,1,0:T(8,128)(2,1)} %bitcast.6), calls=%async_computation.1 | async-start | bytes 1048576 | tf_op jit(solution)/shard_map/all_to_all | solution.py:577
  108.9 36.8 %all-to-all-start.2 = ((bf16[32,8,2560]{2,1,0:T(8,128)(2,1)}), bf16[32,8,2560]{2,1,0:T(8,128)(2,1)S(1)}, u32[]{:S(2)}, u32[]{:S(2)}) async-start(bf16[32,8,2560]{2,1,0:T(8,128)(2,1)} %bitcast.8), calls=%async_computation.2 | async-start | bytes 2621440 | tf_op jit(solution)/shard_map/all_to_all | solution.py:577
  115.0 30.9 %copy-start.4 = (s32[128]{0:T(128)S(1)}, s32[128]{0:T(128)}, u32[]{:S(2)}) copy-start(s32[128]{0:T(128)} %param.12) | copy-start | bytes 1540
  145.8 2.0 %collective-permute-start.10 = (bf16[256,1024]{1,0:T(8,128)(2,1)S(1)}, bf16[256,1024]{1,0:T(8,128)(2,1)S(1)}, u32[]{:S(2)}, u32[]{:S(2)}) collective-permute-start(bf16[256,1024]{1,0:T(8,128)(2,1)S(1)} %slice.19.mine_ref), channel_id=1, source_target_pairs={{0,8},{8,0},{16,24},{24,16},{1,9},{9,1},{17,25},{25,17},{2,10},{10... | collective-permute-start | bytes 1572872 | tf_op jit(solution)/shard_map/ppermute | solution.py:589
  (12 other events, 26.7 us)

commit v10 on v9

--- a/solution.py
+++ b/solution.py
@@ -11,7 +11,7 @@
 LANES = 128
 PAIR = 256
 MIB = 1024 * 1024
-ROOM_WIDE, ROOM_NEAR, ROOM_CORR, ROOM_SMALL = 22, 14, 14, 5
+ROOM_WIDE, ROOM_NEAR, ROOM_CORR, ROOM_SMALL = 26, 18, 14, 5
 BF = jnp.bfloat16
 F32 = jnp.float32
 
@@ -268,7 +268,6 @@
 
 
 def widen_two(ext_ref, edge_ref, f_ref, xlo_ref, xhi_ref, ylo_ref, yhi_ref, low_ref, high_ref, mask_ref=None):
-    pairs = f_ref.shape[0]
     for b in range(3):
         clear_ends(ext_ref, (b,))
         for a in range(3):
@@ -281,7 +280,7 @@
             return value
         return value * twice(mask_ref[mask_start + start : mask_start + start + size, :])
 
-    def body(k, carry):
+    def fill(k):
         ylo = read(ylo_ref, k, 0, MSG, M_YLO)
         yhi = read(yhi_ref, k, 0, MSG, M_YHI)
         low = read(low_ref, k, 0, MSG, M_LOW)
@@ -306,22 +305,27 @@
                         value = pltpu.roll(value, MSG - turn, 0)
                     sides.append(value[0:EDGE])
                 put_pair(edge_ref, (a, b), k, (slice(None),), jnp.concatenate(sides, axis=0))
-        return carry
-
-    lax.fori_loop(0, pairs, body, 0)
+
+    return fill
 
 
 def widen_one(ext_ref, rows_ref):
-    pairs = rows_ref.shape[0]
     for b in range(3):
         clear_ends(ext_ref, (b,))
     row = lax.broadcasted_iota(jnp.int32, (NY, PAIR), 0)
 
-    def body(k, carry):
+    def fill(k):
         edges = rows_ref[k, OUT_MAIN:OUT_ROWS, :].astype(F32)
         for xp in range(NX + 2):
             mid = rows_ref[k, xp * NY : (xp + 1) * NY, :].astype(F32)
             put_shifted(ext_ref, k, xp, mid, edges[xp : xp + 1, :], edges[EDGE + xp : EDGE + xp + 1, :], row)
+
+    return fill
+
+
+def fill_all(fill, pairs):
+    def body(k, carry):
+        fill(k)
         return carry
 
     lax.fori_loop(0, pairs, body, 0)
@@ -348,16 +352,22 @@
     for a in range(3):
         for b in range(3):
             for j in range(2):
-                pieces.append(ext_ref[b, pl.ds(k + j, STEP), a : a + NX].reshape(STEP * NX * NY, PAIR))
+                pieces.append(ext_ref[b, k + j : k + j + STEP, a : a + NX].reshape(STEP * NX * NY, PAIR))
     return dot(jnp.concatenate(pieces, axis=1), w_ref[...])
 
 
-def each_step(pairs, body):
-    def step(t, carry):
-        body(t * STEP)
-        return carry
-
-    lax.fori_loop(0, pairs // STEP, step, 0)
+def each_step(pairs, fill, conv, finish):
+    for k in range(STEP + 1):
+        fill(k)
+    last = None
+    for k in range(0, pairs, STEP):
+        for ahead in range(k + STEP + 1, min(k + 2 * STEP + 1, pairs)):
+            fill(ahead)
+        total = conv(k)
+        if last is not None:
+            finish(*last)
+        last = (k, total)
+    finish(*last)
 
 
 def out_mask(mask_ref):
@@ -370,15 +380,14 @@
 def outer_kernel(f_ref, xlo_ref, xhi_ref, ylo_ref, yhi_ref, low_ref, high_ref, mask_ref, raw_ref,
                  out_ref, outer_ref, ext_ref, edge_ref, w_ref):
     build_band(w_ref, raw_ref, True)
-    widen_two(ext_ref, edge_ref, f_ref, xlo_ref, xhi_ref, ylo_ref, yhi_ref, low_ref, high_ref, mask_ref)
-
-    def body(k):
-        total = conv_wide(ext_ref, edge_ref, w_ref, k)
+    fill = widen_two(ext_ref, edge_ref, f_ref, xlo_ref, xhi_ref, ylo_ref, yhi_ref, low_ref, high_ref, mask_ref)
+
+    def finish(k, total):
         for i in range(STEP):
             out_ref[k + i] = total[i * OUT_ROWS : (i + 1) * OUT_ROWS]
             outer_ref[k + i] = (f_ref[k + i].astype(F32) * twice(mask_ref[0 : NX * NY, :])).astype(BF)
 
-    each_step(f_ref.shape[0], body)
+    each_step(f_ref.shape[0], fill, lambda k: conv_wide(ext_ref, edge_ref, w_ref, k), finish)
 
 
 def correlate(gt_ref, ext_ref, first_x, taps_ref):
@@ -426,10 +435,9 @@
                   raw_ref, grad_ref, act_ref, hg_ref, keep_ref, give_ref,
                   ext_ref, edge_ref, w_ref, gt_ref, taps_ref, packed_ref):
     build_band(w_ref, raw_ref, False)
-    widen_two(ext_ref, edge_ref, f_ref, xlo_ref, xhi_ref, ylo_ref, yhi_ref, low_ref, high_ref)
-
-    def body(k):
-        total = conv_wide(ext_ref, edge_ref, w_ref, k)
+    fill = widen_two(ext_ref, edge_ref, f_ref, xlo_ref, xhi_ref, ylo_ref, yhi_ref, low_ref, high_ref)
+
+    def finish(k, total):
         m = out_mask(mask_ref)
         for i in range(STEP):
             hidden = m * total[i * OUT_ROWS : (i + 1) * OUT_ROWS]
@@ -437,7 +445,7 @@
             act_ref[k + i] = (hidden * sigma).astype(BF)
             hg_ref[k + i] = (m * grad_ref[k + i] * sigma * (1.0 + hidden * (1.0 - sigma))).astype(BF)
 
-    each_step(f_ref.shape[0], body)
+    each_step(f_ref.shape[0], fill, lambda k: conv_wide(ext_ref, edge_ref, w_ref, k), finish)
     turn(gt_ref, hg_ref, NY, channels)
     correlate(gt_ref, ext_ref, 1, taps_ref)
     hand_out(channels, run, core_ref, taps_ref, packed_ref, keep_ref, give_ref)
@@ -469,7 +477,7 @@
 
 
 def corr_kernel(channels, run, core_ref, act_ref, outer_ref, keep_ref, give_ref, ext_ref, gt_ref, taps_ref, packed_ref):
-    widen_one(ext_ref, act_ref)
+    fill_all(widen_one(ext_ref, act_ref), act_ref.shape[0])
     turn(gt_ref, outer_ref, 0, channels)
     correlate(gt_ref, ext_ref, 0, taps_ref)
     hand_out(channels, run, core_ref, taps_ref, packed_ref, keep_ref, give_ref)
@@ -477,15 +485,14 @@
 
 def grid_grad_kernel(hg_ref, raw_ref, outer_ref, perm_ref, take_ref, out_ref, ext_ref, sum_ref, turned_ref, w_ref):
     build_band(w_ref, raw_ref, True)
-    widen_one(ext_ref, hg_ref)
-
-    def body(k):
-        total = conv_inner(ext_ref, w_ref, k)
+    fill = widen_one(ext_ref, hg_ref)
+
+    def finish(k, total):
         rows = NX * NY
         for i in range(STEP):
             sum_ref[k + i] = (outer_ref[k + i].astype(F32) + total[i * rows : (i + 1) * rows]).astype(BF)
 
-    each_step(outer_ref.shape[0], body)
+    each_step(outer_ref.shape[0], fill, lambda k: conv_inner(ext_ref, w_ref, k), finish)
     gather_pairs(sum_ref, turned_ref)
     take = take_ref[...]
     for i in range(perm_ref.shape[0]):
@@ -495,16 +502,15 @@
 
 def block_kernel(act_ref, mask_ref, raw_ref, field_ref, perm_ref, out_ref, ext_ref, sum_ref, turned_ref, w_ref):
     build_band(w_ref, raw_ref, False)
-    widen_one(ext_ref, act_ref)
-
-    def body(k):
-        total = conv_inner(ext_ref, w_ref, k)
+    fill = widen_one(ext_ref, act_ref)
+
+    def finish(k, total):
         m = twice(mask_ref[0 : NX * NY, :])
         rows = NX * NY
         for i in range(STEP):
             sum_ref[k + i] = (field_ref[k + i].astype(F32) + m * total[i * rows : (i + 1) * rows]).astype(BF)
 
-    each_step(field_ref.shape[0], body)
+    each_step(field_ref.shape[0], fill, lambda k: conv_inner(ext_ref, w_ref, k), finish)
     gather_pairs(sum_ref, turned_ref)
     for i in range(perm_ref.shape[0]):
         out_ref[:, i * PAIR : (i + 1) * PAIR] = dot_nt(turned_ref[i], perm_ref[i]).astype(BF)

time: 151 us -> 147 us (0.974)
  Pallas kernels: 63.2 us -> 57.4 us
  waiting for transfers between devices: 36.7 us -> 39.3 us
    all_to_all x3, waiting for transfers between devices: 33.2 us -> 35.8 us  [share(): return lax.all_to_all(parts, axes, split_axis=0, concat_axis=0, tiled=True)]
    pallas_call x1, Pallas kernels: 9.99 us -> 8.33 us  [on_device(): call(outer_kernel, (shape((pairs, OUT_ROWS, PAIR), F32), field_shape), 1....]
    pallas_call x1, Pallas kernels: 9.65 us -> 8.11 us  [on_device(): call(grid_grad_kernel, shape((buffers, back_width), BF), 1.2 * conv_flops...]
  transfers between devices with their start and end apart: 14 -> 14, of which waited for: 6 -> 6; matrix products, arithmetic and copies ran while one was open for 0% -> 0% of each run, Pallas kernels for 28% -> 26%
where the time goes in v10:
time: 147 us; the launch traced here: 146 us
  Pallas kernels  57.4 us (39%)
  waiting for transfers between devices  39.3 us (27%)
  starting transfers between devices  38.1 us (26%)
  local copies, waits for them, and re-layouts  10.1 us (7%)
    all_to_all x3, waiting for transfers between devices, share(): return lax.all_to_all(parts, axes, split_axis=0, concat_axis=0, tiled=True)  35.8 us
    ppermute x8, starting transfers between devices, neighbours(): return (lax.ppermute(upper, axes, ahead), lax.ppermute(lower, axes, behind))  19.3 us
    all_to_all x3, starting transfers between devices, share(): return lax.all_to_all(parts, axes, split_axis=0, concat_axis=0, tiled=True)  16.6 us
    pallas_call x1, Pallas kernels, on_device(): call(functools.partial(hidden_kernel, channels, run), (wide_shape, wide_s...  13.7 us
    unnamed x60, local copies, waits for them, and re-layouts  9.92 us
    pallas_call x1, Pallas kernels, on_device(): call(outer_kernel, (shape((pairs, OUT_ROWS, PAIR), F32), field_shape), 1....  8.33 us
    pallas_call x1, Pallas kernels, on_device(): call(grid_grad_kernel, shape((buffers, back_width), BF), 1.2 * conv_flops...  8.11 us
    pallas_call x1, Pallas kernels, on_device(): call(block_kernel, shape((slots, row_width), BF), 1.2 * conv_flops, 80000...  7.63 us
  transfers between devices with their start and end apart: 14, of which 6 were waited for; matrix products, arithmetic and copies ran while one was open for 0% of the time, Pallas kernels for 26%

profile of v10, /device:TPU:0, one launch (start us, length us, event | category | flops | bytes accessed | tf_op | source)
XLA Modules:
  0.0 146.1 jit_solution(12301955753250154756)
XLA Ops:
  2.3 1.6 %shard_map.138 = bf16[256,1664]{1,0:T(8,128)(2,1)} custom-call(s32[1,128]{1,0:T(1,128)S(1)} %bitcast.16, bf16[128,1536]{1,0:T(8,128)(2,1)S(1)} %copy-done), custom_call_target="tpu_custom_call" | custom-call | flops 100663296 | bytes 1179648 | tf_op jit(solution)/shard_map/pallas_call | solution.py:668
  3.9 7.3 %all-to-all-start = ((bf16[32,8,1664]{2,1,0:T(8,128)(2,1)}), bf16[32,8,1664]{2,1,0:T(8,128)(2,1)S(1)}, u32[]{:S(2)}, u32[]{:S(2)}) async-start(bf16[32,8,1664]{2,1,0:T(8,128)(2,1)} %bitcast.3), calls=%async_computation | async-start | bytes 1703936 | tf_op jit(solution)/shard_map/all_to_all | solution.py:583
  11.2 1.2 shard_map.142.f_ref
  12.5 1.3 collective-permute-start.5
  13.8 3.0 %collective-permute-start.4 = (bf16[8,32,256]{2,1,0:T(8,128)(2,1)S(1)}, bf16[8,32,256]{2,1,0:T(8,128)(2,1)S(1)}, u32[]{:S(2)}, u32[]{:S(2)}) collective-permute-start(bf16[8,32,256]{2,1,0:T(8,128)(2,1)S(1)} %get-tuple-element.45), channel_id=1, source_target_pairs={{0,8},{8,16},{16,24},{1,9},{9,17},{17,25},{2,10},{10,18},{18,26},{... | collective-permute-start | bytes 393224 | tf_op jit(solution)/shard_map/ppermute | solution.py:590
  19.8 4.3 %collective-permute-start.6 = (bf16[8,48,256]{2,1,0:T(8,128)(2,1)}, bf16[8,48,256]{2,1,0:T(8,128)(2,1)}, u32[]{:S(2)}, u32[]{:S(2)}) collective-permute-start(bf16[8,48,256]{2,1,0:T(8,128)(2,1)} %get-tuple-element.27.high_ref), channel_id=1, source_target_pairs={{0,1},{1,2},{2,3},{3,4},{4,5},{5,6},{6,7},{8,9},{9,10},{10,11},{11... | collective-permute-start | bytes 589832 | tf_op jit(solution)/shard_map/ppermute | solution.py:590
  24.1 1.3 collective-permute-start.7
  25.4 9.1 %all-to-all-done = bf16[32,8,1664]{2,1,0:T(8,128)(2,1)S(1)} async-done(((bf16[32,8,1664]{2,1,0:T(8,128)(2,1)}), bf16[32,8,1664]{2,1,0:T(8,128)(2,1)S(1)}, u32[]{:S(2)}, u32[]{:S(2)}) %all-to-all-start) | async-done | bytes 852000 | tf_op jit(solution)/shard_map/all_to_all | solution.py:583
  34.6 1.1 copy-done.13
  35.7 2.3 %shard_map.139 = (bf16[8,256,256]{2,1,0:T(8,128)(2,1)S(1)}, bf16[256,256]{1,0:T(8,128)(2,1)S(1)}) custom-call(s32[1]{0:T(128)} %bitcast.1.me_ref, bf16[256,1664]{1,0:T(8,128)(2,1)S(1)} %bitcast.13, bf16[6,256,256]{2,1,0:T(8,128)(2,1)S(1)} %copy-done.13), custom_call_target="tpu_custom_call" | custom-call | flops 1000000000 | bytes 3000000 | tf_op jit(solution)/shard_map/pallas_call | solution.py:689
  38.1 1.4 collective-permute-start.1
  39.5 3.0 %collective-permute-start = (bf16[8,32,256]{2,1,0:T(8,128)(2,1)S(1)}, bf16[8,32,256]{2,1,0:T(8,128)(2,1)S(1)}, u32[]{:S(2)}, u32[]{:S(2)}) collective-permute-start(bf16[8,32,256]{2,1,0:T(8,128)(2,1)S(1)} %get-tuple-element.47), channel_id=1, source_target_pairs={{0,8},{8,16},{16,24},{1,9},{9,17},{17,25},{2,10},{10,18},{18,26},{... | collective-permute-start | bytes 393224 | tf_op jit(solution)/shard_map/ppermute | solution.py:590
  44.4 3.3 %collective-permute-start.2 = (bf16[8,48,256]{2,1,0:T(8,128)(2,1)S(1)}, bf16[8,48,256]{2,1,0:T(8,128)(2,1)S(1)}, u32[]{:S(2)}, u32[]{:S(2)}) collective-permute-start(bf16[8,48,256]{2,1,0:T(8,128)(2,1)S(1)} %get-tuple-element.25.high_ref), channel_id=1, source_target_pairs={{0,1},{1,2},{2,3},{3,4},{4,5},{5,6},{6,7},{8,9},{9,10},{10,11},{11... | collective-permute-start | bytes 589832 | tf_op jit(solution)/shard_map/ppermute | solution.py:590
  47.7 1.6 %collective-permute-start.3 = (bf16[8,48,256]{2,1,0:T(8,128)(2,1)S(1)}, bf16[8,48,256]{2,1,0:T(8,128)(2,1)S(1)}, u32[]{:S(2)}, u32[]{:S(2)}) collective-permute-start(bf16[8,48,256]{2,1,0:T(8,128)(2,1)S(1)} %get-tuple-element.26.low_ref), channel_id=1, source_target_pairs={{1,0},{2,1},{3,2},{4,3},{5,4},{6,5},{7,6},{9,8},{10,9},{11,10},{12... | collective-permute-start | bytes 589832 | tf_op jit(solution)/shard_map/ppermute | solution.py:590
  49.3 8.3 %shard_map.144 = (f32[8,336,256]{2,1,0:T(8,128)S(1)}, bf16[8,256,256]{2,1,0:T(8,128)(2,1)S(1)}) custom-call(bf16[8,256,256]{2,1,0:T(8,128)(2,1)S(1)} %copy-done.2, bf16[8,32,256]{2,1,0:T(8,128)(2,1)S(1)} %copy-done.11, bf16[8,32,256]{2,1,0:T(8,128)(2,1)S(1)} %copy-done.9, bf16[8,48,256]{2,1,0:T(8,128)(2,1)} %collective-permute-done.6.ylo_ref, ...), custom_call_target="tpu_custom_call" | custom-call | flops 6281389568 | bytes 7000000 | tf_op jit(solution)/shard_map/pallas_call | solution.py:701
  57.7 13.7 %shard_map.145 = (bf16[8,336,256]{2,1,0:T(8,128)(2,1)S(1)}, bf16[8,336,256]{2,1,0:T(8,128)(2,1)S(1)}, f32[128,1024]{1,0:T(8,128)S(1)}, f32[128,1024]{1,0:T(8,128)S(1)}) custom-call(s32[1]{0:T(128)} %bitcast.core_ref, bf16[8,256,256]{2,1,0:T(8,128)(2,1)S(1)} %get-tuple-element.24.f_ref.field_ref, bf16[8,32,256]{2,1,0:T(8,128)(2,1)S(1)} %collective-permute-done.xlo_ref, ...), custom_call_target="tpu_custom_call" | custom-call | flops 11113228288 | bytes 9000000 | tf_op jit(solution)/shard_map/pallas_call | solution.py:714
  71.4 2.0 %collective-permute-start.8 = (f32[128,1024]{1,0:T(8,128)S(1)}, f32[128,1024]{1,0:T(8,128)S(1)}, u32[]{:S(2)}, u32[]{:S(2)}) collective-permute-start(f32[128,1024]{1,0:T(8,128)S(1)} %get-tuple-element.32), channel_id=1, source_target_pairs={{0,8},{8,0},{16,24},{24,16},{1,9},{9,1},{17,25},{25,17},{2,10},{10... | collective-permute-start | bytes 1572872 | tf_op jit(solution)/shard_map/ppermute | solution.py:595
  73.4 6.6 %shard_map.146 = (f32[128,1024]{1,0:T(8,128)S(1)}, f32[128,1024]{1,0:T(8,128)S(1)}) custom-call(s32[1]{0:T(128)} %bitcast.core_ref, bf16[8,336,256]{2,1,0:T(8,128)(2,1)S(1)} %get-tuple-element.39.act_ref, bf16[8,256,256]{2,1,0:T(8,128)(2,1)S(1)} %get-tuple-element.34.outer_ref), custom_call_target="tpu_custom_call" | custom-call | flops 4831838208 | bytes 5000000 | tf_op jit(solution)/shard_map/pallas_call | solution.py:719
  80.2 1.9 %collective-permute-done.9.got1_ref = f32[128,1024]{1,0:T(8,128)S(1)} collective-permute-done((f32[128,1024]{1,0:T(8,128)S(1)}, f32[128,1024]{1,0:T(8,128)S(1)}, u32[]{:S(2)}, u32[]{:S(2)}) %collective-permute-start.9) | collective-permute-done | bytes 524320 | tf_op jit(solution)/shard_map/ppermute | solution.py:595
  82.9 6.3 %all-to-all-start.1 = ((bf16[16,8,2048]{2,1,0:T(8,128)(2,1)}), bf16[16,8,2048]{2,1,0:T(8,128)(2,1)S(1)}, u32[]{:S(2)}, u32[]{:S(2)}) async-start(bf16[16,8,2048]{2,1,0:T(8,128)(2,1)} %bitcast.6), calls=%async_computation.1 | async-start | bytes 1048576 | tf_op jit(solution)/shard_map/all_to_all | solution.py:583
  89.3 1.1 copy-done.14
  90.4 1.3 copy-done.23
  91.8 1.2 copy-done.25
  93.0 8.1 %shard_map.148.back_hbm = bf16[256,2560]{1,0:T(8,128)(2,1)} custom-call(bf16[8,336,256]{2,1,0:T(8,128)(2,1)S(1)} %copy-done.23, bf16[27,96,96]{2,1,0:T(8,128)(2,1)S(1)} %copy-done.6, bf16[8,256,256]{2,1,0:T(8,128)(2,1)S(1)} %copy-done.25, bf16[6,256,256]{2,1,0:T(8,128)(2,1)S(1)} %copy-done.14, bf16[256,256]{1,0:T(8,128)(2,1)S(1)} %copy-done.19), custom_call_target="tpu_custom_call" | custom-call | flops 5798205952 | bytes 6000000 | tf_op jit(solution)/shard_map/pallas_call | solution.py:730
  101.1 3.8 %all-to-all-done.1 = bf16[16,8,2048]{2,1,0:T(8,128)(2,1)S(1)} async-done(((bf16[16,8,2048]{2,1,0:T(8,128)(2,1)}), bf16[16,8,2048]{2,1,0:T(8,128)(2,1)S(1)}, u32[]{:S(2)}, u32[]{:S(2)}) %all-to-all-start.1) | async-done | bytes 524320 | tf_op jit(solution)/shard_map/all_to_all | solution.py:583
  104.9 1.2 shard_map.149
  106.1 2.9 %all-to-all-start.2 = ((bf16[32,8,2560]{2,1,0:T(8,128)(2,1)}), bf16[32,8,2560]{2,1,0:T(8,128)(2,1)S(1)}, u32[]{:S(2)}, u32[]{:S(2)}) async-start(bf16[32,8,2560]{2,1,0:T(8,128)(2,1)} %bitcast.8), calls=%async_computation.2 | async-start | bytes 2621440 | tf_op jit(solution)/shard_map/all_to_all | solution.py:583
  110.2 1.3 copy-done.21
  111.6 7.6 %shard_map.150 = bf16[256,1536]{1,0:T(8,128)(2,1)} custom-call(bf16[8,336,256]{2,1,0:T(8,128)(2,1)S(1)} %copy-done.21, f32[560,128]{1,0:T(8,128)S(1)} %shard_map.141.mask_ref, bf16[27,96,96]{2,1,0:T(8,128)(2,1)S(1)} %copy-done.7, bf16[8,256,256]{2,1,0:T(8,128)(2,1)S(1)} %get-tuple-element.24.f_ref.field_ref, bf16[6,256,256]{2,1,0:T(8,128)(2,1)S(1)} %copy-done.15), custom_call_target="tpu_custom_call" | custom-call | flops 5798205952 | bytes 8000000 | tf_op jit(solution)/shard_map/pallas_call | solution.py:742
  119.2 22.8 %all-to-all-done.2 = bf16[32,8,2560]{2,1,0:T(8,128)(2,1)S(1)} async-done(((bf16[32,8,2560]{2,1,0:T(8,128)(2,1)}), bf16[32,8,2560]{2,1,0:T(8,128)(2,1)S(1)}, u32[]{:S(2)}, u32[]{:S(2)}) %all-to-all-start.2) | async-done | bytes 1310752 | tf_op jit(solution)/shard_map/all_to_all | solution.py:583
  142.2 1.2 shard_map.151
  144.1 2.0 %shard_map.152 = (f32[27,96,96]{2,1,0:T(8,128)}, f32[27,96,96]{2,1,0:T(8,128)}) custom-call(s32[1]{0:T(128)} %bitcast.core_ref, bf16[256,1024]{1,0:T(8,128)(2,1)S(1)} %slice.19.mine_ref, bf16[256,1024]{1,0:T(8,128)(2,1)S(1)} %collective-permute-done.10.other_ref), custom_call_target="tpu_custom_call" | custom-call | flops 1000000 | bytes 4000000 | tf_op jit(solution)/shard_map/pallas_call | solution.py:756
  (76 shorter events, 9.3 us)
Async XLA Ops:
  2.3 8.9 %copy-start.5 = (bf16[16,16,1536]{2,1,0:T(8,128)(2,1)S(1)}, bf16[16,16,1536]{2,1,0:T(8,128)(2,1)}, u32[]{:S(2)}) copy-start(bf16[16,16,1536]{2,1,0:T(8,128)(2,1)} %param.13) | copy-start | bytes 2359300
  2.3 8.9 %copy-start.12 = (bf16[6,256,256]{2,1,0:T(8,128)(2,1)S(1)}, bf16[6,256,256]{2,1,0:T(8,128)(2,1)}, u32[]{:S(2)}) copy-start(bf16[6,256,256]{2,1,0:T(8,128)(2,1)} %constant.38.clone.perm_hbm.perm_ref) | copy-start | bytes 2359300
  3.9 30.7 %all-to-all-start = ((bf16[32,8,1664]{2,1,0:T(8,128)(2,1)}), bf16[32,8,1664]{2,1,0:T(8,128)(2,1)S(1)}, u32[]{:S(2)}, u32[]{:S(2)}) async-start(bf16[32,8,1664]{2,1,0:T(8,128)(2,1)} %bitcast.3), calls=%async_computation | async-start | bytes 1703936 | tf_op jit(solution)/shard_map/all_to_all | solution.py:583
  12.4 22.1 %copy-start.1 = (bf16[8,256,256]{2,1,0:T(8,128)(2,1)}, bf16[8,256,256]{2,1,0:T(8,128)(2,1)S(1)}, u32[]{:S(2)}) copy-start(bf16[8,256,256]{2,1,0:T(8,128)(2,1)S(1)} %shard_map.142.f_ref) | copy-start | bytes 3145732
  12.5 4.4 %collective-permute-start.5 = (bf16[8,32,256]{2,1,0:T(8,128)(2,1)S(1)}, bf16[8,32,256]{2,1,0:T(8,128)(2,1)S(1)}, u32[]{:S(2)}, u32[]{:S(2)}) collective-permute-start(bf16[8,32,256]{2,1,0:T(8,128)(2,1)S(1)} %get-tuple-element.44), channel_id=1, source_target_pairs={{8,0},{16,8},{24,16},{9,1},{17,9},{25,17},{10,2},{18,10},{26,18},{... | collective-permute-start | bytes 393224 | tf_op jit(solution)/shard_map/ppermute | solution.py:590
  13.8 4.0 %collective-permute-start.4 = (bf16[8,32,256]{2,1,0:T(8,128)(2,1)S(1)}, bf16[8,32,256]{2,1,0:T(8,128)(2,1)S(1)}, u32[]{:S(2)}, u32[]{:S(2)}) collective-permute-start(bf16[8,32,256]{2,1,0:T(8,128)(2,1)S(1)} %get-tuple-element.45), channel_id=1, source_target_pairs={{0,8},{8,16},{16,24},{1,9},{9,17},{17,25},{2,10},{10,18},{18,26},{... | collective-permute-start | bytes 393224 | tf_op jit(solution)/shard_map/ppermute | solution.py:590
  16.8 17.7 %copy-start.8 = (bf16[8,32,256]{2,1,0:T(8,128)(2,1)}, bf16[8,32,256]{2,1,0:T(8,128)(2,1)S(1)}, u32[]{:S(2)}) copy-start(bf16[8,32,256]{2,1,0:T(8,128)(2,1)S(1)} %collective-permute-done.5.xhi_ref) | copy-start | bytes 393220
  18.7 15.9 %copy-start.10 = (bf16[8,32,256]{2,1,0:T(8,128)(2,1)}, bf16[8,32,256]{2,1,0:T(8,128)(2,1)S(1)}, u32[]{:S(2)}) copy-start(bf16[8,32,256]{2,1,0:T(8,128)(2,1)S(1)} %collective-permute-done.4.xlo_ref) | copy-start | bytes 393220
  19.8 29.5 %collective-permute-start.6 = (bf16[8,48,256]{2,1,0:T(8,128)(2,1)}, bf16[8,48,256]{2,1,0:T(8,128)(2,1)}, u32[]{:S(2)}, u32[]{:S(2)}) collective-permute-start(bf16[8,48,256]{2,1,0:T(8,128)(2,1)} %get-tuple-element.27.high_ref), channel_id=1, source_target_pairs={{0,1},{1,2},{2,3},{3,4},{4,5},{5,6},{6,7},{8,9},{9,10},{10,11},{11... | collective-permute-start | bytes 589832 | tf_op jit(solution)/shard_map/ppermute | solution.py:590
  24.1 25.2 %collective-permute-start.7 = (bf16[8,48,256]{2,1,0:T(8,128)(2,1)S(1)}, bf16[8,48,256]{2,1,0:T(8,128)(2,1)}, u32[]{:S(2)}, u32[]{:S(2)}) collective-permute-start(bf16[8,48,256]{2,1,0:T(8,128)(2,1)S(1)} %get-tuple-element.28.low_ref), channel_id=1, source_target_pairs={{1,0},{2,1},{3,2},{4,3},{5,4},{6,5},{7,6},{9,8},{10,9},{11,10},{12... | collective-permute-start | bytes 589832 | tf_op jit(solution)/shard_map/ppermute | solution.py:590
  35.7 6.9 %copy-start.26 = (s32[560]{0:T(1024)S(1)}, s32[560]{0:T(1024)}, u32[]{:S(2)}) copy-start(s32[560]{0:T(1024)} %constant.43.clone) | copy-start | bytes 6724
  35.7 6.9 %copy-start.27 = (s32[560]{0:T(1024)S(1)}, s32[560]{0:T(1024)}, u32[]{:S(2)}) copy-start(s32[560]{0:T(1024)} %constant.41.clone) | copy-start | bytes 6724
  35.7 6.9 %copy-start.28 = (s32[560]{0:T(1024)S(1)}, s32[560]{0:T(1024)}, u32[]{:S(2)}) copy-start(s32[560]{0:T(1024)} %constant.40.clone) | copy-start | bytes 6724
  35.7 6.9 %copy-start.29 = (pred[560]{0:T(1024)(128)(4,1)S(1)}, pred[560]{0:T(1024)(128)(4,1)}, u32[]{:S(2)}) copy-start(pred[560]{0:T(1024)(128)(4,1)} %constant.42.clone) | copy-start | bytes 1684
  38.1 5.8 %collective-permute-start.1 = (bf16[8,32,256]{2,1,0:T(8,128)(2,1)S(1)}, bf16[8,32,256]{2,1,0:T(8,128)(2,1)S(1)}, u32[]{:S(2)}, u32[]{:S(2)}) collective-permute-start(bf16[8,32,256]{2,1,0:T(8,128)(2,1)S(1)} %get-tuple-element.46), channel_id=1, source_target_pairs={{8,0},{16,8},{24,16},{9,1},{17,9},{25,17},{10,2},{18,10},{26,18},{... | collective-permute-start | bytes 393224 | tf_op jit(solution)/shard_map/ppermute | solution.py:590
  39.5 4.4 %collective-permute-start = (bf16[8,32,256]{2,1,0:T(8,128)(2,1)S(1)}, bf16[8,32,256]{2,1,0:T(8,128)(2,1)S(1)}, u32[]{:S(2)}, u32[]{:S(2)}) collective-permute-start(bf16[8,32,256]{2,1,0:T(8,128)(2,1)S(1)} %get-tuple-element.47), channel_id=1, source_target_pairs={{0,8},{8,16},{16,24},{1,9},{9,17},{17,25},{2,10},{10,18},{18,26},{... | collective-permute-start | bytes 393224 | tf_op jit(solution)/shard_map/ppermute | solution.py:590
  42.8 6.5 %copy-start.2 = (bf16[8,256,256]{2,1,0:T(8,128)(2,1)S(1)}, bf16[8,256,256]{2,1,0:T(8,128)(2,1)}, u32[]{:S(2)}) copy-start(bf16[8,256,256]{2,1,0:T(8,128)(2,1)} %copy-done.1) | copy-start | bytes 3145732
  42.8 6.5 %copy-start.7 = (bf16[27,96,96]{2,1,0:T(8,128)(2,1)S(1)}, bf16[27,96,96]{2,1,0:T(8,128)(2,1)}, u32[]{:S(2)}) copy-start(bf16[27,96,96]{2,1,0:T(8,128)(2,1)} %raw_ref.7) | copy-start | bytes 1492996
  42.8 6.5 %copy-start.9 = (bf16[8,32,256]{2,1,0:T(8,128)(2,1)S(1)}, bf16[8,32,256]{2,1,0:T(8,128)(2,1)}, u32[]{:S(2)}) copy-start(bf16[8,32,256]{2,1,0:T(8,128)(2,1)} %copy-done.8) | copy-start | bytes 393220
  44.4 13.3 %collective-permute-start.2 = (bf16[8,48,256]{2,1,0:T(8,128)(2,1)S(1)}, bf16[8,48,256]{2,1,0:T(8,128)(2,1)S(1)}, u32[]{:S(2)}, u32[]{:S(2)}) collective-permute-start(bf16[8,48,256]{2,1,0:T(8,128)(2,1)S(1)} %get-tuple-element.25.high_ref), channel_id=1, source_target_pairs={{0,1},{1,2},{2,3},{3,4},{4,5},{5,6},{6,7},{8,9},{9,10},{10,11},{11... | collective-permute-start | bytes 589832 | tf_op jit(solution)/shard_map/ppermute | solution.py:590
  47.6 10.1 %copy-start.6 = (bf16[27,96,96]{2,1,0:T(8,128)(2,1)S(1)}, bf16[27,96,96]{2,1,0:T(8,128)(2,1)}, u32[]{:S(2)}) copy-start(bf16[27,96,96]{2,1,0:T(8,128)(2,1)} %raw_ref.6) | copy-start | bytes 1492996
  47.7 10.0 %collective-permute-start.3 = (bf16[8,48,256]{2,1,0:T(8,128)(2,1)S(1)}, bf16[8,48,256]{2,1,0:T(8,128)(2,1)S(1)}, u32[]{:S(2)}, u32[]{:S(2)}) collective-permute-start(bf16[8,48,256]{2,1,0:T(8,128)(2,1)S(1)} %get-tuple-element.26.low_ref), channel_id=1, source_target_pairs={{1,0},{2,1},{3,2},{4,3},{5,4},{6,5},{7,6},{9,8},{10,9},{11,10},{12... | collective-permute-start | bytes 589832 | tf_op jit(solution)/shard_map/ppermute | solution.py:590
  57.7 15.8 %copy-start.24 = (bf16[8,256,256]{2,1,0:T(8,128)(2,1)}, bf16[8,256,256]{2,1,0:T(8,128)(2,1)S(1)}, u32[]{:S(2)}) copy-start(bf16[8,256,256]{2,1,0:T(8,128)(2,1)S(1)} %get-tuple-element.34.outer_ref) | copy-start | bytes 3145732
  71.4 8.7 %copy-start.20 = (bf16[8,336,256]{2,1,0:T(8,128)(2,1)}, bf16[8,336,256]{2,1,0:T(8,128)(2,1)S(1)}, u32[]{:S(2)}) copy-start(bf16[8,336,256]{2,1,0:T(8,128)(2,1)S(1)} %get-tuple-element.39.act_ref) | copy-start | bytes 4128772
  71.4 8.7 %copy-start.22 = (bf16[8,336,256]{2,1,0:T(8,128)(2,1)}, bf16[8,336,256]{2,1,0:T(8,128)(2,1)S(1)}, u32[]{:S(2)}) copy-start(bf16[8,336,256]{2,1,0:T(8,128)(2,1)S(1)} %get-tuple-element.37.hg_ref) | copy-start | bytes 4128772
  71.4 8.8 %collective-permute-start.8 = (f32[128,1024]{1,0:T(8,128)S(1)}, f32[128,1024]{1,0:T(8,128)S(1)}, u32[]{:S(2)}, u32[]{:S(2)}) collective-permute-start(f32[128,1024]{1,0:T(8,128)S(1)} %get-tuple-element.32), channel_id=1, source_target_pairs={{0,8},{8,0},{16,24},{24,16},{1,9},{9,1},{17,25},{25,17},{2,10},{10... | collective-permute-start | bytes 1572872 | tf_op jit(solution)/shard_map/ppermute | solution.py:595
  80.0 2.0 %collective-permute-start.9 = (f32[128,1024]{1,0:T(8,128)S(1)}, f32[128,1024]{1,0:T(8,128)S(1)}, u32[]{:S(2)}, u32[]{:S(2)}) collective-permute-start(f32[128,1024]{1,0:T(8,128)S(1)} %get-tuple-element.36), channel_id=1, source_target_pairs={{0,8},{8,0},{16,24},{24,16},{1,9},{9,1},{17,25},{25,17},{2,10},{10... | collective-permute-start | bytes 1572872 | tf_op jit(solution)/shard_map/ppermute | solution.py:595
  82.0 7.2 %copy-start.19 = (bf16[256,256]{1,0:T(8,128)(2,1)S(1)}, bf16[256,256]{1,0:T(8,128)(2,1)}, u32[]{:S(2)}) copy-start(bf16[256,256]{1,0:T(8,128)(2,1)} %copy-done.18) | copy-start | bytes 393220
  82.9 22.0 %all-to-all-start.1 = ((bf16[16,8,2048]{2,1,0:T(8,128)(2,1)}), bf16[16,8,2048]{2,1,0:T(8,128)(2,1)S(1)}, u32[]{:S(2)}, u32[]{:S(2)}) async-start(bf16[16,8,2048]{2,1,0:T(8,128)(2,1)} %bitcast.6), calls=%async_computation.1 | async-start | bytes 1048576 | tf_op jit(solution)/shard_map/all_to_all | solution.py:583
  106.1 35.9 %all-to-all-start.2 = ((bf16[32,8,2560]{2,1,0:T(8,128)(2,1)}), bf16[32,8,2560]{2,1,0:T(8,128)(2,1)S(1)}, u32[]{:S(2)}, u32[]{:S(2)}) async-start(bf16[32,8,2560]{2,1,0:T(8,128)(2,1)} %bitcast.8), calls=%async_computation.2 | async-start | bytes 2621440 | tf_op jit(solution)/shard_map/all_to_all | solution.py:583
  111.6 30.6 %copy-start.4 = (s32[128]{0:T(128)S(1)}, s32[128]{0:T(128)}, u32[]{:S(2)}) copy-start(s32[128]{0:T(128)} %param.12) | copy-start | bytes 1540
  142.1 2.0 %collective-permute-start.10 = (bf16[256,1024]{1,0:T(8,128)(2,1)S(1)}, bf16[256,1024]{1,0:T(8,128)(2,1)S(1)}, u32[]{:S(2)}, u32[]{:S(2)}) collective-permute-start(bf16[256,1024]{1,0:T(8,128)(2,1)S(1)} %slice.19.mine_ref), channel_id=1, source_target_pairs={{0,8},{8,0},{16,24},{24,16},{1,9},{9,1},{17,25},{25,17},{2,10},{10... | collective-permute-start | bytes 1572872 | tf_op jit(solution)/shard_map/ppermute | solution.py:595
  (12 other events, 26.9 us)

commit v11 on v10

--- a/solution.py
+++ b/solution.py
@@ -443,10 +443,15 @@
             hidden = m * total[i * OUT_ROWS : (i + 1) * OUT_ROWS]
             sigma = jax.nn.sigmoid(hidden)
             act_ref[k + i] = (hidden * sigma).astype(BF)
-            hg_ref[k + i] = (m * grad_ref[k + i] * sigma * (1.0 + hidden * (1.0 - sigma))).astype(BF)
+            hg = (m * grad_ref[k + i] * sigma * (1.0 + hidden * (1.0 - sigma))).astype(BF)
+            hg_ref[k + i] = hg
+            inner = NX * NY
+            value = hg[NY : NY + inner].T
+            for j in range(2):
+                z = 2 * (k + i) + j
+                gt_ref[:, z * inner : (z + 1) * inner] = value[j * LANES : j * LANES + channels]
 
     each_step(f_ref.shape[0], fill, lambda k: conv_wide(ext_ref, edge_ref, w_ref, k), finish)
-    turn(gt_ref, hg_ref, NY, channels)
     correlate(gt_ref, ext_ref, 1, taps_ref)
     hand_out(channels, run, core_ref, taps_ref, packed_ref, keep_ref, give_ref)
 

time: 147 us -> 147 us (level)
  no operation moved by 1% of the time
where the time goes in v11:
time: 147 us; the launch traced here: 146 us
  Pallas kernels  57.5 us (39%)
  waiting for transfers between devices  39.3 us (27%)
  starting transfers between devices  38.1 us (26%)
  local copies, waits for them, and re-layouts  10.1 us (7%)
    all_to_all x3, waiting for transfers between devices, share(): return lax.all_to_all(parts, axes, split_axis=0, concat_axis=0, tiled=True)  35.8 us
    ppermute x8, starting transfers between devices, neighbours(): return (lax.ppermute(upper, axes, ahead), lax.ppermute(lower, axes, behind))  19.3 us
    all_to_all x3, starting transfers between devices, share(): return lax.all_to_all(parts, axes, split_axis=0, concat_axis=0, tiled=True)  16.6 us
    pallas_call x1, Pallas kernels, on_device(): call(functools.partial(hidden_kernel, channels, run), (wide_shape, wide_s...  13.8 us
    unnamed x60, local copies, waits for them, and re-layouts  9.92 us
    pallas_call x1, Pallas kernels, on_device(): call(outer_kernel, (shape((pairs, OUT_ROWS, PAIR), F32), field_shape), 1....  8.33 us
    pallas_call x1, Pallas kernels, on_device(): call(grid_grad_kernel, shape((buffers, back_width), BF), 1.2 * conv_flops...  8.11 us
    pallas_call x1, Pallas kernels, on_device(): call(block_kernel, shape((slots, row_width), BF), 1.2 * conv_flops, 80000...  7.63 us
  transfers between devices with their start and end apart: 14, of which 6 were waited for; matrix products, arithmetic and copies ran while one was open for 0% of the time, Pallas kernels for 26%

profile of v11, /device:TPU:0, one launch (start us, length us, event | category | flops | bytes accessed | tf_op | source)
XLA Modules:
  0.0 146.2 jit_solution(13832675228797229643)
XLA Ops:
  2.3 1.6 %shard_map.138 = bf16[256,1664]{1,0:T(8,128)(2,1)} custom-call(s32[1,128]{1,0:T(1,128)S(1)} %bitcast.16, bf16[128,1536]{1,0:T(8,128)(2,1)S(1)} %copy-done), custom_call_target="tpu_custom_call" | custom-call | flops 100663296 | bytes 1179648 | tf_op jit(solution)/shard_map/pallas_call | solution.py:673
  3.9 7.3 %all-to-all-start = ((bf16[32,8,1664]{2,1,0:T(8,128)(2,1)}), bf16[32,8,1664]{2,1,0:T(8,128)(2,1)S(1)}, u32[]{:S(2)}, u32[]{:S(2)}) async-start(bf16[32,8,1664]{2,1,0:T(8,128)(2,1)} %bitcast.3), calls=%async_computation | async-start | bytes 1703936 | tf_op jit(solution)/shard_map/all_to_all | solution.py:588
  11.2 1.2 shard_map.142.f_ref
  12.5 1.3 collective-permute-start.5
  13.8 3.0 %collective-permute-start.4 = (bf16[8,32,256]{2,1,0:T(8,128)(2,1)S(1)}, bf16[8,32,256]{2,1,0:T(8,128)(2,1)S(1)}, u32[]{:S(2)}, u32[]{:S(2)}) collective-permute-start(bf16[8,32,256]{2,1,0:T(8,128)(2,1)S(1)} %get-tuple-element.45), channel_id=1, source_target_pairs={{0,8},{8,16},{16,24},{1,9},{9,17},{17,25},{2,10},{10,18},{18,26},{... | collective-permute-start | bytes 393224 | tf_op jit(solution)/shard_map/ppermute | solution.py:595
  19.8 4.3 %collective-permute-start.6 = (bf16[8,48,256]{2,1,0:T(8,128)(2,1)}, bf16[8,48,256]{2,1,0:T(8,128)(2,1)}, u32[]{:S(2)}, u32[]{:S(2)}) collective-permute-start(bf16[8,48,256]{2,1,0:T(8,128)(2,1)} %get-tuple-element.27.high_ref), channel_id=1, source_target_pairs={{0,1},{1,2},{2,3},{3,4},{4,5},{5,6},{6,7},{8,9},{9,10},{10,11},{11... | collective-permute-start | bytes 589832 | tf_op jit(solution)/shard_map/ppermute | solution.py:595
  24.1 1.3 collective-permute-start.7
  25.4 9.1 %all-to-all-done = bf16[32,8,1664]{2,1,0:T(8,128)(2,1)S(1)} async-done(((bf16[32,8,1664]{2,1,0:T(8,128)(2,1)}), bf16[32,8,1664]{2,1,0:T(8,128)(2,1)S(1)}, u32[]{:S(2)}, u32[]{:S(2)}) %all-to-all-start) | async-done | bytes 852000 | tf_op jit(solution)/shard_map/all_to_all | solution.py:588
  34.6 1.1 copy-done.13
  35.7 2.3 %shard_map.139 = (bf16[8,256,256]{2,1,0:T(8,128)(2,1)S(1)}, bf16[256,256]{1,0:T(8,128)(2,1)S(1)}) custom-call(s32[1]{0:T(128)} %bitcast.1.me_ref, bf16[256,1664]{1,0:T(8,128)(2,1)S(1)} %bitcast.13, bf16[6,256,256]{2,1,0:T(8,128)(2,1)S(1)} %copy-done.13), custom_call_target="tpu_custom_call" | custom-call | flops 1000000000 | bytes 3000000 | tf_op jit(solution)/shard_map/pallas_call | solution.py:694
  38.1 1.4 collective-permute-start.1
  39.5 3.0 %collective-permute-start = (bf16[8,32,256]{2,1,0:T(8,128)(2,1)S(1)}, bf16[8,32,256]{2,1,0:T(8,128)(2,1)S(1)}, u32[]{:S(2)}, u32[]{:S(2)}) collective-permute-start(bf16[8,32,256]{2,1,0:T(8,128)(2,1)S(1)} %get-tuple-element.47), channel_id=1, source_target_pairs={{0,8},{8,16},{16,24},{1,9},{9,17},{17,25},{2,10},{10,18},{18,26},{... | collective-permute-start | bytes 393224 | tf_op jit(solution)/shard_map/ppermute | solution.py:595
  44.4 3.3 %collective-permute-start.2 = (bf16[8,48,256]{2,1,0:T(8,128)(2,1)S(1)}, bf16[8,48,256]{2,1,0:T(8,128)(2,1)S(1)}, u32[]{:S(2)}, u32[]{:S(2)}) collective-permute-start(bf16[8,48,256]{2,1,0:T(8,128)(2,1)S(1)} %get-tuple-element.25.high_ref), channel_id=1, source_target_pairs={{0,1},{1,2},{2,3},{3,4},{4,5},{5,6},{6,7},{8,9},{9,10},{10,11},{11... | collective-permute-start | bytes 589832 | tf_op jit(solution)/shard_map/ppermute | solution.py:595
  47.7 1.6 %collective-permute-start.3 = (bf16[8,48,256]{2,1,0:T(8,128)(2,1)S(1)}, bf16[8,48,256]{2,1,0:T(8,128)(2,1)S(1)}, u32[]{:S(2)}, u32[]{:S(2)}) collective-permute-start(bf16[8,48,256]{2,1,0:T(8,128)(2,1)S(1)} %get-tuple-element.26.low_ref), channel_id=1, source_target_pairs={{1,0},{2,1},{3,2},{4,3},{5,4},{6,5},{7,6},{9,8},{10,9},{11,10},{12... | collective-permute-start | bytes 589832 | tf_op jit(solution)/shard_map/ppermute | solution.py:595
  49.3 8.3 %shard_map.144 = (f32[8,336,256]{2,1,0:T(8,128)S(1)}, bf16[8,256,256]{2,1,0:T(8,128)(2,1)S(1)}) custom-call(bf16[8,256,256]{2,1,0:T(8,128)(2,1)S(1)} %copy-done.2, bf16[8,32,256]{2,1,0:T(8,128)(2,1)S(1)} %copy-done.11, bf16[8,32,256]{2,1,0:T(8,128)(2,1)S(1)} %copy-done.9, bf16[8,48,256]{2,1,0:T(8,128)(2,1)} %collective-permute-done.6.ylo_ref, ...), custom_call_target="tpu_custom_call" | custom-call | flops 6281389568 | bytes 7000000 | tf_op jit(solution)/shard_map/pallas_call | solution.py:706
  57.7 13.8 %shard_map.145 = (bf16[8,336,256]{2,1,0:T(8,128)(2,1)S(1)}, bf16[8,336,256]{2,1,0:T(8,128)(2,1)S(1)}, f32[128,1024]{1,0:T(8,128)S(1)}, f32[128,1024]{1,0:T(8,128)S(1)}) custom-call(s32[1]{0:T(128)} %bitcast.core_ref, bf16[8,256,256]{2,1,0:T(8,128)(2,1)S(1)} %get-tuple-element.24.f_ref.field_ref, bf16[8,32,256]{2,1,0:T(8,128)(2,1)S(1)} %collective-permute-done.xlo_ref, ...), custom_call_target="tpu_custom_call" | custom-call | flops 11113228288 | bytes 9000000 | tf_op jit(solution)/shard_map/pallas_call | solution.py:719
  71.5 2.1 %collective-permute-start.8 = (f32[128,1024]{1,0:T(8,128)S(1)}, f32[128,1024]{1,0:T(8,128)S(1)}, u32[]{:S(2)}, u32[]{:S(2)}) collective-permute-start(f32[128,1024]{1,0:T(8,128)S(1)} %get-tuple-element.32), channel_id=1, source_target_pairs={{0,8},{8,0},{16,24},{24,16},{1,9},{9,1},{17,25},{25,17},{2,10},{10... | collective-permute-start | bytes 1572872 | tf_op jit(solution)/shard_map/ppermute | solution.py:600
  73.6 6.6 %shard_map.146 = (f32[128,1024]{1,0:T(8,128)S(1)}, f32[128,1024]{1,0:T(8,128)S(1)}) custom-call(s32[1]{0:T(128)} %bitcast.core_ref, bf16[8,336,256]{2,1,0:T(8,128)(2,1)S(1)} %get-tuple-element.39.act_ref, bf16[8,256,256]{2,1,0:T(8,128)(2,1)S(1)} %get-tuple-element.34.outer_ref), custom_call_target="tpu_custom_call" | custom-call | flops 4831838208 | bytes 5000000 | tf_op jit(solution)/shard_map/pallas_call | solution.py:724
  80.3 1.9 %collective-permute-done.9.got1_ref = f32[128,1024]{1,0:T(8,128)S(1)} collective-permute-done((f32[128,1024]{1,0:T(8,128)S(1)}, f32[128,1024]{1,0:T(8,128)S(1)}, u32[]{:S(2)}, u32[]{:S(2)}) %collective-permute-start.9) | collective-permute-done | bytes 524320 | tf_op jit(solution)/shard_map/ppermute | solution.py:600
  83.0 6.4 %all-to-all-start.1 = ((bf16[16,8,2048]{2,1,0:T(8,128)(2,1)}), bf16[16,8,2048]{2,1,0:T(8,128)(2,1)S(1)}, u32[]{:S(2)}, u32[]{:S(2)}) async-start(bf16[16,8,2048]{2,1,0:T(8,128)(2,1)} %bitcast.6), calls=%async_computation.1 | async-start | bytes 1048576 | tf_op jit(solution)/shard_map/all_to_all | solution.py:588
  89.4 1.1 copy-done.14
  90.6 1.3 copy-done.23
  91.9 1.2 copy-done.25
  93.1 8.1 %shard_map.148.back_hbm = bf16[256,2560]{1,0:T(8,128)(2,1)} custom-call(bf16[8,336,256]{2,1,0:T(8,128)(2,1)S(1)} %copy-done.23, bf16[27,96,96]{2,1,0:T(8,128)(2,1)S(1)} %copy-done.6, bf16[8,256,256]{2,1,0:T(8,128)(2,1)S(1)} %copy-done.25, bf16[6,256,256]{2,1,0:T(8,128)(2,1)S(1)} %copy-done.14, bf16[256,256]{1,0:T(8,128)(2,1)S(1)} %copy-done.19), custom_call_target="tpu_custom_call" | custom-call | flops 5798205952 | bytes 6000000 | tf_op jit(solution)/shard_map/pallas_call | solution.py:735
  101.2 3.8 %all-to-all-done.1 = bf16[16,8,2048]{2,1,0:T(8,128)(2,1)S(1)} async-done(((bf16[16,8,2048]{2,1,0:T(8,128)(2,1)}), bf16[16,8,2048]{2,1,0:T(8,128)(2,1)S(1)}, u32[]{:S(2)}, u32[]{:S(2)}) %all-to-all-start.1) | async-done | bytes 524320 | tf_op jit(solution)/shard_map/all_to_all | solution.py:588
  105.1 1.2 shard_map.149
  106.3 2.9 %all-to-all-start.2 = ((bf16[32,8,2560]{2,1,0:T(8,128)(2,1)}), bf16[32,8,2560]{2,1,0:T(8,128)(2,1)S(1)}, u32[]{:S(2)}, u32[]{:S(2)}) async-start(bf16[32,8,2560]{2,1,0:T(8,128)(2,1)} %bitcast.8), calls=%async_computation.2 | async-start | bytes 2621440 | tf_op jit(solution)/shard_map/all_to_all | solution.py:588
  110.4 1.3 copy-done.21
  111.7 7.6 %shard_map.150 = bf16[256,1536]{1,0:T(8,128)(2,1)} custom-call(bf16[8,336,256]{2,1,0:T(8,128)(2,1)S(1)} %copy-done.21, f32[560,128]{1,0:T(8,128)S(1)} %shard_map.141.mask_ref, bf16[27,96,96]{2,1,0:T(8,128)(2,1)S(1)} %copy-done.7, bf16[8,256,256]{2,1,0:T(8,128)(2,1)S(1)} %get-tuple-element.24.f_ref.field_ref, bf16[6,256,256]{2,1,0:T(8,128)(2,1)S(1)} %copy-done.15), custom_call_target="tpu_custom_call" | custom-call | flops 5798205952 | bytes 8000000 | tf_op jit(solution)/shard_map/pallas_call | solution.py:747
  119.3 22.8 %all-to-all-done.2 = bf16[32,8,2560]{2,1,0:T(8,128)(2,1)S(1)} async-done(((bf16[32,8,2560]{2,1,0:T(8,128)(2,1)}), bf16[32,8,2560]{2,1,0:T(8,128)(2,1)S(1)}, u32[]{:S(2)}, u32[]{:S(2)}) %all-to-all-start.2) | async-done | bytes 1310752 | tf_op jit(solution)/shard_map/all_to_all | solution.py:588
  142.3 1.2 shard_map.151
  144.2 2.0 %shard_map.152 = (f32[27,96,96]{2,1,0:T(8,128)}, f32[27,96,96]{2,1,0:T(8,128)}) custom-call(s32[1]{0:T(128)} %bitcast.core_ref, bf16[256,1024]{1,0:T(8,128)(2,1)S(1)} %slice.19.mine_ref, bf16[256,1024]{1,0:T(8,128)(2,1)S(1)} %collective-permute-done.10.other_ref), custom_call_target="tpu_custom_call" | custom-call | flops 1000000 | bytes 4000000 | tf_op jit(solution)/shard_map/pallas_call | solution.py:761
  (76 shorter events, 9.3 us)
Async XLA Ops:
  2.3 8.9 %copy-start.5 = (bf16[16,16,1536]{2,1,0:T(8,128)(2,1)S(1)}, bf16[16,16,1536]{2,1,0:T(8,128)(2,1)}, u32[]{:S(2)}) copy-start(bf16[16,16,1536]{2,1,0:T(8,128)(2,1)} %param.13) | copy-start | bytes 2359300
  2.3 8.9 %copy-start.12 = (bf16[6,256,256]{2,1,0:T(8,128)(2,1)S(1)}, bf16[6,256,256]{2,1,0:T(8,128)(2,1)}, u32[]{:S(2)}) copy-start(bf16[6,256,256]{2,1,0:T(8,128)(2,1)} %constant.38.clone.perm_hbm.perm_ref) | copy-start | bytes 2359300
  3.9 30.7 %all-to-all-start = ((bf16[32,8,1664]{2,1,0:T(8,128)(2,1)}), bf16[32,8,1664]{2,1,0:T(8,128)(2,1)S(1)}, u32[]{:S(2)}, u32[]{:S(2)}) async-start(bf16[32,8,1664]{2,1,0:T(8,128)(2,1)} %bitcast.3), calls=%async_computation | async-start | bytes 1703936 | tf_op jit(solution)/shard_map/all_to_all | solution.py:588
  12.4 22.1 %copy-start.1 = (bf16[8,256,256]{2,1,0:T(8,128)(2,1)}, bf16[8,256,256]{2,1,0:T(8,128)(2,1)S(1)}, u32[]{:S(2)}) copy-start(bf16[8,256,256]{2,1,0:T(8,128)(2,1)S(1)} %shard_map.142.f_ref) | copy-start | bytes 3145732
  12.5 4.4 %collective-permute-start.5 = (bf16[8,32,256]{2,1,0:T(8,128)(2,1)S(1)}, bf16[8,32,256]{2,1,0:T(8,128)(2,1)S(1)}, u32[]{:S(2)}, u32[]{:S(2)}) collective-permute-start(bf16[8,32,256]{2,1,0:T(8,128)(2,1)S(1)} %get-tuple-element.44), channel_id=1, source_target_pairs={{8,0},{16,8},{24,16},{9,1},{17,9},{25,17},{10,2},{18,10},{26,18},{... | collective-permute-start | bytes 393224 | tf_op jit(solution)/shard_map/ppermute | solution.py:595
  13.8 4.0 %collective-permute-start.4 = (bf16[8,32,256]{2,1,0:T(8,128)(2,1)S(1)}, bf16[8,32,256]{2,1,0:T(8,128)(2,1)S(1)}, u32[]{:S(2)}, u32[]{:S(2)}) collective-permute-start(bf16[8,32,256]{2,1,0:T(8,128)(2,1)S(1)} %get-tuple-element.45), channel_id=1, source_target_pairs={{0,8},{8,16},{16,24},{1,9},{9,17},{17,25},{2,10},{10,18},{18,26},{... | collective-permute-start | bytes 393224 | tf_op jit(solution)/shard_map/ppermute | solution.py:595
  16.8 17.7 %copy-start.8 = (bf16[8,32,256]{2,1,0:T(8,128)(2,1)}, bf16[8,32,256]{2,1,0:T(8,128)(2,1)S(1)}, u32[]{:S(2)}) copy-start(bf16[8,32,256]{2,1,0:T(8,128)(2,1)S(1)} %collective-permute-done.5.xhi_ref) | copy-start | bytes 393220
  18.7 15.9 %copy-start.10 = (bf16[8,32,256]{2,1,0:T(8,128)(2,1)}, bf16[8,32,256]{2,1,0:T(8,128)(2,1)S(1)}, u32[]{:S(2)}) copy-start(bf16[8,32,256]{2,1,0:T(8,128)(2,1)S(1)} %collective-permute-done.4.xlo_ref) | copy-start | bytes 393220
  19.8 29.5 %collective-permute-start.6 = (bf16[8,48,256]{2,1,0:T(8,128)(2,1)}, bf16[8,48,256]{2,1,0:T(8,128)(2,1)}, u32[]{:S(2)}, u32[]{:S(2)}) collective-permute-start(bf16[8,48,256]{2,1,0:T(8,128)(2,1)} %get-tuple-element.27.high_ref), channel_id=1, source_target_pairs={{0,1},{1,2},{2,3},{3,4},{4,5},{5,6},{6,7},{8,9},{9,10},{10,11},{11... | collective-permute-start | bytes 589832 | tf_op jit(solution)/shard_map/ppermute | solution.py:595
  24.1 25.2 %collective-permute-start.7 = (bf16[8,48,256]{2,1,0:T(8,128)(2,1)S(1)}, bf16[8,48,256]{2,1,0:T(8,128)(2,1)}, u32[]{:S(2)}, u32[]{:S(2)}) collective-permute-start(bf16[8,48,256]{2,1,0:T(8,128)(2,1)S(1)} %get-tuple-element.28.low_ref), channel_id=1, source_target_pairs={{1,0},{2,1},{3,2},{4,3},{5,4},{6,5},{7,6},{9,8},{10,9},{11,10},{12... | collective-permute-start | bytes 589832 | tf_op jit(solution)/shard_map/ppermute | solution.py:595
  35.7 6.9 %copy-start.26 = (s32[560]{0:T(1024)S(1)}, s32[560]{0:T(1024)}, u32[]{:S(2)}) copy-start(s32[560]{0:T(1024)} %constant.43.clone) | copy-start | bytes 6724
  35.7 6.9 %copy-start.27 = (s32[560]{0:T(1024)S(1)}, s32[560]{0:T(1024)}, u32[]{:S(2)}) copy-start(s32[560]{0:T(1024)} %constant.41.clone) | copy-start | bytes 6724
  35.7 6.9 %copy-start.28 = (s32[560]{0:T(1024)S(1)}, s32[560]{0:T(1024)}, u32[]{:S(2)}) copy-start(s32[560]{0:T(1024)} %constant.40.clone) | copy-start | bytes 6724
  35.7 6.9 %copy-start.29 = (pred[560]{0:T(1024)(128)(4,1)S(1)}, pred[560]{0:T(1024)(128)(4,1)}, u32[]{:S(2)}) copy-start(pred[560]{0:T(1024)(128)(4,1)} %constant.42.clone) | copy-start | bytes 1684
  38.1 5.8 %collective-permute-start.1 = (bf16[8,32,256]{2,1,0:T(8,128)(2,1)S(1)}, bf16[8,32,256]{2,1,0:T(8,128)(2,1)S(1)}, u32[]{:S(2)}, u32[]{:S(2)}) collective-permute-start(bf16[8,32,256]{2,1,0:T(8,128)(2,1)S(1)} %get-tuple-element.46), channel_id=1, source_target_pairs={{8,0},{16,8},{24,16},{9,1},{17,9},{25,17},{10,2},{18,10},{26,18},{... | collective-permute-start | bytes 393224 | tf_op jit(solution)/shard_map/ppermute | solution.py:595
  39.5 4.4 %collective-permute-start = (bf16[8,32,256]{2,1,0:T(8,128)(2,1)S(1)}, bf16[8,32,256]{2,1,0:T(8,128)(2,1)S(1)}, u32[]{:S(2)}, u32[]{:S(2)}) collective-permute-start(bf16[8,32,256]{2,1,0:T(8,128)(2,1)S(1)} %get-tuple-element.47), channel_id=1, source_target_pairs={{0,8},{8,16},{16,24},{1,9},{9,17},{17,25},{2,10},{10,18},{18,26},{... | collective-permute-start | bytes 393224 | tf_op jit(solution)/shard_map/ppermute | solution.py:595
  42.8 6.5 %copy-start.2 = (bf16[8,256,256]{2,1,0:T(8,128)(2,1)S(1)}, bf16[8,256,256]{2,1,0:T(8,128)(2,1)}, u32[]{:S(2)}) copy-start(bf16[8,256,256]{2,1,0:T(8,128)(2,1)} %copy-done.1) | copy-start | bytes 3145732
  42.8 6.5 %copy-start.7 = (bf16[27,96,96]{2,1,0:T(8,128)(2,1)S(1)}, bf16[27,96,96]{2,1,0:T(8,128)(2,1)}, u32[]{:S(2)}) copy-start(bf16[27,96,96]{2,1,0:T(8,128)(2,1)} %raw_ref.7) | copy-start | bytes 1492996
  42.8 6.5 %copy-start.9 = (bf16[8,32,256]{2,1,0:T(8,128)(2,1)S(1)}, bf16[8,32,256]{2,1,0:T(8,128)(2,1)}, u32[]{:S(2)}) copy-start(bf16[8,32,256]{2,1,0:T(8,128)(2,1)} %copy-done.8) | copy-start | bytes 393220
  44.4 13.3 %collective-permute-start.2 = (bf16[8,48,256]{2,1,0:T(8,128)(2,1)S(1)}, bf16[8,48,256]{2,1,0:T(8,128)(2,1)S(1)}, u32[]{:S(2)}, u32[]{:S(2)}) collective-permute-start(bf16[8,48,256]{2,1,0:T(8,128)(2,1)S(1)} %get-tuple-element.25.high_ref), channel_id=1, source_target_pairs={{0,1},{1,2},{2,3},{3,4},{4,5},{5,6},{6,7},{8,9},{9,10},{10,11},{11... | collective-permute-start | bytes 589832 | tf_op jit(solution)/shard_map/ppermute | solution.py:595
  47.6 10.1 %copy-start.6 = (bf16[27,96,96]{2,1,0:T(8,128)(2,1)S(1)}, bf16[27,96,96]{2,1,0:T(8,128)(2,1)}, u32[]{:S(2)}) copy-start(bf16[27,96,96]{2,1,0:T(8,128)(2,1)} %raw_ref.6) | copy-start | bytes 1492996
  47.7 10.0 %collective-permute-start.3 = (bf16[8,48,256]{2,1,0:T(8,128)(2,1)S(1)}, bf16[8,48,256]{2,1,0:T(8,128)(2,1)S(1)}, u32[]{:S(2)}, u32[]{:S(2)}) collective-permute-start(bf16[8,48,256]{2,1,0:T(8,128)(2,1)S(1)} %get-tuple-element.26.low_ref), channel_id=1, source_target_pairs={{1,0},{2,1},{3,2},{4,3},{5,4},{6,5},{7,6},{9,8},{10,9},{11,10},{12... | collective-permute-start | bytes 589832 | tf_op jit(solution)/shard_map/ppermute | solution.py:595
  57.7 15.9 %copy-start.24 = (bf16[8,256,256]{2,1,0:T(8,128)(2,1)}, bf16[8,256,256]{2,1,0:T(8,128)(2,1)S(1)}, u32[]{:S(2)}) copy-start(bf16[8,256,256]{2,1,0:T(8,128)(2,1)S(1)} %get-tuple-element.34.outer_ref) | copy-start | bytes 3145732
  71.5 8.7 %copy-start.20 = (bf16[8,336,256]{2,1,0:T(8,128)(2,1)}, bf16[8,336,256]{2,1,0:T(8,128)(2,1)S(1)}, u32[]{:S(2)}) copy-start(bf16[8,336,256]{2,1,0:T(8,128)(2,1)S(1)} %get-tuple-element.39.act_ref) | copy-start | bytes 4128772
  71.5 8.7 %copy-start.22 = (bf16[8,336,256]{2,1,0:T(8,128)(2,1)}, bf16[8,336,256]{2,1,0:T(8,128)(2,1)S(1)}, u32[]{:S(2)}) copy-start(bf16[8,336,256]{2,1,0:T(8,128)(2,1)S(1)} %get-tuple-element.37.hg_ref) | copy-start | bytes 4128772
  71.5 8.8 %collective-permute-start.8 = (f32[128,1024]{1,0:T(8,128)S(1)}, f32[128,1024]{1,0:T(8,128)S(1)}, u32[]{:S(2)}, u32[]{:S(2)}) collective-permute-start(f32[128,1024]{1,0:T(8,128)S(1)} %get-tuple-element.32), channel_id=1, source_target_pairs={{0,8},{8,0},{16,24},{24,16},{1,9},{9,1},{17,25},{25,17},{2,10},{10... | collective-permute-start | bytes 1572872 | tf_op jit(solution)/shard_map/ppermute | solution.py:600
  80.2 2.0 %collective-permute-start.9 = (f32[128,1024]{1,0:T(8,128)S(1)}, f32[128,1024]{1,0:T(8,128)S(1)}, u32[]{:S(2)}, u32[]{:S(2)}) collective-permute-start(f32[128,1024]{1,0:T(8,128)S(1)} %get-tuple-element.36), channel_id=1, source_target_pairs={{0,8},{8,0},{16,24},{24,16},{1,9},{9,1},{17,25},{25,17},{2,10},{10... | collective-permute-start | bytes 1572872 | tf_op jit(solution)/shard_map/ppermute | solution.py:600
  82.2 7.3 %copy-start.19 = (bf16[256,256]{1,0:T(8,128)(2,1)S(1)}, bf16[256,256]{1,0:T(8,128)(2,1)}, u32[]{:S(2)}) copy-start(bf16[256,256]{1,0:T(8,128)(2,1)} %copy-done.18) | copy-start | bytes 393220
  83.0 22.0 %all-to-all-start.1 = ((bf16[16,8,2048]{2,1,0:T(8,128)(2,1)}), bf16[16,8,2048]{2,1,0:T(8,128)(2,1)S(1)}, u32[]{:S(2)}, u32[]{:S(2)}) async-start(bf16[16,8,2048]{2,1,0:T(8,128)(2,1)} %bitcast.6), calls=%async_computation.1 | async-start | bytes 1048576 | tf_op jit(solution)/shard_map/all_to_all | solution.py:588
  106.3 35.9 %all-to-all-start.2 = ((bf16[32,8,2560]{2,1,0:T(8,128)(2,1)}), bf16[32,8,2560]{2,1,0:T(8,128)(2,1)S(1)}, u32[]{:S(2)}, u32[]{:S(2)}) async-start(bf16[32,8,2560]{2,1,0:T(8,128)(2,1)} %bitcast.8), calls=%async_computation.2 | async-start | bytes 2621440 | tf_op jit(solution)/shard_map/all_to_all | solution.py:588
  111.7 30.6 %copy-start.4 = (s32[128]{0:T(128)S(1)}, s32[128]{0:T(128)}, u32[]{:S(2)}) copy-start(s32[128]{0:T(128)} %param.12) | copy-start | bytes 1540
  142.2 2.0 %collective-permute-start.10 = (bf16[256,1024]{1,0:T(8,128)(2,1)S(1)}, bf16[256,1024]{1,0:T(8,128)(2,1)S(1)}, u32[]{:S(2)}, u32[]{:S(2)}) collective-permute-start(bf16[256,1024]{1,0:T(8,128)(2,1)S(1)} %slice.19.mine_ref), channel_id=1, source_target_pairs={{0,8},{8,0},{16,24},{24,16},{1,9},{9,1},{17,25},{25,17},{2,10},{10... | collective-permute-start | bytes 1572872 | tf_op jit(solution)/shard_map/ppermute | solution.py:600
  (12 other events, 26.9 us)
